TPU v7x, 32 devices: a whole 2x2x4 slice. The times are simulated.
32 devices in a mesh: wide: 8 (over y, x, core), narrow: 4 (over z).
Axes of the slice: x: 2, y: 2, z: 4, core: 2. Of those that a mesh axis runs over, the one named last changes fastest.
Arguments:
- tokens: bfloat16 [16, 1024, 768], P('wide', 'narrow'), may hold values from -6 to 6
- positions: int32 [16, 1024], P('wide', 'narrow'), may hold values from 0 to 107, as said below
- segments: int32 [16, 1024], P('wide'), may hold values from 0 to 47, as said below
- position_table: bfloat16 [768, 108], P(('wide', 'narrow')), may hold values from -3 to 3
- input_weight: bfloat16 [768, 2304], P(('wide', 'narrow')), may hold values from -0.21875 to 0.21875
- query_bias: bfloat16 [768], P(('wide', 'narrow')), may hold values from -1.796875 to 1.796875
- value_bias: bfloat16 [768], P(('wide', 'narrow')), may hold values from -3 to 3
- output_weight: bfloat16 [768, 768], P(('wide', 'narrow')), may hold values from -1.75 to 1.75
- output_bias: bfloat16 [768], P(('wide', 'narrow')), may hold values from -1.796875 to 1.796875
- first_gain: bfloat16 [768], P(('wide', 'narrow')), may hold values from 0.5 to 1.5
- first_shift: bfloat16 [768], P(('wide', 'narrow')), may hold values from -1.796875 to 1.796875
- up_weight: bfloat16 [768, 3072], P(('wide', 'narrow')), may hold values from -0.21875 to 0.21875
- up_bias: bfloat16 [3072], P(('wide', 'narrow')), may hold values from -3 to 3
- down_weight: bfloat16 [3072, 768], P(('wide', 'narrow')), may hold values from -0.109375 to 0.109375
- down_bias: bfloat16 [768], P(('wide', 'narrow')), may hold values from -1.796875 to 1.796875
- second_gain: bfloat16 [768], P(('wide', 'narrow')), may hold values from 0.5 to 1.5
- second_shift: bfloat16 [768], P(('wide', 'narrow')), may hold values from -1.796875 to 1.796875
- cotangent: bfloat16 [16, 1024, 768], P('wide', 'narrow'), may hold values from -6 to 6
Outputs:
- outputs: bfloat16 [16, 1024, 768], P('wide', 'narrow')
- grad_tokens: bfloat16 [16, 1024, 768], P('wide', 'narrow')
- grad_position_table: float32 [768, 108], P(('wide', 'narrow'))
- grad_input_weight: float32 [768, 2304], P(('wide', 'narrow'))
- grad_query_bias: float32 [768], P(('wide', 'narrow'))
- grad_value_bias: float32 [768], P(('wide', 'narrow'))
- grad_output_weight: float32 [768, 768], P(('wide', 'narrow'))
- grad_output_bias: float32 [768], P(('wide', 'narrow'))
- grad_first_gain: float32 [768], P(('wide', 'narrow'))
- grad_first_shift: float32 [768], P(('wide', 'narrow'))
- grad_up_weight: float32 [768, 3072], P(('wide', 'narrow'))
- grad_up_bias: float32 [3072], P(('wide', 'narrow'))
- grad_down_weight: float32 [3072, 768], P(('wide', 'narrow'))
- grad_down_bias: float32 [768], P(('wide', 'narrow'))
- grad_second_gain: float32 [768], P(('wide', 'narrow'))
- grad_second_shift: float32 [768], P(('wide', 'narrow'))
Inputs may be any that keep to these rules, and one draw needn't show every extreme that they name: `positions`: within each sequence, timesteps of 36, 72 or 108 tokens follow one another; a sequence may begin with the last tokens of a timestep of 36, and the timestep after that has 108 tokens; a token's entry is its index within its timestep. `segments`: sequence s holds episodes 3 s, 3 s + 1 and 3 s + 2 in this order, none empty; the first ends within the sequence's first 256 tokens and the last begins within its last 255.
All inputs are finite; a program needn't handle non-finite values.
Results may differ from a plain program's by a relative error of at most 0.012.
Values may be sent and summed in bfloat16 or wider, within the bound.
No kernel may reach another device: no remote copies, remote signals or barrier semaphores. Data moves between devices by JAX's collectives and lax.ppermute only.
A program may use at most 192 MiB of HBM per device.

v0:
```python
import jax
import jax.numpy as jnp
from jax import lax
from jax.sharding import PartitionSpec as P

HEADS = 12


epsilon = 1e-05
masked_score = -1e30
highest = lax.Precision.HIGHEST


def layer_norm(values, gain_row, shift_row):
    average = jnp.mean(values, axis=-1, keepdims=True)
    centered = values - average
    variance = jnp.mean(centered * centered, axis=-1, keepdims=True)
    return centered * lax.rsqrt(variance + epsilon) * gain_row + shift_row


def gelu_tanh(values):
    return jax.nn.gelu(values, approximate=True)


def product(left, right):
    return jnp.dot(left, right, preferred_element_type=jnp.float32)


def product_left(left, right):
    return lax.dot_general(
        left, right, (((0,), (0,)), ((), ())), preferred_element_type=jnp.float32
    )


def product_right(left, right):
    return lax.dot_general(
        left, right, (((1,), (1,)), ((), ())), preferred_element_type=jnp.float32
    )


def block_mask(segment_rows, query_start, query_rows, key_rows):
    query_places = query_start + jnp.arange(query_rows, dtype=jnp.int32)
    key_places = jnp.arange(key_rows, dtype=jnp.int32)
    query_segments = lax.dynamic_slice_in_dim(segment_rows, query_start, query_rows, 1)
    return (key_places[None, None, :] <= query_places[None, :, None]) & (
        segment_rows[:, None, :] == query_segments[:, :, None]
    )


def block_scores(query_heads, key_heads, allowed):
    score_scale = query_heads.shape[3] ** (-0.5)
    scores = (
        jnp.einsum("gqhd,gkhd->ghqk", query_heads, key_heads, preferred_element_type=jnp.float32)
        * score_scale
    )
    return jnp.where(allowed[:, None], scores, masked_score)


def local(
    tokens,
    positions,
    segments,
    position_table,
    input_weight,
    query_bias,
    value_bias,
    output_weight,
    output_bias,
    first_gain,
    first_shift,
    up_weight,
    up_bias,
    down_weight,
    down_bias,
    second_gain,
    second_shift,
    cotangent,
):
    seq_count, local_rows, model_width = tokens.shape
    full_len = segments.shape[1]
    token_rows = seq_count * local_rows
    head_count = HEADS
    head_width = model_width // head_count
    score_scale = head_width ** (-0.5)
    group = min(seq_count, max(1, 512 // local_rows))
    block_count = seq_count // group
    query_base = lax.axis_index("narrow") * local_rows
    (
        table_full,
        input_full,
        query_bias_full,
        value_bias_full,
        output_full,
        output_bias_full,
        first_gain_full,
        first_shift_full,
    ) = (
        lax.all_gather(position_table, ("wide", "narrow"), axis=0, tiled=True),
        lax.all_gather(input_weight, ("wide", "narrow"), axis=0, tiled=True),
        lax.all_gather(query_bias, ("wide", "narrow"), axis=0, tiled=True),
        lax.all_gather(value_bias, ("wide", "narrow"), axis=0, tiled=True),
        lax.all_gather(output_weight, ("wide", "narrow"), axis=0, tiled=True),
        lax.all_gather(output_bias, ("wide", "narrow"), axis=0, tiled=True),
        lax.all_gather(first_gain, ("wide", "narrow"), axis=0, tiled=True),
        lax.all_gather(first_shift, ("wide", "narrow"), axis=0, tiled=True),
    )
    patch_ids = jnp.arange(table_full.shape[1], dtype=jnp.int32)
    one_hot = positions.reshape(token_rows)[:, None] == patch_ids[None, :]
    embedded = product_right(one_hot.astype(jnp.bfloat16), table_full)
    start = tokens.reshape(token_rows, model_width).astype(jnp.float32) + embedded
    normed_float, norm_one_pull = jax.vjp(
        layer_norm, start, first_gain_full.astype(jnp.float32), first_shift_full.astype(jnp.float32)
    )
    normed_one = normed_float.astype(jnp.bfloat16)
    projected = product(normed_one, input_full)
    query = (projected[:, :model_width] + query_bias_full.astype(jnp.float32)).astype(jnp.bfloat16)
    keys = projected[:, model_width : 2 * model_width].astype(jnp.bfloat16)
    values = (projected[:, 2 * model_width :] + value_bias_full.astype(jnp.float32)).astype(
        jnp.bfloat16
    )
    group_keys, group_values = (
        lax.all_gather(
            keys.reshape(seq_count, local_rows, model_width), "narrow", axis=1, tiled=True
        ),
        lax.all_gather(
            values.reshape(seq_count, local_rows, model_width), "narrow", axis=1, tiled=True
        ),
    )
    key_blocks = group_keys.reshape(block_count, group, full_len, head_count, head_width)
    value_blocks = group_values.reshape(block_count, group, full_len, head_count, head_width)
    query_blocks = query.reshape(block_count, group, local_rows, head_count, head_width)
    segment_blocks = segments.reshape(block_count, group, full_len)

    def attend_block(pieces):
        query_heads, key_heads, value_heads, segment_rows = pieces
        allowed = block_mask(segment_rows, query_base, local_rows, full_len)
        scores = block_scores(query_heads, key_heads, allowed)
        highest_score = jnp.max(scores, axis=-1, keepdims=True)
        log_total = highest_score + jnp.log(
            jnp.sum(jnp.exp(scores - highest_score), axis=-1, keepdims=True)
        )
        probs_low = jnp.exp(scores - log_total).astype(jnp.bfloat16)
        mixed = jnp.einsum(
            "ghqk,gkhd->gqhd", probs_low, value_heads, preferred_element_type=jnp.float32
        )
        return (mixed, log_total)

    attended, log_totals = lax.map(
        attend_block, (query_blocks, key_blocks, value_blocks, segment_blocks)
    )
    attended_low = attended.reshape(token_rows, model_width).astype(jnp.bfloat16)
    middle = start + product(attended_low, output_full) + output_bias_full.astype(jnp.float32)
    up_full, up_bias_full, down_full, down_bias_full, second_gain_full, second_shift_full = (
        lax.all_gather(up_weight, ("wide", "narrow"), axis=0, tiled=True),
        lax.all_gather(up_bias, ("wide", "narrow"), axis=0, tiled=True),
        lax.all_gather(down_weight, ("wide", "narrow"), axis=0, tiled=True),
        lax.all_gather(down_bias, ("wide", "narrow"), axis=0, tiled=True),
        lax.all_gather(second_gain, ("wide", "narrow"), axis=0, tiled=True),
        lax.all_gather(second_shift, ("wide", "narrow"), axis=0, tiled=True),
    )
    normed_float_two, norm_two_pull = jax.vjp(
        layer_norm,
        middle,
        second_gain_full.astype(jnp.float32),
        second_shift_full.astype(jnp.float32),
    )
    normed_two = normed_float_two.astype(jnp.bfloat16)
    hidden = product(normed_two, up_full) + up_bias_full.astype(jnp.float32)
    activated, gelu_pull = jax.vjp(gelu_tanh, hidden)
    activated_low = activated.astype(jnp.bfloat16)
    outputs = (
        middle + product(activated_low, down_full) + down_bias_full.astype(jnp.float32)
    ).astype(jnp.bfloat16)
    up_back, down_back = (
        lax.all_gather(up_weight, ("wide", "narrow"), axis=0, tiled=True),
        lax.all_gather(down_weight, ("wide", "narrow"), axis=0, tiled=True),
    )
    cotangent_rows = cotangent.reshape(token_rows, model_width)
    grad_outputs = cotangent_rows.astype(jnp.float32)
    grad_down = product_left(activated_low, cotangent_rows)
    grad_down_bias = jnp.sum(grad_outputs, axis=0)
    grad_activated = product_right(cotangent_rows, down_back)
    grad_hidden = gelu_pull(grad_activated)[0].astype(jnp.bfloat16)
    grad_up = product_left(normed_two, grad_hidden)
    grad_up_bias = jnp.sum(grad_hidden.astype(jnp.float32), axis=0)
    grad_middle_norm, grad_gain_two, grad_shift_two = norm_two_pull(
        product_right(grad_hidden, up_back)
    )
    grad_middle = grad_outputs + grad_middle_norm
    up_share, up_bias_share, down_share, down_bias_share, gain_two_share, shift_two_share = (
        lax.psum_scatter(grad_up, ("wide", "narrow"), scatter_dimension=0, tiled=True),
        lax.psum_scatter(grad_up_bias, ("wide", "narrow"), scatter_dimension=0, tiled=True),
        lax.psum_scatter(grad_down, ("wide", "narrow"), scatter_dimension=0, tiled=True),
        lax.psum_scatter(grad_down_bias, ("wide", "narrow"), scatter_dimension=0, tiled=True),
        lax.psum_scatter(grad_gain_two, ("wide", "narrow"), scatter_dimension=0, tiled=True),
        lax.psum_scatter(grad_shift_two, ("wide", "narrow"), scatter_dimension=0, tiled=True),
    )
    input_back, output_back = (
        lax.all_gather(input_weight, ("wide", "narrow"), axis=0, tiled=True),
        lax.all_gather(output_weight, ("wide", "narrow"), axis=0, tiled=True),
    )
    grad_branch = grad_middle.astype(jnp.bfloat16)
    grad_output = product_left(attended_low, grad_branch)
    grad_output_bias = jnp.sum(grad_branch.astype(jnp.float32), axis=0)
    grad_attended = product_right(grad_branch, output_back).astype(jnp.bfloat16)
    grad_blocks = grad_attended.reshape(block_count, group, local_rows, head_count, head_width)

    def query_side_grads(pieces):
        query_heads, grad_heads, log_total, key_heads, value_heads, segment_rows = pieces
        allowed = block_mask(segment_rows, query_base, local_rows, full_len)
        scores = block_scores(query_heads, key_heads, allowed)
        probabilities = jnp.exp(scores - log_total)
        grad_probs = jnp.einsum(
            "gqhd,gkhd->ghqk", grad_heads, value_heads, preferred_element_type=jnp.float32
        )
        row_inner = jnp.sum(probabilities * grad_probs, axis=-1, keepdims=True)
        grad_scores = (probabilities * (grad_probs - row_inner)).astype(jnp.bfloat16)
        grad_query_block = (
            jnp.einsum(
                "ghqk,gkhd->gqhd", grad_scores, key_heads, preferred_element_type=jnp.float32
            )
            * score_scale
        )
        return (probabilities, grad_scores, row_inner, grad_query_block)

    def back_block(pieces):
        probabilities, grad_scores, row_inner, grad_query_block = query_side_grads(pieces)
        query_heads, grad_heads = (pieces[0], pieces[1])
        key_sums = (
            jnp.einsum(
                "ghqk,gqhd->gkhd", grad_scores, query_heads, preferred_element_type=jnp.float32
            )
            * score_scale
        )
        value_sums = jnp.einsum(
            "ghqk,gqhd->gkhd",
            probabilities.astype(jnp.bfloat16),
            grad_heads,
            preferred_element_type=jnp.float32,
        )
        return (grad_query_block, key_sums, value_sums)

    grad_query, key_sums, value_sums = lax.map(
        back_block,
        (query_blocks, grad_blocks, log_totals, key_blocks, value_blocks, segment_blocks),
    )
    grad_keys, grad_values = (
        lax.psum_scatter(
            key_sums.reshape(seq_count, full_len, model_width).astype(jnp.bfloat16),
            "narrow",
            scatter_dimension=1,
            tiled=True,
        ).astype(jnp.float32),
        lax.psum_scatter(
            value_sums.reshape(seq_count, full_len, model_width).astype(jnp.bfloat16),
            "narrow",
            scatter_dimension=1,
            tiled=True,
        ).astype(jnp.float32),
    )
    grad_query_low = grad_query.reshape(token_rows, model_width).astype(jnp.bfloat16)
    grad_keys_low = grad_keys.reshape(token_rows, model_width).astype(jnp.bfloat16)
    grad_values_low = grad_values.reshape(token_rows, model_width).astype(jnp.bfloat16)
    grad_projected = jnp.concatenate([grad_query_low, grad_keys_low, grad_values_low], axis=1)
    grad_input = product_left(normed_one, grad_projected)
    grad_query_bias = jnp.sum(grad_query_low.astype(jnp.float32), axis=0)
    grad_value_bias = jnp.sum(grad_values_low.astype(jnp.float32), axis=0)
    grad_start_norm, grad_gain_one, grad_shift_one = norm_one_pull(
        product_right(grad_projected, input_back)
    )
    grad_start = grad_middle + grad_start_norm
    grad_table = lax.dot_general(
        grad_start,
        one_hot.astype(jnp.float32),
        (((0,), (0,)), ((), ())),
        precision=highest,
        preferred_element_type=jnp.float32,
    )
    (
        table_share,
        input_share,
        query_bias_share,
        value_bias_share,
        output_share,
        output_bias_share,
        gain_one_share,
        shift_one_share,
    ) = (
        lax.psum_scatter(grad_table, ("wide", "narrow"), scatter_dimension=0, tiled=True),
        lax.psum_scatter(grad_input, ("wide", "narrow"), scatter_dimension=0, tiled=True),
        lax.psum_scatter(grad_query_bias, ("wide", "narrow"), scatter_dimension=0, tiled=True),
        lax.psum_scatter(grad_value_bias, ("wide", "narrow"), scatter_dimension=0, tiled=True),
        lax.psum_scatter(grad_output, ("wide", "narrow"), scatter_dimension=0, tiled=True),
        lax.psum_scatter(grad_output_bias, ("wide", "narrow"), scatter_dimension=0, tiled=True),
        lax.psum_scatter(grad_gain_one, ("wide", "narrow"), scatter_dimension=0, tiled=True),
        lax.psum_scatter(grad_shift_one, ("wide", "narrow"), scatter_dimension=0, tiled=True),
    )
    return (
        outputs.reshape(seq_count, local_rows, model_width),
        grad_start.astype(jnp.bfloat16).reshape(seq_count, local_rows, model_width),
        table_share,
        input_share,
        query_bias_share,
        value_bias_share,
        output_share,
        output_bias_share,
        gain_one_share,
        shift_one_share,
        up_share,
        up_bias_share,
        down_share,
        down_bias_share,
        gain_two_share,
        shift_two_share,
    )


def solution(mesh):
    placed = (
        P("wide", "narrow", None),
        P("wide", "narrow"),
        P("wide", None),
        P(("wide", "narrow"), None),
        P(("wide", "narrow"), None),
        P(("wide", "narrow")),
        P(("wide", "narrow")),
        P(("wide", "narrow"), None),
        P(("wide", "narrow")),
        P(("wide", "narrow")),
        P(("wide", "narrow")),
        P(("wide", "narrow"), None),
        P(("wide", "narrow")),
        P(("wide", "narrow"), None),
        P(("wide", "narrow")),
        P(("wide", "narrow")),
        P(("wide", "narrow")),
        P("wide", "narrow", None),
    )
    return jax.shard_map(
        local,
        mesh=mesh,
        in_specs=placed,
        out_specs=(
            P("wide", "narrow", None),
            P("wide", "narrow", None),
            P(("wide", "narrow"), None),
            P(("wide", "narrow"), None),
            P(("wide", "narrow")),
            P(("wide", "narrow")),
            P(("wide", "narrow"), None),
            P(("wide", "narrow")),
            P(("wide", "narrow")),
            P(("wide", "narrow")),
            P(("wide", "narrow"), None),
            P(("wide", "narrow")),
            P(("wide", "narrow"), None),
            P(("wide", "narrow")),
            P(("wide", "narrow")),
            P(("wide", "narrow")),
        ),
        check_vma=False,
    )
```

profile of v0, /device:TPU:7, one launch (start us, length us, event | category | flops | bytes accessed | tf_op | source)
XLA Modules:
  0.0 1224.9 jit_solution(65773035846620478)
XLA Ops:
  16.2 40.4 %all-reduce.20 = (bf16[768]{0:T(1024)(128)(2,1)S(1)}, bf16[768]{0:T(1024)(128)(2,1)S(1)}, bf16[768]{0:T(1024)(128)(2,1)S(1)}, bf16[768]{0:T(1024)(128)(2,1)S(1)}...) all-reduce(bf16[768]{0:T(1024)(128)(2,1)S(1)} %dynamic-update-slice, ...), channel_id=1, replica_groups=mesh['wide'=8,'narrow'=4] {'wide','narrow'}, use_global_device_ids=true, to_apply=%add.1 | all-reduce | flops 9216 | bytes 36864
  56.6 60.0 %all_gather.52 = bf16[768,108]{1,0:T(8,128)(2,1)S(1)} all-gather(bf16[24,108]{1,0:T(8,128)(2,1)} %param.21), channel_id=1, replica_groups=mesh['wide'=8,'narrow'=4] {'wide','narrow'}, dimensions={0}, use_global_device_ids=true | all-gather | bytes 171072 | tf_op jit(solution)/shard_map/all_gather | solution.py:98
  116.5 1.6 fusion.43
  118.5 4.3 fusion.34
  123.9 1.3 copy-done.12
  125.4 3.0 fusion.9
  130.5 1.2 compare_and_fusion
  133.1 61.6 %all-gather.11.cloned.1.call-done = bf16[2,1024,768]{2,1,0:T(8,128)(2,1)} async-done(((bf16[2,256,768]{2,1,0:T(8,128)(2,1)}), bf16[2,1024,768]{2,1,0:T(8,128)(2,1)}) %all-gather.11.cloned.1.call-update) | async-done | bytes 3145744 | tf_op jit(solution)/shard_map/all_gather | solution.py:122
  194.7 3.4 copy.56
  198.1 61.0 %all-gather.9.cloned.1.call-done = bf16[2,1024,768]{2,1,0:T(8,128)(2,1)} async-done(((bf16[2,256,768]{2,1,0:T(8,128)(2,1)}), bf16[2,1024,768]{2,1,0:T(8,128)(2,1)}) %all-gather.9.cloned.1.call-update) | async-done | bytes 3145744 | tf_op jit(solution)/shard_map/all_gather | solution.py:125
  259.0 4.6 copy.54
  263.7 12.2 fusion
  275.8 11.8 exponential_reduce_fusion
  287.7 12.3 %fusion.11 = bf16[2,256,12,64]{1,3,2,0:T(8,128)(2,1)S(1)} fusion(bf16[2,1024,12,64]{1,3,2,0:T(8,128)(2,1)} %bitcast.67, f32[2,12,256,1024]{3,2,1,0:T(8,128)} %get-tuple-element.112, f32[2,12,256]{2,1,0:T(8,128)S(1)} %log_add_fusion, pred[2,256,1024]{2,1,0:T(8,128)(4,1)S(1)} %copy-done.5), kind=kOutput, calls=%fused_computation.49 | convolution fusion | flops 830865408 | bytes 29646848 | tf_op jit(solution)/shard_map/while/body/eval_jaxpr/ghqk,gkhd->gqhd/dot_general | solution.py:143
  301.9 12.2 all-gather.13.cloned.1.call-done
  314.1 2.9 fusion.44
  318.5 60.8 %all-gather.15.cloned.1.call-done = bf16[768,3072]{1,0:T(8,128)(2,1)} async-done(((bf16[24,3072]{1,0:T(8,128)(2,1)}), bf16[768,3072]{1,0:T(8,128)(2,1)}) %all-gather.15.cloned.1.call-update) | async-done | bytes 4718608 | tf_op jit(solution)/shard_map/all_gather | solution.py:154
  379.2 8.1 fusion.36
  387.3 57.0 %all-gather.17.cloned.1.call-done = bf16[3072,768]{1,0:T(8,128)(2,1)} async-done(((bf16[96,768]{1,0:T(8,128)(2,1)}), bf16[3072,768]{1,0:T(8,128)(2,1)}) %all-gather.17.cloned.1.call-update) | async-done | bytes 4718608 | tf_op jit(solution)/shard_map/all_gather | solution.py:156
  444.3 9.7 convert_reduce_fusion
  454.0 3.0 multiply_reduce_fusion.1
  460.1 1.7 convolution_convert_fusion.1
  461.8 2.3 copy.59
  464.1 2.9 squeeze.35
  467.0 12.9 %convolution_convert_fusion = bf16[2,12,64,1024]{3,2,1,0:T(8,128)(2,1)} fusion(bf16[2,256,12,64]{1,0,3,2:T(2,128)(2,1)} %squeeze.35, f32[2,12,256,1024]{3,2,1,0:T(8,128)} %get-tuple-element.112, f32[2,12,256]{2,1,0:T(8,128)S(1)} %log_add_fusion, pred[2,256,1024]{2,1,0:T(8,128)(4,1)} %compare_and_fusion), kind=kOutput, calls=%fused_computation.22 | convolution fusion | flops 832045056 | bytes 29646848 | tf_op jit(solution)/shard_map/while/body/eval_jaxpr/ghqk,gqhd->gkhd/dot_general | solution.py:235
  479.9 4.6 copy.65
  484.6 19.6 %multiply_reduce_fusion = (f32[2,12,256]{2,1,0:T(8,128)S(1)}, f32[2,12,256,1024]{3,2,1,0:T(8,128)}) fusion(f32[2,12,256,1024]{3,2,1,0:T(8,128)} %get-tuple-element.112, f32[2,12,256]{2,1,0:T(8,128)S(1)} %log_add_fusion, pred[2,256,1024]{2,1,0:T(8,128)(4,1)} %compare_and_fusion, bf16[2,1024,12,64]{1,3,2,0:T(8,128)(2,1)} %bitcast.68, ...), kind=kOutput, calls=%fused_computation.1 | convolution fusion | flops 836757504 | bytes 54837248 | tf_op jit(solution)/shard_map/while/body/eval_jaxpr/gqhd,gkhd->ghqk/dot_general | solution.py:213
  504.2 17.2 %multiply_convert_fusion = bf16[2,12,256,1024]{3,2,1,0:T(8,128)(2,1)S(1)} fusion(f32[2,12,256,1024]{3,2,1,0:T(8,128)} %get-tuple-element.117, f32[2,12,256,1024]{3,2,1,0:T(8,128)} %get-tuple-element.112, f32[2,12,256]{2,1,0:T(8,128)S(1)} %get-tuple-element.116, f32[2,12,256]{2,1,0:T(8,128)S(1)} %log_add_fusion, pred[2,256,1024]{2,1,0:T(8,128)(4,1)} %compare_and_fusion), kind=kLoop, calls=%fused_computation | loop fusion | flops 37748736 | bytes 63488000 | tf_op jit(solution)/shard_map/while/body/eval_jaxpr/convert_element_type | solution.py:217
  521.5 4.5 multiply_convert_fusion.1
  526.9 4.6 copy.63
  531.6 3.6 fusion.45
  535.5 8.6 convert_reduce_fusion.4
  545.1 1.4 copy.67
  546.6 60.2 %reduce-scatter.10.cloned.1.call-done = bf16[2,256,768]{2,1,0:T(8,128)(2,1)} async-done(((bf16[2,1024,768]{2,1,0:T(8,128)(2,1)}), bf16[2,256,768]{2,1,0:T(8,128)(2,1)}) %reduce-scatter.10.cloned.1.call-update) | async-done | bytes 786448 | tf_op jit(solution)/shard_map/reduce_scatter | solution.py:248
  606.8 2.3 copy.66
  609.1 4.7 multiply_reduce_fusion.2
  615.4 1.3 fusion.40
  616.7 2.3 fusion.21
  619.3 10.2 fusion.37
  629.5 8.9 fusion.35
  639.1 6.6 fusion.13
  647.1 9.2 add_convert_fusion
  656.5 40.6 %all-reduce.19 = (f32[768]{0:T(1024)S(1)}, f32[768]{0:T(1024)S(1)}, f32[768]{0:T(1024)S(1)}, f32[768]{0:T(1024)S(1)}, f32[768]{0:T(1024)S(1)}, /*index=5*/f32[30...) all-reduce(f32[768]{0:T(1024)S(1)} %reduce_sum.218, ...), channel_id=6, replica_groups=mesh['wide'=8,'narrow'=4] {'wide','narrow'}, use_global_device_ids=true, to_apply=%region_16.17.clone | all-reduce | flops 9216 | bytes 73728
  702.3 8.0 reduce-scatter.16.cloned.1.call-done
  710.3 100.0 %reduce-scatter.22.cloned.1.call-done = f32[24,108]{1,0:T(8,128)} async-done(((f32[768,108]{1,0:T(8,128)}), f32[24,108]{1,0:T(8,128)}) %reduce-scatter.22.cloned.1.call-update) | async-done | bytes 10384
  810.2 141.0 %reduce-scatter.20.cloned.1.call-done = f32[96,768]{1,0:T(8,128)} async-done(((f32[3072,768]{1,0:T(8,128)}), f32[96,768]{1,0:T(8,128)}) %reduce-scatter.20.cloned.1.call-update) | async-done | bytes 294928 | tf_op jit(solution)/shard_map/reduce_scatter | solution.py:193
  951.3 142.0 %reduce-scatter.18.cloned.1.call-done = f32[24,3072]{1,0:T(8,128)} async-done(((f32[768,3072]{1,0:T(8,128)}), f32[24,3072]{1,0:T(8,128)}) %reduce-scatter.18.cloned.1.call-update) | async-done | bytes 294928 | tf_op jit(solution)/shard_map/reduce_scatter | solution.py:191
  1093.2 124.7 %reduce-scatter.14.cloned.1.call-done = f32[24,2304]{1,0:T(8,128)} async-done(((f32[768,2304]{1,0:T(8,128)}), f32[24,2304]{1,0:T(8,128)}) %reduce-scatter.14.cloned.1.call-update) | async-done | bytes 221200 | tf_op jit(solution)/shard_map/reduce_scatter | solution.py:290
  (137 shorter events, 32.0 us)
Async XLA Ops:
  7.2 111.3 %all-gather.7.cloned.1.call-start = ((), (), s32[]{:S(2)}) async-start(), calls=%async_computation.7 | async-start | bytes 3649536 | tf_op jit(solution)/shard_map/all_gather | solution.py:99
  7.9 186.8 %all-gather.11.cloned.1.call-start = ((), (), s32[]{:S(2)}) async-start(), calls=%async_computation.9 | async-start | bytes 3932160 | tf_op jit(solution)/shard_map/all_gather | solution.py:122
  56.6 66.3 %copy-start.17 = (f32[768]{0:T(1024)}, f32[768]{0:T(1024)S(1)}, u32[]{:S(2)}) copy-start(f32[768]{0:T(1024)S(1)} %convert_element_type.149) | copy-start | bytes 9220
  118.2 4.7 copy-start.1
  122.9 2.4 copy-start.12
  125.3 5.0 copy-start.16
  125.3 133.8 %all-gather.9.cloned.1.call-start = ((), (), s32[]{:S(2)}) async-start(), calls=%async_computation.8 | async-start | bytes 3932160 | tf_op jit(solution)/shard_map/all_gather | solution.py:125
  128.4 185.7 %all-gather.13.cloned.1.call-start = ((), (), s32[]{:S(2)}) async-start(), calls=%async_computation.10 | async-start | bytes 1216512 | tf_op jit(solution)/shard_map/all_gather | solution.py:102
  129.0 250.3 %all-gather.15.cloned.1.call-start = ((), (), s32[]{:S(2)}) async-start(), calls=%async_computation.11 | async-start | bytes 4866048 | tf_op jit(solution)/shard_map/all_gather | solution.py:154
  129.6 314.7 %all-gather.17.cloned.1.call-start = ((), (), s32[]{:S(2)}) async-start(), calls=%async_computation.12 | async-start | bytes 4866048 | tf_op jit(solution)/shard_map/all_gather | solution.py:156
  130.1 415.0 %reduce-scatter.12.cloned.1.call-start = ((), (), s32[]{:S(2)}) async-start(), calls=%async_computation.14 | async-start | bytes 3932160 | tf_op jit(solution)/shard_map/reduce_scatter | solution.py:254
  263.7 12.2 copy-start.5
  317.0 1.2 copy-start.9
  444.3 9.7 copy-start.10
  444.3 9.7 copy-start.20
  454.0 3.0 copy-start.22
  457.0 1.9 copy-start.7
  457.0 3.1 copy-start.21
  457.7 1.2 copy-start.3
  459.2 0.9 copy-start.14
  484.6 122.2 %reduce-scatter.10.cloned.1.call-start = ((), (), s32[]{:S(2)}) async-start(), calls=%async_computation.13 | async-start | bytes 3932160 | tf_op jit(solution)/shard_map/reduce_scatter | solution.py:248
  504.2 17.2 %copy-start.6 = (bf16[2,256,12,64]{1,0,3,2:T(2,128)(2,1)S(1)}, bf16[2,256,12,64]{1,0,3,2:T(2,128)(2,1)}, u32[]{:S(2)}) copy-start(bf16[2,256,12,64]{1,0,3,2:T(2,128)(2,1)} %squeeze.33) | copy-start | bytes 2359300
  521.5 5.5 copy-start
  531.6 178.7 %reduce-scatter.16.cloned.1.call-start = ((), (), s32[]{:S(2)}) async-start(), calls=%async_computation.16 | async-start | bytes 2433024 | tf_op jit(solution)/shard_map/reduce_scatter | solution.py:293
  535.3 275.0 %reduce-scatter.22.cloned.1.call-start = ((), (), s32[]{:S(2)}) async-start(), calls=%async_computation.19 | async-start | bytes 405504
  544.1 64.9 %copy-start.2 = (f32[512,768]{1,0:T(8,128)S(1)}, f32[512,768]{1,0:T(8,128)}, u32[]{:S(2)}) copy-start(f32[512,768]{1,0:T(8,128)} %copy-done.1) | copy-start | bytes 4718596
  546.6 62.5 %copy-start.15 = (bf16[512,768]{0,1:T(8,128)(2,1)}, bf16[512,768]{0,1:T(8,128)(2,1)S(1)}, u32[]{:S(2)}) copy-start(bf16[512,768]{0,1:T(8,128)(2,1)S(1)} %copy.67) | copy-start | bytes 2359300
  613.8 1.4 copy-start.4
  613.8 1.6 copy-start.8
  619.0 332.3 %reduce-scatter.20.cloned.1.call-start = ((), (), s32[]{:S(2)}) async-start(), calls=%async_computation.18 | async-start | bytes 9732096 | tf_op jit(solution)/shard_map/reduce_scatter | solution.py:193
  629.4 463.8 %reduce-scatter.18.cloned.1.call-start = ((), (), s32[]{:S(2)}) async-start(), calls=%async_computation.17 | async-start | bytes 9732096 | tf_op jit(solution)/shard_map/reduce_scatter | solution.py:191
  638.4 0.7 copy-start.18
  638.5 579.4 %reduce-scatter.14.cloned.1.call-start = ((), (), s32[]{:S(2)}) async-start(), calls=%async_computation.15 | async-start | bytes 7299072 | tf_op jit(solution)/shard_map/reduce_scatter | solution.py:290
  645.7 0.7 copy-start.19
  645.7 1.4 copy-start.11
  647.1 9.2 copy-start.13
Sparse Core Ops, SparseCore 0:
  10.8 61.0 all-gather.6
  125.4 69.2 all-gather.10
  196.9 62.1 all-gather.8
  261.7 52.3 all-gather.12
  316.7 62.4 all-gather.14
  381.9 62.3 all-gather.16
  484.7 59.3 reduce-scatter.11
  546.4 60.2 reduce-scatter.9
  612.6 97.6 reduce-scatter.15
  716.4 93.7 reduce-scatter.21
  816.7 134.5 reduce-scatter.19
  958.6 134.5 reduce-scatter.17
  1099.5 118.3 reduce-scatter.13
where the time goes:
time: 1230 us; the launch traced here: 1220 us
  waiting for transfers between devices  831 us (68%)
  matrix products  147 us (12%)
  blocking collectives  141 us (11%)
  local copies, waits for them, and re-layouts  53 us (4%)
  other arithmetic  37.4 us (3%)
  between operations  14.9 us (1%)
    reduce_scatter x1, waiting for transfers between devices, local(): lax.psum_scatter(grad_up, ('wide', 'narrow'), scatter_dimension=0, tiled=...  142 us
    reduce_scatter x1, waiting for transfers between devices, local(): lax.psum_scatter(grad_down, ('wide', 'narrow'), scatter_dimension=0, tile...  141 us
    reduce_scatter x1, waiting for transfers between devices, local(): lax.psum_scatter(grad_input, ('wide', 'narrow'), scatter_dimension=0, til...  125 us
    unnamed x14, waiting for transfers between devices  102 us
    unnamed x2, blocking collectives  81 us
    all_gather x1, waiting for transfers between devices, local(): lax.all_gather(keys.reshape(seq_count, local_rows, model_width), 'narrow'...  61.6 us
    all_gather x1, waiting for transfers between devices, local(): lax.all_gather(values.reshape(seq_count, local_rows, model_width), 'narro...  61 us
    all_gather x1, waiting for transfers between devices, local(): lax.all_gather(up_weight, ('wide', 'narrow'), axis=0, tiled=True)  60.8 us
  transfers between devices with their start and end apart: 13, of which 11 were waited for; matrix products, arithmetic and copies ran while one was open for 15% of the time, Pallas kernels for 0%

commit v1 on v0

v1 whole, which is shorter than its diff:
```python
import jax
import jax.numpy as jnp
from jax import lax
from jax.sharding import PartitionSpec as P

HEADS = 12
PLACES = 4
epsilon = 1e-05
masked_score = -1e30

f32 = jnp.float32
bf16 = jnp.bfloat16


def layer_norm(values, gain_row, shift_row):
    average = jnp.mean(values, axis=-1, keepdims=True)
    centered = values - average
    variance = jnp.mean(centered * centered, axis=-1, keepdims=True)
    return centered * lax.rsqrt(variance + epsilon) * gain_row + shift_row


def gelu_tanh(values):
    return jax.nn.gelu(values, approximate=True)


def product(left, right):
    return jnp.dot(left, right, preferred_element_type=f32)


def product_left(left, right):
    return lax.dot_general(left, right, (((0,), (0,)), ((), ())), preferred_element_type=f32)


def product_right(left, right):
    return lax.dot_general(left, right, (((1,), (1,)), ((), ())), preferred_element_type=f32)


def swap(values, axis, bits):
    size = lax.axis_size(axis)
    return lax.ppermute(values, axis, [(i, i ^ bits) for i in range(size)])


def wide_bits():
    size, bits, bit = lax.axis_size("wide"), [], 1
    while bit < size:
        bits.append(bit)
        bit *= 2
    return bits


def spread_perm(turn):
    pairs = []
    for w in range(lax.axis_size("wide")):
        for z in range(PLACES):
            core = (0, 1, 1, 0)[z]
            which = turn ^ (z // 2)
            there = (w - w % 2 + core, 2 * (w % 2) + which)
            pairs.append((w * PLACES + z, there[0] * PLACES + there[1]))
    return pairs


def spread(values, place):
    late = place // 2
    got = [
        lax.ppermute(
            lax.dynamic_index_in_dim(values, turn ^ late, 0, keepdims=False),
            ("wide", "narrow"),
            spread_perm(turn),
        )
        for turn in range(2)
    ]
    odd = (place % 2) == 1
    return jnp.where(odd, got[1], got[0]), jnp.where(odd, got[0], got[1])


def unspread(low, high, place):
    odd = (place % 2) == 1
    sent = (jnp.where(odd, high, low), jnp.where(odd, low, high))
    got = [
        lax.ppermute(sent[turn], ("wide", "narrow"), [(b, a) for a, b in spread_perm(turn)])
        for turn in range(2)
    ]
    late = place >= 2
    return jnp.stack([jnp.where(late, got[1], got[0]), jnp.where(late, got[0], got[1])])


def doubling(piece, bits):
    held = {0: piece}
    for bit in bits:
        more = {}
        for index, part in held.items():
            more[index ^ bit] = swap(part, "wide", bit)
        held.update(more)
    return held


def gather(shard, cut, wide, place):
    rows, columns = shard.shape
    pieces = jnp.stack([shard] + [swap(shard, "narrow", k) for k in range(1, PLACES)])
    order = jnp.arange(PLACES) ^ place
    column = jnp.take(pieces, order, axis=0).reshape(PLACES * rows, columns)
    bits = wide_bits()
    halves = []
    for part, way in ((column[:, :cut], bits[1:]), (column[:, cut:], bits[:0:-1])):
        held = doubling(part, list(way))
        held = jnp.stack([held[2 * i] for i in range(len(held))])
        both = jnp.stack([held, swap(held, "wide", 1)], axis=1)
        halves.append(both.reshape((-1,) + part.shape))
    whole = jnp.concatenate(halves, axis=2)
    ranks = jnp.arange(whole.shape[0]) ^ wide
    return jnp.take(whole, ranks, axis=0).reshape(-1, columns)


def scatter(values, cut, wide, place, kind=bf16):
    size = lax.axis_size("wide")
    rows, columns = values.shape
    blocks = values.astype(kind).reshape(size, rows // size, columns)
    blocks = jnp.take(blocks, jnp.arange(size) ^ wide, axis=0)
    blocks = blocks.reshape(size // 2, 2, rows // size, columns)
    kept = blocks[:, 0].astype(f32) + swap(blocks[:, 1], "wide", 1).astype(f32)
    kept = kept.astype(kind)
    bits = wide_bits()
    halves = []
    for part, way in ((kept[:, :, :cut], bits[:0:-1]), (kept[:, :, cut:], bits[1:])):
        held = {2 * i: part[i] for i in range(size // 2)}
        for bit in way:
            keep = {}
            for index, piece in held.items():
                if not index & bit:
                    there = swap(held[index ^ bit], "wide", bit)
                    keep[index] = (piece.astype(f32) + there.astype(f32)).astype(kind)
            held = keep
        halves.append(held[0])
    column = jnp.concatenate(halves, axis=1)
    pieces = column.reshape(PLACES, -1, columns)
    pieces = jnp.take(pieces, jnp.arange(PLACES) ^ place, axis=0)
    total = pieces[0].astype(f32)
    for k in range(1, PLACES):
        total = total + swap(pieces[k], "narrow", k).astype(f32)
    return total


def local(
    tokens,
    positions,
    segments,
    position_table,
    input_weight,
    query_bias,
    value_bias,
    output_weight,
    output_bias,
    first_gain,
    first_shift,
    up_weight,
    up_bias,
    down_weight,
    down_bias,
    second_gain,
    second_shift,
    cotangent,
):
    seq_count, local_rows, width = tokens.shape
    hidden_width = up_weight.shape[1]
    patches = position_table.shape[1]
    full = segments.shape[1]
    head_width = width // HEADS
    scale = head_width ** (-0.5)
    wide = lax.axis_index("wide")
    place = lax.axis_index("narrow")
    core = wide % 2
    first_core = core == 0
    rows = 2 * local_rows

    vectors = (
        query_bias,
        value_bias,
        output_bias,
        first_gain,
        first_shift,
        down_bias,
        second_gain,
        second_shift,
    )
    spare = up_bias.shape[0] // query_bias.shape[0]
    small = jnp.concatenate(
        [position_table] + [v[:, None] for v in vectors] + [up_bias.reshape(-1, spare)], axis=1
    )
    small = jnp.pad(small, ((0, 0), (0, 128 - small.shape[1])))

    low, high = spread(tokens, place)
    mine = jnp.stack([low, high])
    others = swap(mine, "wide", 1)
    pos_low, pos_high = spread(positions, place)
    pos_mine = jnp.stack([pos_low, pos_high])
    pos_others = swap(pos_mine, "wide", 1)
    far = swap(segments, "wide", 1)
    segment = jnp.where((place // 2) == core, segments, far)
    segment = lax.dynamic_index_in_dim(segment, place % 2, 0, keepdims=False)

    def in_order(own, other):
        return jnp.where(
            first_core,
            jnp.concatenate([own[0], other[0], other[1], own[1]]),
            jnp.concatenate([other[0], own[0], own[1], other[1]]),
        )

    def of_core(values):
        blocks = values.reshape((4, local_rows) + values.shape[1:])
        return jnp.where(
            first_core,
            jnp.concatenate([blocks[0], blocks[3]]),
            jnp.concatenate([blocks[1], blocks[2]]),
        )

    def of_other(values):
        blocks = values.reshape((4, local_rows) + values.shape[1:])
        return jnp.where(
            first_core,
            jnp.concatenate([blocks[1], blocks[2]]),
            jnp.concatenate([blocks[0], blocks[3]]),
        )

    cot_low, cot_high = spread(cotangent, place)
    cotangent_rows = jnp.concatenate([cot_low, cot_high])

    in_full = gather(jnp.concatenate([small, input_weight], axis=1), 1280, wide, place)
    small_full, in_full = in_full[:, :128], in_full[:, 128:]
    out_up = gather(
        jnp.concatenate([output_weight, up_weight], axis=1), (width + hidden_width) // 2, wide, place
    )
    out_full, up_full = out_up[:, :width], out_up[:, width:]
    down_full = gather(down_weight, width // 2, wide, place)

    vector_full = small_full[:, patches:].astype(f32)
    (qb, vb, ob, g1, s1, db, g2, s2) = (vector_full[:, i] for i in range(8))
    ub = vector_full[:, 8 : 8 + spare].reshape(hidden_width)
    table_full = small_full[:, :patches]

    tokens_all = in_order(mine, others)
    pos_all = in_order(pos_mine, pos_others)
    one_hot_all = (pos_all[:, None] == jnp.arange(patches, dtype=jnp.int32)[None, :]).astype(bf16)
    start_all = tokens_all.astype(f32) + product_right(one_hot_all, table_full)
    normed_all = layer_norm(start_all, g1, s1).astype(bf16)
    start = of_core(start_all)
    one_hot = of_core(one_hot_all)
    normed_one = of_core(normed_all)
    query = (product(normed_one, in_full[:, :width]) + qb).astype(bf16)
    projected = product(normed_all, in_full[:, width:])
    keys = projected[:, :width].astype(bf16)
    values = (projected[:, width:] + vb).astype(bf16)

    places = of_core(jnp.arange(full, dtype=jnp.int32))
    allowed = (jnp.arange(full)[None, :] <= places[:, None]) & (
        segment[None, :] == of_core(segment)[:, None]
    )
    query_heads = query.reshape(rows, HEADS, head_width)
    key_heads = keys.reshape(full, HEADS, head_width)
    value_heads = values.reshape(full, HEADS, head_width)
    scores = jnp.einsum("qhd,khd->hqk", query_heads, key_heads, preferred_element_type=f32) * scale
    scores = jnp.where(allowed[None], scores, masked_score)
    probabilities = jax.nn.softmax(scores, axis=-1)
    probs_low = probabilities.astype(bf16)
    attended = jnp.einsum("hqk,khd->qhd", probs_low, value_heads, preferred_element_type=f32)
    attended_low = attended.reshape(rows, width).astype(bf16)

    middle = start + product(attended_low, out_full) + ob
    normed_float_two, norm_two_pull = jax.vjp(layer_norm, middle, g2, s2)
    normed_two = normed_float_two.astype(bf16)
    hidden = product(normed_two, up_full) + ub
    activated, gelu_pull = jax.vjp(gelu_tanh, hidden)
    activated_low = activated.astype(bf16)
    outputs = (middle + product(activated_low, down_full) + db).astype(bf16)
    outputs_back = unspread(outputs[:local_rows], outputs[local_rows:], place)

    grad_outputs = cotangent_rows.astype(f32)
    grad_down = product_left(activated_low, cotangent_rows)
    grad_down_bias = jnp.sum(grad_outputs, axis=0)
    grad_hidden = gelu_pull(product_right(cotangent_rows, down_full))[0].astype(bf16)
    grad_up = product_left(normed_two, grad_hidden)
    grad_up_bias = jnp.sum(grad_hidden.astype(f32), axis=0)
    grad_middle_norm, grad_gain_two, grad_shift_two = norm_two_pull(
        product_right(grad_hidden, up_full)
    )
    grad_middle = grad_outputs + grad_middle_norm
    grad_branch = grad_middle.astype(bf16)
    grad_output = product_left(attended_low, grad_branch)
    grad_output_bias = jnp.sum(grad_branch.astype(f32), axis=0)
    grad_attended = product_right(grad_branch, out_full).astype(bf16)
    down_share = scatter(grad_down, width // 2, wide, place)
    out_up_share = scatter(
        jnp.concatenate([grad_output, grad_up], axis=1), (width + hidden_width) // 2, wide, place
    )

    grad_heads = grad_attended.reshape(rows, HEADS, head_width)
    grad_probs = jnp.einsum("qhd,khd->hqk", grad_heads, value_heads, preferred_element_type=f32)
    inner = jnp.sum(probabilities * grad_probs, axis=-1, keepdims=True)
    grad_scores = (probabilities * (grad_probs - inner)).astype(bf16)
    grad_query = (
        jnp.einsum("hqk,khd->qhd", grad_scores, key_heads, preferred_element_type=f32) * scale
    )
    key_sums = (
        jnp.einsum("hqk,qhd->khd", grad_scores, query_heads, preferred_element_type=f32) * scale
    )
    value_sums = jnp.einsum("hqk,qhd->khd", probs_low, grad_heads, preferred_element_type=f32)
    sums = jnp.concatenate(
        [key_sums.reshape(full, width), value_sums.reshape(full, width)], axis=1
    )
    got = swap(of_other(sums).astype(bf16), "wide", 1)
    grad_key_value = (of_core(sums) + got.astype(f32)).astype(bf16)
    grad_query_low = grad_query.reshape(rows, width).astype(bf16)
    grad_projected = jnp.concatenate([grad_query_low, grad_key_value], axis=1)
    grad_input = product_left(normed_one, grad_projected)
    grad_bias = jnp.sum(grad_projected.astype(f32), axis=0)
    _, norm_one_pull = jax.vjp(layer_norm, start, g1, s1)
    grad_start_norm, grad_gain_one, grad_shift_one = norm_one_pull(
        product_right(grad_projected, in_full)
    )
    grad_start = grad_middle + grad_start_norm
    grad_low = grad_start.astype(bf16)
    grad_tokens = unspread(grad_low[:local_rows], grad_low[local_rows:], place)
    grad_table = product_left(grad_low, one_hot)

    in_share = scatter(grad_input, 1152, wide, place)
    small_grads = jnp.concatenate(
        [grad_table]
        + [
            v[:, None]
            for v in (
                grad_bias[:width],
                grad_bias[2 * width :],
                grad_output_bias,
                grad_gain_one,
                grad_shift_one,
                grad_down_bias,
                grad_gain_two,
                grad_shift_two,
            )
        ]
        + [grad_up_bias.reshape(width, spare)],
        axis=1,
    )
    small_share = scatter(small_grads, 64, wide, place, f32)
    tail = [small_share[:, patches + i] for i in range(8)]
    return (
        outputs_back,
        grad_tokens,
        small_share[:, :patches],
        in_share,
        tail[0],
        tail[1],
        out_up_share[:, :width],
        tail[2],
        tail[3],
        tail[4],
        out_up_share[:, width:],
        small_share[:, patches + 8 : patches + 8 + spare].reshape(-1),
        down_share,
        tail[5],
        tail[6],
        tail[7],
    )


def solution(mesh):
    both = ("wide", "narrow")
    matrix = P(both, None)
    vector = P(both)
    block = P("wide", "narrow", None)
    return jax.shard_map(
        local,
        mesh=mesh,
        in_specs=(
            block,
            P("wide", "narrow"),
            P("wide", None),
            matrix,
            matrix,
            vector,
            vector,
            matrix,
            vector,
            vector,
            vector,
            matrix,
            vector,
            matrix,
            vector,
            vector,
            vector,
            block,
        ),
        out_specs=(
            block,
            block,
            matrix,
            matrix,
            vector,
            vector,
            matrix,
            vector,
            vector,
            vector,
            matrix,
            vector,
            matrix,
            vector,
            vector,
            vector,
        ),
        check_vma=False,
    )
```

time: 1230 us -> 625 us (0.51)
  waiting for transfers between devices: 831 us -> 160 us
  blocking collectives: 141 us -> 0 us
  starting transfers between devices: 1.28 us -> 99.4 us
  other arithmetic: 37.4 us -> 113 us
  local copies, waits for them, and re-layouts: 53 us -> 119 us
  matrix products: 147 us -> 120 us
  between operations: 14.9 us -> 2.56 us
    reduce_scatter x6 -> x0, waiting for transfers between devices: 476 us -> none  [the longest x1 142 us: local(): lax.psum_scatter(grad_up, ('wide', 'narrow'), scatter_dimension=0, tiled=...]
    all_gather x6 -> x0, waiting for transfers between devices: 252 us -> none  [the longest x1 61.6 us: local(): lax.all_gather(keys.reshape(seq_count, local_rows, model_width), 'narrow'...]
    ppermute x0 -> x87, waiting for transfers between devices: none -> 160 us  [the longest x77 148 us: swap(): return lax.ppermute(values, axis, [(i, i ^ bits) for i in range(size)])]
    unnamed x14 -> x0, waiting for transfers between devices: 102 us -> none
    ppermute x0 -> x87, starting transfers between devices: none -> 99.4 us  [the longest x77 64.5 us: swap(): return lax.ppermute(values, axis, [(i, i ^ bits) for i in range(size)])]
    unnamed x2 -> x0, blocking collectives: 81 us -> none
    all_gather x1 -> x0, blocking collectives: 60 us -> none  [local(): lax.all_gather(position_table, ('wide', 'narrow'), axis=0, tiled=True)]
    gather x0 -> x15, local copies, waits for them, and re-layouts: none -> 48.7 us  [the longest x4 22.9 us: gather(): return jnp.take(whole, ranks, axis=0).reshape(-1, columns)]
  transfers between devices with their start and end apart: 13 -> 87, of which waited for: 11 -> 38; matrix products, arithmetic and copies ran while one was open for 15% -> 37% of each run, Pallas kernels for 0% -> 0%
where the time goes in v1:
time: 625 us; the launch traced here: 614 us
  waiting for transfers between devices  160 us (26%)
  matrix products  120 us (19%)
  local copies, waits for them, and re-layouts  119 us (19%)
  other arithmetic  113 us (18%)
  starting transfers between devices  99.4 us (16%)
    ppermute x77, waiting for transfers between devices, swap(): return lax.ppermute(values, axis, [(i, i ^ bits) for i in range(size)])  148 us
    ppermute x77, starting transfers between devices, swap(): return lax.ppermute(values, axis, [(i, i ^ bits) for i in range(size)])  64.5 us
    gather x4, local copies, waits for them, and re-layouts, gather(): return jnp.take(whole, ranks, axis=0).reshape(-1, columns)  22.9 us
    ppermute x6, starting transfers between devices, spread(): lax.ppermute(lax.dynamic_index_in_dim(values, turn ^ late, 0, keepdims=Fa...  22.2 us
    dot_general x5, matrix products, product_right(): lax.dot_general(left, right, (((1,), (1,)), ((), ())), preferred_element_...  22 us
    convert_element_type x1, other arithmetic, local(): grad_scores = (probabilities * (grad_probs - inner)).astype(bf16)  18.4 us
    dot_general x5, matrix products, product(): return jnp.dot(left, right, preferred_element_type=f32)  17.9 us
    gather x4, local copies, waits for them, and re-layouts, scatter(): blocks = jnp.take(blocks, jnp.arange(size) ^ wide, axis=0)  17.2 us
  transfers between devices with their start and end apart: 87, of which 38 were waited for; matrix products, arithmetic and copies ran while one was open for 37% of the time, Pallas kernels for 0%

profile of v1, /device:TPU:7, one launch (start us, length us, event | category | flops | bytes accessed | tf_op | source)
XLA Modules:
  0.0 613.9 jit_solution(3374916877762763231)
XLA Ops:
  7.7 5.4 collective-permute-start.4
  35.8 4.9 collective-permute-start
  48.9 4.0 collective-permute-start.42
  58.4 4.4 collective-permute-done.14
  64.2 11.2 %collective-permute-done.42 = bf16[256,768]{0,1:T(8,128)(2,1)} collective-permute-done((bf16[256,768]{0,1:T(8,128)(2,1)S(1)}, bf16[256,768]{0,1:T(8,128)(2,1)}, u32[]{:S(2)}, u32[]{:S(2)}) %collective-permute-start.42) | collective-permute-done | bytes 393248 | tf_op jit(solution)/shard_map/ppermute | solution.py:65
  98.8 3.9 collective-permute-done.23
  108.3 4.9 gather_fusion.1
  113.1 6.3 %copy.124 = bf16[768,2432]{0,1:T(8,128)(2,1)} copy(bf16[768,2432]{1,0:T(8,128)(2,1)} %bitcast.386) | data formatting | bytes 7471104 | tf_op jit(solution)/shard_map/jit(_take)/gather | solution.py:111
  124.5 4.8 fusion.27
  145.1 15.4 %fusion.108 = (f32[12,512]{1,0:T(8,128)}, f32[12,512,1024]{2,1,0:T(8,128)}) fusion(pred[512,1024]{1,0:T(8,128)(4,1)} %fusion.29, bf16[512,12,64]{0,2,1:T(8,128)(2,1)} %bitcast.404, bf16[1024,12,64]{0,2,1:T(8,128)(2,1)} %bitcast.396), kind=kOutput, calls=%fused_computation.367 | convolution fusion | flops 830473216 | bytes 28073984 | tf_op jit(solution)/shard_map/sub | solution.py:262
  160.5 11.9 %fusion.30 = bf16[12,64,512]{2,1,0:T(8,128)(2,1)} fusion(bf16[1024,12,64]{0,2,1:T(8,128)(2,1)} %bitcast.415, f32[12,512,1024]{2,1,0:T(8,128)} %get-tuple-element.205, f32[12,512]{1,0:T(8,128)} %get-tuple-element.204), kind=kOutput, calls=%fused_computation.120 | convolution fusion | flops 818282496 | bytes 27549696 | tf_op jit(solution)/shard_map/hqk,khd->qhd/dot_general | solution.py:264
  185.0 6.3 %gather_fusion.7 = bf16[8,96,3840]{2,1,0:T(8,128)(2,1)} fusion(bf16[8,96,3840]{2,1,0:T(8,128)(2,1)} %pad_maximum_fusion, s32[1024]{0:T(1024)} %get-tuple-element.216), kind=kCustom, calls=%fused_computation.1.clone | custom fusion | bytes 11796512 | tf_op jit(solution)/shard_map/jit(_take)/gather | solution.py:111
  200.2 6.6 %convolution_convert_fusion = bf16[3072,768]{1,0:T(8,128)(2,1)} fusion(bf16[256,768]{0,1:T(8,128)(2,1)S(1)} %copy-done.24, bf16[256,768]{0,1:T(8,128)(2,1)S(1)} %get-tuple-element.136, f32[512,3072]{1,0:T(8,128)S(1)} %fusion.20, f32[3072]{0:T(1024)S(1)} %copy-done.63), kind=kOutput, calls=%fused_computation.45 | convolution fusion | flops 2435579904 | bytes 11808768 | tf_op jit(solution)/shard_map/dot_general | solution.py:31
  206.8 5.5 gather_fusion.12
  215.8 4.2 collective-permute-done.77
  222.6 6.5 %collective-permute-done.79 = bf16[384,384]{1,0:T(8,128)(2,1)S(1)} collective-permute-done((bf16[384,384]{1,0:T(8,128)(2,1)S(1)}, bf16[384,384]{1,0:T(8,128)(2,1)S(1)}, u32[]{:S(2)}, u32[]{:S(2)}) %collective-permute-start.79) | collective-permute-done | bytes 294944 | tf_op jit(solution)/shard_map/ppermute | solution.py:40
  230.7 4.7 collective-permute-done.78
  238.3 6.4 %collective-permute-start.31 = (bf16[96,768]{1,0:T(8,128)(2,1)S(1)}, bf16[96,768]{1,0:T(8,128)(2,1)S(1)}, u32[]{:S(2)}, u32[]{:S(2)}) collective-permute-start(bf16[96,768]{1,0:T(8,128)(2,1)S(1)} %copy-done.48), channel_id=1, source_target_pairs={{0,3},{1,2},{2,1},{3,0},{4,7},{5,6},{6,5},{7,4},{8,11},{9,10},{10,... | collective-permute-start | bytes 442376 | tf_op jit(solution)/shard_map/ppermute | solution.py:40
  244.7 4.2 collective-permute-done.31
  248.9 7.7 %collective-permute-done.30 = bf16[96,768]{1,0:T(8,128)(2,1)S(1)} collective-permute-done((bf16[96,768]{1,0:T(8,128)(2,1)S(1)}, bf16[96,768]{1,0:T(8,128)(2,1)S(1)}, u32[]{:S(2)}, u32[]{:S(2)}) %collective-permute-start.30) | collective-permute-done | bytes 147488 | tf_op jit(solution)/shard_map/ppermute | solution.py:40
  266.3 3.7 collective-permute-done.37
  273.6 3.7 collective-permute-done.36
  277.2 6.4 %collective-permute-done.38 = bf16[384,384]{1,0:T(8,128)(2,1)} collective-permute-done((bf16[384,384]{1,0:T(8,128)(2,1)}, bf16[384,384]{1,0:T(8,128)(2,1)}, u32[]{:S(2)}, u32[]{:S(2)}) %collective-permute-start.38) | collective-permute-done | bytes 294944 | tf_op jit(solution)/shard_map/ppermute | solution.py:40
  285.1 3.6 collective-permute-start.39
  299.1 7.7 %collective-permute-done.85 = bf16[96,768]{1,0:T(8,128)(2,1)S(1)} collective-permute-done((bf16[96,768]{1,0:T(8,128)(2,1)S(1)}, bf16[96,768]{1,0:T(8,128)(2,1)S(1)}, u32[]{:S(2)}, u32[]{:S(2)}) %collective-permute-start.85) | collective-permute-done | bytes 147488 | tf_op jit(solution)/shard_map/ppermute | solution.py:40
  311.0 5.5 gather_fusion.9
  319.5 10.6 %convert_reduce_fusion = (f32[3072]{0:T(1024)}, bf16[512,3072]{1,0:T(8,128)(2,1)S(1)}) fusion(f32[512,3072]{1,0:T(8,128)} %copy-done.13, f32[3072]{0:T(1024)S(1)} %copy-done.64, bf16[3072,768]{1,0:T(8,128)(2,1)S(1)} %bitcast.398, bf16[256,768]{0,1:T(8,128)(2,1)S(1)} %copy-done.24, bf16[256,768]{0,1:T(8,128)(2,1)S(1)} %get-tuple-element.136), kind=kOutput, calls=%fused_computation.33 | convolution fusion | flops 2453664768 | bytes 14966784 | tf_op jit(solution)/shard_map/dot_general | solution.py:35
  330.1 4.4 fusion.111
  334.5 4.6 convolution_convert_fusion.1
  347.7 11.6 %fusion.12 = f32[12,64,1024]{2,1,0:T(8,128)} fusion(bf16[512,12,64]{0,2,1:T(8,128)(2,1)} %bitcast.426, f32[12,512,1024]{2,1,0:T(8,128)} %get-tuple-element.205, f32[12,512]{1,0:T(8,128)S(1)} %copy-done.52), kind=kOutput, calls=%fused_computation.35 | convolution fusion | flops 817889280 | bytes 29122560 | tf_op jit(solution)/shard_map/hqk,qhd->khd/dot_general | solution.py:305
  359.3 17.1 %multiply_reduce_fusion = (f32[12,512]{1,0:T(8,128)}, f32[12,512,1024]{2,1,0:T(8,128)}) fusion(f32[12,512,1024]{2,1,0:T(8,128)} %get-tuple-element.205, f32[12,512]{1,0:T(8,128)S(1)} %copy-done.52, bf16[512,12,64]{0,2,1:T(8,128)(2,1)} %bitcast.427, bf16[1024,12,64]{0,2,1:T(8,128)(2,1)S(1)} %bitcast.416), kind=kOutput, calls=%fused_computation.16 | convolution fusion | flops 824174592 | bytes 52740096 | tf_op jit(solution)/shard_map/qhd,khd->hqk/dot_general | solution.py:296
  376.5 7.6 %add_convert_fusion.3 = bf16[512,768]{0,1:T(8,128)(2,1)S(1)} fusion(f32[512,768]{0,1:T(8,128)S(1)} %get-tuple-element.207, bf16[3072,768]{1,0:T(8,128)(2,1)} %bitcast.399, f32[768]{0:T(1024)S(1)} %copy-done.76, f32[512,3072]{1,0:T(8,128)} %copy-done.13, f32[3072]{0:T(1024)S(1)} %copy-done.65), kind=kOutput, calls=%fused_computation.111 | convolution fusion | flops 2432827392 | bytes 13384704 | tf_op jit(solution)/shard_map/dot_general | solution.py:27
  387.5 4.6 collective-permute-start.41
  396.0 6.3 %gather_fusion.10 = bf16[8,96,3840]{2,1,0:T(8,128)(2,1)} fusion(bf16[8,96,3840]{2,1,0:T(8,128)(2,1)} %pad_maximum_fusion.1, s32[1024]{0:T(1024)} %get-tuple-element.216), kind=kCustom, calls=%fused_computation.5.clone | custom fusion | bytes 11796512 | tf_op jit(solution)/shard_map/jit(_take)/gather | solution.py:118
  405.6 18.4 %multiply_convert_fusion = bf16[12,512,1024]{2,1,0:T(8,128)(2,1)S(1)} fusion(f32[12,512,1024]{2,1,0:T(8,128)} %get-tuple-element.209, f32[12,512]{1,0:T(8,128)S(1)} %copy-done.54, f32[12,512,1024]{2,1,0:T(8,128)} %get-tuple-element.205, f32[12,512]{1,0:T(8,128)S(1)} %copy-done.53), kind=kLoop, calls=%fused_computation.15 | loop fusion | flops 25165824 | bytes 62963712 | tf_op jit(solution)/shard_map/convert_element_type | solution.py:298
  426.4 4.4 select_convert_fusion
  434.8 6.2 %multiply_convert_fusion.2 = bf16[12,64,512]{2,1,0:T(8,128)(2,1)} fusion(bf16[1024,12,64]{0,2,1:T(8,128)(2,1)} %bitcast.397, bf16[12,512,1024]{2,1,0:T(8,128)(2,1)S(1)} %multiply_convert_fusion), kind=kOutput, calls=%fused_computation.109 | convolution fusion | flops 806092800 | bytes 14942208 | tf_op jit(solution)/shard_map/hqk,khd->qhd/dot_general | solution.py:300
  449.6 4.3 add_convert_fusion
  454.0 3.9 fusion.110
  476.7 3.9 concatenate.209
  489.0 3.7 collective-permute-start.46
  514.4 7.5 %collective-permute-start.57 = (bf16[4,96,2304]{2,1,0:T(8,128)(2,1)}, bf16[4,96,2304]{2,1,0:T(8,128)(2,1)}, u32[]{:S(2)}, u32[]{:S(2)}) collective-permute-start(bf16[4,96,2304]{2,1,0:T(8,128)(2,1)} %slice_bitcast_fusion.4), channel_id=1, source_target_pairs={{0,4},{4,0},{8,12},{12,8},{16,20},{20,16},{24,28},{28,24},{1,5},{5... | collective-permute-start | bytes 5308424 | tf_op jit(solution)/shard_map/ppermute | solution.py:40
  525.8 3.5 fusion.16
  538.4 15.7 %collective-permute-done.69 = bf16[96,1920]{1,0:T(8,128)(2,1)S(1)} collective-permute-done((bf16[96,1920]{1,0:T(8,128)(2,1)S(1)}, bf16[96,1920]{1,0:T(8,128)(2,1)S(1)}, u32[]{:S(2)}, u32[]{:S(2)}) %collective-permute-start.69) | collective-permute-done | bytes 368672 | tf_op jit(solution)/shard_map/ppermute | solution.py:40
  554.2 4.6 collective-permute-done.58
  561.2 14.6 %collective-permute-done.70 = bf16[96,1920]{1,0:T(8,128)(2,1)S(1)} collective-permute-done((bf16[96,1920]{1,0:T(8,128)(2,1)S(1)}, bf16[96,1920]{1,0:T(8,128)(2,1)S(1)}, u32[]{:S(2)}, u32[]{:S(2)}) %collective-permute-start.70) | collective-permute-done | bytes 368672 | tf_op jit(solution)/shard_map/ppermute | solution.py:40
  591.7 4.5 collective-permute-done.65
  600.8 11.4 %collective-permute-done.75 = bf16[24,3840]{1,0:T(8,128)(2,1)S(1)} collective-permute-done((bf16[24,3840]{1,0:T(8,128)(2,1)S(1)}, bf16[24,3840]{1,0:T(8,128)(2,1)S(1)}, u32[]{:S(2)}, u32[]{:S(2)}) %collective-permute-start.75) | collective-permute-done | bytes 184352 | tf_op jit(solution)/shard_map/ppermute | solution.py:40
  (527 shorter events, 278.2 us)
Async XLA Ops:
  3.6 42.3 %collective-permute-start.20 = (bf16[24,3840]{1,0:T(8,128)(2,1)}, bf16[24,3840]{1,0:T(8,128)(2,1)}, u32[]{:S(2)}, u32[]{:S(2)}) collective-permute-start(bf16[24,3840]{1,0:T(8,128)(2,1)} %constant_dynamic-update-slice_fusion), channel_id=1, source_target_pairs={{0,3},{1,2},{2,1},{3,0},{4,7},{5,6},{6,5},{7,4},{8,11},{9,10},{10,... | collective-permute-start | bytes 552968 | tf_op jit(solution)/shard_map/ppermute | solution.py:40
  6.9 41.9 %collective-permute-start.19 = (bf16[24,3840]{1,0:T(8,128)(2,1)}, bf16[24,3840]{1,0:T(8,128)(2,1)}, u32[]{:S(2)}, u32[]{:S(2)}) collective-permute-start(bf16[24,3840]{1,0:T(8,128)(2,1)} %constant_dynamic-update-slice_fusion), channel_id=1, source_target_pairs={{0,2},{1,3},{2,0},{3,1},{4,6},{5,7},{6,4},{7,5},{8,10},{9,11},{10,... | collective-permute-start | bytes 552968 | tf_op jit(solution)/shard_map/ppermute | solution.py:40
  7.7 18.9 %collective-permute-start.4 = (s32[256]{0:T(256)S(1)}, s32[256]{0:T(256)S(1)}, u32[]{:S(2)}, u32[]{:S(2)}) collective-permute-start(s32[256]{0:T(256)S(1)} %bitcast.467), channel_id=1, source_target_pairs={{0,0},{1,4},{2,5},{3,1},{4,2},{5,6},{6,7},{7,3},{8,8},{9,12},{10,1... | collective-permute-start | bytes 3080 | tf_op jit(solution)/shard_map/ppermute | solution.py:65
  13.1 14.8 %collective-permute-start.3 = (s32[256]{0:T(256)S(1)}, s32[256]{0:T(256)S(1)}, u32[]{:S(2)}, u32[]{:S(2)}) collective-permute-start(s32[256]{0:T(256)S(1)} %bitcast.466), channel_id=1, source_target_pairs={{0,1},{1,5},{2,4},{3,0},{4,3},{5,7},{6,6},{7,2},{8,9},{9,13},{10,1... | collective-permute-start | bytes 3080 | tf_op jit(solution)/shard_map/ppermute | solution.py:65
  35.3 17.6 %collective-permute-start.18 = (bf16[24,3840]{1,0:T(8,128)(2,1)}, bf16[24,3840]{1,0:T(8,128)(2,1)S(1)}, u32[]{:S(2)}, u32[]{:S(2)}) collective-permute-start(bf16[24,3840]{1,0:T(8,128)(2,1)} %constant_dynamic-update-slice_fusion), channel_id=1, source_target_pairs={{0,1},{1,0},{2,3},{3,2},{4,5},{5,4},{6,7},{7,6},{8,9},{9,8},{10,11... | collective-permute-start | bytes 552968 | tf_op jit(solution)/shard_map/ppermute | solution.py:40
  35.8 19.5 %collective-permute-start = (bf16[256,768]{0,1:T(8,128)(2,1)S(1)}, bf16[256,768]{0,1:T(8,128)(2,1)}, u32[]{:S(2)}, u32[]{:S(2)}) collective-permute-start(bf16[256,768]{0,1:T(8,128)(2,1)S(1)} %bitcast.431), channel_id=1, source_target_pairs={{0,1},{1,5},{2,4},{3,0},{4,3},{5,7},{6,6},{7,2},{8,9},{9,13},{10,1... | collective-permute-start | bytes 1179656 | tf_op jit(solution)/shard_map/ppermute | solution.py:65
  40.7 15.4 %collective-permute-start.1 = (bf16[256,768]{0,1:T(8,128)(2,1)S(1)}, bf16[256,768]{0,1:T(8,128)(2,1)}, u32[]{:S(2)}, u32[]{:S(2)}) collective-permute-start(bf16[256,768]{0,1:T(8,128)(2,1)S(1)} %bitcast.430), channel_id=1, source_target_pairs={{0,0},{1,4},{2,5},{3,1},{4,2},{5,6},{6,7},{7,3},{8,8},{9,12},{10,1... | collective-permute-start | bytes 1179656 | tf_op jit(solution)/shard_map/ppermute | solution.py:65
  45.9 18.1 %collective-permute-start.43 = (bf16[256,768]{0,1:T(8,128)(2,1)S(1)}, bf16[256,768]{0,1:T(8,128)(2,1)}, u32[]{:S(2)}, u32[]{:S(2)}) collective-permute-start(bf16[256,768]{0,1:T(8,128)(2,1)S(1)} %bitcast.429), channel_id=1, source_target_pairs={{0,0},{1,4},{2,5},{3,1},{4,2},{5,6},{6,7},{7,3},{8,8},{9,12},{10,1... | collective-permute-start | bytes 1179656 | tf_op jit(solution)/shard_map/ppermute | solution.py:65
  48.9 26.6 %collective-permute-start.42 = (bf16[256,768]{0,1:T(8,128)(2,1)S(1)}, bf16[256,768]{0,1:T(8,128)(2,1)}, u32[]{:S(2)}, u32[]{:S(2)}) collective-permute-start(bf16[256,768]{0,1:T(8,128)(2,1)S(1)} %bitcast.428), channel_id=1, source_target_pairs={{0,1},{1,5},{2,4},{3,0},{4,3},{5,7},{6,6},{7,2},{8,9},{9,13},{10,1... | collective-permute-start | bytes 1179656 | tf_op jit(solution)/shard_map/ppermute | solution.py:65
  52.9 24.7 %collective-permute-start.13 = (bf16[96,1152]{1,0:T(8,128)(2,1)}, bf16[96,1152]{1,0:T(8,128)(2,1)}, u32[]{:S(2)}, u32[]{:S(2)}) collective-permute-start(bf16[96,1152]{1,0:T(8,128)(2,1)} %get-tuple-element.167), channel_id=1, source_target_pairs={{0,8},{4,12},{8,0},{12,4},{16,24},{20,28},{24,16},{28,20},{1,9},{5... | collective-permute-start | bytes 663560 | tf_op jit(solution)/shard_map/ppermute | solution.py:40
  56.1 22.8 %collective-permute-start.9 = (bf16[96,1280]{1,0:T(8,128)(2,1)S(1)}, bf16[96,1280]{1,0:T(8,128)(2,1)S(1)}, u32[]{:S(2)}, u32[]{:S(2)}) collective-permute-start(bf16[96,1280]{1,0:T(8,128)(2,1)S(1)} %copy-done.46), channel_id=1, source_target_pairs={{0,8},{4,12},{8,0},{12,4},{16,24},{20,28},{24,16},{28,20},{1,9},{5... | collective-permute-start | bytes 737288 | tf_op jit(solution)/shard_map/ppermute | solution.py:40
  62.8 23.8 %collective-permute-start.25 = (bf16[96,1920]{1,0:T(8,128)(2,1)S(1)}, bf16[96,1920]{1,0:T(8,128)(2,1)S(1)}, u32[]{:S(2)}, u32[]{:S(2)}) collective-permute-start(bf16[96,1920]{1,0:T(8,128)(2,1)S(1)} %get-tuple-element.155), channel_id=1, source_target_pairs={{0,8},{4,12},{8,0},{12,4},{16,24},{20,28},{24,16},{28,20},{1,9},{5... | collective-permute-start | bytes 1105928 | tf_op jit(solution)/shard_map/ppermute | solution.py:40
  64.0 15.2 %collective-permute-start.26 = (bf16[96,1920]{1,0:T(8,128)(2,1)S(1)}, bf16[96,1920]{1,0:T(8,128)(2,1)S(1)}, u32[]{:S(2)}, u32[]{:S(2)}) collective-permute-start(bf16[96,1920]{1,0:T(8,128)(2,1)S(1)} %get-tuple-element.155), channel_id=1, source_target_pairs={{0,16},{4,20},{8,24},{12,28},{16,0},{20,4},{24,8},{28,12},{1,17},{... | collective-permute-start | bytes 1105928 | tf_op jit(solution)/shard_map/ppermute | solution.py:40
  77.6 12.3 %collective-permute-start.21 = (bf16[96,1920]{1,0:T(8,128)(2,1)S(1)}, bf16[96,1920]{1,0:T(8,128)(2,1)S(1)}, u32[]{:S(2)}, u32[]{:S(2)}) collective-permute-start(bf16[96,1920]{1,0:T(8,128)(2,1)S(1)} %get-tuple-element.156), channel_id=1, source_target_pairs={{0,8},{4,12},{8,0},{12,4},{16,24},{20,28},{24,16},{28,20},{1,9},{5... | collective-permute-start | bytes 1105928 | tf_op jit(solution)/shard_map/ppermute | solution.py:40
  79.2 12.4 %collective-permute-start.11 = (bf16[96,1280]{1,0:T(8,128)(2,1)S(1)}, bf16[96,1280]{1,0:T(8,128)(2,1)S(1)}, u32[]{:S(2)}, u32[]{:S(2)}) collective-permute-start(bf16[96,1280]{1,0:T(8,128)(2,1)S(1)} %collective-permute-done.9), channel_id=1, source_target_pairs={{0,16},{4,20},{8,24},{12,28},{16,0},{20,4},{24,8},{28,12},{1,17},{... | collective-permute-start | bytes 737288 | tf_op jit(solution)/shard_map/ppermute | solution.py:40
  86.3 12.5 %collective-permute-start.22 = (bf16[96,1920]{1,0:T(8,128)(2,1)S(1)}, bf16[96,1920]{1,0:T(8,128)(2,1)S(1)}, u32[]{:S(2)}, u32[]{:S(2)}) collective-permute-start(bf16[96,1920]{1,0:T(8,128)(2,1)S(1)} %get-tuple-element.156), channel_id=1, source_target_pairs={{0,16},{4,20},{8,24},{12,28},{16,0},{20,4},{24,8},{28,12},{1,17},{... | collective-permute-start | bytes 1105928 | tf_op jit(solution)/shard_map/ppermute | solution.py:40
  86.6 18.1 %collective-permute-start.2 = (bf16[2,256,768]{1,2,0:T(8,128)(2,1)S(1)}, bf16[2,256,768]{1,2,0:T(8,128)(2,1)S(1)}, u32[]{:S(2)}, u32[]{:S(2)}) collective-permute-start(bf16[2,256,768]{1,2,0:T(8,128)(2,1)S(1)} %pad_maximum_fusion.18), channel_id=1, source_target_pairs={{0,4},{4,0},{8,12},{12,8},{16,20},{20,16},{24,28},{28,24},{1,5},{5... | collective-permute-start | bytes 2359304 | tf_op jit(solution)/shard_map/ppermute | solution.py:40
  90.0 12.8 %collective-permute-start.23 = (bf16[96,1920]{1,0:T(8,128)(2,1)S(1)}, bf16[96,1920]{1,0:T(8,128)(2,1)S(1)}, u32[]{:S(2)}, u32[]{:S(2)}) collective-permute-start(bf16[96,1920]{1,0:T(8,128)(2,1)S(1)} %collective-permute-done.21), channel_id=1, source_target_pairs={{0,16},{4,20},{8,24},{12,28},{16,0},{20,4},{24,8},{28,12},{1,17},{... | collective-permute-start | bytes 1105928 | tf_op jit(solution)/shard_map/ppermute | solution.py:40
  91.6 14.0 %collective-permute-start.16 = (bf16[4,96,1152]{2,1,0:T(8,128)(2,1)S(1)}, bf16[4,96,1152]{2,1,0:T(8,128)(2,1)S(1)}, u32[]{:S(2)}, u32[]{:S(2)}) collective-permute-start(bf16[4,96,1152]{2,1,0:T(8,128)(2,1)S(1)} %get-tuple-element.129), channel_id=1, source_target_pairs={{0,4},{4,0},{8,12},{12,8},{16,20},{20,16},{24,28},{28,24},{1,5},{5... | collective-permute-start | bytes 2654216 | tf_op jit(solution)/shard_map/ppermute | solution.py:40
  98.8 78.5 %collective-permute-start.28 = (bf16[4,96,1920]{2,1,0:T(8,128)(2,1)}, bf16[4,96,1920]{2,1,0:T(8,128)(2,1)}, u32[]{:S(2)}, u32[]{:S(2)}) collective-permute-start(bf16[4,96,1920]{2,1,0:T(8,128)(2,1)} %get-tuple-element.121), channel_id=1, source_target_pairs={{0,4},{4,0},{8,12},{12,8},{16,20},{20,16},{24,28},{28,24},{1,5},{5... | collective-permute-start | bytes 4423688 | tf_op jit(solution)/shard_map/ppermute | solution.py:40
  104.7 74.6 %collective-permute-start.24 = (bf16[4,96,1920]{2,1,0:T(8,128)(2,1)}, bf16[4,96,1920]{2,1,0:T(8,128)(2,1)}, u32[]{:S(2)}, u32[]{:S(2)}) collective-permute-start(bf16[4,96,1920]{2,1,0:T(8,128)(2,1)} %get-tuple-element.119), channel_id=1, source_target_pairs={{0,4},{4,0},{8,12},{12,8},{16,20},{20,16},{24,28},{28,24},{1,5},{5... | collective-permute-start | bytes 4423688 | tf_op jit(solution)/shard_map/ppermute | solution.py:40
  221.1 14.3 %collective-permute-start.78 = (bf16[384,384]{1,0:T(8,128)(2,1)S(1)}, bf16[384,384]{1,0:T(8,128)(2,1)S(1)}, u32[]{:S(2)}, u32[]{:S(2)}) collective-permute-start(bf16[384,384]{1,0:T(8,128)(2,1)S(1)} %get-tuple-element.106), channel_id=1, source_target_pairs={{0,16},{4,20},{8,24},{12,28},{16,0},{20,4},{24,8},{28,12},{1,17},{... | collective-permute-start | bytes 884744 | tf_op jit(solution)/shard_map/ppermute | solution.py:40
  222.3 13.1 %collective-permute-start.82 = (bf16[384,384]{1,0:T(8,128)(2,1)S(1)}, bf16[384,384]{1,0:T(8,128)(2,1)S(1)}, u32[]{:S(2)}, u32[]{:S(2)}) collective-permute-start(bf16[384,384]{1,0:T(8,128)(2,1)S(1)} %get-tuple-element.107), channel_id=1, source_target_pairs={{0,8},{4,12},{8,0},{12,4},{16,24},{20,28},{24,16},{28,20},{1,9},{5... | collective-permute-start | bytes 884744 | tf_op jit(solution)/shard_map/ppermute | solution.py:40
  229.5 28.8 %collective-permute-start.81 = (bf16[384,384]{1,0:T(8,128)(2,1)S(1)}, bf16[384,384]{1,0:T(8,128)(2,1)}, u32[]{:S(2)}, u32[]{:S(2)}) collective-permute-start(bf16[384,384]{1,0:T(8,128)(2,1)S(1)} %get-tuple-element.108), channel_id=1, source_target_pairs={{0,8},{4,12},{8,0},{12,4},{16,24},{20,28},{24,16},{28,20},{1,9},{5... | collective-permute-start | bytes 884744 | tf_op jit(solution)/shard_map/ppermute | solution.py:40
  236.6 21.6 %collective-permute-start.83 = (bf16[384,384]{1,0:T(8,128)(2,1)}, bf16[384,384]{1,0:T(8,128)(2,1)}, u32[]{:S(2)}, u32[]{:S(2)}) collective-permute-start(bf16[384,384]{1,0:T(8,128)(2,1)} %get-tuple-element.105), channel_id=1, source_target_pairs={{0,16},{4,20},{8,24},{12,28},{16,0},{20,4},{24,8},{28,12},{1,17},{... | collective-permute-start | bytes 884744 | tf_op jit(solution)/shard_map/ppermute | solution.py:40
  270.1 13.6 %collective-permute-start.38 = (bf16[384,384]{1,0:T(8,128)(2,1)}, bf16[384,384]{1,0:T(8,128)(2,1)}, u32[]{:S(2)}, u32[]{:S(2)}) collective-permute-start(bf16[384,384]{1,0:T(8,128)(2,1)} %collective-permute-done.37), channel_id=1, source_target_pairs={{0,8},{4,12},{8,0},{12,4},{16,24},{20,28},{24,16},{28,20},{1,9},{5... | collective-permute-start | bytes 884744 | tf_op jit(solution)/shard_map/ppermute | solution.py:40
  270.3 18.5 %collective-permute-start.33 = (bf16[384,384]{1,0:T(8,128)(2,1)}, bf16[384,384]{1,0:T(8,128)(2,1)}, u32[]{:S(2)}, u32[]{:S(2)}) collective-permute-start(bf16[384,384]{1,0:T(8,128)(2,1)} %get-tuple-element.163), channel_id=1, source_target_pairs={{0,16},{4,20},{8,24},{12,28},{16,0},{20,4},{24,8},{28,12},{1,17},{... | collective-permute-start | bytes 884744 | tf_op jit(solution)/shard_map/ppermute | solution.py:40
  271.5 17.2 %collective-permute-start.34 = (bf16[384,384]{1,0:T(8,128)(2,1)S(1)}, bf16[384,384]{1,0:T(8,128)(2,1)}, u32[]{:S(2)}, u32[]{:S(2)}) collective-permute-start(bf16[384,384]{1,0:T(8,128)(2,1)S(1)} %collective-permute-done.32), channel_id=1, source_target_pairs={{0,16},{4,20},{8,24},{12,28},{16,0},{20,4},{24,8},{28,12},{1,17},{... | collective-permute-start | bytes 884744 | tf_op jit(solution)/shard_map/ppermute | solution.py:40
  285.1 22.4 %collective-permute-start.39 = (bf16[4,384,384]{2,1,0:T(8,128)(2,1)S(1)}, bf16[4,384,384]{2,1,0:T(8,128)(2,1)S(1)}, u32[]{:S(2)}, u32[]{:S(2)}) collective-permute-start(bf16[4,384,384]{2,1,0:T(8,128)(2,1)S(1)} %get-tuple-element.125), channel_id=1, source_target_pairs={{0,4},{4,0},{8,12},{12,8},{16,20},{20,16},{24,28},{28,24},{1,5},{5... | collective-permute-start | bytes 3538952 | tf_op jit(solution)/shard_map/ppermute | solution.py:40
  290.1 18.0 %collective-permute-start.35 = (bf16[4,384,384]{2,1,0:T(8,128)(2,1)S(1)}, bf16[4,384,384]{2,1,0:T(8,128)(2,1)S(1)}, u32[]{:S(2)}, u32[]{:S(2)}) collective-permute-start(bf16[4,384,384]{2,1,0:T(8,128)(2,1)S(1)} %get-tuple-element.123), channel_id=1, source_target_pairs={{0,4},{4,0},{8,12},{12,8},{16,20},{20,16},{24,28},{28,24},{1,5},{5... | collective-permute-start | bytes 3538952 | tf_op jit(solution)/shard_map/ppermute | solution.py:40
  292.0 14.8 %collective-permute-start.85 = (bf16[96,768]{1,0:T(8,128)(2,1)S(1)}, bf16[96,768]{1,0:T(8,128)(2,1)S(1)}, u32[]{:S(2)}, u32[]{:S(2)}) collective-permute-start(bf16[96,768]{1,0:T(8,128)(2,1)S(1)} %get-tuple-element.159), channel_id=1, source_target_pairs={{0,2},{1,3},{2,0},{3,1},{4,6},{5,7},{6,4},{7,5},{8,10},{9,11},{10,... | collective-permute-start | bytes 442376 | tf_op jit(solution)/shard_map/ppermute | solution.py:40
  385.1 60.3 %collective-permute-start.40 = (bf16[256,768]{0,1:T(8,128)(2,1)}, bf16[256,768]{0,1:T(8,128)(2,1)S(1)}, u32[]{:S(2)}, u32[]{:S(2)}) collective-permute-start(bf16[256,768]{0,1:T(8,128)(2,1)} %get-tuple-element.142), channel_id=1, source_target_pairs={{1,0},{5,1},{4,2},{0,3},{3,4},{7,5},{6,6},{2,7},{9,8},{13,9},{12,1... | collective-permute-start | bytes 1179656 | tf_op jit(solution)/shard_map/ppermute | solution.py:80
  387.5 57.8 %collective-permute-start.41 = (bf16[256,768]{0,1:T(8,128)(2,1)}, bf16[256,768]{0,1:T(8,128)(2,1)}, u32[]{:S(2)}, u32[]{:S(2)}) collective-permute-start(bf16[256,768]{0,1:T(8,128)(2,1)} %get-tuple-element.143), channel_id=1, source_target_pairs={{0,0},{4,1},{5,2},{1,3},{2,4},{6,5},{7,6},{3,7},{8,8},{12,9},{13,1... | collective-permute-start | bytes 1179656 | tf_op jit(solution)/shard_map/ppermute | solution.py:80
  430.8 18.8 %collective-permute-start.44 = (bf16[512,1536]{0,1:T(8,128)(2,1)}, bf16[512,1536]{0,1:T(8,128)(2,1)}, u32[]{:S(2)}, u32[]{:S(2)}) collective-permute-start(bf16[512,1536]{0,1:T(8,128)(2,1)} %select_convert_fusion), channel_id=1, source_target_pairs={{0,4},{4,0},{8,12},{12,8},{16,20},{20,16},{24,28},{28,24},{1,5},{5... | collective-permute-start | bytes 4718600 | tf_op jit(solution)/shard_map/ppermute | solution.py:40
  445.3 80.5 %collective-permute-start.67 = (bf16[4,96,3840]{2,1,0:T(8,128)(2,1)}, bf16[4,96,3840]{2,1,0:T(8,128)(2,1)}, u32[]{:S(2)}, u32[]{:S(2)}) collective-permute-start(bf16[4,96,3840]{2,1,0:T(8,128)(2,1)} %slice_bitcast_fusion), channel_id=1, source_target_pairs={{0,4},{4,0},{8,12},{12,8},{16,20},{20,16},{24,28},{28,24},{1,5},{5... | collective-permute-start | bytes 8847368 | tf_op jit(solution)/shard_map/ppermute | solution.py:40
  487.1 36.3 %collective-permute-start.45 = (bf16[256,768]{0,1:T(8,128)(2,1)}, bf16[256,768]{0,1:T(8,128)(2,1)}, u32[]{:S(2)}, u32[]{:S(2)}) collective-permute-start(bf16[256,768]{0,1:T(8,128)(2,1)} %get-tuple-element.134), channel_id=1, source_target_pairs={{1,0},{5,1},{4,2},{0,3},{3,4},{7,5},{6,6},{2,7},{9,8},{13,9},{12,1... | collective-permute-start | bytes 1179656 | tf_op jit(solution)/shard_map/ppermute | solution.py:80
  489.0 34.4 %collective-permute-start.46 = (bf16[256,768]{0,1:T(8,128)(2,1)}, bf16[256,768]{0,1:T(8,128)(2,1)}, u32[]{:S(2)}, u32[]{:S(2)}) collective-permute-start(bf16[256,768]{0,1:T(8,128)(2,1)} %get-tuple-element.135), channel_id=1, source_target_pairs={{0,0},{4,1},{5,2},{1,3},{2,4},{6,5},{7,6},{3,7},{8,8},{12,9},{13,1... | collective-permute-start | bytes 1179656 | tf_op jit(solution)/shard_map/ppermute | solution.py:80
  514.4 15.0 %collective-permute-start.57 = (bf16[4,96,2304]{2,1,0:T(8,128)(2,1)}, bf16[4,96,2304]{2,1,0:T(8,128)(2,1)}, u32[]{:S(2)}, u32[]{:S(2)}) collective-permute-start(bf16[4,96,2304]{2,1,0:T(8,128)(2,1)} %slice_bitcast_fusion.4), channel_id=1, source_target_pairs={{0,4},{4,0},{8,12},{12,8},{16,20},{20,16},{24,28},{28,24},{1,5},{5... | collective-permute-start | bytes 5308424 | tf_op jit(solution)/shard_map/ppermute | solution.py:40
  532.7 27.8 %collective-permute-start.68 = (bf16[96,1920]{1,0:T(8,128)(2,1)S(1)}, bf16[96,1920]{1,0:T(8,128)(2,1)S(1)}, u32[]{:S(2)}, u32[]{:S(2)}) collective-permute-start(bf16[96,1920]{1,0:T(8,128)(2,1)S(1)} %get-tuple-element.100), channel_id=1, source_target_pairs={{0,16},{4,20},{8,24},{12,28},{16,0},{20,4},{24,8},{28,12},{1,17},{... | collective-permute-start | bytes 1105928 | tf_op jit(solution)/shard_map/ppermute | solution.py:40
  533.9 27.3 %collective-permute-start.72 = (bf16[96,1920]{1,0:T(8,128)(2,1)S(1)}, bf16[96,1920]{1,0:T(8,128)(2,1)S(1)}, u32[]{:S(2)}, u32[]{:S(2)}) collective-permute-start(bf16[96,1920]{1,0:T(8,128)(2,1)S(1)} %get-tuple-element.101), channel_id=1, source_target_pairs={{0,8},{4,12},{8,0},{12,4},{16,24},{20,28},{24,16},{28,20},{1,9},{5... | collective-permute-start | bytes 1105928 | tf_op jit(solution)/shard_map/ppermute | solution.py:40
  534.2 19.9 %collective-permute-start.69 = (bf16[96,1920]{1,0:T(8,128)(2,1)S(1)}, bf16[96,1920]{1,0:T(8,128)(2,1)S(1)}, u32[]{:S(2)}, u32[]{:S(2)}) collective-permute-start(bf16[96,1920]{1,0:T(8,128)(2,1)S(1)} %get-tuple-element.103), channel_id=1, source_target_pairs={{0,16},{4,20},{8,24},{12,28},{16,0},{20,4},{24,8},{28,12},{1,17},{... | collective-permute-start | bytes 1105928 | tf_op jit(solution)/shard_map/ppermute | solution.py:40
  534.7 24.1 %collective-permute-start.58 = (bf16[96,1152]{1,0:T(8,128)(2,1)S(1)}, bf16[96,1152]{1,0:T(8,128)(2,1)S(1)}, u32[]{:S(2)}, u32[]{:S(2)}) collective-permute-start(bf16[96,1152]{1,0:T(8,128)(2,1)S(1)} %get-tuple-element.112), channel_id=1, source_target_pairs={{0,16},{4,20},{8,24},{12,28},{16,0},{20,4},{24,8},{28,12},{1,17},{... | collective-permute-start | bytes 663560 | tf_op jit(solution)/shard_map/ppermute | solution.py:40
  538.3 20.5 %collective-permute-start.62 = (bf16[96,1152]{1,0:T(8,128)(2,1)S(1)}, bf16[96,1152]{1,0:T(8,128)(2,1)S(1)}, u32[]{:S(2)}, u32[]{:S(2)}) collective-permute-start(bf16[96,1152]{1,0:T(8,128)(2,1)S(1)} %get-tuple-element.113), channel_id=1, source_target_pairs={{0,8},{4,12},{8,0},{12,4},{16,24},{20,28},{24,16},{28,20},{1,9},{5... | collective-permute-start | bytes 663560 | tf_op jit(solution)/shard_map/ppermute | solution.py:40
  558.8 27.9 %collective-permute-start.71 = (bf16[96,1920]{1,0:T(8,128)(2,1)}, bf16[96,1920]{1,0:T(8,128)(2,1)}, u32[]{:S(2)}, u32[]{:S(2)}) collective-permute-start(bf16[96,1920]{1,0:T(8,128)(2,1)} %get-tuple-element.102), channel_id=1, source_target_pairs={{0,8},{4,12},{8,0},{12,4},{16,24},{20,28},{24,16},{28,20},{1,9},{5... | collective-permute-start | bytes 1105928 | tf_op jit(solution)/shard_map/ppermute | solution.py:40
  558.8 17.0 %collective-permute-start.70 = (bf16[96,1920]{1,0:T(8,128)(2,1)S(1)}, bf16[96,1920]{1,0:T(8,128)(2,1)S(1)}, u32[]{:S(2)}, u32[]{:S(2)}) collective-permute-start(bf16[96,1920]{1,0:T(8,128)(2,1)S(1)} %fusion.40), channel_id=1, source_target_pairs={{0,8},{4,12},{8,0},{12,4},{16,24},{20,28},{24,16},{28,20},{1,9},{5... | collective-permute-start | bytes 1105928 | tf_op jit(solution)/shard_map/ppermute | solution.py:40
  560.3 20.3 %collective-permute-start.61 = (bf16[96,1152]{1,0:T(8,128)(2,1)S(1)}, bf16[96,1152]{1,0:T(8,128)(2,1)S(1)}, u32[]{:S(2)}, u32[]{:S(2)}) collective-permute-start(bf16[96,1152]{1,0:T(8,128)(2,1)S(1)} %get-tuple-element.114), channel_id=1, source_target_pairs={{0,8},{4,12},{8,0},{12,4},{16,24},{20,28},{24,16},{28,20},{1,9},{5... | collective-permute-start | bytes 663560 | tf_op jit(solution)/shard_map/ppermute | solution.py:40
  560.5 20.0 %collective-permute-start.63 = (bf16[96,1152]{1,0:T(8,128)(2,1)S(1)}, bf16[96,1152]{1,0:T(8,128)(2,1)S(1)}, u32[]{:S(2)}, u32[]{:S(2)}) collective-permute-start(bf16[96,1152]{1,0:T(8,128)(2,1)S(1)} %get-tuple-element.111), channel_id=1, source_target_pairs={{0,16},{4,20},{8,24},{12,28},{16,0},{20,4},{24,8},{28,12},{1,17},{... | collective-permute-start | bytes 663560 | tf_op jit(solution)/shard_map/ppermute | solution.py:40
  591.6 20.6 %collective-permute-start.75 = (bf16[24,3840]{1,0:T(8,128)(2,1)S(1)}, bf16[24,3840]{1,0:T(8,128)(2,1)S(1)}, u32[]{:S(2)}, u32[]{:S(2)}) collective-permute-start(bf16[24,3840]{1,0:T(8,128)(2,1)S(1)} %get-tuple-element.152), channel_id=1, source_target_pairs={{0,2},{1,3},{2,0},{3,1},{4,6},{5,7},{6,4},{7,5},{8,10},{9,11},{10,... | collective-permute-start | bytes 552968 | tf_op jit(solution)/shard_map/ppermute | solution.py:40
  (126 other events, 1469.4 us)

commit v2 on v1

v2 whole, which is shorter than its diff:
```python
import functools

import jax
import jax.numpy as jnp
from jax import lax
from jax.experimental import pallas as pl
from jax.experimental.pallas import tpu as pltpu
from jax.sharding import PartitionSpec as P

HEADS = 12
PLACES = 4
epsilon = 1e-05
masked_score = -1e30

f32 = jnp.float32
bf16 = jnp.bfloat16
MIB = 1 << 20
QUERY_BIAS, VALUE_BIAS, OUTPUT_BIAS, GAIN_ONE, SHIFT_ONE, DOWN_BIAS, GAIN_TWO, SHIFT_TWO = range(8)
SMALL = 128


def dot(left, right):
    return jnp.dot(left, right, preferred_element_type=f32)


def dot_left(left, right):
    return lax.dot_general(left, right, (((0,), (0,)), ((), ())), preferred_element_type=f32)


def dot_right(left, right):
    return lax.dot_general(left, right, (((1,), (1,)), ((), ())), preferred_element_type=f32)


def call(kernel, outs, ins, args, scratch=(), grid=None, limit=48, cost=None):
    return pl.pallas_call(
        kernel,
        out_shape=[shape for shape, _ in outs],
        in_specs=[pl.BlockSpec(memory_space=pltpu.SMEM)] + list(ins),
        out_specs=[spec for _, spec in outs],
        scratch_shapes=list(scratch),
        **({"grid": grid} if grid else {}),
        compiler_params=pltpu.CompilerParams(vmem_limit_bytes=limit * MIB),
        cost_estimate=pl.CostEstimate(
            flops=int(cost[0]), bytes_accessed=int(cost[1]), transcendentals=0
        ),
    )(*args)


def shaped(shape, kind):
    return jax.ShapeDtypeStruct(shape, kind)


def vmem():
    return pl.BlockSpec(memory_space=pltpu.VMEM)


def anywhere():
    return pl.BlockSpec(memory_space=pl.ANY)


def normalise(values):
    average = jnp.mean(values, axis=-1, keepdims=True)
    centered = values - average
    variance = jnp.mean(centered * centered, axis=-1, keepdims=True)
    scale = lax.rsqrt(variance + epsilon)
    return centered * scale, scale


def norm_back(normal, scale, gain, grad):
    inner = grad * gain
    return scale * (
        inner
        - jnp.mean(inner, axis=-1, keepdims=True)
        - normal * jnp.mean(inner * normal, axis=-1, keepdims=True)
    )


def run_copies(copies):
    for copy in copies:
        copy.start()
    for copy in copies:
        copy.wait()


def arrange_kernel(info, a, b, c, d, out):
    place = info[2]
    for k, ref in enumerate((a, b, c, d)):
        out[:, k ^ place] = ref[...]


def arrange(info, pieces):
    two, rows, columns = pieces[0].shape
    return call(
        arrange_kernel,
        [(shaped((two, PLACES, rows, columns), bf16), vmem())],
        [vmem()] * PLACES,
        [info] + list(pieces),
        limit=16,
        cost=(0, 8 * two * rows * columns * 2),
    )[0]


def front_kernel(blocks, patches, info, *refs):
    tokens_in, refs = refs[:4], refs[4:]
    weights_in, refs = refs[:blocks], refs[blocks:]
    (q_out, k_out, v_out, start_out, normed_out, small_out, turned_out, seg_out, spot_out) = refs[:9]
    held, weight, sem = refs[9:]
    core, chip, place = info[0], info[1], info[2]
    block, columns = held.shape[1] - 16, weight.shape[1] - SMALL
    part = columns // 3
    rows = weight.shape[0] // blocks
    copies = []
    for i in range(4):
        side = core if i < 2 else 1 - core
        there = 2 * side + ((i % 2) ^ (place % 2))
        copies.append(pltpu.make_async_copy(tokens_in[i], held.at[there], sem.at[i]))
    for r in range(blocks):
        there = pl.ds(pl.multiple_of((r ^ chip) * rows, rows), rows)
        copies.append(pltpu.make_async_copy(weights_in[r], weight.at[there], sem.at[4 + r]))
    run_copies(copies)
    small = weight[:, columns:]
    small_out[...] = small
    turned_out[...] = small.astype(f32).T
    vector = lambda i: turned_out[patches + i : patches + i + 1, :]
    half = pl.ds(pl.multiple_of(core * part, 128), part)
    query_bias = turned_out[patches + QUERY_BIAS : patches + QUERY_BIAS + 1, half]
    value_bias = turned_out[patches + VALUE_BIAS : patches + VALUE_BIAS + 1, half]
    gain, shift = vector(GAIN_ONE), vector(SHIFT_ONE)
    extra = held[0, block : block + 16, :].astype(f32)
    width = extra.shape[1]
    segment = jnp.concatenate([extra[1:2, :], extra[2:3, : 4 * block - width]], axis=1)
    seg_out[...] = jnp.broadcast_to(segment, seg_out.shape)
    ids = lax.broadcasted_iota(jnp.int32, (SMALL, block), 0).astype(f32)
    for b in range(4):
        here = slice(b * block, (b + 1) * block)
        spot = held[b, block : block + 16, :].astype(f32)[0:1, :block]
        spot_out[:, here] = jnp.broadcast_to(spot, (8, block))
        one_hot = jnp.where(ids == spot, 1.0, 0.0).astype(bf16)
        embedded = lax.dot_general(
            one_hot, small, (((0,), (1,)), ((), ())), preferred_element_type=f32
        )
        start = held[b, :block, :].astype(f32) + embedded
        start_out[here, :] = start
        normal, _ = normalise(start)
        normed = (normal * gain + shift).astype(bf16)
        normed_out[here, :] = normed
        projected = dot(normed, weight[:, :columns])
        query = (projected[:, :part] + query_bias).astype(bf16).astype(f32) * 0.125
        q_out[here, :] = query.astype(bf16)
        k_out[here, :] = projected[:, part : 2 * part].astype(bf16)
        v_out[here, :] = (projected[:, 2 * part :] + value_bias).astype(bf16)


def front(info, tokens, weights, patches):
    blocks = len(weights)
    block, width = tokens[0].shape[0] - 16, tokens[0].shape[1]
    columns = weights[0].shape[1]
    part = (columns - SMALL) // 3
    rows = 4 * block
    return call(
        functools.partial(front_kernel, blocks, patches),
        [
            (shaped((rows, part), bf16), vmem()),
            (shaped((rows, part), bf16), vmem()),
            (shaped((rows, part), bf16), vmem()),
            (shaped((rows, width), f32), vmem()),
            (shaped((rows, width), bf16), vmem()),
            (shaped((width, SMALL), bf16), vmem()),
            (shaped((SMALL, width), f32), vmem()),
            (shaped((8, rows), f32), vmem()),
            (shaped((8, rows), f32), vmem()),
        ],
        [anywhere()] * (4 + blocks),
        [info] + list(tokens) + list(weights),
        scratch=[
            pltpu.VMEM((4, block + 16, width), bf16),
            pltpu.VMEM((width, columns), bf16),
            pltpu.SemaphoreType.DMA((4 + blocks,)),
        ],
        cost=(2 * rows * width * columns, 12 * MIB),
    )


def fill_bias(bias, seg):
    block = bias.shape[1]
    wide = seg[...]
    tall = jnp.broadcast_to(wide[0:1, :], (128, wide.shape[1])).T[:, 0:1]
    base = 0
    for b in range(4):
        many = (b + 1) * block
        key = lax.broadcasted_iota(jnp.int32, (many, block), 0)
        ask = lax.broadcasted_iota(jnp.int32, (many, block), 1) + b * block
        same = tall[:many] == wide[0:1, b * block : (b + 1) * block]
        bias[base : base + many, :] = jnp.where((key <= ask) & same, 0.0, masked_score)
        base += many


def turn(values):
    return values.astype(f32).T.astype(bf16)


def attend_kernel(info, q, k, v, seg, out, total, bias):
    block = bias.shape[1]

    @pl.when(pl.program_id(0) == 0)
    def _():
        fill_bias(bias, seg)

    turned_q, turned_v = turn(q[...]), turn(v[...])
    side = lax.broadcasted_iota(jnp.int32, (128, block), 0) // 64
    base = 0
    for b in range(4):
        many = (b + 1) * block
        here = slice(b * block, (b + 1) * block)
        mixed = []
        for h in range(2):
            ask = jnp.where(side == h, turned_q[:, here].astype(f32), 0.0).astype(bf16)
            scores = dot(k[:many, :], ask) + bias[base : base + many, :]
            top = jnp.max(scores, axis=0, keepdims=True)
            raised = jnp.exp(scores - top)
            mass = jnp.sum(raised, axis=0, keepdims=True)
            total[0, h : h + 1, here] = top + jnp.log(mass)
            part = dot(turned_v[64 * h : 64 * h + 64, :many], raised.astype(bf16))
            mixed.append(part * (1.0 / mass))
        out[here, :] = jnp.concatenate(mixed, axis=0).T.astype(bf16)
        base += many


def attend(info, q, k, v, seg):
    rows, part = q.shape
    pairs = part // 128
    column = pl.BlockSpec((rows, 128), lambda i: (0, i))
    whole = pl.BlockSpec(seg.shape, lambda i: (0, 0))
    return call(
        attend_kernel,
        [
            (shaped((rows, part), bf16), column),
            (shaped((pairs, 8, rows), f32), pl.BlockSpec((1, 8, rows), lambda i: (i, 0, 0))),
        ],
        [column, column, column, whole],
        [info, q, k, v, seg],
        scratch=[pltpu.VMEM((10 * rows // 4, rows // 4), f32)],
        grid=(pairs,),
        cost=(6 * rows * rows * part, 4 * MIB),
    )


def attend_back_kernel(info, q, k, v, o, g, total, seg, dq, dk, dv, bias, dk_sum, dv_sum):
    block = bias.shape[1]

    @pl.when(pl.program_id(0) == 0)
    def _():
        fill_bias(bias, seg)

    wide_g = g[...].astype(f32).T
    product = wide_g * o[...].astype(f32).T
    inner = [jnp.sum(product[64 * h : 64 * h + 64], axis=0, keepdims=True) for h in range(2)]
    turned_q, turned_k = turn(q[...]), turn(k[...])
    turned_g = wide_g.astype(bf16)
    side = lax.broadcasted_iota(jnp.int32, (128, block), 0) // 64
    flat = lax.broadcasted_iota(jnp.int32, (block, 128), 1) // 64
    dk_sum[...] = jnp.zeros_like(dk_sum)
    dv_sum[...] = jnp.zeros_like(dv_sum)
    base = 0
    for b in range(4):
        many = (b + 1) * block
        here = slice(b * block, (b + 1) * block)
        grads = []
        for h in range(2):
            ask = jnp.where(side == h, turned_q[:, here].astype(f32), 0.0).astype(bf16)
            ask_g = jnp.where(side == h, turned_g[:, here].astype(f32), 0.0).astype(bf16)
            scores = dot(k[:many, :], ask) + bias[base : base + many, :]
            probs = jnp.exp(scores - total[0, h : h + 1, here])
            grad_probs = dot(v[:many, :], ask_g)
            grad_scores = (probs * (grad_probs - inner[h][:, here])).astype(bf16)
            own_q = jnp.where(flat == h, q[here, :].astype(f32), 0.0).astype(bf16)
            own_g = jnp.where(flat == h, g[here, :].astype(f32), 0.0).astype(bf16)
            dv_sum[:many, :] += dot(probs.astype(bf16), own_g)
            dk_sum[:many, :] += dot(grad_scores, own_q)
            grads.append(dot(turned_k[64 * h : 64 * h + 64, :many], grad_scores))
        dq[here, :] = (jnp.concatenate(grads, axis=0).T * 0.125).astype(bf16)
        base += many
    dk[...] = dk_sum[...].astype(bf16)
    dv[...] = dv_sum[...].astype(bf16)


def attend_back(info, q, k, v, o, g, total, seg):
    rows, part = q.shape
    pairs = part // 128
    column = pl.BlockSpec((rows, 128), lambda i: (0, i))
    whole = pl.BlockSpec(seg.shape, lambda i: (0, 0))
    out = (shaped((rows, part), bf16), column)
    return call(
        attend_back_kernel,
        [out, out, out],
        [column] * 5 + [pl.BlockSpec((1, 8, rows), lambda i: (i, 0, 0)), whole],
        [info, q, k, v, o, g, total, seg],
        scratch=[
            pltpu.VMEM((10 * rows // 4, rows // 4), f32),
            pltpu.VMEM((rows, 128), f32),
            pltpu.VMEM((rows, 128), f32),
        ],
        grid=(pairs,),
        cost=(15 * rows * rows * part, 6 * MIB),
    )


def cotangent_copies(info, pieces, held, sems):
    core, place = info[0], info[2]
    copies = []
    for i in range(4):
        side = core if i < 2 else 1 - core
        there = 2 * side + ((i % 2) ^ (place % 2))
        copies.append(pltpu.make_async_copy(pieces[i], held.at[there], sems[i]))
    return copies


def gelu_parts(values):
    scale = 0.7978845608028654
    square = values * values
    slope = jnp.tanh(values * (scale + (scale * 0.044715) * square))
    half = 0.5 * (1.0 + slope)
    grad = half + 0.5 * values * (1.0 - slope * slope) * (
        scale + (3.0 * scale * 0.044715) * square
    )
    return values * half, grad


def feed_kernel(blocks, patches, info, *refs):
    att, att_far, start, turned, up_bias, refs = refs[0], refs[1], refs[2], refs[3], refs[4], refs[5:]
    cot_in, refs = refs[:4], refs[4:]
    up_in, refs = refs[:blocks], refs[blocks:]
    down_in, refs = refs[:blocks], refs[blocks:]
    keep_out, send_out, back_out, back_low, middle_out, bias_out, refs = (
        refs[0], refs[1], refs[2], refs[3], refs[4], refs[5], refs[6:],
    )
    up_grads, refs = refs[:blocks], refs[blocks:]
    down_grads, refs = refs[:blocks], refs[blocks:]
    cot, up, down, normed, act, back, out_sum, up_grad, down_grad, sem = refs
    core, chip, place = info[0], info[1], info[2]
    rows, width = start.shape
    tile = rows // 4
    chunk = act.shape[1]
    up_rows = width // blocks
    half_rows = rows // 2
    hidden = 4 * chunk
    copies = cotangent_copies(info, cot_in, cot, [sem.at[i] for i in range(4)])
    count = 4
    for r in range(blocks):
        there = pl.ds(pl.multiple_of((r ^ chip) * up_rows, up_rows), up_rows)
        copies.append(pltpu.make_async_copy(up_in[r], up.at[there], sem.at[count]))
        count += 1
    later = []
    for r in range(blocks):
        if blocks == 4:
            for k in range(PLACES):
                later.append(
                    pltpu.make_async_copy(
                        down_in[r].at[k], down.at[r ^ chip, k ^ place], sem.at[count]
                    )
                )
                count += 1
        else:
            later.append(pltpu.make_async_copy(down_in[r], down, sem.at[count]))
            count += 1
    for copy in copies + later:
        copy.start()
    for copy in copies:
        copy.wait()
    part = width // 2
    vector = lambda i: turned[patches + i : patches + i + 1, :]
    own_rows = pl.ds(pl.multiple_of(core * part, 128), part)
    far_rows = pl.ds(pl.multiple_of((1 - core) * part, 128), part)
    gain, shift, out_bias = vector(GAIN_TWO), vector(SHIFT_TWO), vector(OUTPUT_BIAS)
    for t in range(4):
        here = slice(t * tile, (t + 1) * tile)
        middle = (
            start[here, :]
            + dot(att[here, :], up[own_rows, hidden:])
            + dot(att_far[here, :], up[far_rows, hidden:])
            + out_bias
        )
        middle_out[here, :] = middle
        normal, _ = normalise(middle)
        normed[here, :] = (normal * gain + shift).astype(bf16)
    out_sum[...] = jnp.zeros_like(out_sum)
    back_out[...] = jnp.zeros_like(back_out)
    for copy in later:
        copy.wait()

    def one_chunk(q, carry):
        lanes = pl.ds(pl.multiple_of(q * chunk, 128), chunk)
        down_part = down[q].reshape(chunk, width)
        bias_sum = jnp.zeros((1, chunk), f32)
        for t in range(4):
            here = slice(t * tile, (t + 1) * tile)
            value, slope = gelu_parts(dot(normed[here, :], up[:, lanes]) + up_bias[:, lanes])
            value = value.astype(bf16)
            act[here, :] = value
            out_sum[here, :] += dot(value, down_part)
            grad = (dot_right(cot[t], down_part) * slope).astype(bf16)
            back[here, :] = grad
            bias_sum += jnp.sum(grad.astype(f32), axis=0, keepdims=True)
            back_out[here, :] += dot_right(grad, up[:, lanes])
        bias_out[:, lanes] = jnp.broadcast_to(bias_sum, (8, chunk))
        flat = cot[...].reshape(rows, width)
        down_grad[q] = dot_left(act[...], flat).astype(bf16).reshape(PLACES, chunk // PLACES, width)
        up_grad[:, lanes] = dot_left(normed[...], back[...]).astype(bf16)
        return carry

    lax.fori_loop(0, 4, one_chunk, 0)
    back_low[...] = back_out[...].astype(bf16)
    own = pl.ds(pl.multiple_of(core * half_rows, half_rows), half_rows)
    far = pl.ds(pl.multiple_of((1 - core) * half_rows, half_rows), half_rows)
    keep_out[...] = middle_out[own, :] + out_sum[own, :] + vector(DOWN_BIAS)
    send_out[...] = out_sum[far, :].astype(bf16)
    outs = []
    for r in range(blocks):
        there = pl.ds(pl.multiple_of((r ^ chip) * up_rows, up_rows), up_rows)
        outs.append(pltpu.make_async_copy(up_grad.at[there], up_grads[r], sem.at[r]))
        source = down_grad.at[r ^ chip] if blocks == 4 else down_grad
        outs.append(pltpu.make_async_copy(source, down_grads[r], sem.at[blocks + r]))
    run_copies(outs)


def feed(info, att, att_far, start, turned, up_bias, cots, ups, downs, patches):
    blocks = len(ups)
    rows, width = start.shape
    hidden = up_bias.shape[1]
    chunk = hidden // 4
    down_shape = (4, PLACES, chunk // PLACES, width)
    up_rows = width // blocks
    one = down_shape[1:] if blocks == 4 else down_shape
    return call(
        functools.partial(feed_kernel, blocks, patches),
        [
            (shaped((rows // 2, width), f32), vmem()),
            (shaped((rows // 2, width), bf16), vmem()),
            (shaped((rows, width), f32), vmem()),
            (shaped((rows, width), bf16), vmem()),
            (shaped((rows, width), f32), vmem()),
            (shaped((8, hidden), f32), vmem()),
        ]
        + [(shaped((up_rows, hidden), bf16), anywhere())] * blocks
        + [(shaped(one, bf16), anywhere())] * blocks,
        [vmem()] * 5 + [anywhere()] * (4 + 2 * blocks),
        [info, att, att_far, start, turned, up_bias] + list(cots) + list(ups) + list(downs),
        scratch=[
            pltpu.VMEM((4, rows // 4, width), bf16),
            pltpu.VMEM((width, hidden + width), bf16),
            pltpu.VMEM(down_shape, bf16),
            pltpu.VMEM((rows, width), bf16),
            pltpu.VMEM((rows, chunk), bf16),
            pltpu.VMEM((rows, chunk), bf16),
            pltpu.VMEM((rows, width), f32),
            pltpu.VMEM((width, hidden), bf16),
            pltpu.VMEM(down_shape, bf16),
            pltpu.SemaphoreType.DMA((4 + 5 * blocks,)),
        ],
        limit=56,
        cost=(12 * rows * width * hidden, 30 * MIB),
    )


def middle_kernel(blocks, patches, info, *refs):
    back, back_far, middle, turned, att, refs = refs[0], refs[1], refs[2], refs[3], refs[4], refs[5:]
    cot_in, refs = refs[:4], refs[4:]
    up_in, refs = refs[:blocks], refs[blocks:]
    grad_out, attended_out, keep_out, send_out, sums_out, cot, weight, branch, sem = refs
    core, chip = info[0], info[1]
    rows, width = middle.shape
    tile = rows // 4
    part = width // 2
    up_rows = width // blocks
    hidden = up_in[0].shape[1] - width
    copies = cotangent_copies(info, cot_in, cot, [sem.at[i] for i in range(4)])
    for r in range(blocks):
        there = pl.ds(pl.multiple_of((r ^ chip) * up_rows, up_rows), up_rows)
        copies.append(
            pltpu.make_async_copy(up_in[r].at[:, hidden:], weight.at[there], sem.at[4 + r])
        )
    run_copies(copies)
    gain = turned[patches + GAIN_TWO : patches + GAIN_TWO + 1, :]
    own_rows = pl.ds(pl.multiple_of(core * part, 128), part)
    for t in range(4):
        here = slice(t * tile, (t + 1) * tile)
        grad_normed = back[here, :] + back_far[here, :].astype(f32)
        normal, scale = normalise(middle[here, :])
        grad_outputs = cot[t].astype(f32)
        grad = grad_outputs + norm_back(normal, scale, gain, grad_normed)
        low = grad.astype(bf16)
        branch[here, :] = low
        attended_out[here, :] = dot_right(low, weight[own_rows, :]).astype(bf16)

        @pl.when(core == t // 2)
        def _():
            grad_out[(t % 2) * tile : (t % 2 + 1) * tile, :] = grad
            sums = jnp.concatenate(
                [
                    jnp.sum(low.astype(f32), axis=0, keepdims=True),
                    jnp.sum(grad_outputs, axis=0, keepdims=True),
                    jnp.sum(grad_normed * normal, axis=0, keepdims=True),
                    jnp.sum(grad_normed, axis=0, keepdims=True),
                    jnp.zeros((4, width), f32),
                ],
                axis=0,
            )
            sums_out[...] = sums if t % 2 == 0 else sums_out[...] + sums

    weight_grad = dot_left(att[...], branch[...]).astype(bf16)
    shape = send_out.shape[:1] + (2,) + send_out.shape[1:]
    sorted_grad = weight_grad.reshape(shape) if blocks == 4 else None
    if blocks == 4:
        for c in range(2):

            @pl.when(core == c)
            def _():
                keep_out[...] = sorted_grad[:, c]
                send_out[...] = sorted_grad[:, 1 - c]

    else:
        keep_out[...] = weight_grad
        send_out[...] = weight_grad


def middle_back(info, back, back_far, middle, turned, att, cots, ups, patches):
    blocks = len(ups)
    rows, width = middle.shape
    part = width // 2
    slab = (2, part // 4, width) if blocks == 4 else (part, width)
    return call(
        functools.partial(middle_kernel, blocks, patches),
        [
            (shaped((rows // 2, width), f32), vmem()),
            (shaped((rows, part), bf16), vmem()),
            (shaped(slab, bf16), vmem()),
            (shaped(slab, bf16), vmem()),
            (shaped((8, width), f32), vmem()),
        ],
        [vmem()] * 5 + [anywhere()] * (4 + blocks),
        [info, back, back_far, middle, turned, att] + list(cots) + list(ups),
        scratch=[
            pltpu.VMEM((4, rows // 4, width), bf16),
            pltpu.VMEM((width, width), bf16),
            pltpu.VMEM((rows, width), bf16),
            pltpu.SemaphoreType.DMA((4 + blocks,)),
        ],
        cost=(4 * rows * width * part, 14 * MIB),
    )


def project_kernel(blocks, info, *refs):
    dq, dk, dv, refs = refs[0], refs[1], refs[2], refs[3:]
    weights_in, refs = refs[:blocks], refs[blocks:]
    keep_out, send_out, weight, sem = refs
    core, chip = info[0], info[1]
    rows, part = dq.shape
    width = weight.shape[0]
    up_rows = width // blocks
    half_rows = rows // 2
    copies = []
    for r in range(blocks):
        there = pl.ds(pl.multiple_of((r ^ chip) * up_rows, up_rows), up_rows)
        copies.append(
            pltpu.make_async_copy(
                weights_in[r].at[:, : 3 * part], weight.at[there], sem.at[r]
            )
        )
    run_copies(copies)

    def product(first):
        here = pl.ds(pl.multiple_of(first, 128), half_rows)
        return (
            dot_right(dq[here, :], weight[:, :part])
            + dot_right(dk[here, :], weight[:, part : 2 * part])
            + dot_right(dv[here, :], weight[:, 2 * part :])
        )

    send_out[...] = product((1 - core) * half_rows).astype(bf16)
    keep_out[...] = product(core * half_rows)


def project_back(info, dq, dk, dv, weights, width):
    blocks = len(weights)
    rows, part = dq.shape
    return call(
        functools.partial(project_kernel, blocks),
        [
            (shaped((rows // 2, width), f32), vmem()),
            (shaped((rows // 2, width), bf16), vmem()),
        ],
        [vmem()] * 3 + [anywhere()] * blocks,
        [info, dq, dk, dv] + list(weights),
        scratch=[
            pltpu.VMEM((width, 3 * part), bf16),
            pltpu.SemaphoreType.DMA((blocks,)),
        ],
        cost=(6 * rows * width * part, 8 * MIB),
    )


def start_kernel(blocks, patches, info, *refs):
    (keep, far, start, grad_middle, turned, sums, up_bias_rows, spots, normed, dq, dk, dv) = refs[:12]
    refs = refs[12:]
    low_out, refs = refs[0], refs[1:]
    grads, refs = refs[:blocks], refs[blocks:]
    held, rows_held, sem = refs
    core, chip = info[0], info[1]
    rows, part = dq.shape
    half_rows, width = keep.shape
    up_rows = width // blocks
    columns = 3 * part
    for i, ref in enumerate((dq, dk, dv)):
        held[:, i * part : (i + 1) * part] = dot_left(normed[...], ref[...]).astype(bf16)
    gain = turned[patches + GAIN_ONE : patches + GAIN_ONE + 1, :]
    own = pl.ds(pl.multiple_of(core * half_rows, half_rows), half_rows)
    grad_normed = keep[...] + far[...].astype(f32)
    normal, scale = normalise(start[own, :])
    grad = grad_middle[...] + norm_back(normal, scale, gain, grad_normed)
    low = grad.astype(bf16)
    low_out[...] = low
    ids = lax.broadcasted_iota(jnp.int32, (SMALL, half_rows), 0).astype(f32)
    mine = spots[0:1, pl.ds(pl.multiple_of(core * half_rows, 128), half_rows)]
    one_hot = jnp.where(ids == mine, 1.0, 0.0).astype(bf16)
    rows_held[...] = dot(one_hot, low)
    half = pl.ds(pl.multiple_of(core * part, 128), part)
    rows_held[patches : patches + 8, :] = jnp.zeros((8, width), f32)

    def put(i, row):
        rows_held[patches + i : patches + i + 1, :] = row

    rows_held[patches + QUERY_BIAS : patches + QUERY_BIAS + 1, half] = jnp.sum(
        dq[...].astype(f32), axis=0, keepdims=True
    )
    rows_held[patches + VALUE_BIAS : patches + VALUE_BIAS + 1, half] = jnp.sum(
        dv[...].astype(f32), axis=0, keepdims=True
    )
    put(OUTPUT_BIAS, sums[0:1, :])
    put(DOWN_BIAS, sums[1:2, :])
    put(GAIN_TWO, sums[2:3, :])
    put(SHIFT_TWO, sums[3:4, :])
    put(GAIN_ONE, jnp.sum(grad_normed * normal, axis=0, keepdims=True))
    put(SHIFT_ONE, jnp.sum(grad_normed, axis=0, keepdims=True))
    spare = up_bias_rows.shape[0]
    rows_held[patches + 8 : patches + 8 + spare, :] = up_bias_rows[...]
    held[:, columns:] = rows_held[...].T.astype(bf16)
    copies = []
    for r in range(blocks):
        there = pl.ds(pl.multiple_of((r ^ chip) * up_rows, up_rows), up_rows)
        copies.append(pltpu.make_async_copy(held.at[there], grads[r], sem.at[r]))
    run_copies(copies)


def start_back(
    info, blocks, keep, far, start, grad_middle, turned, sums, up_bias_rows, spots, normed, dq, dk, dv, patches
):
    half_rows, width = keep.shape
    rows, part = dq.shape
    columns = 3 * part + SMALL
    return call(
        functools.partial(start_kernel, blocks, patches),
        [(shaped((half_rows, width), bf16), vmem())]
        + [(shaped((width // blocks, columns), bf16), anywhere())] * blocks,
        [vmem()] * 12,
        [info, keep, far, start, grad_middle, turned, sums, up_bias_rows, spots, normed, dq, dk, dv],
        scratch=[
            pltpu.VMEM((width, columns), bf16),
            pltpu.VMEM((SMALL, width), f32),
            pltpu.SemaphoreType.DMA((blocks,)),
        ],
        cost=(6 * rows * width * part, 14 * MIB),
    )


def split_kernel(groups, info, *refs):
    place = info[2]
    inputs, outs = refs[: sum(groups)], refs[sum(groups) :]
    base, column = 0, 0
    for count in groups:
        total = inputs[base][...].astype(f32)
        for ref in inputs[base + 1 : base + count]:
            total = total + ref[...].astype(f32)
        base += count
        lanes = total.shape[-1]
        outs[PLACES][:, :, :, column : column + lanes] = total
        column += lanes
    for k in range(PLACES):
        outs[k][...] = outs[PLACES][:, k ^ place].astype(outs[k].dtype)


def split(info, groups):
    two, places, rows, _ = groups[0][0].shape
    columns = sum(group[0].shape[3] for group in groups)
    one = (two, rows, columns)
    outs = [(shaped(one, f32 if k == 0 else bf16), vmem()) for k in range(places)]
    outs.append((shaped((two, places, rows, columns), f32), vmem()))
    arrays = [array for group in groups for array in group]
    return call(
        functools.partial(split_kernel, [len(group) for group in groups]),
        outs,
        [vmem()] * len(arrays),
        [info] + arrays,
        limit=32,
        cost=(0, 8 * two * places * rows * columns),
    )[:places]


def swap(values, axis, bits):
    size = lax.axis_size(axis)
    return lax.ppermute(values, axis, [(i, i ^ bits) for i in range(size)])


def spread_perm(turn):
    pairs = []
    for w in range(lax.axis_size("wide")):
        for z in range(PLACES):
            there = (w - w % 2 + z // 2, 2 * (w % 2) + (turn ^ (z % 2)))
            pairs.append((w * PLACES + z, there[0] * PLACES + there[1]))
    return pairs


def spread(values, place):
    mine = [
        lax.ppermute(
            lax.dynamic_index_in_dim(values, turn ^ (place % 2), 0, keepdims=False),
            ("wide", "narrow"),
            spread_perm(turn),
        )
        for turn in range(2)
    ]
    return mine + [swap(part, "wide", 1) for part in mine]


def unspread(blocks, place):
    got = [
        lax.ppermute(
            lax.dynamic_index_in_dim(blocks, turn ^ (place % 2), 0, keepdims=False),
            ("wide", "narrow"),
            [(b, a) for a, b in spread_perm(turn)],
        )
        for turn in range(2)
    ]
    odd = (place % 2) == 1
    return jnp.stack([jnp.where(odd, got[1], got[0]), jnp.where(odd, got[0], got[1])])


def along(piece, bits):
    held = {0: piece}
    for bit in bits:
        held.update({index ^ (bit // 2): swap(part, "wide", bit) for index, part in list(held.items())})
    return [held[index] for index in range(len(held))]


def direct(piece, chips):
    return [piece] + [swap(piece, "wide", 2 * index) for index in range(1, chips)]


def fold(pieces, bits):
    held = dict(enumerate(pieces))
    for number, bit in enumerate(bits):
        step = bit // 2
        got = {i: swap(held[i ^ step], "wide", bit) for i in held if not i & step}
        if number == len(bits) - 1:
            return [held[0], got[0]]
        held = {i: (held[i].astype(f32) + got[i].astype(f32)).astype(bf16) for i in got}
    return [held[0]]


def after(values, *others):
    return lax.optimization_barrier((values,) + others)[0]


def local(
    tokens,
    positions,
    segments,
    position_table,
    input_weight,
    query_bias,
    value_bias,
    output_weight,
    output_bias,
    first_gain,
    first_shift,
    up_weight,
    up_bias,
    down_weight,
    down_bias,
    second_gain,
    second_shift,
    cotangent,
):
    size = lax.axis_size("wide")
    chips = size // 2
    bits = [2**i for i in range(1, size.bit_length() - 1)]
    seq_count, block, width = tokens.shape
    hidden = up_weight.shape[1]
    patches = position_table.shape[1]
    full = segments.shape[1]
    rows = width // (size * PLACES)
    part = width // 2
    own_hidden = hidden // 2
    wide, place = lax.axis_index("wide"), lax.axis_index("narrow")
    core, chip = wide % 2, wide // 2
    first_core = core == 0
    blocks = 4 if chips == 4 else 1
    info = jnp.stack([core, chip if blocks == 4 else 0 * chip, place, chip]).astype(jnp.int32)

    def pick(values, index, axis=0):
        return lax.dynamic_index_in_dim(values, index, axis, keepdims=False)

    def by_chip(pieces):
        flat = [piece.reshape((-1,) + piece.shape[-1:]) for piece in pieces]
        if blocks == 4:
            return flat
        whole = jnp.take(jnp.stack(flat), jnp.arange(chips) ^ chip, axis=0)
        return [whole.reshape((-1,) + flat[0].shape[1:])]

    def by_distance(outs, shape):
        if blocks == 4:
            return [out.reshape(shape) for out in outs]
        whole = outs[0].reshape((chips,) + shape)
        return [pick(whole, index ^ chip) for index in range(chips)]

    relative = (segments - segments[:, :1]).astype(bf16)
    extra = [
        jnp.pad(positions.astype(bf16), ((0, 0), (0, width - block)))[:, None],
        relative[:, None, :width],
        jnp.pad(relative[:, width:], ((0, 0), (0, 2 * width - full)))[:, None],
        jnp.zeros((seq_count, 13, width), bf16),
    ]
    packed = jnp.concatenate([tokens] + extra, axis=1)

    vectors = (
        query_bias,
        value_bias,
        output_bias,
        first_gain,
        first_shift,
        down_bias,
        second_gain,
        second_shift,
    )
    spare = up_bias.shape[0] // rows
    small = jnp.concatenate(
        [position_table] + [v[:, None] for v in vectors] + [up_bias.reshape(rows, spare)], axis=1
    )
    small = jnp.pad(small, ((0, 0), (0, SMALL - small.shape[1])))

    def pair(keep, send):
        got = swap(send, "wide", 1)
        return jnp.where(first_core, jnp.stack([keep, got]), jnp.stack([got, keep]))

    def in_halves(index):
        cut = pick(input_weight.reshape(rows, 3, 2, part), index, 2).reshape(rows, 3 * part)
        return jnp.concatenate([cut, small], axis=1)

    def up_halves(index):
        cut = pick(up_weight.reshape(rows, chips, 2, -1), index, 2).reshape(rows, own_hidden)
        return jnp.concatenate([cut, output_weight], axis=1)

    def narrow_pieces(piece):
        return [piece] + [swap(piece, "narrow", k) for k in range(1, PLACES)]

    in_pair = pair(in_halves(core), in_halves(1 - core))
    in_piece = arrange(info, narrow_pieces(in_pair))
    in_chips = direct(in_piece, chips) if blocks == 4 else along(in_piece, bits)
    in_blocks = by_chip(in_chips)
    token_blocks = spread(packed, place)

    up_pair = pair(up_halves(core), up_halves(1 - core))
    up_pair = after(up_pair, in_piece)
    up_piece = arrange(info, narrow_pieces(up_pair))
    up_blocks = by_chip(along(up_piece, bits[::-1]))
    down_pieces = jnp.stack(narrow_pieces(after(down_weight, up_piece)))
    if blocks == 4:
        down_blocks = along(down_pieces, bits)
    else:
        down_pieces = jnp.take(down_pieces, jnp.arange(PLACES) ^ place, axis=0)
        down_blocks = by_chip(along(down_pieces, bits))
        down_blocks = [down_blocks[0].reshape(4, PLACES, -1, width)]
    cots = spread(cotangent, place)

    q, k, v, start, normed, small_full, turned, seg, spots = front(
        info, token_blocks, in_blocks, patches
    )
    att, total = attend(info, q, k, v, seg)
    att_far = swap(att, "wide", 1)
    bias = small_full[:, patches + 8 : patches + 8 + spare]
    up_bias_own = pick(bias.reshape(chips, 2, -1), core, 1).reshape(1, own_hidden).astype(f32)
    fed = feed(
        info, att, att_far, start, turned, up_bias_own, cots, up_blocks, down_blocks, patches
    )
    keep, send, back, back_low, middle, bias_grad = fed[:6]
    up_grads, down_grads = fed[6 : 6 + blocks], fed[6 + blocks :]
    back_far = swap(back_low, "wide", 1)
    out_far = swap(send, "wide", 1)
    outputs = (keep + out_far.astype(f32)).astype(bf16).reshape(2, block, width)
    outputs = unspread(outputs, place)

    down_sum = fold(
        by_distance(down_grads, (1, PLACES, own_hidden // (chips * PLACES), width)), bits[::-1]
    )
    down_cut = split(info, [down_sum])
    down_share = down_cut[0][0]
    for index in range(1, PLACES):
        down_share = down_share + swap(down_cut[index], "narrow", index)[0].astype(f32)

    grad_middle, grad_att, out_keep, out_send, sums = middle_back(
        info, back, back_far, middle, turned, att, cots, up_blocks, patches
    )
    if blocks == 1:
        shape = (chips // 2, 2, PLACES * rows, width)
        out_keep = pick(out_keep.reshape(shape), core, 1)
        out_send = pick(out_send.reshape(shape), 1 - core, 1)
    out_got = swap(out_send, "wide", 1)
    out_grad = jnp.where(
        first_core,
        jnp.concatenate([out_keep, out_got]),
        jnp.concatenate([out_got, out_keep]),
    ).reshape(chips, PLACES, rows, 2, part)
    out_grad = jnp.swapaxes(jnp.swapaxes(out_grad, 2, 3), 1, 2)
    out_pieces = [pick(out_grad, index ^ chip) for index in range(chips)]
    up_pieces = by_distance(up_grads, (2, PLACES, rows, own_hidden))
    up_cut = split(info, [fold(up_pieces, bits), fold(out_pieces, bits)])

    def narrow_sum(cut):
        whole = cut[0]
        for index in range(1, PLACES):
            whole = whole + swap(cut[index], "narrow", index).astype(f32)
        return whole

    up_total = narrow_sum(up_cut)
    up_keep = pick(up_total[:, :, :own_hidden], core)
    up_got = swap(pick(up_total[:, :, :own_hidden], 1 - core).astype(bf16), "wide", 1).astype(f32)
    up_both = [up_keep.reshape(rows, chips, 1, -1), up_got.reshape(rows, chips, 1, -1)]
    up_share = jnp.where(
        first_core, jnp.concatenate(up_both, axis=2), jnp.concatenate(up_both[::-1], axis=2)
    ).reshape(rows, hidden)
    out_share = jnp.concatenate([up_total[0, :, own_hidden:], up_total[1, :, own_hidden:]], axis=1)

    dq, dk, dv = attend_back(info, q, k, v, att, grad_att, total, seg)
    start_keep, start_send = project_back(info, dq, dk, dv, in_blocks, width)
    start_far = swap(start_send, "wide", 1)
    bias_rows = bias_grad[0].reshape(chips, 1, rows * PLACES, spare)
    mine = (jnp.arange(2) == core)[None, :, None, None]
    bias_rows = jnp.where(mine, bias_rows, 0.0).reshape(width, spare).T
    started = start_back(
        info, blocks, start_keep, start_far, start, grad_middle, turned, sums, bias_rows,
        spots, normed, dq, dk, dv, patches,
    )
    grad_tokens = unspread(started[0].reshape(2, block, width), place)
    columns = 3 * part + SMALL
    in_pieces = by_distance(started[1:], (2, PLACES, rows, columns))
    if blocks == 4:
        in_sum = [in_pieces[0]] + [swap(in_pieces[i], "wide", 2 * i) for i in range(1, chips)]
    else:
        in_sum = fold(in_pieces, bits)
    in_total = narrow_sum(split(info, [in_sum]))
    in_keep = pick(in_total, core)
    in_got = swap(pick(in_total, 1 - core).astype(bf16), "wide", 1).astype(f32)
    in_both = [
        in_keep[:, : 3 * part].reshape(rows, 3, 1, part),
        in_got[:, : 3 * part].reshape(rows, 3, 1, part),
    ]
    in_share = jnp.where(
        first_core, jnp.concatenate(in_both, axis=2), jnp.concatenate(in_both[::-1], axis=2)
    ).reshape(rows, 3 * width)
    small_share = in_keep[:, 3 * part :] + in_got[:, 3 * part :]
    tail = [small_share[:, patches + i] for i in range(8)]
    return (
        outputs,
        grad_tokens,
        small_share[:, :patches],
        in_share,
        tail[QUERY_BIAS],
        tail[VALUE_BIAS],
        out_share,
        tail[OUTPUT_BIAS],
        tail[GAIN_ONE],
        tail[SHIFT_ONE],
        up_share,
        small_share[:, patches + 8 : patches + 8 + spare].reshape(-1),
        down_share,
        tail[DOWN_BIAS],
        tail[GAIN_TWO],
        tail[SHIFT_TWO],
    )


def solution(mesh):
    both = ("wide", "narrow")
    matrix = P(both, None)
    vector = P(both)
    block = P("wide", "narrow", None)
    gains = [matrix, matrix] + [vector] * 2 + [matrix] + [vector] * 3 + [matrix, vector, matrix]
    gains += [vector] * 3
    return jax.shard_map(
        local,
        mesh=mesh,
        in_specs=tuple([block, P("wide", "narrow"), P("wide", None)] + gains + [block]),
        out_specs=tuple([block, block] + gains),
        check_vma=False,
    )
```

time: 625 us -> 383 us (0.61)
  matrix products: 120 us -> 0 us
  Pallas kernels: 0 us -> 104 us
  other arithmetic: 113 us -> 16 us
  local copies, waits for them, and re-layouts: 119 us -> 35.1 us
  waiting for transfers between devices: 160 us -> 127 us
  starting transfers between devices: 99.4 us -> 91.9 us
    dot_general x20 -> x0, matrix products: 105 us -> none  [the longest x5 22 us: product_right(): lax.dot_general(left, right, (((1,), (1,)), ((), ())), preferred_element_...]
    pallas_call x0 -> x12, Pallas kernels: none -> 104 us  [call(): pl.pallas_call(kernel, out_shape=[shape for shape, _ in outs], in_specs=[...]
    gather x15 -> x0, local copies, waits for them, and re-layouts: 48.7 us -> none  [the longest x4 22.9 us: gather(): return jnp.take(whole, ranks, axis=0).reshape(-1, columns)]
    ppermute x77 -> x52, waiting for transfers between devices: 148 us -> 102 us  [swap(): return lax.ppermute(values, axis, [(i, i ^ bits) for i in range(size)])]
    convert_element_type x19 -> x10, other arithmetic: 42.2 us -> 5.7 us  [the longest x5 4.84 us: fold(): (held[i].astype(f32) + got[i].astype(f32)).astype(bf16)]
    select_n x26 -> x5, other arithmetic: 27.4 us -> 2.5 us  [the longest x1 1.24 us: local(): jnp.where(first_core, jnp.concatenate(up_both, axis=2), jnp.concatenate(u...]
    sub x1 -> x0, matrix products: 15.4 us -> none  [local(): probabilities = jax.nn.softmax(scores, axis=-1)]
    ppermute x10 -> x8, waiting for transfers between devices: 11.7 us -> 25.1 us  [the longest x4 12.8 us: spread(): lax.ppermute(lax.dynamic_index_in_dim(values, turn ^ place % 2, 0, keepdi...]
  transfers between devices with their start and end apart: 87 -> 60, of which waited for: 38 -> 23; matrix products, arithmetic and copies ran while one was open for 37% -> 9% of each run, Pallas kernels for 0% -> 17%
where the time goes in v2:
time: 383 us; the launch traced here: 376 us
  waiting for transfers between devices  127 us (33%)
  Pallas kernels  104 us (27%)
  starting transfers between devices  91.9 us (24%)
  local copies, waits for them, and re-layouts  35.1 us (9%)
  other arithmetic  16 us (4%)
    pallas_call x12, Pallas kernels, call(): pl.pallas_call(kernel, out_shape=[shape for shape, _ in outs], in_specs=[...  104 us
    ppermute x52, waiting for transfers between devices, swap(): return lax.ppermute(values, axis, [(i, i ^ bits) for i in range(size)])  102 us
    ppermute x52, starting transfers between devices, swap(): return lax.ppermute(values, axis, [(i, i ^ bits) for i in range(size)])  70.1 us
    ppermute x4, waiting for transfers between devices, spread(): lax.ppermute(lax.dynamic_index_in_dim(values, turn ^ place % 2, 0, keepdi...  12.8 us
    ppermute x4, waiting for transfers between devices, unspread(): lax.ppermute(lax.dynamic_index_in_dim(blocks, turn ^ place % 2, 0, keepdi...  12.2 us
    ppermute x4, starting transfers between devices, unspread(): lax.ppermute(lax.dynamic_index_in_dim(blocks, turn ^ place % 2, 0, keepdi...  11.4 us
    ppermute x4, starting transfers between devices, spread(): lax.ppermute(lax.dynamic_index_in_dim(values, turn ^ place % 2, 0, keepdi...  10.3 us
  transfers between devices with their start and end apart: 60, of which 23 were waited for; matrix products, arithmetic and copies ran while one was open for 9% of the time, Pallas kernels for 17%

profile of v2, /device:TPU:7, one launch (start us, length us, event | category | flops | bytes accessed | tf_op | source)
XLA Modules:
  0.0 376.4 jit_solution(7550107007429576238)
XLA Ops:
  13.8 4.5 %collective-permute-start.12 = (bf16[256,768]{1,0:T(8,128)(2,1)}, bf16[256,768]{1,0:T(8,128)(2,1)S(1)}, u32[]{:S(2)}, u32[]{:S(2)}) collective-permute-start(bf16[256,768]{1,0:T(8,128)(2,1)} %get-tuple-element.147), channel_id=1, source_target_pairs={{0,0},{1,1},{2,4},{3,5},{4,2},{5,3},{6,6},{7,7},{8,8},{9,9},{10,12... | collective-permute-start | bytes 1179656 | tf_op jit(solution)/shard_map/ppermute | solution.py:724
  20.1 2.2 collective-permute-start.7
  22.4 5.7 %collective-permute-done.5.b = bf16[2,24,1280]{2,1,0:T(8,128)(2,1)S(1)} collective-permute-done((bf16[2,24,1280]{2,1,0:T(8,128)(2,1)S(1)}, bf16[2,24,1280]{2,1,0:T(8,128)(2,1)S(1)}, u32[]{:S(2)}, u32[]{:S(2)}) %collective-permute-start.5) | collective-permute-done | bytes 122912 | tf_op jit(solution)/shard_map/ppermute | solution.py:710
  28.1 5.7 %collective-permute-done.6.c = bf16[2,24,1280]{2,1,0:T(8,128)(2,1)S(1)} collective-permute-done((bf16[2,24,1280]{2,1,0:T(8,128)(2,1)S(1)}, bf16[2,24,1280]{2,1,0:T(8,128)(2,1)S(1)}, u32[]{:S(2)}, u32[]{:S(2)}) %collective-permute-start.6) | collective-permute-done | bytes 122912 | tf_op jit(solution)/shard_map/ppermute | solution.py:710
  34.4 5.5 %collective-permute-start.17 = (bf16[2,24,2304]{2,1,0:T(8,128)(2,1)S(1)}, bf16[2,24,2304]{2,1,0:T(8,128)(2,1)S(1)}, u32[]{:S(2)}, u32[]{:S(2)}) collective-permute-start(bf16[2,24,2304]{2,1,0:T(8,128)(2,1)S(1)} %maximum_select_fusion.3.a), channel_id=1, source_target_pairs={{0,1},{1,0},{2,3},{3,2},{4,5},{5,4},{6,7},{7,6},{8,9},{9,8},{10,11... | collective-permute-start | bytes 663560 | tf_op jit(solution)/shard_map/ppermute | solution.py:710
  39.9 1.7 collective-permute-start.18
  43.4 2.8 collective-permute-start
  46.2 2.1 collective-permute-done.17.b
  48.9 3.0 collective-permute-start.1
  51.8 6.2 %collective-permute-done.19.d = bf16[2,24,2304]{2,1,0:T(8,128)(2,1)S(1)} collective-permute-done((bf16[2,24,2304]{2,1,0:T(8,128)(2,1)S(1)}, bf16[2,24,2304]{2,1,0:T(8,128)(2,1)S(1)}, u32[]{:S(2)}, u32[]{:S(2)}) %collective-permute-start.19) | collective-permute-done | bytes 221216 | tf_op jit(solution)/shard_map/ppermute | solution.py:710
  59.2 12.8 %collective-permute-done.13.refs_6_ = bf16[256,768]{1,0:T(8,128)(2,1)S(1)} collective-permute-done((bf16[256,768]{1,0:T(8,128)(2,1)S(1)}, bf16[256,768]{1,0:T(8,128)(2,1)S(1)}, u32[]{:S(2)}, u32[]{:S(2)}) %collective-permute-start.13) | collective-permute-done | bytes 393248 | tf_op jit(solution)/shard_map/ppermute | solution.py:724
  72.1 12.7 %collective-permute-start.23 = (bf16[96,768]{1,0:T(8,128)(2,1)S(1)}, bf16[96,768]{1,0:T(8,128)(2,1)S(1)}, u32[]{:S(2)}, u32[]{:S(2)}) collective-permute-start(bf16[96,768]{1,0:T(8,128)(2,1)S(1)} %copy-done.50), channel_id=1, source_target_pairs={{0,1},{1,0},{2,3},{3,2},{4,5},{5,4},{6,7},{7,6},{8,9},{9,8},{10,11... | collective-permute-start | bytes 442376 | tf_op jit(solution)/shard_map/ppermute | solution.py:710
  84.8 2.2 collective-permute-start.25
  87.6 10.2 %collective-permute-done.24 = bf16[96,768]{1,0:T(8,128)(2,1)S(1)} collective-permute-done((bf16[96,768]{1,0:T(8,128)(2,1)S(1)}, bf16[96,768]{1,0:T(8,128)(2,1)S(1)}, u32[]{:S(2)}, u32[]{:S(2)}) %collective-permute-start.24) | collective-permute-done | bytes 147488 | tf_op jit(solution)/shard_map/ppermute | solution.py:710
  101.2 8.9 %collective-permute-done.10 = bf16[2,4,24,1280]{3,2,1,0:T(8,128)(2,1)S(1)} collective-permute-done((bf16[2,4,24,1280]{3,2,1,0:T(8,128)(2,1)S(1)}, bf16[2,4,24,1280]{3,2,1,0:T(8,128)(2,1)S(1)}, u32[]{:S(2)}, u32[]{:S(2)}) %collective-permute-start.10) | collective-permute-done | bytes 491552 | tf_op jit(solution)/shard_map/ppermute | solution.py:710
  110.1 2.3 collective-permute-start.15
  113.9 9.2 %shard_map.298 = (bf16[1024,384]{1,0:T(8,128)(2,1)S(1)}, bf16[1024,384]{1,0:T(8,128)(2,1)S(1)}, bf16[1024,384]{1,0:T(8,128)(2,1)}, f32[1024,768]{1,0:T(8,128)}, ...) custom-call(s32[4]{0:T(128)S(1)} %pad_add_fusion.info, ...), custom_call_target="tpu_custom_call" | custom-call | flops 2013265920 | bytes 12582912 | tf_op jit(solution)/shard_map/pallas_call | solution.py:35
  125.0 13.2 %shard_map.299 = (bf16[1024,384]{1,0:T(8,128)(2,1)S(1)}, f32[3,8,1024]{2,1,0:T(8,128)S(1)}) custom-call(s32[4]{0:T(128)S(1)} %pad_add_fusion.info, bf16[1024,384]{1,0:T(8,128)(2,1)S(1)} %get-tuple-element.70.q, bf16[1024,384]{1,0:T(8,128)(2,1)S(1)} %get-tuple-element.71.k, bf16[1024,384]{1,0:T(8,128)(2,1)S(1)} %copy-done.35, f32[8,1024]{1,0:T(8,128)S(1)} %get-tuple-element.73.seg), custom_call_target="tpu_custom_call" | custom-call | flops 2415919104 | bytes 4194304 | tf_op jit(solution)/shard_map/pallas_call | solution.py:35
  140.4 5.9 %collective-permute-done.26.refs_14_ = bf16[4,96,768]{2,1,0:T(8,128)(2,1)} collective-permute-done((bf16[4,96,768]{2,1,0:T(8,128)(2,1)}, bf16[4,96,768]{2,1,0:T(8,128)(2,1)}, u32[]{:S(2)}, u32[]{:S(2)}) %collective-permute-start.26) | collective-permute-done | bytes 589856 | tf_op jit(solution)/shard_map/ppermute | solution.py:710
  147.6 6.7 %collective-permute-done.27.refs_15_ = bf16[4,96,768]{2,1,0:T(8,128)(2,1)} collective-permute-done((bf16[4,96,768]{2,1,0:T(8,128)(2,1)}, bf16[4,96,768]{2,1,0:T(8,128)(2,1)}, u32[]{:S(2)}, u32[]{:S(2)}) %collective-permute-start.27) | collective-permute-done | bytes 589856 | tf_op jit(solution)/shard_map/ppermute | solution.py:710
  154.3 12.6 %collective-permute-done.28.refs_16_ = bf16[4,96,768]{2,1,0:T(8,128)(2,1)} collective-permute-done((bf16[4,96,768]{2,1,0:T(8,128)(2,1)}, bf16[4,96,768]{2,1,0:T(8,128)(2,1)}, u32[]{:S(2)}, u32[]{:S(2)}) %collective-permute-start.28) | collective-permute-done | bytes 589856 | tf_op jit(solution)/shard_map/ppermute | solution.py:710
  166.9 36.9 %shard_map.301 = (f32[512,768]{1,0:T(8,128)}, bf16[512,768]{1,0:T(8,128)(2,1)}, f32[1024,768]{1,0:T(8,128)}, bf16[1024,768]{1,0:T(8,128)(2,1)}, f32[1024,768]{1,...) custom-call(s32[4]{0:T(128)} %copy-done.19, ...), custom_call_target="tpu_custom_call" | custom-call | flops 14495514624 | bytes 31457280 | tf_op jit(solution)/shard_map/pallas_call | solution.py:35
  205.6 2.0 collective-permute-start.32
  210.3 7.2 %collective-permute-done.55 = bf16[1,4,96,768]{3,2,1,0:T(8,128)(2,1)S(1)} collective-permute-done((bf16[1,4,96,768]{3,2,1,0:T(8,128)(2,1)}, bf16[1,4,96,768]{3,2,1,0:T(8,128)(2,1)S(1)}, u32[]{:S(2)}, u32[]{:S(2)}) %collective-permute-start.55) | collective-permute-done | bytes 589856 | tf_op jit(solution)/shard_map/ppermute | solution.py:710
  217.5 4.4 %collective-permute-start.29 = (bf16[512,768]{1,0:T(8,128)(2,1)}, bf16[512,768]{1,0:T(8,128)(2,1)S(1)}, u32[]{:S(2)}, u32[]{:S(2)}) collective-permute-start(bf16[512,768]{1,0:T(8,128)(2,1)} %get-tuple-element.81), channel_id=1, source_target_pairs={{0,4},{4,0},{8,12},{12,8},{16,20},{20,16},{24,28},{28,24},{1,5},{5... | collective-permute-start | bytes 2359304 | tf_op jit(solution)/shard_map/ppermute | solution.py:710
  225.2 10.3 %collective-permute-done.43 = bf16[2,4,24,1536]{3,2,1,0:T(8,128)(2,1)} collective-permute-done((bf16[2,4,24,1536]{3,2,1,0:T(8,128)(2,1)}, bf16[2,4,24,1536]{3,2,1,0:T(8,128)(2,1)}, u32[]{:S(2)}, u32[]{:S(2)}) %collective-permute-start.43) | collective-permute-done | bytes 589856 | tf_op jit(solution)/shard_map/ppermute | solution.py:710
  238.9 11.4 %shard_map.302 = (f32[512,768]{1,0:T(8,128)}, bf16[1024,384]{1,0:T(8,128)(2,1)S(1)}, bf16[2,96,768]{2,1,0:T(8,128)(2,1)S(1)}, bf16[2,96,768]{2,1,0:T(8,128)(2,1)}, f32[8,768]{1,0:T(8,128)S(1)}) custom-call(s32[4]{0:T(128)S(1)} %copy-done.20, f32[1024,768]{1,0:T(8,128)} %get-tuple-element.82.refs_0_, bf16[1024,768]{1,0:T(8,128)(2,1)} %collective-permute-done.32.refs_1_, ...), custom_call_target="tpu_custom_call" | custom-call | flops 1207959552 | bytes 14680064 | tf_op jit(solution)/shard_map/pallas_call | solution.py:35
  254.2 4.7 %collective-permute-start.31 = (bf16[256,768]{1,0:T(8,128)(2,1)}, bf16[256,768]{1,0:T(8,128)(2,1)}, u32[]{:S(2)}, u32[]{:S(2)}) collective-permute-start(bf16[256,768]{1,0:T(8,128)(2,1)} %get-tuple-element.145), channel_id=1, source_target_pairs={{0,0},{1,1},{4,2},{5,3},{2,4},{3,5},{6,6},{7,7},{8,8},{9,9},{12,10... | collective-permute-start | bytes 1179656 | tf_op jit(solution)/shard_map/ppermute | solution.py:736
  260.2 1.8 shard_map.308
  264.3 1.7 copy.91
  266.0 3.8 %collective-permute-start.58 = (bf16[1,96,768]{2,1,0:T(8,128)(2,1)}, bf16[1,96,768]{2,1,0:T(8,128)(2,1)}, u32[]{:S(2)}, u32[]{:S(2)}) collective-permute-start(bf16[1,96,768]{2,1,0:T(8,128)(2,1)} %copy-done.30), channel_id=1, source_target_pairs={{0,2},{1,3},{2,0},{3,1},{4,6},{5,7},{6,4},{7,5},{8,10},{9,11},{10,... | collective-permute-start | bytes 442376 | tf_op jit(solution)/shard_map/ppermute | solution.py:710
  273.0 6.5 %collective-permute-done.31 = bf16[256,768]{1,0:T(8,128)(2,1)} collective-permute-done((bf16[256,768]{1,0:T(8,128)(2,1)}, bf16[256,768]{1,0:T(8,128)(2,1)}, u32[]{:S(2)}, u32[]{:S(2)}) %collective-permute-start.31) | collective-permute-done | bytes 393248 | tf_op jit(solution)/shard_map/ppermute | solution.py:736
  284.9 4.0 %collective-permute-done.59 = bf16[1,96,768]{2,1,0:T(8,128)(2,1)S(1)} collective-permute-done((bf16[1,96,768]{2,1,0:T(8,128)(2,1)S(1)}, bf16[1,96,768]{2,1,0:T(8,128)(2,1)S(1)}, u32[]{:S(2)}, u32[]{:S(2)}) %collective-permute-start.59) | collective-permute-done | bytes 147488 | tf_op jit(solution)/shard_map/ppermute | solution.py:710
  288.9 1.8 add_bitcast_fusion
  290.7 1.9 shard_map.307
  293.5 2.7 collective-permute-start.52
  296.2 13.0 %shard_map.303 = (bf16[1024,384]{1,0:T(8,128)(2,1)S(1)}, bf16[1024,384]{1,0:T(8,128)(2,1)S(1)}, bf16[1024,384]{1,0:T(8,128)(2,1)S(1)}) custom-call(s32[4]{0:T(128)S(1)} %copy-done.20, bf16[1024,384]{1,0:T(8,128)(2,1)S(1)} %copy-done.32, bf16[1024,384]{1,0:T(8,128)(2,1)S(1)} %copy-done.34, bf16[1024,384]{1,0:T(8,128)(2,1)S(1)} %copy-done.36, ...), custom_call_target="tpu_custom_call" | custom-call | flops 6039797760 | bytes 6291456 | tf_op jit(solution)/shard_map/pallas_call | solution.py:35
  309.3 4.6 %shard_map.304 = (f32[512,768]{1,0:T(8,128)}, bf16[512,768]{1,0:T(8,128)(2,1)S(1)}) custom-call(s32[4]{0:T(128)S(1)} %copy-done.20, bf16[1024,384]{1,0:T(8,128)(2,1)S(1)} %get-tuple-element.87.refs_0_.refs_9_, bf16[1024,384]{1,0:T(8,128)(2,1)S(1)} %get-tuple-element.88.refs_1_.refs_10_, bf16[1024,384]{1,0:T(8,128)(2,1)S(1)} %get-tuple-element.89.refs_2_.refs_11_, ...), custom_call_target="tpu_custom_call" | custom-call | flops 1811939328 | bytes 8388608 | tf_op jit(solution)/shard_map/pallas_call | solution.py:35
  316.5 8.9 %shard_map.305 = (bf16[512,768]{1,0:T(8,128)(2,1)S(1)}, bf16[192,1280]{1,0:T(8,128)(2,1)S(1)}, bf16[192,1280]{1,0:T(8,128)(2,1)S(1)}, bf16[192,1280]{1,0:T(8,128)(2,1)S(1)}, bf16[192,1280]{1,0:T(8,128)(2,1)S(1)}) custom-call(s32[4]{0:T(128)S(1)} %copy-done.20, f32[512,768]{1,0:T(8,128)} %get-tuple-element.90.refs_0_, ...), custom_call_target="tpu_custom_call" | custom-call | flops 1811939328 | bytes 14680064 | tf_op jit(solution)/shard_map/pallas_call | solution.py:35
  326.3 3.1 collective-permute-start.34
  329.4 2.1 collective-permute-start.35
  339.4 1.9 select_n.180
  341.3 5.8 %collective-permute-done.35 = bf16[256,768]{1,0:T(8,128)(2,1)} collective-permute-done((bf16[256,768]{1,0:T(8,128)(2,1)}, bf16[256,768]{1,0:T(8,128)(2,1)}, u32[]{:S(2)}, u32[]{:S(2)}) %collective-permute-start.35) | collective-permute-done | bytes 393248 | tf_op jit(solution)/shard_map/ppermute | solution.py:736
  348.2 7.3 %collective-permute-done.38.refs_3_ = bf16[2,4,24,1280]{3,2,1,0:T(8,128)(2,1)S(1)} collective-permute-done((bf16[2,4,24,1280]{3,2,1,0:T(8,128)(2,1)S(1)}, bf16[2,4,24,1280]{3,2,1,0:T(8,128)(2,1)S(1)}, u32[]{:S(2)}, u32[]{:S(2)}) %collective-permute-start.38) | collective-permute-done | bytes 491552 | tf_op jit(solution)/shard_map/ppermute | solution.py:710
  355.6 1.9 shard_map.306
  358.3 2.6 collective-permute-start.40
  363.9 5.5 %collective-permute-done.41 = bf16[2,24,1280]{2,1,0:T(8,128)(2,1)S(1)} collective-permute-done((bf16[2,24,1280]{2,1,0:T(8,128)(2,1)S(1)}, bf16[2,24,1280]{2,1,0:T(8,128)(2,1)S(1)}, u32[]{:S(2)}, u32[]{:S(2)}) %collective-permute-start.41) | collective-permute-done | bytes 122912 | tf_op jit(solution)/shard_map/ppermute | solution.py:710
  369.5 3.1 collective-permute-start.42
  (288 shorter events, 77.4 us)
Async XLA Ops:
  13.8 45.1 %collective-permute-start.12 = (bf16[256,768]{1,0:T(8,128)(2,1)}, bf16[256,768]{1,0:T(8,128)(2,1)S(1)}, u32[]{:S(2)}, u32[]{:S(2)}) collective-permute-start(bf16[256,768]{1,0:T(8,128)(2,1)} %get-tuple-element.147), channel_id=1, source_target_pairs={{0,0},{1,1},{2,4},{3,5},{4,2},{5,3},{6,6},{7,7},{8,8},{9,9},{10,12... | collective-permute-start | bytes 1179656 | tf_op jit(solution)/shard_map/ppermute | solution.py:724
  20.1 13.7 %collective-permute-start.6 = (bf16[2,24,1280]{2,1,0:T(8,128)(2,1)S(1)}, bf16[2,24,1280]{2,1,0:T(8,128)(2,1)S(1)}, u32[]{:S(2)}, u32[]{:S(2)}) collective-permute-start(bf16[2,24,1280]{2,1,0:T(8,128)(2,1)S(1)} %maximum_select_fusion.4.a), channel_id=1, source_target_pairs={{0,2},{1,3},{2,0},{3,1},{4,6},{5,7},{6,4},{7,5},{8,10},{9,11},{10,... | collective-permute-start | bytes 368648 | tf_op jit(solution)/shard_map/ppermute | solution.py:710
  20.1 13.7 %collective-permute-start.7 = (bf16[2,24,1280]{2,1,0:T(8,128)(2,1)S(1)}, bf16[2,24,1280]{2,1,0:T(8,128)(2,1)S(1)}, u32[]{:S(2)}, u32[]{:S(2)}) collective-permute-start(bf16[2,24,1280]{2,1,0:T(8,128)(2,1)S(1)} %maximum_select_fusion.4.a), channel_id=1, source_target_pairs={{0,3},{1,2},{2,1},{3,0},{4,7},{5,6},{6,5},{7,4},{8,11},{9,10},{10,... | collective-permute-start | bytes 368648 | tf_op jit(solution)/shard_map/ppermute | solution.py:710
  34.4 13.9 %collective-permute-start.17 = (bf16[2,24,2304]{2,1,0:T(8,128)(2,1)S(1)}, bf16[2,24,2304]{2,1,0:T(8,128)(2,1)S(1)}, u32[]{:S(2)}, u32[]{:S(2)}) collective-permute-start(bf16[2,24,2304]{2,1,0:T(8,128)(2,1)S(1)} %maximum_select_fusion.3.a), channel_id=1, source_target_pairs={{0,1},{1,0},{2,3},{3,2},{4,5},{5,4},{6,7},{7,6},{8,9},{9,8},{10,11... | collective-permute-start | bytes 663560 | tf_op jit(solution)/shard_map/ppermute | solution.py:710
  42.1 15.9 %collective-permute-start.19 = (bf16[2,24,2304]{2,1,0:T(8,128)(2,1)S(1)}, bf16[2,24,2304]{2,1,0:T(8,128)(2,1)S(1)}, u32[]{:S(2)}, u32[]{:S(2)}) collective-permute-start(bf16[2,24,2304]{2,1,0:T(8,128)(2,1)S(1)} %maximum_select_fusion.3.a), channel_id=1, source_target_pairs={{0,3},{1,2},{2,1},{3,0},{4,7},{5,6},{6,5},{7,4},{8,11},{9,10},{10,... | collective-permute-start | bytes 663560 | tf_op jit(solution)/shard_map/ppermute | solution.py:710
  43.4 41.5 %collective-permute-start = (bf16[272,768]{1,0:T(8,128)(2,1)S(1)}, bf16[272,768]{1,0:T(8,128)(2,1)S(1)}, u32[]{:S(2)}, u32[]{:S(2)}) collective-permute-start(bf16[272,768]{1,0:T(8,128)(2,1)S(1)} %get-tuple-element.137), channel_id=1, source_target_pairs={{0,0},{1,1},{2,4},{3,5},{4,2},{5,3},{6,6},{7,7},{8,8},{9,9},{10,12... | collective-permute-start | bytes 1253384 | tf_op jit(solution)/shard_map/ppermute | solution.py:724
  48.3 23.8 %collective-permute-start.13 = (bf16[256,768]{1,0:T(8,128)(2,1)S(1)}, bf16[256,768]{1,0:T(8,128)(2,1)S(1)}, u32[]{:S(2)}, u32[]{:S(2)}) collective-permute-start(bf16[256,768]{1,0:T(8,128)(2,1)S(1)} %copy-done.49), channel_id=1, source_target_pairs={{0,1},{1,0},{2,5},{3,4},{4,3},{5,2},{6,7},{7,6},{8,9},{9,8},{10,13... | collective-permute-start | bytes 1179656 | tf_op jit(solution)/shard_map/ppermute | solution.py:724
  48.9 36.0 %collective-permute-start.1 = (bf16[272,768]{1,0:T(8,128)(2,1)S(1)}, bf16[272,768]{1,0:T(8,128)(2,1)S(1)}, u32[]{:S(2)}, u32[]{:S(2)}) collective-permute-start(bf16[272,768]{1,0:T(8,128)(2,1)S(1)} %get-tuple-element.136), channel_id=1, source_target_pairs={{0,1},{1,0},{2,5},{3,4},{4,3},{5,2},{6,7},{7,6},{8,9},{9,8},{10,13... | collective-permute-start | bytes 1253384 | tf_op jit(solution)/shard_map/ppermute | solution.py:724
  58.1 41.7 %collective-permute-start.8 = (bf16[2,4,24,1280]{3,2,1,0:T(8,128)(2,1)S(1)}, bf16[2,4,24,1280]{3,2,1,0:T(8,128)(2,1)S(1)}, u32[]{:S(2)}, u32[]{:S(2)}) collective-permute-start(bf16[2,4,24,1280]{3,2,1,0:T(8,128)(2,1)S(1)} %shard_map.297), channel_id=1, source_target_pairs={{0,8},{4,12},{8,0},{12,4},{16,24},{20,28},{24,16},{28,20},{1,9},{5... | collective-permute-start | bytes 1474568 | tf_op jit(solution)/shard_map/ppermute | solution.py:710
  58.9 64.2 %collective-permute-start.21 = (bf16[2,4,24,2304]{3,2,1,0:T(8,128)(2,1)S(1)}, bf16[2,4,24,2304]{3,2,1,0:T(8,128)(2,1)}, u32[]{:S(2)}, u32[]{:S(2)}) collective-permute-start(bf16[2,4,24,2304]{3,2,1,0:T(8,128)(2,1)S(1)} %shard_map.300), channel_id=1, source_target_pairs={{0,16},{4,20},{8,24},{12,28},{16,0},{20,4},{24,8},{28,12},{1,17},{... | collective-permute-start | bytes 2654216 | tf_op jit(solution)/shard_map/ppermute | solution.py:710
  72.1 15.3 %collective-permute-start.23 = (bf16[96,768]{1,0:T(8,128)(2,1)S(1)}, bf16[96,768]{1,0:T(8,128)(2,1)S(1)}, u32[]{:S(2)}, u32[]{:S(2)}) collective-permute-start(bf16[96,768]{1,0:T(8,128)(2,1)S(1)} %copy-done.50), channel_id=1, source_target_pairs={{0,1},{1,0},{2,3},{3,2},{4,5},{5,4},{6,7},{7,6},{8,9},{9,8},{10,11... | collective-permute-start | bytes 442376 | tf_op jit(solution)/shard_map/ppermute | solution.py:710
  84.8 13.0 %collective-permute-start.24 = (bf16[96,768]{1,0:T(8,128)(2,1)S(1)}, bf16[96,768]{1,0:T(8,128)(2,1)S(1)}, u32[]{:S(2)}, u32[]{:S(2)}) collective-permute-start(bf16[96,768]{1,0:T(8,128)(2,1)S(1)} %copy-done.50), channel_id=1, source_target_pairs={{0,2},{1,3},{2,0},{3,1},{4,6},{5,7},{6,4},{7,5},{8,10},{9,11},{10,... | collective-permute-start | bytes 442376 | tf_op jit(solution)/shard_map/ppermute | solution.py:710
  84.8 13.2 %collective-permute-start.25 = (bf16[96,768]{1,0:T(8,128)(2,1)S(1)}, bf16[96,768]{1,0:T(8,128)(2,1)S(1)}, u32[]{:S(2)}, u32[]{:S(2)}) collective-permute-start(bf16[96,768]{1,0:T(8,128)(2,1)S(1)} %copy-done.50), channel_id=1, source_target_pairs={{0,3},{1,2},{2,1},{3,0},{4,7},{5,6},{6,5},{7,4},{8,11},{9,10},{10,... | collective-permute-start | bytes 442376 | tf_op jit(solution)/shard_map/ppermute | solution.py:710
  87.4 13.4 %collective-permute-start.9 = (bf16[2,4,24,1280]{3,2,1,0:T(8,128)(2,1)S(1)}, bf16[2,4,24,1280]{3,2,1,0:T(8,128)(2,1)S(1)}, u32[]{:S(2)}, u32[]{:S(2)}) collective-permute-start(bf16[2,4,24,1280]{3,2,1,0:T(8,128)(2,1)S(1)} %shard_map.297), channel_id=1, source_target_pairs={{0,16},{4,20},{8,24},{12,28},{16,0},{20,4},{24,8},{28,12},{1,17},{... | collective-permute-start | bytes 1474568 | tf_op jit(solution)/shard_map/ppermute | solution.py:710
  97.9 12.2 %collective-permute-start.10 = (bf16[2,4,24,1280]{3,2,1,0:T(8,128)(2,1)S(1)}, bf16[2,4,24,1280]{3,2,1,0:T(8,128)(2,1)S(1)}, u32[]{:S(2)}, u32[]{:S(2)}) collective-permute-start(bf16[2,4,24,1280]{3,2,1,0:T(8,128)(2,1)S(1)} %shard_map.297), channel_id=1, source_target_pairs={{0,24},{4,28},{8,16},{12,20},{16,8},{20,12},{24,0},{28,4},{1,25},{... | collective-permute-start | bytes 1474568 | tf_op jit(solution)/shard_map/ppermute | solution.py:710
  98.1 14.3 %collective-permute-start.2 = (bf16[272,768]{1,0:T(8,128)(2,1)S(1)}, bf16[272,768]{1,0:T(8,128)(2,1)S(1)}, u32[]{:S(2)}, u32[]{:S(2)}) collective-permute-start(bf16[272,768]{1,0:T(8,128)(2,1)S(1)} %collective-permute-done.refs_0_), channel_id=1, source_target_pairs={{0,4},{4,0},{8,12},{12,8},{16,20},{20,16},{24,28},{28,24},{1,5},{5... | collective-permute-start | bytes 1253384 | tf_op jit(solution)/shard_map/ppermute | solution.py:710
  99.8 12.9 %collective-permute-start.3 = (bf16[272,768]{1,0:T(8,128)(2,1)S(1)}, bf16[272,768]{1,0:T(8,128)(2,1)S(1)}, u32[]{:S(2)}, u32[]{:S(2)}) collective-permute-start(bf16[272,768]{1,0:T(8,128)(2,1)S(1)} %collective-permute-done.1.refs_1_), channel_id=1, source_target_pairs={{0,4},{4,0},{8,12},{12,8},{16,20},{20,16},{24,28},{28,24},{1,5},{5... | collective-permute-start | bytes 1253384 | tf_op jit(solution)/shard_map/ppermute | solution.py:710
  100.8 38.1 %collective-permute-start.14 = (bf16[256,768]{1,0:T(8,128)(2,1)S(1)}, bf16[256,768]{1,0:T(8,128)(2,1)S(1)}, u32[]{:S(2)}, u32[]{:S(2)}) collective-permute-start(bf16[256,768]{1,0:T(8,128)(2,1)S(1)} %collective-permute-done.12.refs_5_), channel_id=1, source_target_pairs={{0,4},{4,0},{8,12},{12,8},{16,20},{20,16},{24,28},{28,24},{1,5},{5... | collective-permute-start | bytes 1179656 | tf_op jit(solution)/shard_map/ppermute | solution.py:710
  110.1 29.4 %collective-permute-start.15 = (bf16[256,768]{1,0:T(8,128)(2,1)S(1)}, bf16[256,768]{1,0:T(8,128)(2,1)S(1)}, u32[]{:S(2)}, u32[]{:S(2)}) collective-permute-start(bf16[256,768]{1,0:T(8,128)(2,1)S(1)} %collective-permute-done.13.refs_6_), channel_id=1, source_target_pairs={{0,4},{4,0},{8,12},{12,8},{16,20},{20,16},{24,28},{28,24},{1,5},{5... | collective-permute-start | bytes 1179656 | tf_op jit(solution)/shard_map/ppermute | solution.py:710
  112.4 41.9 %collective-permute-start.20 = (bf16[2,4,24,2304]{3,2,1,0:T(8,128)(2,1)S(1)}, bf16[2,4,24,2304]{3,2,1,0:T(8,128)(2,1)S(1)}, u32[]{:S(2)}, u32[]{:S(2)}) collective-permute-start(bf16[2,4,24,2304]{3,2,1,0:T(8,128)(2,1)S(1)} %shard_map.300), channel_id=1, source_target_pairs={{0,8},{4,12},{8,0},{12,4},{16,24},{20,28},{24,16},{28,20},{1,9},{5... | collective-permute-start | bytes 2654216 | tf_op jit(solution)/shard_map/ppermute | solution.py:710
  112.7 33.7 %collective-permute-start.26 = (bf16[4,96,768]{2,1,0:T(8,128)(2,1)}, bf16[4,96,768]{2,1,0:T(8,128)(2,1)}, u32[]{:S(2)}, u32[]{:S(2)}) collective-permute-start(bf16[4,96,768]{2,1,0:T(8,128)(2,1)} %pad_maximum_fusion.2.refs_13_), channel_id=1, source_target_pairs={{0,8},{4,12},{8,0},{12,4},{16,24},{20,28},{24,16},{28,20},{1,9},{5... | collective-permute-start | bytes 1769480 | tf_op jit(solution)/shard_map/ppermute | solution.py:710
  123.2 43.7 %collective-permute-start.22 = (bf16[2,4,24,2304]{3,2,1,0:T(8,128)(2,1)}, bf16[2,4,24,2304]{3,2,1,0:T(8,128)(2,1)}, u32[]{:S(2)}, u32[]{:S(2)}) collective-permute-start(bf16[2,4,24,2304]{3,2,1,0:T(8,128)(2,1)} %collective-permute-done.21), channel_id=1, source_target_pairs={{0,8},{4,12},{8,0},{12,4},{16,24},{20,28},{24,16},{28,20},{1,9},{5... | collective-permute-start | bytes 2654216 | tf_op jit(solution)/shard_map/ppermute | solution.py:710
  138.9 15.4 %collective-permute-start.11 = (bf16[1024,384]{1,0:T(8,128)(2,1)S(1)}, bf16[1024,384]{1,0:T(8,128)(2,1)}, u32[]{:S(2)}, u32[]{:S(2)}) collective-permute-start(bf16[1024,384]{1,0:T(8,128)(2,1)S(1)} %get-tuple-element.74.refs_0_.refs_4_.o), channel_id=1, source_target_pairs={{0,4},{4,0},{8,12},{12,8},{16,20},{20,16},{24,28},{28,24},{1,5},{5... | collective-permute-start | bytes 2359304 | tf_op jit(solution)/shard_map/ppermute | solution.py:710
  139.7 14.6 %collective-permute-start.27 = (bf16[4,96,768]{2,1,0:T(8,128)(2,1)}, bf16[4,96,768]{2,1,0:T(8,128)(2,1)}, u32[]{:S(2)}, u32[]{:S(2)}) collective-permute-start(bf16[4,96,768]{2,1,0:T(8,128)(2,1)} %pad_maximum_fusion.2.refs_13_), channel_id=1, source_target_pairs={{0,16},{4,20},{8,24},{12,28},{16,0},{20,4},{24,8},{28,12},{1,17},{... | collective-permute-start | bytes 1769480 | tf_op jit(solution)/shard_map/ppermute | solution.py:710
  146.4 20.6 %collective-permute-start.28 = (bf16[4,96,768]{2,1,0:T(8,128)(2,1)}, bf16[4,96,768]{2,1,0:T(8,128)(2,1)}, u32[]{:S(2)}, u32[]{:S(2)}) collective-permute-start(bf16[4,96,768]{2,1,0:T(8,128)(2,1)} %collective-permute-done.26.refs_14_), channel_id=1, source_target_pairs={{0,16},{4,20},{8,24},{12,28},{16,0},{20,4},{24,8},{28,12},{1,17},{... | collective-permute-start | bytes 1769480 | tf_op jit(solution)/shard_map/ppermute | solution.py:710
  203.9 13.6 %collective-permute-start.55 = (bf16[1,4,96,768]{3,2,1,0:T(8,128)(2,1)}, bf16[1,4,96,768]{3,2,1,0:T(8,128)(2,1)S(1)}, u32[]{:S(2)}, u32[]{:S(2)}) collective-permute-start(bf16[1,4,96,768]{3,2,1,0:T(8,128)(2,1)} %bitcast.173), channel_id=1, source_target_pairs={{0,16},{4,20},{8,24},{12,28},{16,0},{20,4},{24,8},{28,12},{1,17},{... | collective-permute-start | bytes 1769480 | tf_op jit(solution)/shard_map/ppermute | solution.py:710
  204.3 49.9 %collective-permute-start.54 = (bf16[1,4,96,768]{3,2,1,0:T(8,128)(2,1)}, bf16[1,4,96,768]{3,2,1,0:T(8,128)(2,1)}, u32[]{:S(2)}, u32[]{:S(2)}) collective-permute-start(bf16[1,4,96,768]{3,2,1,0:T(8,128)(2,1)} %bitcast.170), channel_id=1, source_target_pairs={{0,16},{4,20},{8,24},{12,28},{16,0},{20,4},{24,8},{28,12},{1,17},{... | collective-permute-start | bytes 1769480 | tf_op jit(solution)/shard_map/ppermute | solution.py:710
  205.6 31.8 %collective-permute-start.32 = (bf16[1024,768]{1,0:T(8,128)(2,1)}, bf16[1024,768]{1,0:T(8,128)(2,1)}, u32[]{:S(2)}, u32[]{:S(2)}) collective-permute-start(bf16[1024,768]{1,0:T(8,128)(2,1)} %get-tuple-element.83), channel_id=1, source_target_pairs={{0,4},{4,0},{8,12},{12,8},{16,20},{20,16},{24,28},{28,24},{1,5},{5... | collective-permute-start | bytes 4718600 | tf_op jit(solution)/shard_map/ppermute | solution.py:710
  207.6 15.5 %collective-permute-start.44 = (bf16[2,4,24,1536]{3,2,1,0:T(8,128)(2,1)}, bf16[2,4,24,1536]{3,2,1,0:T(8,128)(2,1)S(1)}, u32[]{:S(2)}, u32[]{:S(2)}) collective-permute-start(bf16[2,4,24,1536]{3,2,1,0:T(8,128)(2,1)} %bitcast.172), channel_id=1, source_target_pairs={{0,8},{4,12},{8,0},{12,4},{16,24},{20,28},{24,16},{28,20},{1,9},{5... | collective-permute-start | bytes 1769480 | tf_op jit(solution)/shard_map/ppermute | solution.py:710
  208.7 26.8 %collective-permute-start.43 = (bf16[2,4,24,1536]{3,2,1,0:T(8,128)(2,1)}, bf16[2,4,24,1536]{3,2,1,0:T(8,128)(2,1)}, u32[]{:S(2)}, u32[]{:S(2)}) collective-permute-start(bf16[2,4,24,1536]{3,2,1,0:T(8,128)(2,1)} %bitcast.171), channel_id=1, source_target_pairs={{0,8},{4,12},{8,0},{12,4},{16,24},{20,28},{24,16},{28,20},{1,9},{5... | collective-permute-start | bytes 1769480 | tf_op jit(solution)/shard_map/ppermute | solution.py:710
  217.5 19.6 %collective-permute-start.29 = (bf16[512,768]{1,0:T(8,128)(2,1)}, bf16[512,768]{1,0:T(8,128)(2,1)S(1)}, u32[]{:S(2)}, u32[]{:S(2)}) collective-permute-start(bf16[512,768]{1,0:T(8,128)(2,1)} %get-tuple-element.81), channel_id=1, source_target_pairs={{0,4},{4,0},{8,12},{12,8},{16,20},{20,16},{24,28},{28,24},{1,5},{5... | collective-permute-start | bytes 2359304 | tf_op jit(solution)/shard_map/ppermute | solution.py:710
  223.1 37.0 %collective-permute-start.56 = (bf16[1,4,96,768]{3,2,1,0:T(8,128)(2,1)S(1)}, bf16[1,4,96,768]{3,2,1,0:T(8,128)(2,1)S(1)}, u32[]{:S(2)}, u32[]{:S(2)}) collective-permute-start(bf16[1,4,96,768]{3,2,1,0:T(8,128)(2,1)S(1)} %fusion), channel_id=1, source_target_pairs={{0,8},{4,12},{8,0},{12,4},{16,24},{20,28},{24,16},{28,20},{1,9},{5... | collective-permute-start | bytes 1769480 | tf_op jit(solution)/shard_map/ppermute | solution.py:710
  235.5 55.2 %collective-permute-start.45 = (bf16[2,4,24,1536]{3,2,1,0:T(8,128)(2,1)}, bf16[2,4,24,1536]{3,2,1,0:T(8,128)(2,1)S(1)}, u32[]{:S(2)}, u32[]{:S(2)}) collective-permute-start(bf16[2,4,24,1536]{3,2,1,0:T(8,128)(2,1)} %fusion.2), channel_id=1, source_target_pairs={{0,16},{4,20},{8,24},{12,28},{16,0},{20,4},{24,8},{28,12},{1,17},{... | collective-permute-start | bytes 1769480 | tf_op jit(solution)/shard_map/ppermute | solution.py:710
  250.3 15.7 %collective-permute-start.46 = (bf16[2,96,768]{2,1,0:T(8,128)(2,1)}, bf16[2,96,768]{2,1,0:T(8,128)(2,1)}, u32[]{:S(2)}, u32[]{:S(2)}) collective-permute-start(bf16[2,96,768]{2,1,0:T(8,128)(2,1)} %get-tuple-element.111), channel_id=1, source_target_pairs={{0,4},{4,0},{8,12},{12,8},{16,20},{20,16},{24,28},{28,24},{1,5},{5... | collective-permute-start | bytes 884744 | tf_op jit(solution)/shard_map/ppermute | solution.py:710
  252.8 19.3 %collective-permute-start.30 = (bf16[256,768]{1,0:T(8,128)(2,1)}, bf16[256,768]{1,0:T(8,128)(2,1)}, u32[]{:S(2)}, u32[]{:S(2)}) collective-permute-start(bf16[256,768]{1,0:T(8,128)(2,1)} %get-tuple-element.144), channel_id=1, source_target_pairs={{1,0},{0,1},{5,2},{4,3},{3,4},{2,5},{7,6},{6,7},{9,8},{8,9},{13,10... | collective-permute-start | bytes 1179656 | tf_op jit(solution)/shard_map/ppermute | solution.py:736
  254.2 25.2 %collective-permute-start.31 = (bf16[256,768]{1,0:T(8,128)(2,1)}, bf16[256,768]{1,0:T(8,128)(2,1)}, u32[]{:S(2)}, u32[]{:S(2)}) collective-permute-start(bf16[256,768]{1,0:T(8,128)(2,1)} %get-tuple-element.145), channel_id=1, source_target_pairs={{0,0},{1,1},{4,2},{5,3},{2,4},{3,5},{6,6},{7,7},{8,8},{9,9},{12,10... | collective-permute-start | bytes 1179656 | tf_op jit(solution)/shard_map/ppermute | solution.py:736
  263.3 21.7 %collective-permute-start.57 = (bf16[1,96,768]{2,1,0:T(8,128)(2,1)}, bf16[1,96,768]{2,1,0:T(8,128)(2,1)}, u32[]{:S(2)}, u32[]{:S(2)}) collective-permute-start(bf16[1,96,768]{2,1,0:T(8,128)(2,1)} %get-tuple-element.121), channel_id=1, source_target_pairs={{0,1},{1,0},{2,3},{3,2},{4,5},{5,4},{6,7},{7,6},{8,9},{9,8},{10,11... | collective-permute-start | bytes 442376 | tf_op jit(solution)/shard_map/ppermute | solution.py:710
  266.0 18.9 %collective-permute-start.58 = (bf16[1,96,768]{2,1,0:T(8,128)(2,1)}, bf16[1,96,768]{2,1,0:T(8,128)(2,1)}, u32[]{:S(2)}, u32[]{:S(2)}) collective-permute-start(bf16[1,96,768]{2,1,0:T(8,128)(2,1)} %copy-done.30), channel_id=1, source_target_pairs={{0,2},{1,3},{2,0},{3,1},{4,6},{5,7},{6,4},{7,5},{8,10},{9,11},{10,... | collective-permute-start | bytes 442376 | tf_op jit(solution)/shard_map/ppermute | solution.py:710
  272.1 10.5 %collective-permute-start.47 = (bf16[2,4,24,384]{3,2,1,0:T(8,128)(2,1)S(1)}, bf16[2,4,24,384]{3,2,1,0:T(8,128)(2,1)S(1)}, u32[]{:S(2)}, u32[]{:S(2)}) collective-permute-start(bf16[2,4,24,384]{3,2,1,0:T(8,128)(2,1)S(1)} %get-tuple-element.151), channel_id=1, source_target_pairs={{0,8},{4,12},{8,0},{12,4},{16,24},{20,28},{24,16},{28,20},{1,9},{5... | collective-permute-start | bytes 442376 | tf_op jit(solution)/shard_map/ppermute | solution.py:710
  292.6 22.0 %collective-permute-start.50 = (bf16[2,24,1920]{2,1,0:T(8,128)(2,1)S(1)}, bf16[2,24,1920]{2,1,0:T(8,128)(2,1)S(1)}, u32[]{:S(2)}, u32[]{:S(2)}) collective-permute-start(bf16[2,24,1920]{2,1,0:T(8,128)(2,1)S(1)} %get-tuple-element.113), channel_id=1, source_target_pairs={{0,1},{1,0},{2,3},{3,2},{4,5},{5,4},{6,7},{7,6},{8,9},{9,8},{10,11... | collective-permute-start | bytes 552968 | tf_op jit(solution)/shard_map/ppermute | solution.py:710
  292.6 22.0 %collective-permute-start.51 = (bf16[2,24,1920]{2,1,0:T(8,128)(2,1)S(1)}, bf16[2,24,1920]{2,1,0:T(8,128)(2,1)S(1)}, u32[]{:S(2)}, u32[]{:S(2)}) collective-permute-start(bf16[2,24,1920]{2,1,0:T(8,128)(2,1)S(1)} %get-tuple-element.114), channel_id=1, source_target_pairs={{0,2},{1,3},{2,0},{3,1},{4,6},{5,7},{6,4},{7,5},{8,10},{9,11},{10,... | collective-permute-start | bytes 552968 | tf_op jit(solution)/shard_map/ppermute | solution.py:710
  293.5 21.1 %collective-permute-start.52 = (bf16[2,24,1920]{2,1,0:T(8,128)(2,1)S(1)}, bf16[2,24,1920]{2,1,0:T(8,128)(2,1)S(1)}, u32[]{:S(2)}, u32[]{:S(2)}) collective-permute-start(bf16[2,24,1920]{2,1,0:T(8,128)(2,1)S(1)} %get-tuple-element.115), channel_id=1, source_target_pairs={{0,3},{1,2},{2,1},{3,0},{4,7},{5,6},{6,5},{7,4},{8,11},{9,10},{10,... | collective-permute-start | bytes 552968 | tf_op jit(solution)/shard_map/ppermute | solution.py:710
  315.3 18.6 %collective-permute-start.53 = (bf16[24,1536]{1,0:T(8,128)(2,1)}, bf16[24,1536]{1,0:T(8,128)(2,1)}, u32[]{:S(2)}, u32[]{:S(2)}) collective-permute-start(bf16[24,1536]{1,0:T(8,128)(2,1)} %fusion.8), channel_id=1, source_target_pairs={{0,4},{4,0},{8,12},{12,8},{16,20},{20,16},{24,28},{28,24},{1,5},{5... | collective-permute-start | bytes 221192 | tf_op jit(solution)/shard_map/ppermute | solution.py:710
  326.3 15.0 %collective-permute-start.34 = (bf16[256,768]{1,0:T(8,128)(2,1)}, bf16[256,768]{1,0:T(8,128)(2,1)}, u32[]{:S(2)}, u32[]{:S(2)}) collective-permute-start(bf16[256,768]{1,0:T(8,128)(2,1)} %get-tuple-element.140), channel_id=1, source_target_pairs={{1,0},{0,1},{5,2},{4,3},{3,4},{2,5},{7,6},{6,7},{9,8},{8,9},{13,10... | collective-permute-start | bytes 1179656 | tf_op jit(solution)/shard_map/ppermute | solution.py:736
  329.4 17.6 %collective-permute-start.35 = (bf16[256,768]{1,0:T(8,128)(2,1)}, bf16[256,768]{1,0:T(8,128)(2,1)}, u32[]{:S(2)}, u32[]{:S(2)}) collective-permute-start(bf16[256,768]{1,0:T(8,128)(2,1)} %get-tuple-element.141), channel_id=1, source_target_pairs={{0,0},{1,1},{4,2},{5,3},{2,4},{3,5},{6,6},{7,7},{8,8},{9,9},{12,10... | collective-permute-start | bytes 1179656 | tf_op jit(solution)/shard_map/ppermute | solution.py:736
  332.3 15.9 %collective-permute-start.36 = (bf16[2,4,24,1280]{3,2,1,0:T(8,128)(2,1)S(1)}, bf16[2,4,24,1280]{3,2,1,0:T(8,128)(2,1)S(1)}, u32[]{:S(2)}, u32[]{:S(2)}) collective-permute-start(bf16[2,4,24,1280]{3,2,1,0:T(8,128)(2,1)S(1)} %bitcast.142), channel_id=1, source_target_pairs={{0,8},{4,12},{8,0},{12,4},{16,24},{20,28},{24,16},{28,20},{1,9},{5... | collective-permute-start | bytes 1474568 | tf_op jit(solution)/shard_map/ppermute | solution.py:710
  332.7 15.5 %collective-permute-start.37 = (bf16[2,4,24,1280]{3,2,1,0:T(8,128)(2,1)S(1)}, bf16[2,4,24,1280]{3,2,1,0:T(8,128)(2,1)S(1)}, u32[]{:S(2)}, u32[]{:S(2)}) collective-permute-start(bf16[2,4,24,1280]{3,2,1,0:T(8,128)(2,1)S(1)} %bitcast.141), channel_id=1, source_target_pairs={{0,16},{4,20},{8,24},{12,28},{16,0},{20,4},{24,8},{28,12},{1,17},{... | collective-permute-start | bytes 1474568 | tf_op jit(solution)/shard_map/ppermute | solution.py:710
  334.0 21.6 %collective-permute-start.38 = (bf16[2,4,24,1280]{3,2,1,0:T(8,128)(2,1)S(1)}, bf16[2,4,24,1280]{3,2,1,0:T(8,128)(2,1)S(1)}, u32[]{:S(2)}, u32[]{:S(2)}) collective-permute-start(bf16[2,4,24,1280]{3,2,1,0:T(8,128)(2,1)S(1)} %bitcast.140), channel_id=1, source_target_pairs={{0,24},{4,28},{8,16},{12,20},{16,8},{20,12},{24,0},{28,4},{1,25},{... | collective-permute-start | bytes 1474568 | tf_op jit(solution)/shard_map/ppermute | solution.py:710
  (66 other events, 849.8 us)

commit v3 on v2

--- a/solution.py
+++ b/solution.py
@@ -15,6 +15,7 @@
 f32 = jnp.float32
 bf16 = jnp.bfloat16
 MIB = 1 << 20
+LOAD, HELD = "load", "held"
 QUERY_BIAS, VALUE_BIAS, OUTPUT_BIAS, GAIN_ONE, SHIFT_ONE, DOWN_BIAS, GAIN_TWO, SHIFT_TWO = range(8)
 SMALL = 128
 
@@ -31,13 +32,38 @@
     return lax.dot_general(left, right, (((1,), (1,)), ((), ())), preferred_element_type=f32)
 
 
-def call(kernel, outs, ins, args, scratch=(), grid=None, limit=48, cost=None):
+def call(kernel, outs, ins, args, scratch=(), grid=None, limit=14, cost=None):
+    loads = []
+    specs = [pl.BlockSpec(memory_space=pltpu.SMEM)]
+    for index, (spec, array) in enumerate(zip(ins, args[1:], strict=True)):
+        if spec == LOAD:
+            whole = False
+            spec = pl.BlockSpec(memory_space=pl.ANY if whole else pltpu.VMEM)
+            if whole:
+                loads.append(index)
+        elif spec == HELD:
+            spec = pl.BlockSpec(memory_space=pl.ANY)
+        specs.append(spec)
+    count, news = len(ins), len(loads)
+
+    def loaded(info, *refs):
+        refs, held, sem = list(refs[: -1 - news]), refs[-1 - news : -1], refs[-1]
+        copies = []
+        for i, index in enumerate(loads):
+            copies.append(pltpu.make_async_copy(refs[index], held[i], sem.at[i]))
+            refs[index] = held[i]
+        run_copies(copies)
+        kernel(info, *refs)
+
+    extra = [pltpu.VMEM(args[1 + i].shape, args[1 + i].dtype) for i in loads]
+    if loads:
+        extra.append(pltpu.SemaphoreType.DMA((news,)))
     return pl.pallas_call(
-        kernel,
+        loaded if loads else kernel,
         out_shape=[shape for shape, _ in outs],
-        in_specs=[pl.BlockSpec(memory_space=pltpu.SMEM)] + list(ins),
+        in_specs=specs,
         out_specs=[spec for _, spec in outs],
-        scratch_shapes=list(scratch),
+        scratch_shapes=list(scratch) + extra,
         **({"grid": grid} if grid else {}),
         compiler_params=pltpu.CompilerParams(vmem_limit_bytes=limit * MIB),
         cost_estimate=pl.CostEstimate(
@@ -82,22 +108,156 @@
         copy.wait()
 
 
-def arrange_kernel(info, a, b, c, d, out):
+def pack_kernel(patches, info, weight, table, rows_in, spare_in, up, out_weight, ins_keep, ins_send, ups_keep, ups_send):
+    core = info[0]
+    part = weight.shape[1] // 6
+    small = jnp.zeros((weight.shape[0], SMALL), f32)
+    turned = rows_in[...].astype(f32).T
+    count = patches + turned.shape[1]
+    small = jnp.concatenate(
+        [
+            table[...].astype(f32),
+            turned,
+            spare_in[...].astype(f32),
+            small[:, count + spare_in.shape[1] :],
+        ],
+        axis=1,
+    ).astype(bf16)
+    columns = 3 * part
+    own = ups_keep.shape[1] - out_weight.shape[1]
+    for ref, up_ref, side in ((ins_keep, ups_keep, core), (ins_send, ups_send, 1 - core)):
+        for i in range(3):
+            there = pl.ds(pl.multiple_of((2 * i + side) * part, 128), part)
+            ref[:, i * part : (i + 1) * part] = weight[:, there]
+        ref[:, columns:] = small
+        if up is not None:
+            step = own // 4
+            for q in range(4):
+                there = pl.ds(pl.multiple_of((2 * q + side) * step, 128), step)
+                up_ref[:, q * step : (q + 1) * step] = up[:, there]
+        up_ref[:, own:] = out_weight[...]
+
+
+def pack(info, weight, table, rows_in, spare_in, up, out_weight, patches):
+    rows, columns = weight.shape[0], weight.shape[1] // 2 + SMALL
+    own = up.shape[1] // 2 + out_weight.shape[1]
+    return call(
+        functools.partial(pack_kernel, patches),
+        [(shaped((rows, columns), bf16), vmem())] * 2 + [(shaped((rows, own), bf16), vmem())] * 2,
+        [vmem()] * 6,
+        [info, weight, table, rows_in, spare_in, up, out_weight],
+        limit=8,
+        cost=(0, MIB),
+    )
+
+
+def sent_kernel(info, tokens, positions, segments, first, second, extra):
     place = info[2]
-    for k, ref in enumerate((a, b, c, d)):
-        out[:, k ^ place] = ref[...]
-
-
-def arrange(info, pieces):
-    two, rows, columns = pieces[0].shape
-    return call(
-        arrange_kernel,
-        [(shaped((two, PLACES, rows, columns), bf16), vmem())],
-        [vmem()] * PLACES,
+    block, width = tokens.shape[1], tokens.shape[2]
+    full = segments.shape[1]
+    extra[...] = jnp.zeros_like(extra)
+    for k, out in enumerate((first, second)):
+        index = k ^ (place % 2)
+        row = segments[pl.ds(index, 1), :]
+        row = (row - row[:, 0:1]).astype(f32)
+        extra[0:1, :block] = positions[pl.ds(index, 1), :].astype(f32)
+        extra[1:2, :] = row[:, :width]
+        extra[2:3, : full - width] = row[:, width:]
+        out[:block, :] = tokens[index]
+        out[block:, :] = extra[...].astype(bf16)
+
+
+def sent(info, tokens, positions, segments):
+    _, block, width = tokens.shape
+    one = (shaped((block + 16, width), bf16), vmem())
+    return call(
+        sent_kernel,
+        [one, one],
+        [vmem()] * 3,
+        [info, tokens, positions, segments],
+        scratch=[pltpu.VMEM((16, width), f32)],
+        limit=8,
+        cost=(0, 2 * MIB),
+    )
+
+
+def arrange_kernel(slot, shift, info, *refs):
+    ins, out = refs[:-1], refs[-1]
+    lead = len(out.shape) - 3
+    place = lax.rem(info[slot] >> shift, len(ins))
+    for k, ref in enumerate(ins):
+        out[(slice(None),) * lead + (k ^ place,)] = ref[...]
+
+
+def arrange(info, pieces, shift=0, slot=2):
+    shape = pieces[0].shape
+    shape = shape[:-2] + (len(pieces),) + shape[-2:]
+    total = 1
+    for extent in shape:
+        total *= extent
+    return call(
+        functools.partial(arrange_kernel, slot, shift),
+        [(shaped(shape, bf16), vmem())],
+        [vmem()] * len(pieces),
         [info] + list(pieces),
-        limit=16,
-        cost=(0, 8 * two * rows * columns * 2),
+        limit=8,
+        cost=(0, 4 * total),
     )[0]
+
+
+def cut_kernel(info, x, y, first, second):
+    half = first.shape[0]
+    first[...] = y[:half]
+    second[...] = x[half:]
+
+
+def cut(info, x, y):
+    one = shaped((x.shape[0] // 2,) + x.shape[1:], bf16)
+    return call(cut_kernel, [(one, vmem())] * 2, [LOAD] * 2, [info, x, y], limit=8, cost=(0, MIB))
+
+
+def add_kernel(info, a, b, c, d, first, second):
+    first[...] = (a[...].astype(f32) + b[...].astype(f32)).astype(bf16)
+    second[...] = (c[...].astype(f32) + d[...].astype(f32)).astype(bf16)
+
+
+def add_pairs(info, a, b, c, d):
+    out = (shaped(a.shape, bf16), vmem())
+    return call(add_kernel, [out] * 2, [LOAD] * 4, [info, a, b, c, d], limit=8, cost=(0, MIB))
+
+
+def pick_kernel(info, blocks, first, second):
+    odd = lax.rem(info[2], 2)
+    first[...] = blocks[odd]
+    second[...] = blocks[1 - odd]
+
+
+def pick_turns(info, blocks):
+    out = (shaped(blocks.shape[1:], bf16), vmem())
+    return call(pick_kernel, [out] * 2, [LOAD], [info, blocks], limit=8, cost=(0, MIB))
+
+
+def output_kernel(patches, info, middle, keep, far, turned, first, second):
+    core, odd = info[0], lax.rem(info[2], 2)
+    half = keep.shape[0]
+    block = half // 2
+    bias = turned[patches + DOWN_BIAS : patches + DOWN_BIAS + 1, :]
+    for ref, which in ((first, odd), (second, 1 - odd)):
+        here = pl.ds(pl.multiple_of(which * block, block), block)
+        there = pl.ds(pl.multiple_of(core * half + which * block, block), block)
+        ref[...] = (middle[there, :] + keep[here, :] + far[here, :].astype(f32) + bias).astype(bf16)
+
+
+def output_turns(info, middle, keep, far, turned, patches):
+    out = (shaped((keep.shape[0] // 2, keep.shape[1]), bf16), vmem())
+    return call(
+        functools.partial(output_kernel, patches),
+        [out] * 2,
+        [LOAD] * 4,
+        [info, middle, keep, far, turned],
+        limit=8,
+        cost=(0, 6 * MIB),
+    )
 
 
 def front_kernel(blocks, patches, info, *refs):
@@ -170,7 +330,7 @@
             (shaped((8, rows), f32), vmem()),
             (shaped((8, rows), f32), vmem()),
         ],
-        [anywhere()] * (4 + blocks),
+        [HELD] * (4 + blocks),
         [info] + list(tokens) + list(weights),
         scratch=[
             pltpu.VMEM((4, block + 16, width), bf16),
@@ -326,159 +486,268 @@
     return values * half, grad
 
 
-def feed_kernel(blocks, patches, info, *refs):
-    att, att_far, start, turned, up_bias, refs = refs[0], refs[1], refs[2], refs[3], refs[4], refs[5:]
-    cot_in, refs = refs[:4], refs[4:]
-    up_in, refs = refs[:blocks], refs[blocks:]
-    down_in, refs = refs[:blocks], refs[blocks:]
-    keep_out, send_out, back_out, back_low, middle_out, bias_out, refs = (
-        refs[0], refs[1], refs[2], refs[3], refs[4], refs[5], refs[6:],
-    )
-    up_grads, refs = refs[:blocks], refs[blocks:]
-    down_grads, refs = refs[:blocks], refs[blocks:]
-    cot, up, down, normed, act, back, out_sum, up_grad, down_grad, sem = refs
-    core, chip, place = info[0], info[1], info[2]
+def piece_copies(pieces, target, info, sem, lanes=None):
+    chip = info[1]
+    rows = pieces[0].shape[0]
+    copies, base = [], 0
+    for i, ref in enumerate(pieces):
+        distance = min(i, 3)
+        begin = pl.multiple_of((distance ^ chip) * rows, rows)
+        if i == 4:
+            begin = pl.multiple_of(begin + rows // 2, rows // 2)
+        source = ref if lanes is None else ref.at[:, lanes]
+        there = target.at[pl.ds(begin, ref.shape[0])]
+        copies.append(pltpu.make_async_copy(source, there, sem.at[i]))
+    return copies
+
+
+def hidden_places(core, hidden, width, chips):
+    spare = 2 * hidden // width
+    share = hidden // chips
+    unit = lax.broadcasted_iota(jnp.int32, (hidden, 1), 0)
+    chip, rest = unit // share, lax.rem(unit, share)
+    row = (2 * chip + core) * (share // spare) + rest // spare
+    lane = lax.broadcasted_iota(jnp.int32, (hidden, width), 1)
+    return jnp.where(lane == row, 1.0, 0.0).astype(bf16)
+
+
+def middle_kernel(count, patches, chips, info, att, att_far, start, turned, *refs):
+    up_in, refs = refs[:count], refs[count:]
+    middle_out, normed_out, bias_out, weight, sem = refs
+    core = info[0]
     rows, width = start.shape
-    tile = rows // 4
-    chunk = act.shape[1]
-    up_rows = width // blocks
-    half_rows = rows // 2
-    hidden = 4 * chunk
-    copies = cotangent_copies(info, cot_in, cot, [sem.at[i] for i in range(4)])
-    count = 4
-    for r in range(blocks):
-        there = pl.ds(pl.multiple_of((r ^ chip) * up_rows, up_rows), up_rows)
-        copies.append(pltpu.make_async_copy(up_in[r], up.at[there], sem.at[count]))
-        count += 1
-    later = []
-    for r in range(blocks):
-        if blocks == 4:
-            for k in range(PLACES):
-                later.append(
-                    pltpu.make_async_copy(
-                        down_in[r].at[k], down.at[r ^ chip, k ^ place], sem.at[count]
-                    )
-                )
-                count += 1
-        else:
-            later.append(pltpu.make_async_copy(down_in[r], down, sem.at[count]))
-            count += 1
-    for copy in copies + later:
+    part, tile = width // 2, rows // 4
+    hidden = up_in[0].shape[1] - width
+    copies = piece_copies(up_in, weight, info, sem, slice(hidden, hidden + width))
+    for copy in copies:
         copy.start()
+    spare = 2 * hidden // width
+    biases = turned[patches + 8 : patches + 8 + spare, :].astype(bf16)
+    spread_out = dot_right(biases, hidden_places(core, hidden, width, chips))
+    turns = lax.rem(lax.broadcasted_iota(jnp.int32, (spare, hidden), 1), spare)
+    ranks = lax.broadcasted_iota(jnp.int32, (spare, hidden), 0)
+    bias = jnp.sum(jnp.where(turns == ranks, spread_out, 0.0), axis=0, keepdims=True)
+    bias_out[...] = jnp.broadcast_to(bias, bias_out.shape)
     for copy in copies:
         copy.wait()
-    part = width // 2
     vector = lambda i: turned[patches + i : patches + i + 1, :]
-    own_rows = pl.ds(pl.multiple_of(core * part, 128), part)
-    far_rows = pl.ds(pl.multiple_of((1 - core) * part, 128), part)
+    own = pl.ds(pl.multiple_of(core * part, 128), part)
+    far = pl.ds(pl.multiple_of((1 - core) * part, 128), part)
     gain, shift, out_bias = vector(GAIN_TWO), vector(SHIFT_TWO), vector(OUTPUT_BIAS)
     for t in range(4):
         here = slice(t * tile, (t + 1) * tile)
-        middle = (
-            start[here, :]
-            + dot(att[here, :], up[own_rows, hidden:])
-            + dot(att_far[here, :], up[far_rows, hidden:])
-            + out_bias
-        )
+        mixed = dot(att[here, :], weight[own, :]) + dot(att_far[here, :], weight[far, :])
+        middle = start[here, :] + mixed + out_bias
         middle_out[here, :] = middle
         normal, _ = normalise(middle)
-        normed[here, :] = (normal * gain + shift).astype(bf16)
+        normed_out[here, :] = (normal * gain + shift).astype(bf16)
+
+
+def middle_front(info, att, att_far, start, turned, ups, patches, chips):
+    rows, width = start.shape
+    count = len(ups)
+    return call(
+        functools.partial(middle_kernel, count, patches, chips),
+        [
+            (shaped((rows, width), f32), vmem()),
+            (shaped((rows, width), bf16), vmem()),
+            (shaped((8, ups[0].shape[1] - width), f32), vmem()),
+        ],
+        [LOAD] * 4 + [HELD] * count,
+        [info, att, att_far, start, turned] + list(ups),
+        scratch=[pltpu.VMEM((width, width), bf16), pltpu.SemaphoreType.DMA((count,))],
+        cost=(2 * rows * width * width, 12 * MIB),
+    )
+
+
+def feed_front_kernel(ups, downs, blocks, info, normed, up_bias, *refs):
+    cot_in, refs = refs[:4], refs[4:]
+    up_in, refs = refs[:ups], refs[ups:]
+    down_in, refs = refs[:downs], refs[downs:]
+    keep_out, send_out, slope_out, refs = refs[0], refs[1], refs[2], refs[3:]
+    cut = 2 if blocks == 4 else 1
+    down_grads, refs = refs[: cut * blocks], refs[cut * blocks :]
+    cot, up, down, out_sum, down_grad, cot_sem, up_sem, down_sem = refs
+    core, chip = info[0], info[1]
+    rows, width = normed.shape
+    hidden = up.shape[1]
+    chunk = hidden // 4
+    early = piece_copies(up_in, up, info, up_sem, slice(0, hidden))
+    late = cotangent_copies(info, cot_in, cot, [cot_sem.at[i] for i in range(4)])
+    late += piece_copies(down_in, down, info, down_sem)
+    for copy in early + late:
+        copy.start()
+    for copy in early + late:
+        copy.wait()
     out_sum[...] = jnp.zeros_like(out_sum)
-    back_out[...] = jnp.zeros_like(back_out)
-    for copy in later:
-        copy.wait()
 
     def one_chunk(q, carry):
         lanes = pl.ds(pl.multiple_of(q * chunk, 128), chunk)
-        down_part = down[q].reshape(chunk, width)
-        bias_sum = jnp.zeros((1, chunk), f32)
-        for t in range(4):
-            here = slice(t * tile, (t + 1) * tile)
-            value, slope = gelu_parts(dot(normed[here, :], up[:, lanes]) + up_bias[:, lanes])
-            value = value.astype(bf16)
-            act[here, :] = value
-            out_sum[here, :] += dot(value, down_part)
-            grad = (dot_right(cot[t], down_part) * slope).astype(bf16)
-            back[here, :] = grad
-            bias_sum += jnp.sum(grad.astype(f32), axis=0, keepdims=True)
-            back_out[here, :] += dot_right(grad, up[:, lanes])
-        bias_out[:, lanes] = jnp.broadcast_to(bias_sum, (8, chunk))
+        down_part = down[pl.ds(q * PLACES, PLACES)].reshape(chunk, width)
+        value, slope = gelu_parts(dot(normed[...], up[:, lanes]) + up_bias[0:1, lanes])
+        value = value.astype(bf16)
+        slope_out[:, lanes] = slope.astype(bf16)
+        out_sum[...] += dot(value, down_part)
         flat = cot[...].reshape(rows, width)
-        down_grad[q] = dot_left(act[...], flat).astype(bf16).reshape(PLACES, chunk // PLACES, width)
-        up_grad[:, lanes] = dot_left(normed[...], back[...]).astype(bf16)
+        grad = dot_left(value, flat).astype(bf16)
+        down_grad[pl.ds(q * PLACES, PLACES)] = grad.reshape(PLACES, chunk // PLACES, width)
         return carry
 
     lax.fori_loop(0, 4, one_chunk, 0)
-    back_low[...] = back_out[...].astype(bf16)
-    own = pl.ds(pl.multiple_of(core * half_rows, half_rows), half_rows)
-    far = pl.ds(pl.multiple_of((1 - core) * half_rows, half_rows), half_rows)
-    keep_out[...] = middle_out[own, :] + out_sum[own, :] + vector(DOWN_BIAS)
+    outs = []
+    if blocks == 4:
+        for r in range(blocks):
+            for h in range(2):
+                there = pl.ds((r ^ chip) * PLACES + 2 * h, 2)
+                i = 2 * r + h
+                outs.append(pltpu.make_async_copy(down_grad.at[there], down_grads[i], down_sem.at[i]))
+    else:
+        outs.append(pltpu.make_async_copy(down_grad, down_grads[0], down_sem.at[0]))
+    for copy in outs:
+        copy.start()
+    half = rows // 2
+    own = pl.ds(pl.multiple_of(core * half, half), half)
+    far = pl.ds(pl.multiple_of((1 - core) * half, half), half)
+    keep_out[...] = out_sum[own, :]
     send_out[...] = out_sum[far, :].astype(bf16)
-    outs = []
-    for r in range(blocks):
-        there = pl.ds(pl.multiple_of((r ^ chip) * up_rows, up_rows), up_rows)
-        outs.append(pltpu.make_async_copy(up_grad.at[there], up_grads[r], sem.at[r]))
-        source = down_grad.at[r ^ chip] if blocks == 4 else down_grad
-        outs.append(pltpu.make_async_copy(source, down_grads[r], sem.at[blocks + r]))
-    run_copies(outs)
-
-
-def feed(info, att, att_far, start, turned, up_bias, cots, ups, downs, patches):
-    blocks = len(ups)
-    rows, width = start.shape
+    for copy in outs:
+        copy.wait()
+
+
+def feed_front(info, normed, up_bias, cots, ups, downs, blocks):
+    rows, width = normed.shape
     hidden = up_bias.shape[1]
-    chunk = hidden // 4
-    down_shape = (4, PLACES, chunk // PLACES, width)
-    up_rows = width // blocks
-    one = down_shape[1:] if blocks == 4 else down_shape
-    return call(
-        functools.partial(feed_kernel, blocks, patches),
+    whole = (4 * PLACES, hidden // (4 * PLACES), width)
+    grads = [(2,) + whole[1:]] * 8 if blocks == 4 else [whole]
+    return call(
+        functools.partial(feed_front_kernel, len(ups), len(downs), blocks),
         [
             (shaped((rows // 2, width), f32), vmem()),
             (shaped((rows // 2, width), bf16), vmem()),
+            (shaped((rows, hidden), bf16), vmem()),
+        ]
+        + [(shaped(one, bf16), anywhere()) for one in grads],
+        [LOAD] * 2 + [HELD] * (4 + len(ups) + len(downs)),
+        [info, normed, up_bias] + list(cots) + list(ups) + list(downs),
+        scratch=[
+            pltpu.VMEM((4, rows // 4, width), bf16),
+            pltpu.VMEM((width, hidden), bf16),
+            pltpu.VMEM(whole, bf16),
+            pltpu.VMEM((rows, width), f32),
+            pltpu.VMEM(whole, bf16),
+            pltpu.SemaphoreType.DMA((4,)),
+            pltpu.SemaphoreType.DMA((len(ups),)),
+            pltpu.SemaphoreType.DMA((8,)),
+        ],
+        limit=20,
+        cost=(6 * rows * width * hidden, 24 * MIB),
+    )
+
+
+def feed_back_kernel(ups, downs, info, slope, *refs):
+    cot_in, refs = refs[:4], refs[4:]
+    up_in, refs = refs[:ups], refs[ups:]
+    down_in, refs = refs[:downs], refs[downs:]
+    back_out, low_out, grad_out, bias_out, cot, up, down, cot_sem, up_sem, down_sem = refs
+    rows, hidden = slope.shape
+    width = up.shape[0]
+    chunk = hidden // 4
+    copies = cotangent_copies(info, cot_in, cot, [cot_sem.at[i] for i in range(4)])
+    copies += piece_copies(down_in, down, info, down_sem)
+    copies += piece_copies(up_in, up, info, up_sem, slice(0, hidden))
+    run_copies(copies)
+    back_out[...] = jnp.zeros_like(back_out)
+
+    def one_chunk(q, carry):
+        lanes = pl.ds(pl.multiple_of(q * chunk, 128), chunk)
+        down_part = down[pl.ds(q * PLACES, PLACES)].reshape(chunk, width)
+        flat = cot[...].reshape(rows, width)
+        grad = (dot_right(flat, down_part) * slope[:, lanes].astype(f32)).astype(bf16)
+        grad_out[:, lanes] = grad
+        bias_out[:, lanes] = jnp.broadcast_to(
+            jnp.sum(grad.astype(f32), axis=0, keepdims=True), (8, chunk)
+        )
+        back_out[...] += dot_right(grad, up[:, lanes])
+        return carry
+
+    lax.fori_loop(0, 4, one_chunk, 0)
+    low_out[...] = back_out[...].astype(bf16)
+
+
+def feed_back(info, slope, cots, ups, downs, width):
+    rows, hidden = slope.shape
+    whole = (4 * PLACES, hidden // (4 * PLACES), width)
+    return call(
+        functools.partial(feed_back_kernel, len(ups), len(downs)),
+        [
             (shaped((rows, width), f32), vmem()),
             (shaped((rows, width), bf16), vmem()),
-            (shaped((rows, width), f32), vmem()),
+            (shaped((rows, hidden), bf16), vmem()),
             (shaped((8, hidden), f32), vmem()),
-        ]
-        + [(shaped((up_rows, hidden), bf16), anywhere())] * blocks
-        + [(shaped(one, bf16), anywhere())] * blocks,
-        [vmem()] * 5 + [anywhere()] * (4 + 2 * blocks),
-        [info, att, att_far, start, turned, up_bias] + list(cots) + list(ups) + list(downs),
+        ],
+        [LOAD] + [HELD] * (4 + len(ups) + len(downs)),
+        [info, slope] + list(cots) + list(ups) + list(downs),
         scratch=[
             pltpu.VMEM((4, rows // 4, width), bf16),
-            pltpu.VMEM((width, hidden + width), bf16),
-            pltpu.VMEM(down_shape, bf16),
-            pltpu.VMEM((rows, width), bf16),
-            pltpu.VMEM((rows, chunk), bf16),
-            pltpu.VMEM((rows, chunk), bf16),
-            pltpu.VMEM((rows, width), f32),
             pltpu.VMEM((width, hidden), bf16),
-            pltpu.VMEM(down_shape, bf16),
-            pltpu.SemaphoreType.DMA((4 + 5 * blocks,)),
+            pltpu.VMEM(whole, bf16),
+            pltpu.SemaphoreType.DMA((4,)),
+            pltpu.SemaphoreType.DMA((len(ups),)),
+            pltpu.SemaphoreType.DMA((len(downs),)),
         ],
-        limit=56,
-        cost=(12 * rows * width * hidden, 30 * MIB),
-    )
-
-
-def middle_kernel(blocks, patches, info, *refs):
+        limit=20,
+        cost=(4 * rows * width * hidden, 24 * MIB),
+    )
+
+
+def weight_kernel(pieces, cut, count, info, left, *refs):
+    parts, outs = refs[:count], refs[count : count + pieces * cut]
+    held, sem = refs[count + pieces * cut :][:2]
+    chip = info[1]
+    width = left.shape[1]
+    base = 0
+    for ref in parts:
+        for begin in range(0, ref.shape[1], 384):
+            size = min(384, ref.shape[1] - begin)
+            product = dot_left(left[...], ref[:, begin : begin + size]).astype(bf16)
+            held[:, base : base + size] = product
+            base += size
+    copies = []
+    rows = width // (pieces * cut)
+    for r in range(pieces):
+        for h in range(cut):
+            there = pl.ds(pl.multiple_of(((r ^ chip) * cut + h) * rows, rows), rows)
+            i = cut * r + h
+            copies.append(pltpu.make_async_copy(held.at[there], outs[i], sem.at[i]))
+    run_copies(copies)
+
+
+def weight_grad(info, left, parts, pieces, cut=1):
+    rows, width = left.shape
+    columns = sum(part.shape[1] for part in parts)
+    count = pieces * cut
+    return call(
+        functools.partial(weight_kernel, pieces, cut, len(parts)),
+        [(shaped((width // count, columns), bf16), anywhere())] * count,
+        [LOAD] * (1 + len(parts)),
+        [info, left] + list(parts),
+        scratch=[pltpu.VMEM((width, columns), bf16), pltpu.SemaphoreType.DMA((count,))],
+        cost=(2 * rows * width * columns, 8 * MIB),
+    )
+
+
+def middle_back_kernel(count, blocks, patches, info, *refs):
     back, back_far, middle, turned, att, refs = refs[0], refs[1], refs[2], refs[3], refs[4], refs[5:]
     cot_in, refs = refs[:4], refs[4:]
-    up_in, refs = refs[:blocks], refs[blocks:]
-    grad_out, attended_out, keep_out, send_out, sums_out, cot, weight, branch, sem = refs
+    up_in, refs = refs[:count], refs[count:]
+    grad_out, attended_out, keep_out, send_out, sums_out, cot, weight, branch, sem, up_sem = refs
     core, chip = info[0], info[1]
     rows, width = middle.shape
     tile = rows // 4
     part = width // 2
-    up_rows = width // blocks
     hidden = up_in[0].shape[1] - width
     copies = cotangent_copies(info, cot_in, cot, [sem.at[i] for i in range(4)])
-    for r in range(blocks):
-        there = pl.ds(pl.multiple_of((r ^ chip) * up_rows, up_rows), up_rows)
-        copies.append(
-            pltpu.make_async_copy(up_in[r].at[:, hidden:], weight.at[there], sem.at[4 + r])
-        )
+    copies += piece_copies(up_in, weight, info, up_sem, slice(hidden, hidden + width))
     run_copies(copies)
     gain = turned[patches + GAIN_TWO : patches + GAIN_TWO + 1, :]
     own_rows = pl.ds(pl.multiple_of(core * part, 128), part)
@@ -523,13 +792,13 @@
         send_out[...] = weight_grad
 
 
-def middle_back(info, back, back_far, middle, turned, att, cots, ups, patches):
-    blocks = len(ups)
+def middle_back(info, back, back_far, middle, turned, att, cots, ups, patches, blocks):
+    count = len(ups)
     rows, width = middle.shape
     part = width // 2
     slab = (2, part // 4, width) if blocks == 4 else (part, width)
     return call(
-        functools.partial(middle_kernel, blocks, patches),
+        functools.partial(middle_back_kernel, count, blocks, patches),
         [
             (shaped((rows // 2, width), f32), vmem()),
             (shaped((rows, part), bf16), vmem()),
@@ -537,13 +806,14 @@
             (shaped(slab, bf16), vmem()),
             (shaped((8, width), f32), vmem()),
         ],
-        [vmem()] * 5 + [anywhere()] * (4 + blocks),
+        [LOAD] * 5 + [HELD] * (4 + count),
         [info, back, back_far, middle, turned, att] + list(cots) + list(ups),
         scratch=[
             pltpu.VMEM((4, rows // 4, width), bf16),
             pltpu.VMEM((width, width), bf16),
             pltpu.VMEM((rows, width), bf16),
-            pltpu.SemaphoreType.DMA((4 + blocks,)),
+            pltpu.SemaphoreType.DMA((4,)),
+            pltpu.SemaphoreType.DMA((count,)),
         ],
         cost=(4 * rows * width * part, 14 * MIB),
     )
@@ -589,7 +859,7 @@
             (shaped((rows // 2, width), f32), vmem()),
             (shaped((rows // 2, width), bf16), vmem()),
         ],
-        [vmem()] * 3 + [anywhere()] * blocks,
+        [LOAD] * 3 + [HELD] * blocks,
         [info, dq, dk, dv] + list(weights),
         scratch=[
             pltpu.VMEM((width, 3 * part), bf16),
@@ -599,8 +869,8 @@
     )
 
 
-def start_kernel(blocks, patches, info, *refs):
-    (keep, far, start, grad_middle, turned, sums, up_bias_rows, spots, normed, dq, dk, dv) = refs[:12]
+def start_kernel(blocks, patches, chips, info, *refs):
+    (keep, far, start, grad_middle, turned, sums, bias_grad, spots, dq, dv, out_keep, out_got) = refs[:12]
     refs = refs[12:]
     low_out, refs = refs[0], refs[1:]
     grads, refs = refs[:blocks], refs[blocks:]
@@ -609,9 +879,6 @@
     rows, part = dq.shape
     half_rows, width = keep.shape
     up_rows = width // blocks
-    columns = 3 * part
-    for i, ref in enumerate((dq, dk, dv)):
-        held[:, i * part : (i + 1) * part] = dot_left(normed[...], ref[...]).astype(bf16)
     gain = turned[patches + GAIN_ONE : patches + GAIN_ONE + 1, :]
     own = pl.ds(pl.multiple_of(core * half_rows, half_rows), half_rows)
     grad_normed = keep[...] + far[...].astype(f32)
@@ -641,9 +908,23 @@
     put(SHIFT_TWO, sums[3:4, :])
     put(GAIN_ONE, jnp.sum(grad_normed * normal, axis=0, keepdims=True))
     put(SHIFT_ONE, jnp.sum(grad_normed, axis=0, keepdims=True))
-    spare = up_bias_rows.shape[0]
-    rows_held[patches + 8 : patches + 8 + spare, :] = up_bias_rows[...]
-    held[:, columns:] = rows_held[...].T.astype(bf16)
+    hidden = bias_grad.shape[1]
+    spare = 2 * hidden // width
+    turns = lax.rem(lax.broadcasted_iota(jnp.int32, (spare, hidden), 1), spare)
+    ranks = lax.broadcasted_iota(jnp.int32, (spare, hidden), 0)
+    biases = jnp.where(turns == ranks, bias_grad[0:1, :], 0.0)
+    high = biases.astype(bf16)
+    both = jnp.concatenate([high.astype(f32), biases - high.astype(f32)]).astype(bf16)
+    placed = dot(both, hidden_places(core, hidden, width, chips))
+    rows_held[patches + 8 : patches + 8 + spare, :] = placed[:spare] + placed[spare:]
+    held[:, :SMALL] = rows_held[...].T.astype(bf16)
+    if blocks == 4:
+        slab = up_rows // 2
+        for x in range(2):
+            for side, ref in ((core, out_keep), (1 - core, out_got)):
+                begin = pl.multiple_of((2 * side + x) * up_rows, up_rows)
+                held[pl.ds(begin, slab), SMALL:] = ref[x, :, : width // 2]
+                held[pl.ds(begin + slab, slab), SMALL:] = ref[x, :, width // 2 :]
     copies = []
     for r in range(blocks):
         there = pl.ds(pl.multiple_of((r ^ chip) * up_rows, up_rows), up_rows)
@@ -651,58 +932,59 @@
     run_copies(copies)
 
 
-def start_back(
-    info, blocks, keep, far, start, grad_middle, turned, sums, up_bias_rows, spots, normed, dq, dk, dv, patches
-):
-    half_rows, width = keep.shape
-    rows, part = dq.shape
-    columns = 3 * part + SMALL
-    return call(
-        functools.partial(start_kernel, blocks, patches),
+def start_back(info, blocks, args, patches, chips):
+    half_rows, width = args[0].shape
+    columns = SMALL + width // 2 if blocks == 4 else SMALL
+    return call(
+        functools.partial(start_kernel, blocks, patches, chips),
         [(shaped((half_rows, width), bf16), vmem())]
         + [(shaped((width // blocks, columns), bf16), anywhere())] * blocks,
-        [vmem()] * 12,
-        [info, keep, far, start, grad_middle, turned, sums, up_bias_rows, spots, normed, dq, dk, dv],
+        [LOAD] * len(args),
+        [info] + list(args),
         scratch=[
             pltpu.VMEM((width, columns), bf16),
             pltpu.VMEM((SMALL, width), f32),
             pltpu.SemaphoreType.DMA((blocks,)),
         ],
-        cost=(6 * rows * width * part, 14 * MIB),
-    )
-
-
-def split_kernel(groups, info, *refs):
-    place = info[2]
-    inputs, outs = refs[: sum(groups)], refs[sum(groups) :]
-    base, column = 0, 0
-    for count in groups:
-        total = inputs[base][...].astype(f32)
-        for ref in inputs[base + 1 : base + count]:
+        cost=(2 * half_rows * width * SMALL, 10 * MIB),
+    )
+
+
+def split_kernel(terms, parts, shift, count, info, *refs):
+    place = lax.rem(info[2] >> shift, count)
+    outs, held = refs[terms * parts : terms * parts + count], refs[terms * parts + count]
+    totals = []
+    for part in range(parts):
+        total = refs[part * terms][...].astype(f32)
+        for ref in refs[part * terms + 1 : (part + 1) * terms]:
             total = total + ref[...].astype(f32)
-        base += count
-        lanes = total.shape[-1]
-        outs[PLACES][:, :, :, column : column + lanes] = total
-        column += lanes
-    for k in range(PLACES):
-        outs[k][...] = outs[PLACES][:, k ^ place].astype(outs[k].dtype)
-
-
-def split(info, groups):
-    two, places, rows, _ = groups[0][0].shape
-    columns = sum(group[0].shape[3] for group in groups)
-    one = (two, rows, columns)
-    outs = [(shaped(one, f32 if k == 0 else bf16), vmem()) for k in range(places)]
-    outs.append((shaped((two, places, rows, columns), f32), vmem()))
-    arrays = [array for group in groups for array in group]
-    return call(
-        functools.partial(split_kernel, [len(group) for group in groups]),
+        totals.append(total)
+    held[...] = (totals[0] if parts == 1 else jnp.concatenate(totals)).reshape(held.shape)
+    lead = (slice(None),) * (len(held.shape) - 3)
+    for k in range(count):
+        outs[k][...] = held[lead + (k ^ place,)].astype(outs[k].dtype)
+
+
+def split(info, parts, shape, shift=0):
+    columns = parts[0][0].shape[-1]
+    count = shape[-2]
+    outs = [
+        (shaped(shape[:-2] + (shape[-1], columns), f32 if k == 0 else bf16), vmem())
+        for k in range(count)
+    ]
+    arrays = [array.reshape(-1, columns) for part in parts for array in part]
+    total = 1
+    for extent in shape + (columns,):
+        total *= extent
+    return call(
+        functools.partial(split_kernel, len(parts[0]), len(parts), shift, count),
         outs,
-        [vmem()] * len(arrays),
+        [LOAD] * len(arrays),
         [info] + arrays,
-        limit=32,
-        cost=(0, 8 * two * places * rows * columns),
-    )[:places]
+        scratch=[pltpu.VMEM(shape + (columns,), f32)],
+        limit=16,
+        cost=(0, 8 * total),
+    )
 
 
 def swap(values, axis, bits):
@@ -719,27 +1001,14 @@
     return pairs
 
 
-def spread(values, place):
-    mine = [
-        lax.ppermute(
-            lax.dynamic_index_in_dim(values, turn ^ (place % 2), 0, keepdims=False),
-            ("wide", "narrow"),
-            spread_perm(turn),
-        )
-        for turn in range(2)
+def unspread(turns):
+    return [
+        lax.ppermute(part, ("wide", "narrow"), [(b, a) for a, b in spread_perm(turn)])
+        for turn, part in enumerate(turns)
     ]
-    return mine + [swap(part, "wide", 1) for part in mine]
-
-
-def unspread(blocks, place):
-    got = [
-        lax.ppermute(
-            lax.dynamic_index_in_dim(blocks, turn ^ (place % 2), 0, keepdims=False),
-            ("wide", "narrow"),
-            [(b, a) for a, b in spread_perm(turn)],
-        )
-        for turn in range(2)
-    ]
+
+
+def unspread_join(got, place):
     odd = (place % 2) == 1
     return jnp.stack([jnp.where(odd, got[1], got[0]), jnp.where(odd, got[0], got[1])])
 
@@ -768,6 +1037,38 @@
 
 def after(values, *others):
     return lax.optimization_barrier((values,) + others)[0]
+
+
+def together(*values):
+    return lax.optimization_barrier(values)
+
+
+class Fold:
+    def __init__(self, info, pieces, bits):
+        self.info, self.pieces, self.bits = info, pieces, bits
+        if len(pieces[0]) == 2:
+            own, x, y, d = pieces
+            self.near = [swap(d[0], "wide", 2), swap(x[0], "wide", 2), swap(d[1], "wide", 4), swap(y[1], "wide", 4)]
+
+    def second(self, *values):
+        if len(self.pieces[0]) == 2:
+            own, x, y, d = self.pieces
+            count = len(values)
+            values = together(*values, *self.near)
+            values, self.near = values[:count], values[count:]
+            first, second = add_pairs(self.info, y[0], self.near[0], x[1], self.near[2])
+            self.far = [swap(first, "wide", 4), swap(second, "wide", 2)]
+        return values
+
+    def last(self, *values):
+        if len(self.pieces[0]) == 1:
+            self.parts = [fold([piece[0] for piece in self.pieces], self.bits)]
+            return values
+        count = len(values)
+        *values, one, two = together(*values, *self.far)
+        own = self.pieces[0]
+        self.parts = [[own[0], self.near[1], one], [own[1], self.near[3], two]]
+        return values
 
 
 def local(
@@ -822,15 +1123,6 @@
         whole = outs[0].reshape((chips,) + shape)
         return [pick(whole, index ^ chip) for index in range(chips)]
 
-    relative = (segments - segments[:, :1]).astype(bf16)
-    extra = [
-        jnp.pad(positions.astype(bf16), ((0, 0), (0, width - block)))[:, None],
-        relative[:, None, :width],
-        jnp.pad(relative[:, width:], ((0, 0), (0, 2 * width - full)))[:, None],
-        jnp.zeros((seq_count, 13, width), bf16),
-    ]
-    packed = jnp.concatenate([tokens] + extra, axis=1)
-
     vectors = (
         query_bias,
         value_bias,
@@ -842,131 +1134,213 @@
         second_shift,
     )
     spare = up_bias.shape[0] // rows
-    small = jnp.concatenate(
-        [position_table] + [v[:, None] for v in vectors] + [up_bias.reshape(rows, spare)], axis=1
-    )
-    small = jnp.pad(small, ((0, 0), (0, SMALL - small.shape[1])))
+    if blocks == 4:
+        up_sorted = up_weight
+    else:
+        up_sorted = up_weight.reshape(rows, 4, chips // 4, 2, -1)
+        up_sorted = jnp.swapaxes(up_sorted, 2, 3).reshape(rows, hidden)
+    in_keep, in_send, up_keep, up_send = pack(
+        info,
+        input_weight,
+        position_table,
+        jnp.stack(vectors),
+        up_bias.reshape(rows, spare),
+        up_sorted,
+        output_weight,
+        patches,
+    )
+
+    def cross_one(piece):
+        if blocks == 4:
+            return [piece, swap(piece, "wide", 2), swap(piece, "wide", 4)]
+        return along(piece, bits)
+
+    def cross_two(pieces):
+        if blocks == 4:
+            own, x, y = pieces
+            first, second = cut(info, x, y)
+            return [own, x, y, swap(first, "wide", 2), swap(second, "wide", 4)]
+        return pieces
+
+    def gather_sum(pieces):
+        if blocks == 4:
+            return [pieces[0]] + [swap(pieces[i], "wide", 2 * i) for i in range(1, chips)]
+        return fold(pieces, bits)
 
     def pair(keep, send):
-        got = swap(send, "wide", 1)
-        return jnp.where(first_core, jnp.stack([keep, got]), jnp.stack([got, keep]))
-
-    def in_halves(index):
-        cut = pick(input_weight.reshape(rows, 3, 2, part), index, 2).reshape(rows, 3 * part)
-        return jnp.concatenate([cut, small], axis=1)
-
-    def up_halves(index):
-        cut = pick(up_weight.reshape(rows, chips, 2, -1), index, 2).reshape(rows, own_hidden)
-        return jnp.concatenate([cut, output_weight], axis=1)
+        return arrange(info, [keep, swap(send, "wide", 1)], 0, 0)
 
     def narrow_pieces(piece):
         return [piece] + [swap(piece, "narrow", k) for k in range(1, PLACES)]
 
-    in_pair = pair(in_halves(core), in_halves(1 - core))
+    def place_axis(piece):
+        return piece.reshape(piece.shape[:-4] + (PLACES,) + piece.shape[-2:])
+
+    def halves(outs, shape):
+        if blocks == 4:
+            shape = (shape[0] // 2,) + shape[1:]
+            return [[out.reshape(shape) for out in outs[2 * r : 2 * r + 2]] for r in range(4)]
+        whole = outs[0].reshape((chips,) + shape)
+        return [[pick(whole, index ^ chip)] for index in range(chips)]
+
+    in_pair = pair(in_keep, in_send)
+    up_pair = pair(up_keep, up_send)
     in_piece = arrange(info, narrow_pieces(in_pair))
     in_chips = direct(in_piece, chips) if blocks == 4 else along(in_piece, bits)
     in_blocks = by_chip(in_chips)
-    token_blocks = spread(packed, place)
-
-    up_pair = pair(up_halves(core), up_halves(1 - core))
-    up_pair = after(up_pair, in_piece)
-    up_piece = arrange(info, narrow_pieces(up_pair))
-    up_blocks = by_chip(along(up_piece, bits[::-1]))
-    down_pieces = jnp.stack(narrow_pieces(after(down_weight, up_piece)))
-    if blocks == 4:
-        down_blocks = along(down_pieces, bits)
-    else:
-        down_pieces = jnp.take(down_pieces, jnp.arange(PLACES) ^ place, axis=0)
-        down_blocks = by_chip(along(down_pieces, bits))
-        down_blocks = [down_blocks[0].reshape(4, PLACES, -1, width)]
-    cots = spread(cotangent, place)
-
+    plane = blocks == 4
+    first, second = sent(info, tokens, positions, segments)
+    down_half = arrange(info, [down_weight, swap(down_weight, "narrow", 2)], 1)
+    in_got = [in_pair] + [swap(in_pair, "narrow", k) for k in range(1, PLACES)]
+    down_got = swap(down_half, "narrow", 1)
+    in_piece, down_got, up_pair, first = together(arrange(info, in_got), down_got, up_pair, first)
+    in_chips = direct(in_piece, chips) if plane else along(in_piece, bits)
+    up_got = swap(up_pair, "narrow", 2)
+    low = lax.ppermute(first, ("wide", "narrow"), spread_perm(0))
+    down_piece = place_axis(arrange(info, [down_half, down_got]))
+    up_half = arrange(info, [up_pair, up_got], 1)
+    down_piece, second, up_half, low, *in_chips = together(
+        down_piece, second, up_half, low, *in_chips
+    )
+    up_got = swap(up_half, "narrow", 1)
+    in_blocks = by_chip(in_chips)
+    plane = blocks == 4
+    first, second = sent(info, tokens, positions, segments)
+    in_got = [in_pair] + [swap(in_pair, "narrow", k) for k in range(1, PLACES)]
+    down_half = [down_weight, swap(down_weight, "narrow", 2)]
+    in_piece, down_half, up_pair = together(
+        arrange(info, in_got), arrange(info, down_half, 1), up_pair
+    )
+    in_chips = direct(in_piece, chips) if plane else along(in_piece, bits)
+    up_got, down_got, first = together(
+        swap(up_pair, "narrow", 2), swap(down_half, "narrow", 1), first
+    )
+    low = lax.ppermute(first, ("wide", "narrow"), spread_perm(0))
+    up_half = arrange(info, [up_pair, up_got], 1)
+    up_got = swap(up_half, "narrow", 1)
+    down_piece = place_axis(arrange(info, [down_half, down_got]))
+    down_piece, second, *in_chips = together(down_piece, second, *in_chips)
+    in_blocks = by_chip(in_chips)
+    down_chips = cross_one(down_piece)
+    high = lax.ppermute(second, ("wide", "narrow"), spread_perm(1))
+    low, high, up_got, *down_chips = together(low, high, up_got, *down_chips)
+    token_blocks = [low, high, swap(low, "wide", 1), swap(high, "wide", 1)]
+    up_piece = place_axis(arrange(info, [up_half, up_got]))
+    up_chips = cross_one(up_piece)
+    down_chips = cross_two(down_chips)
     q, k, v, start, normed, small_full, turned, seg, spots = front(
         info, token_blocks, in_blocks, patches
     )
+    q, k, v, seg, cotangent, *down_chips = together(q, k, v, seg, cotangent, *down_chips)
+    cot_low, cot_high = (
+        lax.ppermute(block, ("wide", "narrow"), spread_perm(turn))
+        for turn, block in enumerate(pick_turns(info, cotangent))
+    )
     att, total = attend(info, q, k, v, seg)
+    att, cot_low, cot_high, *up_chips = together(att, cot_low, cot_high, *up_chips)
     att_far = swap(att, "wide", 1)
-    bias = small_full[:, patches + 8 : patches + 8 + spare]
-    up_bias_own = pick(bias.reshape(chips, 2, -1), core, 1).reshape(1, own_hidden).astype(f32)
-    fed = feed(
-        info, att, att_far, start, turned, up_bias_own, cots, up_blocks, down_blocks, patches
-    )
-    keep, send, back, back_low, middle, bias_grad = fed[:6]
-    up_grads, down_grads = fed[6 : 6 + blocks], fed[6 + blocks :]
+    up_chips = cross_two(up_chips)
+    cots = [cot_low, cot_high, swap(cot_low, "wide", 1), swap(cot_high, "wide", 1)]
+    if plane:
+        up_blocks = [part.reshape((-1,) + part.shape[-1:]) for part in up_chips]
+        down_blocks = down_chips
+    else:
+        up_blocks = by_chip(up_chips)
+        down_blocks = [by_chip(down_chips)[0].reshape(4 * PLACES, -1, width)]
+    middle, normed_two, up_bias_own = middle_front(
+        info, att, att_far, start, turned, up_blocks, patches, chips
+    )
+    keep, send, slope, *down_grads = feed_front(
+        info, normed_two, up_bias_own, cots, up_blocks, down_blocks, blocks
+    )
+    down_rows = own_hidden // (chips * PLACES)
+    down_fold = Fold(info, halves(down_grads, (PLACES, down_rows, width)), bits)
+    fed = feed_back(info, slope, cots, up_blocks, down_blocks, width)
+    back, back_low, grad_hidden, bias_grad, send, normed_two = down_fold.second(
+        *fed, send, normed_two
+    )
     back_far = swap(back_low, "wide", 1)
     out_far = swap(send, "wide", 1)
-    outputs = (keep + out_far.astype(f32)).astype(bf16).reshape(2, block, width)
-    outputs = unspread(outputs, place)
-
-    down_sum = fold(
-        by_distance(down_grads, (1, PLACES, own_hidden // (chips * PLACES), width)), bits[::-1]
-    )
-    down_cut = split(info, [down_sum])
-    down_share = down_cut[0][0]
-    for index in range(1, PLACES):
-        down_share = down_share + swap(down_cut[index], "narrow", index)[0].astype(f32)
-
+    up_grads = weight_grad(info, normed_two, [grad_hidden], blocks, 2 if plane else 1)
+    back_far, out_far, *up_grads = down_fold.last(back_far, out_far, *up_grads)
+    up_fold = Fold(info, halves(up_grads, (2, PLACES, rows, own_hidden)), bits)
+    down_keep, down_send = split(info, down_fold.parts, (2, 2, down_rows))
+    down_got = swap(down_send, "narrow", 1)
     grad_middle, grad_att, out_keep, out_send, sums = middle_back(
-        info, back, back_far, middle, turned, att, cots, up_blocks, patches
+        info, back, back_far, middle, turned, att, cots, up_blocks, patches, blocks
     )
     if blocks == 1:
         shape = (chips // 2, 2, PLACES * rows, width)
         out_keep = pick(out_keep.reshape(shape), core, 1)
         out_send = pick(out_send.reshape(shape), 1 - core, 1)
+    grad_att, out_send, out_far, down_got = up_fold.second(grad_att, out_send, out_far, down_got)
     out_got = swap(out_send, "wide", 1)
-    out_grad = jnp.where(
-        first_core,
-        jnp.concatenate([out_keep, out_got]),
-        jnp.concatenate([out_got, out_keep]),
-    ).reshape(chips, PLACES, rows, 2, part)
-    out_grad = jnp.swapaxes(jnp.swapaxes(out_grad, 2, 3), 1, 2)
-    out_pieces = [pick(out_grad, index ^ chip) for index in range(chips)]
-    up_pieces = by_distance(up_grads, (2, PLACES, rows, own_hidden))
-    up_cut = split(info, [fold(up_pieces, bits), fold(out_pieces, bits)])
-
-    def narrow_sum(cut):
+    out_turns = unspread(output_turns(info, middle, keep, out_far, turned, patches))
+    dq, dk, dv = attend_back(info, q, k, v, att, grad_att, total, seg)
+    dq, dk, dv, out_got, normed, *out_turns = up_fold.last(
+        dq, dk, dv, out_got, normed, *out_turns
+    )
+    outputs = unspread_join(out_turns, place)
+    down_keep, down_send = split(info, [[down_keep, down_got]], (2, down_rows), 1)
+    down_got = swap(down_send, "narrow", 2)
+    up_keep, up_send = split(info, up_fold.parts, (2, 2, 2, rows))
+    up_got = swap(up_send, "narrow", 1)
+    start_keep, start_send = project_back(info, dq, dk, dv, in_blocks, width)
+    start_send, down_got, up_got = together(start_send, down_got, up_got)
+    start_far = swap(start_send, "wide", 1)
+    up_keep, up_send = split(info, [[up_keep, up_got]], (2, 2, rows), 1)
+    up_got = swap(up_send, "narrow", 2)
+    in_grads = weight_grad(info, normed, [dq, dk, dv], blocks)
+    start_far, up_got, *in_grads = together(start_far, up_got, *in_grads)
+    in_sum = gather_sum(by_distance(in_grads, (2, PLACES, rows, 3 * part)))
+    args = [start_keep, start_far, start, grad_middle, turned, sums, bias_grad, spots, dq, dv]
+    started = start_back(info, blocks, args + [out_keep, out_got], patches, chips)
+    grad_blocks, *small_grads = started
+    grad_turns = unspread(pick_turns(info, grad_blocks.reshape(2, block, width)))
+    down_got, up_got, *rest = together(down_got, up_got, *grad_turns, *in_sum[1:], *small_grads)
+    grad_tokens = unspread_join(rest[:2], place)
+    in_sum, small_grads = [in_sum[0], *rest[2 : 1 + len(in_sum)]], rest[1 + len(in_sum) :]
+    if plane:
+        small_sum = gather_sum(by_distance(small_grads, (2, PLACES, rows, SMALL + part)))
+    else:
+        out_grad = jnp.where(
+            first_core,
+            jnp.concatenate([out_keep, out_got]),
+            jnp.concatenate([out_got, out_keep]),
+        ).reshape(chips, PLACES, rows, 2, part)
+        out_grad = jnp.transpose(out_grad, (0, 3, 1, 2, 4)).reshape(width, part)
+        small_grads = jnp.concatenate([small_grads[0], out_grad], axis=1)
+        small_sum = gather_sum(by_distance([small_grads], (2, PLACES, rows, SMALL + part)))
+
+    def narrow_sum(parts):
+        cut = split(info, [parts], (2, PLACES, rows))
         whole = cut[0]
         for index in range(1, PLACES):
             whole = whole + swap(cut[index], "narrow", index).astype(f32)
         return whole
 
-    up_total = narrow_sum(up_cut)
-    up_keep = pick(up_total[:, :, :own_hidden], core)
-    up_got = swap(pick(up_total[:, :, :own_hidden], 1 - core).astype(bf16), "wide", 1).astype(f32)
+    down_share = down_keep + down_got.astype(f32)
+    up_total = up_keep + up_got.astype(f32)
+    up_keep = pick(up_total, core)
+    up_got = swap(pick(up_total, 1 - core).astype(bf16), "wide", 1).astype(f32)
     up_both = [up_keep.reshape(rows, chips, 1, -1), up_got.reshape(rows, chips, 1, -1)]
     up_share = jnp.where(
         first_core, jnp.concatenate(up_both, axis=2), jnp.concatenate(up_both[::-1], axis=2)
     ).reshape(rows, hidden)
-    out_share = jnp.concatenate([up_total[0, :, own_hidden:], up_total[1, :, own_hidden:]], axis=1)
-
-    dq, dk, dv = attend_back(info, q, k, v, att, grad_att, total, seg)
-    start_keep, start_send = project_back(info, dq, dk, dv, in_blocks, width)
-    start_far = swap(start_send, "wide", 1)
-    bias_rows = bias_grad[0].reshape(chips, 1, rows * PLACES, spare)
-    mine = (jnp.arange(2) == core)[None, :, None, None]
-    bias_rows = jnp.where(mine, bias_rows, 0.0).reshape(width, spare).T
-    started = start_back(
-        info, blocks, start_keep, start_far, start, grad_middle, turned, sums, bias_rows,
-        spots, normed, dq, dk, dv, patches,
-    )
-    grad_tokens = unspread(started[0].reshape(2, block, width), place)
-    columns = 3 * part + SMALL
-    in_pieces = by_distance(started[1:], (2, PLACES, rows, columns))
-    if blocks == 4:
-        in_sum = [in_pieces[0]] + [swap(in_pieces[i], "wide", 2 * i) for i in range(1, chips)]
-    else:
-        in_sum = fold(in_pieces, bits)
-    in_total = narrow_sum(split(info, [in_sum]))
+    in_total = narrow_sum(in_sum)
+    small_total = narrow_sum(small_sum)
     in_keep = pick(in_total, core)
     in_got = swap(pick(in_total, 1 - core).astype(bf16), "wide", 1).astype(f32)
+    small_far = swap(pick(small_total, 1 - core)[:, :SMALL].astype(bf16), "wide", 1)
+    small_share = pick(small_total, core)[:, :SMALL] + small_far.astype(f32)
+    out_share = jnp.concatenate([small_total[0, :, SMALL:], small_total[1, :, SMALL:]], axis=1)
     in_both = [
-        in_keep[:, : 3 * part].reshape(rows, 3, 1, part),
-        in_got[:, : 3 * part].reshape(rows, 3, 1, part),
+        in_keep.reshape(rows, 3, 1, part),
+        in_got.reshape(rows, 3, 1, part),
     ]
     in_share = jnp.where(
         first_core, jnp.concatenate(in_both, axis=2), jnp.concatenate(in_both[::-1], axis=2)
     ).reshape(rows, 3 * width)
-    small_share = in_keep[:, 3 * part :] + in_got[:, 3 * part :]
     tail = [small_share[:, patches + i] for i in range(8)]
     return (
         outputs,

time: 383 us -> 326 us (0.85)
  the two profiles are of different devices: /device:TPU:7 before, /device:TPU:0 now
where the time goes in v3:
time: 326 us; the launch traced here: 320 us
  waiting for transfers between devices  107 us (33%)
  Pallas kernels  102 us (31%)
  starting transfers between devices  92.7 us (28%)
  local copies, waits for them, and re-layouts  12.6 us (4%)
  other arithmetic  5.36 us (2%)
    pallas_call x33, Pallas kernels, call(): pl.pallas_call(loaded if loads else kernel, out_shape=[shape for shape, _...  102 us
    ppermute x60, waiting for transfers between devices, swap(): return lax.ppermute(values, axis, [(i, i ^ bits) for i in range(size)])  87 us
    ppermute x60, starting transfers between devices, swap(): return lax.ppermute(values, axis, [(i, i ^ bits) for i in range(size)])  85.4 us
    ppermute x4, waiting for transfers between devices, unspread(): lax.ppermute(part, ('wide', 'narrow'), [(b, a) for a, b in spread_perm(tu...  13.3 us
  transfers between devices with their start and end apart: 68, of which 25 were waited for; matrix products, arithmetic and copies ran while one was open for 2% of the time, Pallas kernels for 26%

profile of v3, /device:TPU:0, one launch (start us, length us, event | category | flops | bytes accessed | tf_op | source)
XLA Modules:
  0.0 320.5 jit_solution(4893826162524524441)
XLA Ops:
  6.7 3.7 %collective-permute-start.4 = (bf16[96,768]{1,0:T(8,128)(2,1)}, bf16[96,768]{1,0:T(8,128)(2,1)S(1)}, u32[]{:S(2)}, u32[]{:S(2)}) collective-permute-start(bf16[96,768]{1,0:T(8,128)(2,1)} %refs_0_.1), channel_id=1, source_target_pairs={{0,2},{1,3},{2,0},{3,1},{4,6},{5,7},{6,4},{7,5},{8,10},{9,11},{10,... | collective-permute-start | bytes 442376 | tf_op jit(solution)/shard_map/ppermute | solution.py:992
  11.0 1.6 collective-permute-start.1
  13.8 1.6 collective-permute-start.3
  19.8 6.7 %collective-permute-done.2.refs_2_ = bf16[2,24,1280]{2,1,0:T(8,128)(2,1)S(1)} collective-permute-done((bf16[2,24,1280]{2,1,0:T(8,128)(2,1)S(1)}, bf16[2,24,1280]{2,1,0:T(8,128)(2,1)S(1)}, u32[]{:S(2)}, u32[]{:S(2)}) %collective-permute-start.2) | collective-permute-done | bytes 122912 | tf_op jit(solution)/shard_map/ppermute | solution.py:992
  27.0 1.8 collective-permute-start.10
  30.6 3.1 collective-permute-start.7
  33.6 1.9 collective-permute-start.6
  35.5 8.5 %collective-permute-done.6.refs_1_ = bf16[2,24,2304]{2,1,0:T(8,128)(2,1)S(1)} collective-permute-done((bf16[2,24,2304]{2,1,0:T(8,128)(2,1)S(1)}, bf16[2,24,2304]{2,1,0:T(8,128)(2,1)S(1)}, u32[]{:S(2)}, u32[]{:S(2)}) %collective-permute-start.6) | collective-permute-done | bytes 221216 | tf_op jit(solution)/shard_map/ppermute | solution.py:992
  45.4 5.0 %collective-permute-done.10 = bf16[2,4,24,1280]{3,2,1,0:T(8,128)(2,1)S(1)} collective-permute-done((bf16[2,4,24,1280]{3,2,1,0:T(8,128)(2,1)S(1)}, bf16[2,4,24,1280]{3,2,1,0:T(8,128)(2,1)S(1)}, u32[]{:S(2)}, u32[]{:S(2)}) %collective-permute-start.10) | collective-permute-done | bytes 491552 | tf_op jit(solution)/shard_map/ppermute | solution.py:992
  52.9 1.5 collective-permute-start.15
  55.0 3.7 %collective-permute-start.13 = (bf16[2,2,24,2304]{3,2,1,0:T(8,128)(2,1)S(1)}, bf16[2,2,24,2304]{3,2,1,0:T(8,128)(2,1)S(1)}, u32[]{:S(2)}, u32[]{:S(2)}) collective-permute-start(bf16[2,2,24,2304]{3,2,1,0:T(8,128)(2,1)S(1)} %shard_map.304.refs_0_), channel_id=1, source_target_pairs={{0,1},{1,0},{2,3},{3,2},{4,5},{5,4},{6,7},{7,6},{8,9},{9,8},{10,11... | collective-permute-start | bytes 1327112 | tf_op jit(solution)/shard_map/ppermute | solution.py:992
  59.5 12.4 %collective-permute-done.13.refs_1_ = bf16[2,2,24,2304]{3,2,1,0:T(8,128)(2,1)S(1)} collective-permute-done((bf16[2,2,24,2304]{3,2,1,0:T(8,128)(2,1)S(1)}, bf16[2,2,24,2304]{3,2,1,0:T(8,128)(2,1)S(1)}, u32[]{:S(2)}, u32[]{:S(2)}) %collective-permute-start.13) | collective-permute-done | bytes 442400 | tf_op jit(solution)/shard_map/ppermute | solution.py:992
  71.9 6.4 %collective-permute-done.12.refs_1_ = bf16[272,768]{1,0:T(8,128)(2,1)S(1)} collective-permute-done((bf16[272,768]{1,0:T(8,128)(2,1)S(1)}, bf16[272,768]{1,0:T(8,128)(2,1)S(1)}, u32[]{:S(2)}, u32[]{:S(2)}) %collective-permute-start.12) | collective-permute-done | bytes 417824 | tf_op jit(solution)/shard_map/ppermute | solution.py:1225
  78.3 5.5 %collective-permute-start.16 = (bf16[272,768]{1,0:T(8,128)(2,1)S(1)}, bf16[272,768]{1,0:T(8,128)(2,1)S(1)}, u32[]{:S(2)}, u32[]{:S(2)}) collective-permute-start(bf16[272,768]{1,0:T(8,128)(2,1)S(1)} %collective-permute-done.8.refs_0_), channel_id=1, source_target_pairs={{0,4},{4,0},{8,12},{12,8},{16,20},{20,16},{24,28},{28,24},{1,5},{5... | collective-permute-start | bytes 1253384 | tf_op jit(solution)/shard_map/ppermute | solution.py:992
  86.2 1.6 collective-permute-start.18
  87.8 1.5 collective-permute-start.19
  89.3 7.5 %shard_map.305 = (bf16[1024,384]{1,0:T(8,128)(2,1)S(1)}, bf16[1024,384]{1,0:T(8,128)(2,1)S(1)}, bf16[1024,384]{1,0:T(8,128)(2,1)S(1)}, f32[1024,768]{1,0:T(8,128...) custom-call(s32[4]{0:T(128)S(1)} %pad_add_fusion.info, ...), custom_call_target="tpu_custom_call" | custom-call | flops 2013265920 | bytes 12582912 | tf_op jit(solution)/shard_map/pallas_call | solution.py:61
  96.8 16.1 %collective-permute-done.18.refs_12_ = bf16[2,96,768]{2,1,0:T(8,128)(2,1)S(1)} collective-permute-done((bf16[2,96,768]{2,1,0:T(8,128)(2,1)S(1)}, bf16[2,96,768]{2,1,0:T(8,128)(2,1)S(1)}, u32[]{:S(2)}, u32[]{:S(2)}) %collective-permute-start.18) | collective-permute-done | bytes 294944 | tf_op jit(solution)/shard_map/ppermute | solution.py:992
  114.7 13.2 %shard_map.307 = (bf16[1024,384]{1,0:T(8,128)(2,1)S(1)}, f32[3,8,1024]{2,1,0:T(8,128)S(1)}) custom-call(s32[4]{0:T(128)S(1)} %pad_add_fusion.info, bf16[1024,384]{1,0:T(8,128)(2,1)S(1)} %get-tuple-element.231.q, bf16[1024,384]{1,0:T(8,128)(2,1)S(1)} %get-tuple-element.232.k, bf16[1024,384]{1,0:T(8,128)(2,1)S(1)} %get-tuple-element.233.v, ...), custom_call_target="tpu_custom_call" | custom-call | flops 2415919104 | bytes 4194304 | tf_op jit(solution)/shard_map/pallas_call | solution.py:61
  128.0 3.1 collective-permute-start.24
  131.7 1.5 collective-permute-start.25
  134.2 9.6 %collective-permute-done.25 = bf16[1,4,24,2304]{3,2,1,0:T(8,128)(2,1)S(1)} collective-permute-done((bf16[1,4,24,2304]{3,2,1,0:T(8,128)(2,1)S(1)}, bf16[1,4,24,2304]{3,2,1,0:T(8,128)(2,1)S(1)}, u32[]{:S(2)}, u32[]{:S(2)}) %collective-permute-start.25) | collective-permute-done | bytes 442400 | tf_op jit(solution)/shard_map/ppermute | solution.py:992
  145.0 4.2 %shard_map.311 = (f32[1024,768]{1,0:T(8,128)S(1)}, bf16[1024,768]{1,0:T(8,128)(2,1)S(1)}, f32[8,1536]{1,0:T(8,128)S(1)}) custom-call(s32[4]{0:T(128)S(1)} %pad_add_fusion.info, bf16[1024,384]{1,0:T(8,128)(2,1)S(1)} %get-tuple-element.240.att.refs_4_.o, bf16[1024,384]{1,0:T(8,128)(2,1)S(1)} %collective-permute-done.24.att_far, ...), custom_call_target="tpu_custom_call" | custom-call | flops 1207959552 | bytes 12582912 | tf_op jit(solution)/shard_map/pallas_call | solution.py:61
  149.3 15.1 %shard_map.312 = (f32[512,768]{1,0:T(8,128)S(1)}, bf16[512,768]{1,0:T(8,128)(2,1)S(1)}, bf16[1024,1536]{1,0:T(8,128)(2,1)S(1)}, bf16[2,96,768]{2,1,0:T(8,128)(2,...) custom-call(s32[4]{0:T(128)S(1)} %pad_add_fusion.info, ...), custom_call_target="tpu_custom_call" | custom-call | flops 7247757312 | bytes 25165824 | tf_op jit(solution)/shard_map/pallas_call | solution.py:61
  168.5 10.1 %shard_map.313 = (f32[1024,768]{1,0:T(8,128)S(1)}, bf16[1024,768]{1,0:T(8,128)(2,1)S(1)}, bf16[1024,1536]{1,0:T(8,128)(2,1)S(1)}, f32[8,1536]{1,0:T(8,128)S(1)}) custom-call(s32[4]{0:T(128)S(1)} %pad_add_fusion.info, bf16[1024,1536]{1,0:T(8,128)(2,1)S(1)} %get-tuple-element.257.slope, bf16[256,768]{1,0:T(8,128)(2,1)S(1)} %collective-permute-done.20.refs_0_.refs_5_, ...), custom_call_target="tpu_custom_call" | custom-call | flops 4831838208 | bytes 25165824 | tf_op jit(solution)/shard_map/pallas_call | solution.py:61
  182.4 4.6 %shard_map.314 = (bf16[96,1536]{1,0:T(8,128)(2,1)S(1)}, bf16[96,1536]{1,0:T(8,128)(2,1)S(1)}, bf16[96,1536]{1,0:T(8,128)(2,1)S(1)}, bf16[96,1536]{1,0:T(8,128)(2...) custom-call(s32[4]{0:T(128)S(1)} %pad_add_fusion.info, ...), custom_call_target="tpu_custom_call" | custom-call | flops 2415919104 | bytes 8388608 | tf_op jit(solution)/shard_map/pallas_call | solution.py:61
  187.0 3.2 %collective-permute-done.35 = bf16[2,96,768]{2,1,0:T(8,128)(2,1)S(1)} collective-permute-done((bf16[2,96,768]{2,1,0:T(8,128)(2,1)S(1)}, bf16[2,96,768]{2,1,0:T(8,128)(2,1)S(1)}, u32[]{:S(2)}, u32[]{:S(2)}) %collective-permute-start.35) | collective-permute-done | bytes 294944 | tf_op jit(solution)/shard_map/ppermute | solution.py:992
  191.4 4.8 %collective-permute-start.37 = (bf16[2,96,768]{2,1,0:T(8,128)(2,1)S(1)}, bf16[2,96,768]{2,1,0:T(8,128)(2,1)S(1)}, u32[]{:S(2)}, u32[]{:S(2)}) collective-permute-start(bf16[2,96,768]{2,1,0:T(8,128)(2,1)S(1)} %get-tuple-element.297), channel_id=1, source_target_pairs={{0,1},{1,0},{2,3},{3,2},{4,5},{5,4},{6,7},{7,6},{8,9},{9,8},{10,11... | collective-permute-start | bytes 884744 | tf_op jit(solution)/shard_map/ppermute | solution.py:992
  200.2 6.2 %shard_map.316 = (f32[512,768]{1,0:T(8,128)S(1)}, bf16[1024,384]{1,0:T(8,128)(2,1)S(1)}, bf16[2,96,768]{2,1,0:T(8,128)(2,1)S(1)}, bf16[2,96,768]{2,1,0:T(8,128)(2,1)S(1)}, f32[8,768]{1,0:T(8,128)S(1)}) custom-call(s32[4]{0:T(128)S(1)} %pad_add_fusion.info, f32[1024,768]{1,0:T(8,128)S(1)} %get-tuple-element.267.refs_0_, ...), custom_call_target="tpu_custom_call" | custom-call | flops 1207959552 | bytes 14680064 | tf_op jit(solution)/shard_map/pallas_call | solution.py:61
  206.5 3.5 %collective-permute-done.39 = bf16[1,4,24,1536]{3,2,1,0:T(8,128)(2,1)S(1)} collective-permute-done((bf16[1,4,24,1536]{3,2,1,0:T(8,128)(2,1)S(1)}, bf16[1,4,24,1536]{3,2,1,0:T(8,128)(2,1)S(1)}, u32[]{:S(2)}, u32[]{:S(2)}) %collective-permute-start.39) | collective-permute-done | bytes 294944 | tf_op jit(solution)/shard_map/ppermute | solution.py:992
  216.2 4.1 %collective-permute-start.42 = (bf16[2,96,768]{2,1,0:T(8,128)(2,1)S(1)}, bf16[2,96,768]{2,1,0:T(8,128)(2,1)S(1)}, u32[]{:S(2)}, u32[]{:S(2)}) collective-permute-start(bf16[2,96,768]{2,1,0:T(8,128)(2,1)S(1)} %get-tuple-element.307), channel_id=1, source_target_pairs={{0,4},{4,0},{8,12},{12,8},{16,20},{20,16},{24,28},{28,24},{1,5},{5... | collective-permute-start | bytes 884744 | tf_op jit(solution)/shard_map/ppermute | solution.py:992
  220.2 13.0 %shard_map.318 = (bf16[1024,384]{1,0:T(8,128)(2,1)S(1)}, bf16[1024,384]{1,0:T(8,128)(2,1)S(1)}, bf16[1024,384]{1,0:T(8,128)(2,1)S(1)}) custom-call(s32[4]{0:T(128)S(1)} %pad_add_fusion.info, bf16[1024,384]{1,0:T(8,128)(2,1)S(1)} %get-tuple-element.231.q, bf16[1024,384]{1,0:T(8,128)(2,1)S(1)} %get-tuple-element.232.k, ...), custom_call_target="tpu_custom_call" | custom-call | flops 6039797760 | bytes 6291456 | tf_op jit(solution)/shard_map/pallas_call | solution.py:61
  235.6 6.0 %collective-permute-start.47 = (bf16[96,768]{1,0:T(8,128)(2,1)S(1)}, bf16[96,768]{1,0:T(8,128)(2,1)S(1)}, u32[]{:S(2)}, u32[]{:S(2)}) collective-permute-start(bf16[96,768]{1,0:T(8,128)(2,1)S(1)} %get-tuple-element.327), channel_id=1, source_target_pairs={{0,2},{1,3},{2,0},{3,1},{4,6},{5,7},{6,4},{7,5},{8,10},{9,11},{10,... | collective-permute-start | bytes 442376 | tf_op jit(solution)/shard_map/ppermute | solution.py:992
  241.6 3.4 %shard_map.321 = (f32[512,768]{1,0:T(8,128)S(1)}, bf16[512,768]{1,0:T(8,128)(2,1)S(1)}) custom-call(s32[4]{0:T(128)S(1)} %pad_add_fusion.info, bf16[1024,384]{1,0:T(8,128)(2,1)S(1)} %get-tuple-element.321.refs_0_.refs_8_, bf16[1024,384]{1,0:T(8,128)(2,1)S(1)} %get-tuple-element.322.refs_1_, bf16[1024,384]{1,0:T(8,128)(2,1)S(1)} %get-tuple-element.323.refs_2_.refs_9_, ...), custom_call_target="tpu_custom_call" | custom-call | flops 1811939328 | bytes 8388608 | tf_op jit(solution)/shard_map/pallas_call | solution.py:61
  245.0 2.4 collective-permute-done.47
  248.8 1.6 collective-permute-start.50
  250.4 4.2 %shard_map.325 = (bf16[192,1152]{1,0:T(8,128)(2,1)S(1)}, bf16[192,1152]{1,0:T(8,128)(2,1)}, bf16[192,1152]{1,0:T(8,128)(2,1)S(1)}, bf16[192,1152]{1,0:T(8,128)(2,1)S(1)}) custom-call(s32[4]{0:T(128)S(1)} %pad_add_fusion.info, bf16[1024,768]{1,0:T(8,128)(2,1)S(1)} %get-tuple-element.340.left, bf16[1024,384]{1,0:T(8,128)(2,1)S(1)} %get-tuple-element.321.refs_0_.refs_8_, ...), custom_call_target="tpu_custom_call" | custom-call | flops 1811939328 | bytes 8388608 | tf_op jit(solution)/shard_map/pallas_call | solution.py:61
  254.6 4.1 %collective-permute-done.50 = bf16[2,24,1536]{2,1,0:T(8,128)(2,1)S(1)} collective-permute-done((bf16[2,24,1536]{2,1,0:T(8,128)(2,1)S(1)}, bf16[2,24,1536]{2,1,0:T(8,128)(2,1)S(1)}, u32[]{:S(2)}, u32[]{:S(2)}) %collective-permute-start.50) | collective-permute-done | bytes 147488 | tf_op jit(solution)/shard_map/ppermute | solution.py:992
  262.3 4.5 %shard_map.326 = (bf16[512,768]{1,0:T(8,128)(2,1)S(1)}, bf16[192,512]{1,0:T(8,128)(2,1)S(1)}, bf16[192,512]{1,0:T(8,128)(2,1)}, bf16[192,512]{1,0:T(8,128)(2,1)}, bf16[192,512]{1,0:T(8,128)(2,1)S(1)}) custom-call(s32[4]{0:T(128)S(1)} %pad_add_fusion.info, f32[512,768]{1,0:T(8,128)S(1)} %get-tuple-element.346.refs_0_, ...), custom_call_target="tpu_custom_call" | custom-call | flops 100663296 | bytes 10485760 | tf_op jit(solution)/shard_map/pallas_call | solution.py:61
  268.2 4.5 %collective-permute-start.51 = (bf16[256,768]{1,0:T(8,128)(2,1)}, bf16[256,768]{1,0:T(8,128)(2,1)}, u32[]{:S(2)}, u32[]{:S(2)}) collective-permute-start(bf16[256,768]{1,0:T(8,128)(2,1)} %get-tuple-element.355), channel_id=1, source_target_pairs={{0,0},{1,1},{4,2},{5,3},{2,4},{3,5},{6,6},{7,7},{8,8},{9,9},{12,10... | collective-permute-start | bytes 1179656 | tf_op jit(solution)/shard_map/ppermute | solution.py:1006
  273.9 13.3 %collective-permute-done.52 = bf16[256,768]{1,0:T(8,128)(2,1)} collective-permute-done((bf16[256,768]{1,0:T(8,128)(2,1)}, bf16[256,768]{1,0:T(8,128)(2,1)}, u32[]{:S(2)}, u32[]{:S(2)}) %collective-permute-start.52) | collective-permute-done | bytes 393248 | tf_op jit(solution)/shard_map/ppermute | solution.py:1006
  291.0 3.0 collective-permute-start.63
  297.9 1.8 collective-permute-start.65
  302.5 2.1 collective-permute-done.65
  306.0 1.7 collective-permute-done.58
  309.5 2.1 collective-permute-start.60
  314.1 1.6 collective-permute-done.60
  315.7 1.8 collective-permute-done.61
  (190 shorter events, 74.4 us)
Async XLA Ops:
  6.7 12.4 %collective-permute-start.4 = (bf16[96,768]{1,0:T(8,128)(2,1)}, bf16[96,768]{1,0:T(8,128)(2,1)S(1)}, u32[]{:S(2)}, u32[]{:S(2)}) collective-permute-start(bf16[96,768]{1,0:T(8,128)(2,1)} %refs_0_.1), channel_id=1, source_target_pairs={{0,2},{1,3},{2,0},{3,1},{4,6},{5,7},{6,4},{7,5},{8,10},{9,11},{10,... | collective-permute-start | bytes 442376 | tf_op jit(solution)/shard_map/ppermute | solution.py:992
  12.6 13.8 %collective-permute-start.2 = (bf16[2,24,1280]{2,1,0:T(8,128)(2,1)S(1)}, bf16[2,24,1280]{2,1,0:T(8,128)(2,1)S(1)}, u32[]{:S(2)}, u32[]{:S(2)}) collective-permute-start(bf16[2,24,1280]{2,1,0:T(8,128)(2,1)S(1)} %shard_map.298.refs_0_), channel_id=1, source_target_pairs={{0,2},{1,3},{2,0},{3,1},{4,6},{5,7},{6,4},{7,5},{8,10},{9,11},{10,... | collective-permute-start | bytes 368648 | tf_op jit(solution)/shard_map/ppermute | solution.py:992
  13.8 12.6 %collective-permute-start.3 = (bf16[2,24,1280]{2,1,0:T(8,128)(2,1)S(1)}, bf16[2,24,1280]{2,1,0:T(8,128)(2,1)S(1)}, u32[]{:S(2)}, u32[]{:S(2)}) collective-permute-start(bf16[2,24,1280]{2,1,0:T(8,128)(2,1)S(1)} %shard_map.298.refs_0_), channel_id=1, source_target_pairs={{0,3},{1,2},{2,1},{3,0},{4,7},{5,6},{6,5},{7,4},{8,11},{9,10},{10,... | collective-permute-start | bytes 368648 | tf_op jit(solution)/shard_map/ppermute | solution.py:992
  27.0 23.3 %collective-permute-start.10 = (bf16[2,4,24,1280]{3,2,1,0:T(8,128)(2,1)S(1)}, bf16[2,4,24,1280]{3,2,1,0:T(8,128)(2,1)S(1)}, u32[]{:S(2)}, u32[]{:S(2)}) collective-permute-start(bf16[2,4,24,1280]{3,2,1,0:T(8,128)(2,1)S(1)} %shard_map.299), channel_id=1, source_target_pairs={{0,16},{4,20},{8,24},{12,28},{16,0},{20,4},{24,8},{28,12},{1,17},{... | collective-permute-start | bytes 1474568 | tf_op jit(solution)/shard_map/ppermute | solution.py:992
  28.8 21.5 %collective-permute-start.11 = (bf16[2,4,24,1280]{3,2,1,0:T(8,128)(2,1)S(1)}, bf16[2,4,24,1280]{3,2,1,0:T(8,128)(2,1)S(1)}, u32[]{:S(2)}, u32[]{:S(2)}) collective-permute-start(bf16[2,4,24,1280]{3,2,1,0:T(8,128)(2,1)S(1)} %shard_map.299), channel_id=1, source_target_pairs={{0,24},{4,28},{8,16},{12,20},{16,8},{20,12},{24,0},{28,4},{1,25},{... | collective-permute-start | bytes 1474568 | tf_op jit(solution)/shard_map/ppermute | solution.py:992
  30.3 21.3 %collective-permute-start.9 = (bf16[2,4,24,1280]{3,2,1,0:T(8,128)(2,1)S(1)}, bf16[2,4,24,1280]{3,2,1,0:T(8,128)(2,1)S(1)}, u32[]{:S(2)}, u32[]{:S(2)}) collective-permute-start(bf16[2,4,24,1280]{3,2,1,0:T(8,128)(2,1)S(1)} %shard_map.299), channel_id=1, source_target_pairs={{0,8},{4,12},{8,0},{12,4},{16,24},{20,28},{24,16},{28,20},{1,9},{5... | collective-permute-start | bytes 1474568 | tf_op jit(solution)/shard_map/ppermute | solution.py:992
  30.6 14.2 %collective-permute-start.7 = (bf16[2,96,768]{2,1,0:T(8,128)(2,1)S(1)}, bf16[2,96,768]{2,1,0:T(8,128)(2,1)S(1)}, u32[]{:S(2)}, u32[]{:S(2)}) collective-permute-start(bf16[2,96,768]{2,1,0:T(8,128)(2,1)S(1)} %shard_map.300.refs_0_), channel_id=1, source_target_pairs={{0,1},{1,0},{2,3},{3,2},{4,5},{5,4},{6,7},{7,6},{8,9},{9,8},{10,11... | collective-permute-start | bytes 884744 | tf_op jit(solution)/shard_map/ppermute | solution.py:992
  33.6 10.4 %collective-permute-start.6 = (bf16[2,24,2304]{2,1,0:T(8,128)(2,1)S(1)}, bf16[2,24,2304]{2,1,0:T(8,128)(2,1)S(1)}, u32[]{:S(2)}, u32[]{:S(2)}) collective-permute-start(bf16[2,24,2304]{2,1,0:T(8,128)(2,1)S(1)} %shard_map.301.refs_0_), channel_id=1, source_target_pairs={{0,2},{1,3},{2,0},{3,1},{4,6},{5,7},{6,4},{7,5},{8,10},{9,11},{10,... | collective-permute-start | bytes 663560 | tf_op jit(solution)/shard_map/ppermute | solution.py:992
  51.5 26.8 %collective-permute-start.14 = (bf16[4,96,768]{2,1,0:T(8,128)(2,1)S(1)}, bf16[4,96,768]{2,1,0:T(8,128)(2,1)S(1)}, u32[]{:S(2)}, u32[]{:S(2)}) collective-permute-start(bf16[4,96,768]{2,1,0:T(8,128)(2,1)S(1)} %bitcast.99), channel_id=1, source_target_pairs={{0,8},{4,12},{8,0},{12,4},{16,24},{20,28},{24,16},{28,20},{1,9},{5... | collective-permute-start | bytes 1769480 | tf_op jit(solution)/shard_map/ppermute | solution.py:992
  52.9 25.4 %collective-permute-start.15 = (bf16[4,96,768]{2,1,0:T(8,128)(2,1)S(1)}, bf16[4,96,768]{2,1,0:T(8,128)(2,1)S(1)}, u32[]{:S(2)}, u32[]{:S(2)}) collective-permute-start(bf16[4,96,768]{2,1,0:T(8,128)(2,1)S(1)} %bitcast.100), channel_id=1, source_target_pairs={{0,16},{4,20},{8,24},{12,28},{16,0},{20,4},{24,8},{28,12},{1,17},{... | collective-permute-start | bytes 1769480 | tf_op jit(solution)/shard_map/ppermute | solution.py:992
  55.0 16.9 %collective-permute-start.13 = (bf16[2,2,24,2304]{3,2,1,0:T(8,128)(2,1)S(1)}, bf16[2,2,24,2304]{3,2,1,0:T(8,128)(2,1)S(1)}, u32[]{:S(2)}, u32[]{:S(2)}) collective-permute-start(bf16[2,2,24,2304]{3,2,1,0:T(8,128)(2,1)S(1)} %shard_map.304.refs_0_), channel_id=1, source_target_pairs={{0,1},{1,0},{2,3},{3,2},{4,5},{5,4},{6,7},{7,6},{8,9},{9,8},{10,11... | collective-permute-start | bytes 1327112 | tf_op jit(solution)/shard_map/ppermute | solution.py:992
  59.4 18.9 %collective-permute-start.12 = (bf16[272,768]{1,0:T(8,128)(2,1)S(1)}, bf16[272,768]{1,0:T(8,128)(2,1)S(1)}, u32[]{:S(2)}, u32[]{:S(2)}) collective-permute-start(bf16[272,768]{1,0:T(8,128)(2,1)S(1)} %get-tuple-element.213), channel_id=1, source_target_pairs={{0,1},{1,0},{2,5},{3,4},{4,3},{5,2},{6,7},{7,6},{8,9},{9,8},{10,13... | collective-permute-start | bytes 1253384 | tf_op jit(solution)/shard_map/ppermute | solution.py:1225
  84.5 43.4 %collective-permute-start.22 = (bf16[2,4,24,2304]{3,2,1,0:T(8,128)(2,1)S(1)}, bf16[2,4,24,2304]{3,2,1,0:T(8,128)(2,1)S(1)}, u32[]{:S(2)}, u32[]{:S(2)}) collective-permute-start(bf16[2,4,24,2304]{3,2,1,0:T(8,128)(2,1)S(1)} %bitcast.76), channel_id=1, source_target_pairs={{0,8},{4,12},{8,0},{12,4},{16,24},{20,28},{24,16},{28,20},{1,9},{5... | collective-permute-start | bytes 2654216 | tf_op jit(solution)/shard_map/ppermute | solution.py:992
  85.1 42.8 %collective-permute-start.23 = (bf16[2,4,24,2304]{3,2,1,0:T(8,128)(2,1)S(1)}, bf16[2,4,24,2304]{3,2,1,0:T(8,128)(2,1)S(1)}, u32[]{:S(2)}, u32[]{:S(2)}) collective-permute-start(bf16[2,4,24,2304]{3,2,1,0:T(8,128)(2,1)S(1)} %bitcast.77), channel_id=1, source_target_pairs={{0,16},{4,20},{8,24},{12,28},{16,0},{20,4},{24,8},{28,12},{1,17},{... | collective-permute-start | bytes 2654216 | tf_op jit(solution)/shard_map/ppermute | solution.py:992
  86.2 26.7 %collective-permute-start.18 = (bf16[2,96,768]{2,1,0:T(8,128)(2,1)S(1)}, bf16[2,96,768]{2,1,0:T(8,128)(2,1)S(1)}, u32[]{:S(2)}, u32[]{:S(2)}) collective-permute-start(bf16[2,96,768]{2,1,0:T(8,128)(2,1)S(1)} %get-tuple-element.229), channel_id=1, source_target_pairs={{0,8},{4,12},{8,0},{12,4},{16,24},{20,28},{24,16},{28,20},{1,9},{5... | collective-permute-start | bytes 884744 | tf_op jit(solution)/shard_map/ppermute | solution.py:992
  87.8 25.4 %collective-permute-start.19 = (bf16[2,96,768]{2,1,0:T(8,128)(2,1)S(1)}, bf16[2,96,768]{2,1,0:T(8,128)(2,1)S(1)}, u32[]{:S(2)}, u32[]{:S(2)}) collective-permute-start(bf16[2,96,768]{2,1,0:T(8,128)(2,1)S(1)} %get-tuple-element.230), channel_id=1, source_target_pairs={{0,16},{4,20},{8,24},{12,28},{16,0},{20,4},{24,8},{28,12},{1,17},{... | collective-permute-start | bytes 884744 | tf_op jit(solution)/shard_map/ppermute | solution.py:992
  113.8 14.2 %collective-permute-start.20 = (bf16[256,768]{1,0:T(8,128)(2,1)S(1)}, bf16[256,768]{1,0:T(8,128)(2,1)S(1)}, u32[]{:S(2)}, u32[]{:S(2)}) collective-permute-start(bf16[256,768]{1,0:T(8,128)(2,1)S(1)} %get-tuple-element.237), channel_id=1, source_target_pairs={{0,0},{1,1},{2,4},{3,5},{4,2},{5,3},{6,6},{7,7},{8,8},{9,9},{10,12... | collective-permute-start | bytes 1179656 | tf_op jit(solution)/shard_map/ppermute | solution.py:1236
  114.6 13.3 %collective-permute-start.21 = (bf16[256,768]{1,0:T(8,128)(2,1)S(1)}, bf16[256,768]{1,0:T(8,128)(2,1)S(1)}, u32[]{:S(2)}, u32[]{:S(2)}) collective-permute-start(bf16[256,768]{1,0:T(8,128)(2,1)S(1)} %get-tuple-element.238), channel_id=1, source_target_pairs={{0,1},{1,0},{2,5},{3,4},{4,3},{5,2},{6,7},{7,6},{8,9},{9,8},{10,13... | collective-permute-start | bytes 1179656 | tf_op jit(solution)/shard_map/ppermute | solution.py:1236
  128.0 17.1 %collective-permute-start.24 = (bf16[1024,384]{1,0:T(8,128)(2,1)S(1)}, bf16[1024,384]{1,0:T(8,128)(2,1)S(1)}, u32[]{:S(2)}, u32[]{:S(2)}) collective-permute-start(bf16[1024,384]{1,0:T(8,128)(2,1)S(1)} %get-tuple-element.240.att.refs_4_.o), channel_id=1, source_target_pairs={{0,4},{4,0},{8,12},{12,8},{16,20},{20,16},{24,28},{28,24},{1,5},{5... | collective-permute-start | bytes 2359304 | tf_op jit(solution)/shard_map/ppermute | solution.py:992
  131.7 12.2 %collective-permute-start.25 = (bf16[1,4,24,2304]{3,2,1,0:T(8,128)(2,1)S(1)}, bf16[1,4,24,2304]{3,2,1,0:T(8,128)(2,1)S(1)}, u32[]{:S(2)}, u32[]{:S(2)}) collective-permute-start(bf16[1,4,24,2304]{3,2,1,0:T(8,128)(2,1)S(1)} %get-tuple-element.246), channel_id=1, source_target_pairs={{0,8},{4,12},{8,0},{12,4},{16,24},{20,28},{24,16},{28,20},{1,9},{5... | collective-permute-start | bytes 1327112 | tf_op jit(solution)/shard_map/ppermute | solution.py:992
  133.2 11.8 %collective-permute-start.26 = (bf16[1,4,24,2304]{3,2,1,0:T(8,128)(2,1)S(1)}, bf16[1,4,24,2304]{3,2,1,0:T(8,128)(2,1)S(1)}, u32[]{:S(2)}, u32[]{:S(2)}) collective-permute-start(bf16[1,4,24,2304]{3,2,1,0:T(8,128)(2,1)S(1)} %get-tuple-element.247), channel_id=1, source_target_pairs={{0,16},{4,20},{8,24},{12,28},{16,0},{20,4},{24,8},{28,12},{1,17},{... | collective-permute-start | bytes 1327112 | tf_op jit(solution)/shard_map/ppermute | solution.py:992
  133.7 15.5 %collective-permute-start.27 = (bf16[256,768]{1,0:T(8,128)(2,1)S(1)}, bf16[256,768]{1,0:T(8,128)(2,1)S(1)}, u32[]{:S(2)}, u32[]{:S(2)}) collective-permute-start(bf16[256,768]{1,0:T(8,128)(2,1)S(1)} %collective-permute-done.20.refs_0_.refs_5_), channel_id=1, source_target_pairs={{0,4},{4,0},{8,12},{12,8},{16,20},{20,16},{24,28},{28,24},{1,5},{5... | collective-permute-start | bytes 1179656 | tf_op jit(solution)/shard_map/ppermute | solution.py:992
  133.7 15.5 %collective-permute-start.28 = (bf16[256,768]{1,0:T(8,128)(2,1)S(1)}, bf16[256,768]{1,0:T(8,128)(2,1)S(1)}, u32[]{:S(2)}, u32[]{:S(2)}) collective-permute-start(bf16[256,768]{1,0:T(8,128)(2,1)S(1)} %collective-permute-done.21.refs_1_.refs_6_), channel_id=1, source_target_pairs={{0,4},{4,0},{8,12},{12,8},{16,20},{20,16},{24,28},{28,24},{1,5},{5... | collective-permute-start | bytes 1179656 | tf_op jit(solution)/shard_map/ppermute | solution.py:992
  164.4 14.2 %collective-permute-start.29 = (bf16[2,96,768]{2,1,0:T(8,128)(2,1)S(1)}, bf16[2,96,768]{2,1,0:T(8,128)(2,1)S(1)}, u32[]{:S(2)}, u32[]{:S(2)}) collective-permute-start(bf16[2,96,768]{2,1,0:T(8,128)(2,1)S(1)} %get-tuple-element.263), channel_id=1, source_target_pairs={{0,8},{4,12},{8,0},{12,4},{16,24},{20,28},{24,16},{28,20},{1,9},{5... | collective-permute-start | bytes 884744 | tf_op jit(solution)/shard_map/ppermute | solution.py:992
  165.0 13.6 %collective-permute-start.30 = (bf16[2,96,768]{2,1,0:T(8,128)(2,1)S(1)}, bf16[2,96,768]{2,1,0:T(8,128)(2,1)S(1)}, u32[]{:S(2)}, u32[]{:S(2)}) collective-permute-start(bf16[2,96,768]{2,1,0:T(8,128)(2,1)S(1)} %get-tuple-element.264), channel_id=1, source_target_pairs={{0,8},{4,12},{8,0},{12,4},{16,24},{20,28},{24,16},{28,20},{1,9},{5... | collective-permute-start | bytes 884744 | tf_op jit(solution)/shard_map/ppermute | solution.py:992
  166.5 12.1 %collective-permute-start.31 = (bf16[2,96,768]{2,1,0:T(8,128)(2,1)S(1)}, bf16[2,96,768]{2,1,0:T(8,128)(2,1)S(1)}, u32[]{:S(2)}, u32[]{:S(2)}) collective-permute-start(bf16[2,96,768]{2,1,0:T(8,128)(2,1)S(1)} %get-tuple-element.265), channel_id=1, source_target_pairs={{0,16},{4,20},{8,24},{12,28},{16,0},{20,4},{24,8},{28,12},{1,17},{... | collective-permute-start | bytes 884744 | tf_op jit(solution)/shard_map/ppermute | solution.py:992
  167.0 13.0 %collective-permute-start.32 = (bf16[2,96,768]{2,1,0:T(8,128)(2,1)S(1)}, bf16[2,96,768]{2,1,0:T(8,128)(2,1)S(1)}, u32[]{:S(2)}, u32[]{:S(2)}) collective-permute-start(bf16[2,96,768]{2,1,0:T(8,128)(2,1)S(1)} %get-tuple-element.266), channel_id=1, source_target_pairs={{0,16},{4,20},{8,24},{12,28},{16,0},{20,4},{24,8},{28,12},{1,17},{... | collective-permute-start | bytes 884744 | tf_op jit(solution)/shard_map/ppermute | solution.py:992
  180.0 10.4 %collective-permute-start.33 = (bf16[1024,768]{1,0:T(8,128)(2,1)S(1)}, bf16[1024,768]{1,0:T(8,128)(2,1)S(1)}, u32[]{:S(2)}, u32[]{:S(2)}) collective-permute-start(bf16[1024,768]{1,0:T(8,128)(2,1)S(1)} %get-tuple-element.268), channel_id=1, source_target_pairs={{0,4},{4,0},{8,12},{12,8},{16,20},{20,16},{24,28},{28,24},{1,5},{5... | collective-permute-start | bytes 4718600 | tf_op jit(solution)/shard_map/ppermute | solution.py:992
  180.0 10.4 %collective-permute-start.34 = (bf16[512,768]{1,0:T(8,128)(2,1)S(1)}, bf16[512,768]{1,0:T(8,128)(2,1)S(1)}, u32[]{:S(2)}, u32[]{:S(2)}) collective-permute-start(bf16[512,768]{1,0:T(8,128)(2,1)S(1)} %get-tuple-element.269), channel_id=1, source_target_pairs={{0,4},{4,0},{8,12},{12,8},{16,20},{20,16},{24,28},{28,24},{1,5},{5... | collective-permute-start | bytes 2359304 | tf_op jit(solution)/shard_map/ppermute | solution.py:992
  191.4 15.1 %collective-permute-start.37 = (bf16[2,96,768]{2,1,0:T(8,128)(2,1)S(1)}, bf16[2,96,768]{2,1,0:T(8,128)(2,1)S(1)}, u32[]{:S(2)}, u32[]{:S(2)}) collective-permute-start(bf16[2,96,768]{2,1,0:T(8,128)(2,1)S(1)} %get-tuple-element.297), channel_id=1, source_target_pairs={{0,1},{1,0},{2,3},{3,2},{4,5},{5,4},{6,7},{7,6},{8,9},{9,8},{10,11... | collective-permute-start | bytes 884744 | tf_op jit(solution)/shard_map/ppermute | solution.py:992
  196.2 10.3 %collective-permute-start.38 = (bf16[1,4,24,1536]{3,2,1,0:T(8,128)(2,1)S(1)}, bf16[1,4,24,1536]{3,2,1,0:T(8,128)(2,1)S(1)}, u32[]{:S(2)}, u32[]{:S(2)}) collective-permute-start(bf16[1,4,24,1536]{3,2,1,0:T(8,128)(2,1)S(1)} %bitcast.138), channel_id=1, source_target_pairs={{0,8},{4,12},{8,0},{12,4},{16,24},{20,28},{24,16},{28,20},{1,9},{5... | collective-permute-start | bytes 884744 | tf_op jit(solution)/shard_map/ppermute | solution.py:992
  196.8 13.3 %collective-permute-start.39 = (bf16[1,4,24,1536]{3,2,1,0:T(8,128)(2,1)S(1)}, bf16[1,4,24,1536]{3,2,1,0:T(8,128)(2,1)S(1)}, u32[]{:S(2)}, u32[]{:S(2)}) collective-permute-start(bf16[1,4,24,1536]{3,2,1,0:T(8,128)(2,1)S(1)} %bitcast.137), channel_id=1, source_target_pairs={{0,8},{4,12},{8,0},{12,4},{16,24},{20,28},{24,16},{28,20},{1,9},{5... | collective-permute-start | bytes 884744 | tf_op jit(solution)/shard_map/ppermute | solution.py:992
  198.2 11.8 %collective-permute-start.40 = (bf16[1,4,24,1536]{3,2,1,0:T(8,128)(2,1)S(1)}, bf16[1,4,24,1536]{3,2,1,0:T(8,128)(2,1)S(1)}, u32[]{:S(2)}, u32[]{:S(2)}) collective-permute-start(bf16[1,4,24,1536]{3,2,1,0:T(8,128)(2,1)S(1)} %bitcast.136), channel_id=1, source_target_pairs={{0,16},{4,20},{8,24},{12,28},{16,0},{20,4},{24,8},{28,12},{1,17},{... | collective-permute-start | bytes 884744 | tf_op jit(solution)/shard_map/ppermute | solution.py:992
  199.7 11.8 %collective-permute-start.41 = (bf16[1,4,24,1536]{3,2,1,0:T(8,128)(2,1)S(1)}, bf16[1,4,24,1536]{3,2,1,0:T(8,128)(2,1)S(1)}, u32[]{:S(2)}, u32[]{:S(2)}) collective-permute-start(bf16[1,4,24,1536]{3,2,1,0:T(8,128)(2,1)S(1)} %bitcast.135), channel_id=1, source_target_pairs={{0,16},{4,20},{8,24},{12,28},{16,0},{20,4},{24,8},{28,12},{1,17},{... | collective-permute-start | bytes 884744 | tf_op jit(solution)/shard_map/ppermute | solution.py:992
  212.2 21.0 %collective-permute-start.45 = (bf16[1,4,24,1536]{3,2,1,0:T(8,128)(2,1)S(1)}, bf16[1,4,24,1536]{3,2,1,0:T(8,128)(2,1)S(1)}, u32[]{:S(2)}, u32[]{:S(2)}) collective-permute-start(bf16[1,4,24,1536]{3,2,1,0:T(8,128)(2,1)S(1)} %get-tuple-element.317), channel_id=1, source_target_pairs={{0,16},{4,20},{8,24},{12,28},{16,0},{20,4},{24,8},{28,12},{1,17},{... | collective-permute-start | bytes 884744 | tf_op jit(solution)/shard_map/ppermute | solution.py:992
  213.7 19.6 %collective-permute-start.46 = (bf16[1,4,24,1536]{3,2,1,0:T(8,128)(2,1)S(1)}, bf16[1,4,24,1536]{3,2,1,0:T(8,128)(2,1)S(1)}, u32[]{:S(2)}, u32[]{:S(2)}) collective-permute-start(bf16[1,4,24,1536]{3,2,1,0:T(8,128)(2,1)S(1)} %get-tuple-element.318), channel_id=1, source_target_pairs={{0,8},{4,12},{8,0},{12,4},{16,24},{20,28},{24,16},{28,20},{1,9},{5... | collective-permute-start | bytes 884744 | tf_op jit(solution)/shard_map/ppermute | solution.py:992
  215.1 18.2 %collective-permute-start.43 = (bf16[256,768]{1,0:T(8,128)(2,1)S(1)}, bf16[256,768]{1,0:T(8,128)(2,1)S(1)}, u32[]{:S(2)}, u32[]{:S(2)}) collective-permute-start(bf16[256,768]{1,0:T(8,128)(2,1)S(1)} %get-tuple-element.311), channel_id=1, source_target_pairs={{0,0},{1,1},{4,2},{5,3},{2,4},{3,5},{6,6},{7,7},{8,8},{9,9},{12,10... | collective-permute-start | bytes 1179656 | tf_op jit(solution)/shard_map/ppermute | solution.py:1006
  215.7 17.5 %collective-permute-start.44 = (bf16[256,768]{1,0:T(8,128)(2,1)S(1)}, bf16[256,768]{1,0:T(8,128)(2,1)S(1)}, u32[]{:S(2)}, u32[]{:S(2)}) collective-permute-start(bf16[256,768]{1,0:T(8,128)(2,1)S(1)} %get-tuple-element.312), channel_id=1, source_target_pairs={{1,0},{0,1},{5,2},{4,3},{3,4},{2,5},{7,6},{6,7},{9,8},{8,9},{13,10... | collective-permute-start | bytes 1179656 | tf_op jit(solution)/shard_map/ppermute | solution.py:1006
  216.2 17.1 %collective-permute-start.42 = (bf16[2,96,768]{2,1,0:T(8,128)(2,1)S(1)}, bf16[2,96,768]{2,1,0:T(8,128)(2,1)S(1)}, u32[]{:S(2)}, u32[]{:S(2)}) collective-permute-start(bf16[2,96,768]{2,1,0:T(8,128)(2,1)S(1)} %get-tuple-element.307), channel_id=1, source_target_pairs={{0,4},{4,0},{8,12},{12,8},{16,20},{20,16},{24,28},{28,24},{1,5},{5... | collective-permute-start | bytes 884744 | tf_op jit(solution)/shard_map/ppermute | solution.py:992
  234.3 13.2 %collective-permute-start.48 = (bf16[2,2,24,1536]{3,2,1,0:T(8,128)(2,1)S(1)}, bf16[2,2,24,1536]{3,2,1,0:T(8,128)(2,1)S(1)}, u32[]{:S(2)}, u32[]{:S(2)}) collective-permute-start(bf16[2,2,24,1536]{3,2,1,0:T(8,128)(2,1)S(1)} %get-tuple-element.334), channel_id=1, source_target_pairs={{0,1},{1,0},{2,3},{3,2},{4,5},{5,4},{6,7},{7,6},{8,9},{9,8},{10,11... | collective-permute-start | bytes 884744 | tf_op jit(solution)/shard_map/ppermute | solution.py:992
  235.6 11.8 %collective-permute-start.47 = (bf16[96,768]{1,0:T(8,128)(2,1)S(1)}, bf16[96,768]{1,0:T(8,128)(2,1)S(1)}, u32[]{:S(2)}, u32[]{:S(2)}) collective-permute-start(bf16[96,768]{1,0:T(8,128)(2,1)S(1)} %get-tuple-element.327), channel_id=1, source_target_pairs={{0,2},{1,3},{2,0},{3,1},{4,6},{5,7},{6,4},{7,5},{8,10},{9,11},{10,... | collective-permute-start | bytes 442376 | tf_op jit(solution)/shard_map/ppermute | solution.py:992
  247.4 11.3 %collective-permute-start.49 = (bf16[512,768]{1,0:T(8,128)(2,1)S(1)}, bf16[512,768]{1,0:T(8,128)(2,1)S(1)}, u32[]{:S(2)}, u32[]{:S(2)}) collective-permute-start(bf16[512,768]{1,0:T(8,128)(2,1)S(1)} %get-tuple-element.336), channel_id=1, source_target_pairs={{0,4},{4,0},{8,12},{12,8},{16,20},{20,16},{24,28},{28,24},{1,5},{5... | collective-permute-start | bytes 2359304 | tf_op jit(solution)/shard_map/ppermute | solution.py:992
  258.8 28.5 %collective-permute-start.53 = (bf16[2,4,24,1152]{3,2,1,0:T(8,128)(2,1)}, bf16[2,4,24,1152]{3,2,1,0:T(8,128)(2,1)S(1)}, u32[]{:S(2)}, u32[]{:S(2)}) collective-permute-start(bf16[2,4,24,1152]{3,2,1,0:T(8,128)(2,1)} %bitcast.45), channel_id=1, source_target_pairs={{0,8},{4,12},{8,0},{12,4},{16,24},{20,28},{24,16},{28,20},{1,9},{5... | collective-permute-start | bytes 1327112 | tf_op jit(solution)/shard_map/ppermute | solution.py:992
  260.2 27.1 %collective-permute-start.54 = (bf16[2,4,24,1152]{3,2,1,0:T(8,128)(2,1)S(1)}, bf16[2,4,24,1152]{3,2,1,0:T(8,128)(2,1)S(1)}, u32[]{:S(2)}, u32[]{:S(2)}) collective-permute-start(bf16[2,4,24,1152]{3,2,1,0:T(8,128)(2,1)S(1)} %bitcast.134), channel_id=1, source_target_pairs={{0,16},{4,20},{8,24},{12,28},{16,0},{20,4},{24,8},{28,12},{1,17},{... | collective-permute-start | bytes 1327112 | tf_op jit(solution)/shard_map/ppermute | solution.py:992
  260.8 26.5 %collective-permute-start.55 = (bf16[2,4,24,1152]{3,2,1,0:T(8,128)(2,1)S(1)}, bf16[2,4,24,1152]{3,2,1,0:T(8,128)(2,1)S(1)}, u32[]{:S(2)}, u32[]{:S(2)}) collective-permute-start(bf16[2,4,24,1152]{3,2,1,0:T(8,128)(2,1)S(1)} %bitcast.133), channel_id=1, source_target_pairs={{0,24},{4,28},{8,16},{12,20},{16,8},{20,12},{24,0},{28,4},{1,25},{... | collective-permute-start | bytes 1327112 | tf_op jit(solution)/shard_map/ppermute | solution.py:992
  272.7 14.5 %collective-permute-start.52 = (bf16[256,768]{1,0:T(8,128)(2,1)}, bf16[256,768]{1,0:T(8,128)(2,1)}, u32[]{:S(2)}, u32[]{:S(2)}) collective-permute-start(bf16[256,768]{1,0:T(8,128)(2,1)} %get-tuple-element.356), channel_id=1, source_target_pairs={{1,0},{0,1},{5,2},{4,3},{3,4},{2,5},{7,6},{6,7},{9,8},{8,9},{13,10... | collective-permute-start | bytes 1179656 | tf_op jit(solution)/shard_map/ppermute | solution.py:1006
  288.0 18.0 %collective-permute-start.56 = (bf16[2,4,24,512]{3,2,1,0:T(8,128)(2,1)}, bf16[2,4,24,512]{3,2,1,0:T(8,128)(2,1)S(1)}, u32[]{:S(2)}, u32[]{:S(2)}) collective-permute-start(bf16[2,4,24,512]{3,2,1,0:T(8,128)(2,1)} %bitcast.50), channel_id=1, source_target_pairs={{0,8},{4,12},{8,0},{12,4},{16,24},{20,28},{24,16},{28,20},{1,9},{5... | collective-permute-start | bytes 589832 | tf_op jit(solution)/shard_map/ppermute | solution.py:992
  289.4 16.6 %collective-permute-start.57 = (bf16[2,4,24,512]{3,2,1,0:T(8,128)(2,1)}, bf16[2,4,24,512]{3,2,1,0:T(8,128)(2,1)S(1)}, u32[]{:S(2)}, u32[]{:S(2)}) collective-permute-start(bf16[2,4,24,512]{3,2,1,0:T(8,128)(2,1)} %bitcast.52), channel_id=1, source_target_pairs={{0,16},{4,20},{8,24},{12,28},{16,0},{20,4},{24,8},{28,12},{1,17},{... | collective-permute-start | bytes 589832 | tf_op jit(solution)/shard_map/ppermute | solution.py:992
  (38 other events, 239.5 us)

commit v4 on v3

--- a/solution.py
+++ b/solution.py
@@ -108,47 +108,42 @@
         copy.wait()
 
 
-def pack_kernel(patches, info, weight, table, rows_in, spare_in, up, out_weight, ins_keep, ins_send, ups_keep, ups_send):
+def pack_in_kernel(patches, info, weight, table, rows_in, keep, send):
     core = info[0]
     part = weight.shape[1] // 6
-    small = jnp.zeros((weight.shape[0], SMALL), f32)
     turned = rows_in[...].astype(f32).T
-    count = patches + turned.shape[1]
-    small = jnp.concatenate(
-        [
-            table[...].astype(f32),
-            turned,
-            spare_in[...].astype(f32),
-            small[:, count + spare_in.shape[1] :],
-        ],
-        axis=1,
-    ).astype(bf16)
-    columns = 3 * part
-    own = ups_keep.shape[1] - out_weight.shape[1]
-    for ref, up_ref, side in ((ins_keep, ups_keep, core), (ins_send, ups_send, 1 - core)):
+    empty = jnp.zeros((weight.shape[0], SMALL - patches - turned.shape[1]), f32)
+    small = jnp.concatenate([table[...].astype(f32), turned, empty], axis=1).astype(bf16)
+    for ref, side in ((keep, core), (send, 1 - core)):
         for i in range(3):
             there = pl.ds(pl.multiple_of((2 * i + side) * part, 128), part)
             ref[:, i * part : (i + 1) * part] = weight[:, there]
-        ref[:, columns:] = small
-        if up is not None:
-            step = own // 4
-            for q in range(4):
-                there = pl.ds(pl.multiple_of((2 * q + side) * step, 128), step)
-                up_ref[:, q * step : (q + 1) * step] = up[:, there]
-        up_ref[:, own:] = out_weight[...]
-
-
-def pack(info, weight, table, rows_in, spare_in, up, out_weight, patches):
+        ref[:, 3 * part :] = small
+
+
+def pack_in(info, weight, table, rows_in):
     rows, columns = weight.shape[0], weight.shape[1] // 2 + SMALL
-    own = up.shape[1] // 2 + out_weight.shape[1]
-    return call(
-        functools.partial(pack_kernel, patches),
-        [(shaped((rows, columns), bf16), vmem())] * 2 + [(shaped((rows, own), bf16), vmem())] * 2,
-        [vmem()] * 6,
-        [info, weight, table, rows_in, spare_in, up, out_weight],
+    return call(
+        functools.partial(pack_in_kernel, table.shape[1]),
+        [(shaped((rows, columns), bf16), vmem())] * 2,
+        [vmem()] * 3,
+        [info, weight, table, rows_in],
         limit=8,
         cost=(0, MIB),
     )
+
+
+def pack_up_kernel(info, up, keep, send):
+    step = keep.shape[1] // 4
+    for ref, side in ((keep, info[0]), (send, 1 - info[0])):
+        for q in range(4):
+            there = pl.ds(pl.multiple_of((2 * q + side) * step, 128), step)
+            ref[:, q * step : (q + 1) * step] = up[:, there]
+
+
+def pack_up(info, up):
+    out = (shaped((up.shape[0], up.shape[1] // 2), bf16), vmem())
+    return call(pack_up_kernel, [out] * 2, [vmem()], [info, up], limit=8, cost=(0, MIB))
 
 
 def sent_kernel(info, tokens, positions, segments, first, second, extra):
@@ -205,6 +200,51 @@
     )[0]
 
 
+def settle_kernel(info, own, far, out):
+    odd = lax.rem(info[2], 2)
+    block = out.shape[1]
+    rows = own.shape[1] - block
+    for k, ref in enumerate((own, far)):
+        for high in range(2):
+            out[2 * high + (k ^ odd)] = ref[high, :block, :]
+    both = (own, far)
+    for high in range(2):
+        pair = [ref[high, block:, :].astype(f32) for ref in both]
+        for low in range(2):
+            row = jnp.where(odd == low, pair[0], pair[1]).astype(bf16)
+            begin = (2 * high + low) * rows
+            out[PLACES, begin : begin + rows, :] = row
+
+
+def settle(info, own, far):
+    _, rows, width = own.shape
+    block = rows * PLACES // (PLACES + 1)
+    return call(
+        settle_kernel,
+        [(shaped((PLACES + 1, block, width), bf16), vmem())],
+        [vmem()] * 2,
+        [info, own, far],
+        limit=8,
+        cost=(0, 2 * MIB),
+    )[0]
+
+
+def last_kernel(info, own, x, y, d, out):
+    for distance, ref in enumerate((own, x, y, d)):
+        out[distance ^ info[1]] = ref[ref.shape[0] - 1]
+
+
+def last_blocks(info, own, x, y, d):
+    return call(
+        last_kernel,
+        [(shaped((4,) + own.shape[1:], bf16), vmem())],
+        [vmem()] * 4,
+        [info, own, x, y, d],
+        limit=8,
+        cost=(0, MIB),
+    )[0]
+
+
 def cut_kernel(info, x, y, first, second):
     half = first.shape[0]
     first[...] = y[:half]
@@ -212,8 +252,12 @@
 
 
 def cut(info, x, y):
-    one = shaped((x.shape[0] // 2,) + x.shape[1:], bf16)
-    return call(cut_kernel, [(one, vmem())] * 2, [LOAD] * 2, [info, x, y], limit=8, cost=(0, MIB))
+    half = x.shape[0] // 2
+    outs = [
+        (shaped((half,) + x.shape[1:], bf16), vmem()),
+        (shaped((x.shape[0] - half,) + x.shape[1:], bf16), vmem()),
+    ]
+    return call(cut_kernel, outs, [LOAD] * 2, [info, x, y], limit=8, cost=(0, MIB))
 
 
 def add_kernel(info, a, b, c, d, first, second):
@@ -501,61 +545,85 @@
     return copies
 
 
+def block_copies(pieces, target, info, sem):
+    if len(pieces) == 1:
+        return [pltpu.make_async_copy(pieces[0], target, sem.at[0])]
+    copies = []
+    for i, ref in enumerate(pieces):
+        begin = (min(i, 3) ^ info[1]) * PLACES + (2 if i == 4 else 0)
+        count = 2 if i >= 3 else PLACES
+        copies.append(
+            pltpu.make_async_copy(ref.at[pl.ds(0, count)], target.at[pl.ds(begin, count)], sem.at[i])
+        )
+    return copies
+
+
 def hidden_places(core, hidden, width, chips):
     spare = 2 * hidden // width
     share = hidden // chips
+    device = share // PLACES
+    rows = device // spare
     unit = lax.broadcasted_iota(jnp.int32, (hidden, 1), 0)
-    chip, rest = unit // share, lax.rem(unit, share)
-    row = (2 * chip + core) * (share // spare) + rest // spare
+    rest = lax.rem(unit, share)
+    row = ((2 * (unit // share) + core) * PLACES + rest // device) * rows + lax.rem(rest, rows)
     lane = lax.broadcasted_iota(jnp.int32, (hidden, width), 1)
     return jnp.where(lane == row, 1.0, 0.0).astype(bf16)
 
 
-def middle_kernel(count, patches, chips, info, att, att_far, start, turned, *refs):
-    up_in, refs = refs[:count], refs[count:]
-    middle_out, normed_out, bias_out, weight, sem = refs
+def hidden_turns(spare, hidden, chips):
+    device = hidden // (chips * PLACES)
+    unit = lax.broadcasted_iota(jnp.int32, (spare, hidden), 1)
+    return lax.rem(unit, device) // (device // spare) == lax.broadcasted_iota(
+        jnp.int32, (spare, hidden), 0
+    )
+
+
+def middle_kernel(patches, chips, hidden, info, att, att_far, start, turned, *refs):
+    weights, refs = refs[:-4], refs[-4:]
+    middle_out, normed_out, bias_out, weight_out = refs
     core = info[0]
     rows, width = start.shape
     part, tile = width // 2, rows // 4
-    hidden = up_in[0].shape[1] - width
-    copies = piece_copies(up_in, weight, info, sem, slice(hidden, hidden + width))
-    for copy in copies:
-        copy.start()
+    if len(weights) == 2:
+        block = weights[0].shape[1]
+        for side, ref in ((core, weights[0]), (1 - core, weights[1])):
+            for q in range(4):
+                begin = pl.multiple_of((2 * q + side) * block, block)
+                weight_out[pl.ds(begin, block), :] = ref[q]
+    else:
+        weight_out[...] = weights[0][...]
     spare = 2 * hidden // width
     biases = turned[patches + 8 : patches + 8 + spare, :].astype(bf16)
     spread_out = dot_right(biases, hidden_places(core, hidden, width, chips))
-    turns = lax.rem(lax.broadcasted_iota(jnp.int32, (spare, hidden), 1), spare)
-    ranks = lax.broadcasted_iota(jnp.int32, (spare, hidden), 0)
-    bias = jnp.sum(jnp.where(turns == ranks, spread_out, 0.0), axis=0, keepdims=True)
+    bias = jnp.sum(
+        jnp.where(hidden_turns(spare, hidden, chips), spread_out, 0.0), axis=0, keepdims=True
+    )
     bias_out[...] = jnp.broadcast_to(bias, bias_out.shape)
-    for copy in copies:
-        copy.wait()
     vector = lambda i: turned[patches + i : patches + i + 1, :]
     own = pl.ds(pl.multiple_of(core * part, 128), part)
     far = pl.ds(pl.multiple_of((1 - core) * part, 128), part)
     gain, shift, out_bias = vector(GAIN_TWO), vector(SHIFT_TWO), vector(OUTPUT_BIAS)
     for t in range(4):
         here = slice(t * tile, (t + 1) * tile)
-        mixed = dot(att[here, :], weight[own, :]) + dot(att_far[here, :], weight[far, :])
+        mixed = dot(att[here, :], weight_out[own, :]) + dot(att_far[here, :], weight_out[far, :])
         middle = start[here, :] + mixed + out_bias
         middle_out[here, :] = middle
         normal, _ = normalise(middle)
         normed_out[here, :] = (normal * gain + shift).astype(bf16)
 
 
-def middle_front(info, att, att_far, start, turned, ups, patches, chips):
+def middle_front(info, att, att_far, start, turned, weights, hidden, patches, chips):
     rows, width = start.shape
-    count = len(ups)
-    return call(
-        functools.partial(middle_kernel, count, patches, chips),
+    return call(
+        functools.partial(middle_kernel, patches, chips, hidden),
         [
             (shaped((rows, width), f32), vmem()),
             (shaped((rows, width), bf16), vmem()),
-            (shaped((8, ups[0].shape[1] - width), f32), vmem()),
+            (shaped((8, hidden), f32), vmem()),
+            (shaped((width, width), bf16), vmem()),
         ],
-        [LOAD] * 4 + [HELD] * count,
-        [info, att, att_far, start, turned] + list(ups),
-        scratch=[pltpu.VMEM((width, width), bf16), pltpu.SemaphoreType.DMA((count,))],
+        [LOAD] * (4 + len(weights)),
+        [info, att, att_far, start, turned] + list(weights),
         cost=(2 * rows * width * width, 12 * MIB),
     )
 
@@ -572,9 +640,9 @@
     rows, width = normed.shape
     hidden = up.shape[1]
     chunk = hidden // 4
-    early = piece_copies(up_in, up, info, up_sem, slice(0, hidden))
+    early = piece_copies(up_in, up, info, up_sem)
     late = cotangent_copies(info, cot_in, cot, [cot_sem.at[i] for i in range(4)])
-    late += piece_copies(down_in, down, info, down_sem)
+    late += block_copies(down_in, down, info, down_sem)
     for copy in early + late:
         copy.start()
     for copy in early + late:
@@ -653,8 +721,8 @@
     width = up.shape[0]
     chunk = hidden // 4
     copies = cotangent_copies(info, cot_in, cot, [cot_sem.at[i] for i in range(4)])
-    copies += piece_copies(down_in, down, info, down_sem)
-    copies += piece_copies(up_in, up, info, up_sem, slice(0, hidden))
+    copies += block_copies(down_in, down, info, down_sem)
+    copies += piece_copies(up_in, up, info, up_sem)
     run_copies(copies)
     back_out[...] = jnp.zeros_like(back_out)
 
@@ -736,19 +804,14 @@
     )
 
 
-def middle_back_kernel(count, blocks, patches, info, *refs):
-    back, back_far, middle, turned, att, refs = refs[0], refs[1], refs[2], refs[3], refs[4], refs[5:]
+def middle_back_kernel(blocks, patches, info, back, back_far, middle, turned, att, weight, *refs):
     cot_in, refs = refs[:4], refs[4:]
-    up_in, refs = refs[:count], refs[count:]
-    grad_out, attended_out, keep_out, send_out, sums_out, cot, weight, branch, sem, up_sem = refs
-    core, chip = info[0], info[1]
+    grad_out, attended_out, keep_out, send_out, sums_out, cot, branch, sem = refs
+    core = info[0]
     rows, width = middle.shape
     tile = rows // 4
     part = width // 2
-    hidden = up_in[0].shape[1] - width
-    copies = cotangent_copies(info, cot_in, cot, [sem.at[i] for i in range(4)])
-    copies += piece_copies(up_in, weight, info, up_sem, slice(hidden, hidden + width))
-    run_copies(copies)
+    run_copies(cotangent_copies(info, cot_in, cot, [sem.at[i] for i in range(4)]))
     gain = turned[patches + GAIN_TWO : patches + GAIN_TWO + 1, :]
     own_rows = pl.ds(pl.multiple_of(core * part, 128), part)
     for t in range(4):
@@ -792,13 +855,12 @@
         send_out[...] = weight_grad
 
 
-def middle_back(info, back, back_far, middle, turned, att, cots, ups, patches, blocks):
-    count = len(ups)
+def middle_back(info, back, back_far, middle, turned, att, weight, cots, patches, blocks):
     rows, width = middle.shape
     part = width // 2
     slab = (2, part // 4, width) if blocks == 4 else (part, width)
     return call(
-        functools.partial(middle_back_kernel, count, blocks, patches),
+        functools.partial(middle_back_kernel, blocks, patches),
         [
             (shaped((rows // 2, width), f32), vmem()),
             (shaped((rows, part), bf16), vmem()),
@@ -806,14 +868,12 @@
             (shaped(slab, bf16), vmem()),
             (shaped((8, width), f32), vmem()),
         ],
-        [LOAD] * 5 + [HELD] * (4 + count),
-        [info, back, back_far, middle, turned, att] + list(cots) + list(ups),
+        [LOAD] * 6 + [HELD] * 4,
+        [info, back, back_far, middle, turned, att, weight] + list(cots),
         scratch=[
             pltpu.VMEM((4, rows // 4, width), bf16),
-            pltpu.VMEM((width, width), bf16),
             pltpu.VMEM((rows, width), bf16),
             pltpu.SemaphoreType.DMA((4,)),
-            pltpu.SemaphoreType.DMA((count,)),
         ],
         cost=(4 * rows * width * part, 14 * MIB),
     )
@@ -910,9 +970,7 @@
     put(SHIFT_ONE, jnp.sum(grad_normed, axis=0, keepdims=True))
     hidden = bias_grad.shape[1]
     spare = 2 * hidden // width
-    turns = lax.rem(lax.broadcasted_iota(jnp.int32, (spare, hidden), 1), spare)
-    ranks = lax.broadcasted_iota(jnp.int32, (spare, hidden), 0)
-    biases = jnp.where(turns == ranks, bias_grad[0:1, :], 0.0)
+    biases = jnp.where(hidden_turns(spare, hidden, chips), bias_grad[0:1, :], 0.0)
     high = biases.astype(bf16)
     both = jnp.concatenate([high.astype(f32), biases - high.astype(f32)]).astype(bf16)
     placed = dot(both, hidden_places(core, hidden, width, chips))
@@ -1001,11 +1059,8 @@
     return pairs
 
 
-def unspread(turns):
-    return [
-        lax.ppermute(part, ("wide", "narrow"), [(b, a) for a, b in spread_perm(turn)])
-        for turn, part in enumerate(turns)
-    ]
+def unspread_turn(part, turn):
+    return lax.ppermute(part, ("wide", "narrow"), [(b, a) for a, b in spread_perm(turn)])
 
 
 def unspread_join(got, place):
@@ -1134,21 +1189,11 @@
         second_shift,
     )
     spare = up_bias.shape[0] // rows
-    if blocks == 4:
-        up_sorted = up_weight
-    else:
+    plane = blocks == 4
+    up_sorted = up_weight
+    if not plane:
         up_sorted = up_weight.reshape(rows, 4, chips // 4, 2, -1)
         up_sorted = jnp.swapaxes(up_sorted, 2, 3).reshape(rows, hidden)
-    in_keep, in_send, up_keep, up_send = pack(
-        info,
-        input_weight,
-        position_table,
-        jnp.stack(vectors),
-        up_bias.reshape(rows, spare),
-        up_sorted,
-        output_weight,
-        patches,
-    )
 
     def cross_one(piece):
         if blocks == 4:
@@ -1167,12 +1212,6 @@
             return [pieces[0]] + [swap(pieces[i], "wide", 2 * i) for i in range(1, chips)]
         return fold(pieces, bits)
 
-    def pair(keep, send):
-        return arrange(info, [keep, swap(send, "wide", 1)], 0, 0)
-
-    def narrow_pieces(piece):
-        return [piece] + [swap(piece, "narrow", k) for k in range(1, PLACES)]
-
     def place_axis(piece):
         return piece.reshape(piece.shape[:-4] + (PLACES,) + piece.shape[-2:])
 
@@ -1183,63 +1222,70 @@
         whole = outs[0].reshape((chips,) + shape)
         return [[pick(whole, index ^ chip)] for index in range(chips)]
 
-    in_pair = pair(in_keep, in_send)
-    up_pair = pair(up_keep, up_send)
-    in_piece = arrange(info, narrow_pieces(in_pair))
-    in_chips = direct(in_piece, chips) if blocks == 4 else along(in_piece, bits)
+    rows_in = jnp.concatenate([jnp.stack(vectors), up_bias.reshape(spare, rows)])
+    in_keep, in_send = pack_in(info, input_weight, position_table, rows_in)
+    in_far = swap(in_send, "wide", 1)
+    raw_parts = together(down_weight, output_weight, up_sorted, tokens, in_keep)
+    raw = jnp.concatenate(raw_parts[:2]) if plane else raw_parts[0]
+    up_keep, up_send = pack_up(info, raw_parts[2])
+    first, second = sent(info, raw_parts[3], positions, segments)
+    in_far, raw, up_send, first = together(in_far, raw, up_send, first)
+
+    in_pair = arrange(info, [in_keep, in_far], 0, 0)
+    in_got = [in_pair] + [swap(in_pair, "narrow", k) for k in range(1, PLACES)]
+    raw_far = swap(raw, "narrow", 2)
+    up_far = swap(up_send, "wide", 1)
+    up_far, raw_far, first, *in_got = together(up_far, raw_far, first, *in_got)
+
+    in_piece = arrange(info, in_got)
+    in_chips = direct(in_piece, chips) if plane else along(in_piece, bits)
+    raw_half = arrange(info, [raw, raw_far], 1)
+    raw_far = swap(raw_half, "narrow", 1)
+    low = lax.ppermute(first, ("wide", "narrow"), spread_perm(0))
+    up_pair = arrange(info, [up_keep, up_far], 0, 0)
+    low, raw_far, up_pair, second = together(low, raw_far, up_pair, second)
+
+    up_far = swap(up_pair, "narrow", 2)
+    high = lax.ppermute(second, ("wide", "narrow"), spread_perm(1))
+    if plane:
+        raw_far, *in_chips = together(settle(info, raw_half, raw_far), *in_chips)
+        down_chips = cross_one(raw_far)
+    else:
+        down_chips = along(place_axis(arrange(info, [raw_half, raw_far])), bits)
+    high, up_far = together(high, up_far)
+
+    up_half = arrange(info, [up_pair, up_far], 1)
+    up_far = swap(up_half, "narrow", 1)
+    low_far, high_far = swap(low, "wide", 1), swap(high, "wide", 1)
+    low_far, high_far, cotangent = together(low_far, high_far, cotangent)
+    token_blocks = [low, high, low_far, high_far]
+    cot_first, cot_second = pick_turns(info, cotangent)
+    cot_low = lax.ppermute(cot_first, ("wide", "narrow"), spread_perm(0))
     in_blocks = by_chip(in_chips)
-    plane = blocks == 4
-    first, second = sent(info, tokens, positions, segments)
-    down_half = arrange(info, [down_weight, swap(down_weight, "narrow", 2)], 1)
-    in_got = [in_pair] + [swap(in_pair, "narrow", k) for k in range(1, PLACES)]
-    down_got = swap(down_half, "narrow", 1)
-    in_piece, down_got, up_pair, first = together(arrange(info, in_got), down_got, up_pair, first)
-    in_chips = direct(in_piece, chips) if plane else along(in_piece, bits)
-    up_got = swap(up_pair, "narrow", 2)
-    low = lax.ppermute(first, ("wide", "narrow"), spread_perm(0))
-    down_piece = place_axis(arrange(info, [down_half, down_got]))
-    up_half = arrange(info, [up_pair, up_got], 1)
-    down_piece, second, up_half, low, *in_chips = together(
-        down_piece, second, up_half, low, *in_chips
-    )
-    up_got = swap(up_half, "narrow", 1)
-    in_blocks = by_chip(in_chips)
-    plane = blocks == 4
-    first, second = sent(info, tokens, positions, segments)
-    in_got = [in_pair] + [swap(in_pair, "narrow", k) for k in range(1, PLACES)]
-    down_half = [down_weight, swap(down_weight, "narrow", 2)]
-    in_piece, down_half, up_pair = together(
-        arrange(info, in_got), arrange(info, down_half, 1), up_pair
-    )
-    in_chips = direct(in_piece, chips) if plane else along(in_piece, bits)
-    up_got, down_got, first = together(
-        swap(up_pair, "narrow", 2), swap(down_half, "narrow", 1), first
-    )
-    low = lax.ppermute(first, ("wide", "narrow"), spread_perm(0))
-    up_half = arrange(info, [up_pair, up_got], 1)
-    up_got = swap(up_half, "narrow", 1)
-    down_piece = place_axis(arrange(info, [down_half, down_got]))
-    down_piece, second, *in_chips = together(down_piece, second, *in_chips)
-    in_blocks = by_chip(in_chips)
-    down_chips = cross_one(down_piece)
-    high = lax.ppermute(second, ("wide", "narrow"), spread_perm(1))
-    low, high, up_got, *down_chips = together(low, high, up_got, *down_chips)
-    token_blocks = [low, high, swap(low, "wide", 1), swap(high, "wide", 1)]
-    up_piece = place_axis(arrange(info, [up_half, up_got]))
-    up_chips = cross_one(up_piece)
-    down_chips = cross_two(down_chips)
     q, k, v, start, normed, small_full, turned, seg, spots = front(
         info, token_blocks, in_blocks, patches
     )
-    q, k, v, seg, cotangent, *down_chips = together(q, k, v, seg, cotangent, *down_chips)
-    cot_low, cot_high = (
-        lax.ppermute(block, ("wide", "narrow"), spread_perm(turn))
-        for turn, block in enumerate(pick_turns(info, cotangent))
-    )
+    q, k, v, seg, cot_second, up_far, *down_chips = together(
+        q, k, v, seg, cot_second, up_far, *down_chips
+    )
+
+    up_chips = cross_one(place_axis(arrange(info, [up_half, up_far])))
+    cot_high = lax.ppermute(cot_second, ("wide", "narrow"), spread_perm(1))
+    if plane:
+        down_chips = cross_two(down_chips)
     att, total = attend(info, q, k, v, seg)
-    att, cot_low, cot_high, *up_chips = together(att, cot_low, cot_high, *up_chips)
+    count = len(down_chips)
+    att, cot_low, cot_high, *rest = together(att, cot_low, cot_high, *down_chips, *up_chips)
+    down_chips, up_chips = rest[:count], rest[count:]
+
     att_far = swap(att, "wide", 1)
-    up_chips = cross_two(up_chips)
+    if plane:
+        out_rows = last_blocks(info, *down_chips[:3], down_chips[4])
+        out_weights = [out_rows, swap(out_rows, "wide", 1)]
+    else:
+        out_weights = [lax.all_gather(output_weight, ("wide", "narrow"), axis=0, tiled=True)]
+    if plane:
+        up_chips = cross_two(up_chips)
     cots = [cot_low, cot_high, swap(cot_low, "wide", 1), swap(cot_high, "wide", 1)]
     if plane:
         up_blocks = [part.reshape((-1,) + part.shape[-1:]) for part in up_chips]
@@ -1247,8 +1293,8 @@
     else:
         up_blocks = by_chip(up_chips)
         down_blocks = [by_chip(down_chips)[0].reshape(4 * PLACES, -1, width)]
-    middle, normed_two, up_bias_own = middle_front(
-        info, att, att_far, start, turned, up_blocks, patches, chips
+    middle, normed_two, up_bias_own, out_full = middle_front(
+        info, att, att_far, start, turned, out_weights, own_hidden, patches, chips
     )
     keep, send, slope, *down_grads = feed_front(
         info, normed_two, up_bias_own, cots, up_blocks, down_blocks, blocks
@@ -1267,7 +1313,7 @@
     down_keep, down_send = split(info, down_fold.parts, (2, 2, down_rows))
     down_got = swap(down_send, "narrow", 1)
     grad_middle, grad_att, out_keep, out_send, sums = middle_back(
-        info, back, back_far, middle, turned, att, cots, up_blocks, patches, blocks
+        info, back, back_far, middle, turned, att, out_full, cots, patches, blocks
     )
     if blocks == 1:
         shape = (chips // 2, 2, PLACES * rows, width)
@@ -1275,31 +1321,32 @@
         out_send = pick(out_send.reshape(shape), 1 - core, 1)
     grad_att, out_send, out_far, down_got = up_fold.second(grad_att, out_send, out_far, down_got)
     out_got = swap(out_send, "wide", 1)
-    out_turns = unspread(output_turns(info, middle, keep, out_far, turned, patches))
+    out_turns = output_turns(info, middle, keep, out_far, turned, patches)
+    out_turns = [unspread_turn(part, turn) for turn, part in enumerate(out_turns)]
     dq, dk, dv = attend_back(info, q, k, v, att, grad_att, total, seg)
     dq, dk, dv, out_got, normed, *out_turns = up_fold.last(
         dq, dk, dv, out_got, normed, *out_turns
     )
-    outputs = unspread_join(out_turns, place)
+    start_keep, start_send = project_back(info, dq, dk, dv, in_blocks, width)
+    start_far = swap(start_send, "wide", 1)
+    normed, start_keep = together(normed, start_keep)
+    in_grads = weight_grad(info, normed, [dq, dk, dv], blocks)
+    start_far, *in_grads = together(start_far, *in_grads)
+    in_sum = gather_sum(by_distance(in_grads, (2, PLACES, rows, 3 * part)))
     down_keep, down_send = split(info, [[down_keep, down_got]], (2, down_rows), 1)
+    up_keep, up_send = split(info, up_fold.parts, (2, 2, 2, rows))
+    start_far, down_send, up_send = together(start_far, down_send, up_send)
     down_got = swap(down_send, "narrow", 2)
-    up_keep, up_send = split(info, up_fold.parts, (2, 2, 2, rows))
     up_got = swap(up_send, "narrow", 1)
-    start_keep, start_send = project_back(info, dq, dk, dv, in_blocks, width)
-    start_send, down_got, up_got = together(start_send, down_got, up_got)
-    start_far = swap(start_send, "wide", 1)
+    args = [start_keep, start_far, start, grad_middle, turned, sums, bias_grad, spots, dq, dv]
+    started = start_back(info, blocks, args + [out_keep, out_got], patches, chips)
+    down_got, up_got, grad_blocks, *small_grads = together(down_got, up_got, *started)
     up_keep, up_send = split(info, [[up_keep, up_got]], (2, 2, rows), 1)
     up_got = swap(up_send, "narrow", 2)
-    in_grads = weight_grad(info, normed, [dq, dk, dv], blocks)
-    start_far, up_got, *in_grads = together(start_far, up_got, *in_grads)
-    in_sum = gather_sum(by_distance(in_grads, (2, PLACES, rows, 3 * part)))
-    args = [start_keep, start_far, start, grad_middle, turned, sums, bias_grad, spots, dq, dv]
-    started = start_back(info, blocks, args + [out_keep, out_got], patches, chips)
-    grad_blocks, *small_grads = started
-    grad_turns = unspread(pick_turns(info, grad_blocks.reshape(2, block, width)))
-    down_got, up_got, *rest = together(down_got, up_got, *grad_turns, *in_sum[1:], *small_grads)
-    grad_tokens = unspread_join(rest[:2], place)
-    in_sum, small_grads = [in_sum[0], *rest[2 : 1 + len(in_sum)]], rest[1 + len(in_sum) :]
+    grad_first, grad_second = pick_turns(info, grad_blocks.reshape(2, block, width))
+    grad_first = unspread_turn(grad_first, 0)
+    up_got, grad_second, *rest = together(up_got, grad_second, *in_sum[1:], *small_grads)
+    in_sum, small_grads = [in_sum[0], *rest[: len(in_sum) - 1]], rest[len(in_sum) - 1 :]
     if plane:
         small_sum = gather_sum(by_distance(small_grads, (2, PLACES, rows, SMALL + part)))
     else:
@@ -1312,13 +1359,19 @@
         small_grads = jnp.concatenate([small_grads[0], out_grad], axis=1)
         small_sum = gather_sum(by_distance([small_grads], (2, PLACES, rows, SMALL + part)))
 
-    def narrow_sum(parts):
-        cut = split(info, [parts], (2, PLACES, rows))
+    def narrow_sum(cut):
         whole = cut[0]
         for index in range(1, PLACES):
             whole = whole + swap(cut[index], "narrow", index).astype(f32)
         return whole
 
+    in_cut = split(info, [in_sum], (2, PLACES, rows))
+    down_keep, up_keep, grad_first, *rest = together(
+        down_keep, up_keep, grad_first, *out_turns, *in_cut
+    )
+    out_turns, in_cut = rest[:2], rest[2:]
+    outputs = unspread_join(out_turns, place)
+    grad_tokens = unspread_join([grad_first, unspread_turn(grad_second, 1)], place)
     down_share = down_keep + down_got.astype(f32)
     up_total = up_keep + up_got.astype(f32)
     up_keep = pick(up_total, core)
@@ -1327,8 +1380,8 @@
     up_share = jnp.where(
         first_core, jnp.concatenate(up_both, axis=2), jnp.concatenate(up_both[::-1], axis=2)
     ).reshape(rows, hidden)
-    in_total = narrow_sum(in_sum)
-    small_total = narrow_sum(small_sum)
+    in_total = narrow_sum(in_cut)
+    small_total = narrow_sum(split(info, [small_sum], (2, PLACES, rows)))
     in_keep = pick(in_total, core)
     in_got = swap(pick(in_total, 1 - core).astype(bf16), "wide", 1).astype(f32)
     small_far = swap(pick(small_total, 1 - core)[:, :SMALL].astype(bf16), "wide", 1)
@@ -1354,7 +1407,7 @@
         tail[GAIN_ONE],
         tail[SHIFT_ONE],
         up_share,
-        small_share[:, patches + 8 : patches + 8 + spare].reshape(-1),
+        small_share[:, patches + 8 : patches + 8 + spare].T.reshape(-1),
         down_share,
         tail[DOWN_BIAS],
         tail[GAIN_TWO],

time: 326 us -> 289 us (0.89)
  the two profiles are of different devices: /device:TPU:0 before, /device:TPU:9 now
where the time goes in v4:
time: 289 us; the launch traced here: 284 us
  Pallas kernels  104 us (36%)
  starting transfers between devices  81.8 us (28%)
  waiting for transfers between devices  78.7 us (27%)
  local copies, waits for them, and re-layouts  11.4 us (4%)
  other arithmetic  6.7 us (2%)
    pallas_call x35, Pallas kernels, call(): pl.pallas_call(loaded if loads else kernel, out_shape=[shape for shape, _...  104 us
    ppermute x61, waiting for transfers between devices, swap(): return lax.ppermute(values, axis, [(i, i ^ bits) for i in range(size)])  73.5 us
    ppermute x61, starting transfers between devices, swap(): return lax.ppermute(values, axis, [(i, i ^ bits) for i in range(size)])  59.1 us
    ppermute x4, starting transfers between devices, unspread_turn(): lax.ppermute(part, ('wide', 'narrow'), [(b, a) for a, b in spread_perm(tu...  14.5 us
    unnamed x34, local copies, waits for them, and re-layouts  5.8 us
  transfers between devices with their start and end apart: 69, of which 23 were waited for; matrix products, arithmetic and copies ran while one was open for 3% of the time, Pallas kernels for 29%

profile of v4, /device:TPU:9, one launch (start us, length us, event | category | flops | bytes accessed | tf_op | source)
XLA Modules:
  0.0 284.0 jit_solution(4694626126319937204)
XLA Ops:
  10.8 2.4 collective-permute-start.2
  14.0 2.5 collective-permute-start.5
  18.5 2.3 collective-permute-done.3.refs_1_
  20.9 8.5 %collective-permute-done.4.refs_2_ = bf16[2,24,1280]{2,1,0:T(8,128)(2,1)S(1)} collective-permute-done((bf16[2,24,1280]{2,1,0:T(8,128)(2,1)S(1)}, bf16[2,24,1280]{2,1,0:T(8,128)(2,1)S(1)}, u32[]{:S(2)}, u32[]{:S(2)}) %collective-permute-start.4) | collective-permute-done | bytes 122912 | tf_op jit(solution)/shard_map/ppermute | solution.py:1050
  29.4 2.6 collective-permute-done.5.refs_3_
  32.0 2.7 collective-permute-start.6
  35.3 2.9 %collective-permute-start.7 = (bf16[2,120,768]{2,1,0:T(8,128)(2,1)S(1)}, bf16[2,120,768]{2,1,0:T(8,128)(2,1)S(1)}, u32[]{:S(2)}, u32[]{:S(2)}) collective-permute-start(bf16[2,120,768]{2,1,0:T(8,128)(2,1)S(1)} %shard_map.301.own), channel_id=1, source_target_pairs={{0,1},{1,0},{2,3},{3,2},{4,5},{5,4},{6,7},{7,6},{8,9},{9,8},{10,11... | collective-permute-start | bytes 1105928 | tf_op jit(solution)/shard_map/ppermute | solution.py:1050
  42.1 10.0 %collective-permute-done.7.far = bf16[2,120,768]{2,1,0:T(8,128)(2,1)S(1)} collective-permute-done((bf16[2,120,768]{2,1,0:T(8,128)(2,1)S(1)}, bf16[2,120,768]{2,1,0:T(8,128)(2,1)S(1)}, u32[]{:S(2)}, u32[]{:S(2)}) %collective-permute-start.7) | collective-permute-done | bytes 368672 | tf_op jit(solution)/shard_map/ppermute | solution.py:1050
  52.8 7.4 %collective-permute-done.13 = bf16[2,4,24,1280]{3,2,1,0:T(8,128)(2,1)S(1)} collective-permute-done((bf16[2,4,24,1280]{3,2,1,0:T(8,128)(2,1)S(1)}, bf16[2,4,24,1280]{3,2,1,0:T(8,128)(2,1)S(1)}, u32[]{:S(2)}, u32[]{:S(2)}) %collective-permute-start.13) | collective-permute-done | bytes 491552 | tf_op jit(solution)/shard_map/ppermute | solution.py:1050
  62.1 5.6 %collective-permute-done.9.refs_1_ = bf16[2,24,1536]{2,1,0:T(8,128)(2,1)S(1)} collective-permute-done((bf16[2,24,1536]{2,1,0:T(8,128)(2,1)S(1)}, bf16[2,24,1536]{2,1,0:T(8,128)(2,1)S(1)}, u32[]{:S(2)}, u32[]{:S(2)}) %collective-permute-start.9) | collective-permute-done | bytes 147488 | tf_op jit(solution)/shard_map/ppermute | solution.py:1050
  68.5 3.2 %collective-permute-start.15 = (bf16[2,2,24,1536]{3,2,1,0:T(8,128)(2,1)S(1)}, bf16[2,2,24,1536]{3,2,1,0:T(8,128)(2,1)S(1)}, u32[]{:S(2)}, u32[]{:S(2)}) collective-permute-start(bf16[2,2,24,1536]{3,2,1,0:T(8,128)(2,1)S(1)} %shard_map.307.refs_0_), channel_id=1, source_target_pairs={{0,1},{1,0},{2,3},{3,2},{4,5},{5,4},{6,7},{7,6},{8,9},{9,8},{10,11... | collective-permute-start | bytes 884744 | tf_op jit(solution)/shard_map/ppermute | solution.py:1050
  72.4 7.4 %shard_map.305 = (bf16[1024,384]{1,0:T(8,128)(2,1)S(1)}, bf16[1024,384]{1,0:T(8,128)(2,1)S(1)}, bf16[1024,384]{1,0:T(8,128)(2,1)S(1)}, f32[1024,768]{1,0:T(8,128...) custom-call(s32[4]{0:T(128)S(1)} %pad_add_fusion.info, ...), custom_call_target="tpu_custom_call" | custom-call | flops 2013265920 | bytes 12582912 | tf_op jit(solution)/shard_map/pallas_call | solution.py:61
  84.1 1.4 collective-permute-start.19
  85.5 3.3 %collective-permute-done.20.refs_12_ = bf16[2,96,768]{2,1,0:T(8,128)(2,1)S(1)} collective-permute-done((bf16[2,96,768]{2,1,0:T(8,128)(2,1)S(1)}, bf16[2,96,768]{2,1,0:T(8,128)(2,1)S(1)}, u32[]{:S(2)}, u32[]{:S(2)}) %collective-permute-start.20) | collective-permute-done | bytes 294944 | tf_op jit(solution)/shard_map/ppermute | solution.py:1050
  88.8 4.1 %collective-permute-start.18 = (bf16[256,768]{1,0:T(8,128)(2,1)S(1)}, bf16[256,768]{1,0:T(8,128)(2,1)S(1)}, u32[]{:S(2)}, u32[]{:S(2)}) collective-permute-start(bf16[256,768]{1,0:T(8,128)(2,1)S(1)} %get-tuple-element.276), channel_id=1, source_target_pairs={{0,0},{1,1},{2,4},{3,5},{4,2},{5,3},{6,6},{7,7},{8,8},{9,9},{10,12... | collective-permute-start | bytes 1179656 | tf_op jit(solution)/shard_map/ppermute | solution.py:1263
  93.0 13.2 %shard_map.308 = (bf16[1024,384]{1,0:T(8,128)(2,1)S(1)}, f32[3,8,1024]{2,1,0:T(8,128)S(1)}) custom-call(s32[4]{0:T(128)S(1)} %pad_add_fusion.info, bf16[1024,384]{1,0:T(8,128)(2,1)S(1)} %get-tuple-element.271.q, bf16[1024,384]{1,0:T(8,128)(2,1)S(1)} %get-tuple-element.272.k, bf16[1024,384]{1,0:T(8,128)(2,1)S(1)} %get-tuple-element.273.v, ...), custom_call_target="tpu_custom_call" | custom-call | flops 2415919104 | bytes 4194304 | tf_op jit(solution)/shard_map/pallas_call | solution.py:61
  106.3 1.6 collective-permute-start.24
  112.2 4.1 %shard_map.312 = (f32[1024,768]{1,0:T(8,128)S(1)}, bf16[1024,768]{1,0:T(8,128)(2,1)S(1)}, f32[8,1536]{1,0:T(8,128)S(1)}, bf16[768,768]{1,0:T(8,128)(2,1)S(1)}) custom-call(s32[4]{0:T(128)S(1)} %pad_add_fusion.info, bf16[1024,384]{1,0:T(8,128)(2,1)S(1)} %get-tuple-element.284.att.o, bf16[1024,384]{1,0:T(8,128)(2,1)S(1)} %collective-permute-done.24.att_far, ...), custom_call_target="tpu_custom_call" | custom-call | flops 1207959552 | bytes 12582912 | tf_op jit(solution)/shard_map/pallas_call | solution.py:61
  116.4 1.5 collective-permute-done.28
  118.8 15.4 %shard_map.314 = (f32[512,768]{1,0:T(8,128)S(1)}, bf16[512,768]{1,0:T(8,128)(2,1)S(1)}, bf16[1024,1536]{1,0:T(8,128)(2,1)S(1)}, bf16[2,96,768]{2,1,0:T(8,128)(2,...) custom-call(s32[4]{0:T(128)S(1)} %pad_add_fusion.info, ...), custom_call_target="tpu_custom_call" | custom-call | flops 7247757312 | bytes 25165824 | tf_op jit(solution)/shard_map/pallas_call | solution.py:61
  134.2 1.3 collective-permute-start.30
  137.2 10.4 %shard_map.315 = (f32[1024,768]{1,0:T(8,128)S(1)}, bf16[1024,768]{1,0:T(8,128)(2,1)S(1)}, bf16[1024,1536]{1,0:T(8,128)(2,1)S(1)}, f32[8,1536]{1,0:T(8,128)S(1)}) custom-call(s32[4]{0:T(128)S(1)} %pad_add_fusion.info, bf16[1024,1536]{1,0:T(8,128)(2,1)S(1)} %get-tuple-element.302.slope, bf16[256,768]{1,0:T(8,128)(2,1)S(1)} %collective-permute-done.18.refs_0_, ...), custom_call_target="tpu_custom_call" | custom-call | flops 4831838208 | bytes 25165824 | tf_op jit(solution)/shard_map/pallas_call | solution.py:61
  148.4 3.1 %collective-permute-start.34 = (bf16[1024,768]{1,0:T(8,128)(2,1)S(1)}, bf16[1024,768]{1,0:T(8,128)(2,1)S(1)}, u32[]{:S(2)}, u32[]{:S(2)}) collective-permute-start(bf16[1024,768]{1,0:T(8,128)(2,1)S(1)} %get-tuple-element.313), channel_id=1, source_target_pairs={{0,4},{4,0},{8,12},{12,8},{16,20},{20,16},{24,28},{28,24},{1,5},{5... | collective-permute-start | bytes 4718600 | tf_op jit(solution)/shard_map/ppermute | solution.py:1050
  152.2 1.3 collective-permute-start.36
  154.7 4.6 %shard_map.316 = (bf16[96,1536]{1,0:T(8,128)(2,1)S(1)}, bf16[96,1536]{1,0:T(8,128)(2,1)S(1)}, bf16[96,1536]{1,0:T(8,128)(2,1)S(1)}, bf16[96,1536]{1,0:T(8,128)(2...) custom-call(s32[4]{0:T(128)S(1)} %pad_add_fusion.info, ...), custom_call_target="tpu_custom_call" | custom-call | flops 2415919104 | bytes 8388608 | tf_op jit(solution)/shard_map/pallas_call | solution.py:61
  165.9 6.1 %shard_map.319 = (f32[512,768]{1,0:T(8,128)S(1)}, bf16[1024,384]{1,0:T(8,128)(2,1)S(1)}, bf16[2,96,768]{2,1,0:T(8,128)(2,1)S(1)}, bf16[2,96,768]{2,1,0:T(8,128)(2,1)S(1)}, f32[8,768]{1,0:T(8,128)S(1)}) custom-call(s32[4]{0:T(128)S(1)} %pad_add_fusion.info, f32[1024,768]{1,0:T(8,128)S(1)} %get-tuple-element.336.back, ...), custom_call_target="tpu_custom_call" | custom-call | flops 1207959552 | bytes 14680064 | tf_op jit(solution)/shard_map/pallas_call | solution.py:61
  172.0 3.8 %collective-permute-done.40 = bf16[1,4,24,1536]{3,2,1,0:T(8,128)(2,1)S(1)} collective-permute-done((bf16[1,4,24,1536]{3,2,1,0:T(8,128)(2,1)S(1)}, bf16[1,4,24,1536]{3,2,1,0:T(8,128)(2,1)S(1)}, u32[]{:S(2)}, u32[]{:S(2)}) %collective-permute-start.40) | collective-permute-done | bytes 294944 | tf_op jit(solution)/shard_map/ppermute | solution.py:1050
  179.9 5.8 %collective-permute-start.44 = (bf16[256,768]{1,0:T(8,128)(2,1)S(1)}, bf16[256,768]{1,0:T(8,128)(2,1)S(1)}, u32[]{:S(2)}, u32[]{:S(2)}) collective-permute-start(bf16[256,768]{1,0:T(8,128)(2,1)S(1)} %get-tuple-element.361), channel_id=1, source_target_pairs={{0,0},{1,1},{4,2},{5,3},{2,4},{3,5},{6,6},{7,7},{8,8},{9,9},{12,10... | collective-permute-start | bytes 1179656 | tf_op jit(solution)/shard_map/ppermute | solution.py:1063
  185.9 13.0 %shard_map.321 = (bf16[1024,384]{1,0:T(8,128)(2,1)S(1)}, bf16[1024,384]{1,0:T(8,128)(2,1)S(1)}, bf16[1024,384]{1,0:T(8,128)(2,1)S(1)}) custom-call(s32[4]{0:T(128)S(1)} %pad_add_fusion.info, bf16[1024,384]{1,0:T(8,128)(2,1)S(1)} %get-tuple-element.271.q, bf16[1024,384]{1,0:T(8,128)(2,1)S(1)} %get-tuple-element.272.k, ...), custom_call_target="tpu_custom_call" | custom-call | flops 6039797760 | bytes 6291456 | tf_op jit(solution)/shard_map/pallas_call | solution.py:61
  198.9 4.8 %collective-permute-done.45 = bf16[256,768]{1,0:T(8,128)(2,1)S(1)} collective-permute-done((bf16[256,768]{1,0:T(8,128)(2,1)S(1)}, bf16[256,768]{1,0:T(8,128)(2,1)S(1)}, u32[]{:S(2)}, u32[]{:S(2)}) %collective-permute-start.45) | collective-permute-done | bytes 393248 | tf_op jit(solution)/shard_map/ppermute | solution.py:1063
  204.5 3.4 %shard_map.325 = (f32[512,768]{1,0:T(8,128)S(1)}, bf16[512,768]{1,0:T(8,128)(2,1)S(1)}) custom-call(s32[4]{0:T(128)S(1)} %pad_add_fusion.info, bf16[1024,384]{1,0:T(8,128)(2,1)S(1)} %get-tuple-element.374.refs_0_.refs_8_, bf16[1024,384]{1,0:T(8,128)(2,1)S(1)} %get-tuple-element.375.refs_1_, bf16[1024,384]{1,0:T(8,128)(2,1)S(1)} %get-tuple-element.376.refs_2_.refs_9_, ...), custom_call_target="tpu_custom_call" | custom-call | flops 1811939328 | bytes 8388608 | tf_op jit(solution)/shard_map/pallas_call | solution.py:61
  209.6 4.4 %shard_map.326 = (bf16[192,1152]{1,0:T(8,128)(2,1)S(1)}, bf16[192,1152]{1,0:T(8,128)(2,1)S(1)}, bf16[192,1152]{1,0:T(8,128)(2,1)S(1)}, bf16[192,1152]{1,0:T(8,128)(2,1)S(1)}) custom-call(s32[4]{0:T(128)S(1)} %pad_add_fusion.info, bf16[1024,768]{1,0:T(8,128)(2,1)S(1)} %get-tuple-element.380.left, bf16[1024,384]{1,0:T(8,128)(2,1)S(1)} %get-tuple-element.374.refs_0_.refs_8_, ...), custom_call_target="tpu_custom_call" | custom-call | flops 1811939328 | bytes 8388608 | tf_op jit(solution)/shard_map/pallas_call | solution.py:61
  215.5 1.3 collective-permute-start.55
  216.8 3.0 %collective-permute-start.49 = (bf16[96,768]{1,0:T(8,128)(2,1)S(1)}, bf16[96,768]{1,0:T(8,128)(2,1)S(1)}, u32[]{:S(2)}, u32[]{:S(2)}) collective-permute-start(bf16[96,768]{1,0:T(8,128)(2,1)S(1)} %get-tuple-element.388), channel_id=1, source_target_pairs={{0,2},{1,3},{2,0},{3,1},{4,6},{5,7},{6,4},{7,5},{8,10},{9,11},{10,... | collective-permute-start | bytes 442376 | tf_op jit(solution)/shard_map/ppermute | solution.py:1050
  219.8 4.7 %shard_map.327 = (bf16[512,768]{1,0:T(8,128)(2,1)S(1)}, bf16[192,512]{1,0:T(8,128)(2,1)S(1)}, bf16[192,512]{1,0:T(8,128)(2,1)S(1)}, bf16[192,512]{1,0:T(8,128)(2,1)S(1)}, bf16[192,512]{1,0:T(8,128)(2,1)S(1)}) custom-call(s32[4]{0:T(128)S(1)} %pad_add_fusion.info, f32[512,768]{1,0:T(8,128)S(1)} %get-tuple-element.390.refs_0_, ...), custom_call_target="tpu_custom_call" | custom-call | flops 100663296 | bytes 10485760 | tf_op jit(solution)/shard_map/pallas_call | solution.py:61
  224.5 2.9 %collective-permute-done.49 = bf16[96,768]{1,0:T(8,128)(2,1)S(1)} collective-permute-done((bf16[96,768]{1,0:T(8,128)(2,1)S(1)}, bf16[96,768]{1,0:T(8,128)(2,1)S(1)}, u32[]{:S(2)}, u32[]{:S(2)}) %collective-permute-start.49) | collective-permute-done | bytes 147488 | tf_op jit(solution)/shard_map/ppermute | solution.py:1050
  228.8 5.2 %collective-permute-start.51 = (bf16[256,768]{1,0:T(8,128)(2,1)S(1)}, bf16[256,768]{1,0:T(8,128)(2,1)}, u32[]{:S(2)}, u32[]{:S(2)}) collective-permute-start(bf16[256,768]{1,0:T(8,128)(2,1)S(1)} %get-tuple-element.406), channel_id=1, source_target_pairs={{0,0},{1,1},{4,2},{5,3},{2,4},{3,5},{6,6},{7,7},{8,8},{9,9},{12,10... | collective-permute-start | bytes 1179656 | tf_op jit(solution)/shard_map/ppermute | solution.py:1063
  234.0 4.9 %collective-permute-done.52 = bf16[2,24,1536]{2,1,0:T(8,128)(2,1)S(1)} collective-permute-done((bf16[2,24,1536]{2,1,0:T(8,128)(2,1)S(1)}, bf16[2,24,1536]{2,1,0:T(8,128)(2,1)S(1)}, u32[]{:S(2)}, u32[]{:S(2)}) %collective-permute-start.52) | collective-permute-done | bytes 147488 | tf_op jit(solution)/shard_map/ppermute | solution.py:1050
  240.4 1.3 collective-permute-start.59
  241.6 2.8 collective-permute-done.57
  244.5 5.1 %collective-permute-done.59 = bf16[2,4,24,512]{3,2,1,0:T(8,128)(2,1)S(1)} collective-permute-done((bf16[2,4,24,512]{3,2,1,0:T(8,128)(2,1)S(1)}, bf16[2,4,24,512]{3,2,1,0:T(8,128)(2,1)S(1)}, u32[]{:S(2)}, u32[]{:S(2)}) %collective-permute-start.59) | collective-permute-done | bytes 196640 | tf_op jit(solution)/shard_map/ppermute | solution.py:1050
  249.5 1.3 shard_map.331
  250.9 3.1 %collective-permute-start.61 = (bf16[2,24,512]{2,1,0:T(8,128)(2,1)}, bf16[2,24,512]{2,1,0:T(8,128)(2,1)}, u32[]{:S(2)}, u32[]{:S(2)}) collective-permute-start(bf16[2,24,512]{2,1,0:T(8,128)(2,1)} %get-tuple-element.436), channel_id=1, source_target_pairs={{0,2},{1,3},{2,0},{3,1},{4,6},{5,7},{6,4},{7,5},{8,10},{9,11},{10,... | collective-permute-start | bytes 147464 | tf_op jit(solution)/shard_map/ppermute | solution.py:1050
  254.3 3.4 %collective-permute-start.56 = (bf16[256,768]{1,0:T(8,128)(2,1)S(1)}, bf16[256,768]{1,0:T(8,128)(2,1)}, u32[]{:S(2)}, u32[]{:S(2)}) collective-permute-start(bf16[256,768]{1,0:T(8,128)(2,1)S(1)} %get-tuple-element.428), channel_id=1, source_target_pairs={{1,0},{0,1},{5,2},{4,3},{3,4},{2,5},{7,6},{6,7},{9,8},{8,9},{13,10... | collective-permute-start | bytes 1179656 | tf_op jit(solution)/shard_map/ppermute | solution.py:1063
  257.8 1.6 shard_map.330
  261.7 3.9 %collective-permute-start.64 = (bf16[2,24,1152]{2,1,0:T(8,128)(2,1)}, bf16[2,24,1152]{2,1,0:T(8,128)(2,1)S(1)}, u32[]{:S(2)}, u32[]{:S(2)}) collective-permute-start(bf16[2,24,1152]{2,1,0:T(8,128)(2,1)} %get-tuple-element.439), channel_id=1, source_target_pairs={{0,1},{1,0},{2,3},{3,2},{4,5},{5,4},{6,7},{7,6},{8,9},{9,8},{10,11... | collective-permute-start | bytes 331784 | tf_op jit(solution)/shard_map/ppermute | solution.py:1050
  267.4 1.3 collective-permute-start.66
  272.6 6.2 %collective-permute-done.66 = bf16[2,24,1152]{2,1,0:T(8,128)(2,1)S(1)} collective-permute-done((bf16[2,24,1152]{2,1,0:T(8,128)(2,1)}, bf16[2,24,1152]{2,1,0:T(8,128)(2,1)S(1)}, u32[]{:S(2)}, u32[]{:S(2)}) %collective-permute-start.66) | collective-permute-done | bytes 110624 | tf_op jit(solution)/shard_map/ppermute | solution.py:1050
  (194 shorter events, 66.1 us)
Async XLA Ops:
  10.8 21.2 %collective-permute-start.2 = (bf16[120,768]{1,0:T(8,128)(2,1)S(1)}, bf16[120,768]{1,0:T(8,128)(2,1)S(1)}, u32[]{:S(2)}, u32[]{:S(2)}) collective-permute-start(bf16[120,768]{1,0:T(8,128)(2,1)S(1)} %pad_maximum_fusion.2.refs_0_), channel_id=1, source_target_pairs={{0,2},{1,3},{2,0},{3,1},{4,6},{5,7},{6,4},{7,5},{8,10},{9,11},{10,... | collective-permute-start | bytes 552968 | tf_op jit(solution)/shard_map/ppermute | solution.py:1050
  14.0 15.4 %collective-permute-start.4 = (bf16[2,24,1280]{2,1,0:T(8,128)(2,1)S(1)}, bf16[2,24,1280]{2,1,0:T(8,128)(2,1)S(1)}, u32[]{:S(2)}, u32[]{:S(2)}) collective-permute-start(bf16[2,24,1280]{2,1,0:T(8,128)(2,1)S(1)} %shard_map.300.refs_0_), channel_id=1, source_target_pairs={{0,2},{1,3},{2,0},{3,1},{4,6},{5,7},{6,4},{7,5},{8,10},{9,11},{10,... | collective-permute-start | bytes 368648 | tf_op jit(solution)/shard_map/ppermute | solution.py:1050
  14.0 18.0 %collective-permute-start.5 = (bf16[2,24,1280]{2,1,0:T(8,128)(2,1)S(1)}, bf16[2,24,1280]{2,1,0:T(8,128)(2,1)S(1)}, u32[]{:S(2)}, u32[]{:S(2)}) collective-permute-start(bf16[2,24,1280]{2,1,0:T(8,128)(2,1)S(1)} %shard_map.300.refs_0_), channel_id=1, source_target_pairs={{0,3},{1,2},{2,1},{3,0},{4,7},{5,6},{6,5},{7,4},{8,11},{9,10},{10,... | collective-permute-start | bytes 368648 | tf_op jit(solution)/shard_map/ppermute | solution.py:1050
  32.0 20.1 %collective-permute-start.6 = (bf16[272,768]{1,0:T(8,128)(2,1)S(1)}, bf16[272,768]{1,0:T(8,128)(2,1)S(1)}, u32[]{:S(2)}, u32[]{:S(2)}) collective-permute-start(bf16[272,768]{1,0:T(8,128)(2,1)S(1)} %get-tuple-element.243), channel_id=1, source_target_pairs={{0,0},{1,1},{2,4},{3,5},{4,2},{5,3},{6,6},{7,7},{8,8},{9,9},{10,12... | collective-permute-start | bytes 1253384 | tf_op jit(solution)/shard_map/ppermute | solution.py:1244
  35.3 16.8 %collective-permute-start.7 = (bf16[2,120,768]{2,1,0:T(8,128)(2,1)S(1)}, bf16[2,120,768]{2,1,0:T(8,128)(2,1)S(1)}, u32[]{:S(2)}, u32[]{:S(2)}) collective-permute-start(bf16[2,120,768]{2,1,0:T(8,128)(2,1)S(1)} %shard_map.301.own), channel_id=1, source_target_pairs={{0,1},{1,0},{2,3},{3,2},{4,5},{5,4},{6,7},{7,6},{8,9},{9,8},{10,11... | collective-permute-start | bytes 1105928 | tf_op jit(solution)/shard_map/ppermute | solution.py:1050
  38.9 13.9 %collective-permute-start.12 = (bf16[2,4,24,1280]{3,2,1,0:T(8,128)(2,1)S(1)}, bf16[2,4,24,1280]{3,2,1,0:T(8,128)(2,1)S(1)}, u32[]{:S(2)}, u32[]{:S(2)}) collective-permute-start(bf16[2,4,24,1280]{3,2,1,0:T(8,128)(2,1)S(1)} %shard_map.304), channel_id=1, source_target_pairs={{0,8},{4,12},{8,0},{12,4},{16,24},{20,28},{24,16},{28,20},{1,9},{5... | collective-permute-start | bytes 1474568 | tf_op jit(solution)/shard_map/ppermute | solution.py:1050
  40.1 20.1 %collective-permute-start.13 = (bf16[2,4,24,1280]{3,2,1,0:T(8,128)(2,1)S(1)}, bf16[2,4,24,1280]{3,2,1,0:T(8,128)(2,1)S(1)}, u32[]{:S(2)}, u32[]{:S(2)}) collective-permute-start(bf16[2,4,24,1280]{3,2,1,0:T(8,128)(2,1)S(1)} %shard_map.304), channel_id=1, source_target_pairs={{0,16},{4,20},{8,24},{12,28},{16,0},{20,4},{24,8},{28,12},{1,17},{... | collective-permute-start | bytes 1474568 | tf_op jit(solution)/shard_map/ppermute | solution.py:1050
  41.4 18.8 %collective-permute-start.14 = (bf16[2,4,24,1280]{3,2,1,0:T(8,128)(2,1)S(1)}, bf16[2,4,24,1280]{3,2,1,0:T(8,128)(2,1)S(1)}, u32[]{:S(2)}, u32[]{:S(2)}) collective-permute-start(bf16[2,4,24,1280]{3,2,1,0:T(8,128)(2,1)S(1)} %shard_map.304), channel_id=1, source_target_pairs={{0,24},{4,28},{8,16},{12,20},{16,8},{20,12},{24,0},{28,4},{1,25},{... | collective-permute-start | bytes 1474568 | tf_op jit(solution)/shard_map/ppermute | solution.py:1050
  52.1 15.8 %collective-permute-start.8 = (bf16[272,768]{1,0:T(8,128)(2,1)S(1)}, bf16[272,768]{1,0:T(8,128)(2,1)S(1)}, u32[]{:S(2)}, u32[]{:S(2)}) collective-permute-start(bf16[272,768]{1,0:T(8,128)(2,1)S(1)} %get-tuple-element.249), channel_id=1, source_target_pairs={{0,1},{1,0},{2,5},{3,4},{4,3},{5,2},{6,7},{7,6},{8,9},{9,8},{10,13... | collective-permute-start | bytes 1253384 | tf_op jit(solution)/shard_map/ppermute | solution.py:1249
  52.1 15.5 %collective-permute-start.9 = (bf16[2,24,1536]{2,1,0:T(8,128)(2,1)S(1)}, bf16[2,24,1536]{2,1,0:T(8,128)(2,1)S(1)}, u32[]{:S(2)}, u32[]{:S(2)}) collective-permute-start(bf16[2,24,1536]{2,1,0:T(8,128)(2,1)S(1)} %shard_map.302.refs_0_), channel_id=1, source_target_pairs={{0,2},{1,3},{2,0},{3,1},{4,6},{5,7},{6,4},{7,5},{8,10},{9,11},{10,... | collective-permute-start | bytes 442376 | tf_op jit(solution)/shard_map/ppermute | solution.py:1050
  60.2 19.6 %collective-permute-start.16 = (bf16[5,96,768]{2,1,0:T(8,128)(2,1)S(1)}, bf16[5,96,768]{2,1,0:T(8,128)(2,1)S(1)}, u32[]{:S(2)}, u32[]{:S(2)}) collective-permute-start(bf16[5,96,768]{2,1,0:T(8,128)(2,1)S(1)} %shard_map.303.own.refs_9_), channel_id=1, source_target_pairs={{0,8},{4,12},{8,0},{12,4},{16,24},{20,28},{24,16},{28,20},{1,9},{5... | collective-permute-start | bytes 2211848 | tf_op jit(solution)/shard_map/ppermute | solution.py:1050
  61.0 18.9 %collective-permute-start.17 = (bf16[5,96,768]{2,1,0:T(8,128)(2,1)S(1)}, bf16[5,96,768]{2,1,0:T(8,128)(2,1)S(1)}, u32[]{:S(2)}, u32[]{:S(2)}) collective-permute-start(bf16[5,96,768]{2,1,0:T(8,128)(2,1)S(1)} %shard_map.303.own.refs_9_), channel_id=1, source_target_pairs={{0,16},{4,20},{8,24},{12,28},{16,0},{20,4},{24,8},{28,12},{1,17},{... | collective-permute-start | bytes 2211848 | tf_op jit(solution)/shard_map/ppermute | solution.py:1050
  62.1 9.7 %collective-permute-start.10 = (bf16[272,768]{1,0:T(8,128)(2,1)S(1)}, bf16[272,768]{1,0:T(8,128)(2,1)S(1)}, u32[]{:S(2)}, u32[]{:S(2)}) collective-permute-start(bf16[272,768]{1,0:T(8,128)(2,1)S(1)} %collective-permute-done.6.refs_0_), channel_id=1, source_target_pairs={{0,4},{4,0},{8,12},{12,8},{16,20},{20,16},{24,28},{28,24},{1,5},{5... | collective-permute-start | bytes 1253384 | tf_op jit(solution)/shard_map/ppermute | solution.py:1050
  68.5 11.3 %collective-permute-start.15 = (bf16[2,2,24,1536]{3,2,1,0:T(8,128)(2,1)S(1)}, bf16[2,2,24,1536]{3,2,1,0:T(8,128)(2,1)S(1)}, u32[]{:S(2)}, u32[]{:S(2)}) collective-permute-start(bf16[2,2,24,1536]{3,2,1,0:T(8,128)(2,1)S(1)} %shard_map.307.refs_0_), channel_id=1, source_target_pairs={{0,1},{1,0},{2,3},{3,2},{4,5},{5,4},{6,7},{7,6},{8,9},{9,8},{10,11... | collective-permute-start | bytes 884744 | tf_op jit(solution)/shard_map/ppermute | solution.py:1050
  82.3 23.9 %collective-permute-start.22 = (bf16[2,4,24,1536]{3,2,1,0:T(8,128)(2,1)S(1)}, bf16[2,4,24,1536]{3,2,1,0:T(8,128)(2,1)S(1)}, u32[]{:S(2)}, u32[]{:S(2)}) collective-permute-start(bf16[2,4,24,1536]{3,2,1,0:T(8,128)(2,1)S(1)} %bitcast.78), channel_id=1, source_target_pairs={{0,8},{4,12},{8,0},{12,4},{16,24},{20,28},{24,16},{28,20},{1,9},{5... | collective-permute-start | bytes 1769480 | tf_op jit(solution)/shard_map/ppermute | solution.py:1050
  82.6 23.6 %collective-permute-start.23 = (bf16[2,4,24,1536]{3,2,1,0:T(8,128)(2,1)S(1)}, bf16[2,4,24,1536]{3,2,1,0:T(8,128)(2,1)S(1)}, u32[]{:S(2)}, u32[]{:S(2)}) collective-permute-start(bf16[2,4,24,1536]{3,2,1,0:T(8,128)(2,1)S(1)} %bitcast.79), channel_id=1, source_target_pairs={{0,16},{4,20},{8,24},{12,28},{16,0},{20,4},{24,8},{28,12},{1,17},{... | collective-permute-start | bytes 1769480 | tf_op jit(solution)/shard_map/ppermute | solution.py:1050
  83.9 22.4 %collective-permute-start.21 = (bf16[3,96,768]{2,1,0:T(8,128)(2,1)S(1)}, bf16[3,96,768]{2,1,0:T(8,128)(2,1)S(1)}, u32[]{:S(2)}, u32[]{:S(2)}) collective-permute-start(bf16[3,96,768]{2,1,0:T(8,128)(2,1)S(1)} %get-tuple-element.282), channel_id=1, source_target_pairs={{0,16},{4,20},{8,24},{12,28},{16,0},{20,4},{24,8},{28,12},{1,17},{... | collective-permute-start | bytes 1327112 | tf_op jit(solution)/shard_map/ppermute | solution.py:1050
  84.1 22.1 %collective-permute-start.19 = (bf16[256,768]{1,0:T(8,128)(2,1)S(1)}, bf16[256,768]{1,0:T(8,128)(2,1)S(1)}, u32[]{:S(2)}, u32[]{:S(2)}) collective-permute-start(bf16[256,768]{1,0:T(8,128)(2,1)S(1)} %get-tuple-element.277), channel_id=1, source_target_pairs={{0,1},{1,0},{2,5},{3,4},{4,3},{5,2},{6,7},{7,6},{8,9},{9,8},{10,13... | collective-permute-start | bytes 1179656 | tf_op jit(solution)/shard_map/ppermute | solution.py:1273
  88.8 17.4 %collective-permute-start.18 = (bf16[256,768]{1,0:T(8,128)(2,1)S(1)}, bf16[256,768]{1,0:T(8,128)(2,1)S(1)}, u32[]{:S(2)}, u32[]{:S(2)}) collective-permute-start(bf16[256,768]{1,0:T(8,128)(2,1)S(1)} %get-tuple-element.276), channel_id=1, source_target_pairs={{0,0},{1,1},{2,4},{3,5},{4,2},{5,3},{6,6},{7,7},{8,8},{9,9},{10,12... | collective-permute-start | bytes 1179656 | tf_op jit(solution)/shard_map/ppermute | solution.py:1263
  108.5 10.3 %collective-permute-start.26 = (bf16[256,768]{1,0:T(8,128)(2,1)S(1)}, bf16[256,768]{1,0:T(8,128)(2,1)S(1)}, u32[]{:S(2)}, u32[]{:S(2)}) collective-permute-start(bf16[256,768]{1,0:T(8,128)(2,1)S(1)} %collective-permute-done.18.refs_0_), channel_id=1, source_target_pairs={{0,4},{4,0},{8,12},{12,8},{16,20},{20,16},{24,28},{28,24},{1,5},{5... | collective-permute-start | bytes 1179656 | tf_op jit(solution)/shard_map/ppermute | solution.py:1050
  109.0 9.8 %collective-permute-start.27 = (bf16[256,768]{1,0:T(8,128)(2,1)S(1)}, bf16[256,768]{1,0:T(8,128)(2,1)S(1)}, u32[]{:S(2)}, u32[]{:S(2)}) collective-permute-start(bf16[256,768]{1,0:T(8,128)(2,1)S(1)} %collective-permute-done.19.refs_1_), channel_id=1, source_target_pairs={{0,4},{4,0},{8,12},{12,8},{16,20},{20,16},{24,28},{28,24},{1,5},{5... | collective-permute-start | bytes 1179656 | tf_op jit(solution)/shard_map/ppermute | solution.py:1050
  134.2 13.4 %collective-permute-start.30 = (bf16[2,96,768]{2,1,0:T(8,128)(2,1)S(1)}, bf16[2,96,768]{2,1,0:T(8,128)(2,1)S(1)}, u32[]{:S(2)}, u32[]{:S(2)}) collective-permute-start(bf16[2,96,768]{2,1,0:T(8,128)(2,1)S(1)} %get-tuple-element.308), channel_id=1, source_target_pairs={{0,8},{4,12},{8,0},{12,4},{16,24},{20,28},{24,16},{28,20},{1,9},{5... | collective-permute-start | bytes 884744 | tf_op jit(solution)/shard_map/ppermute | solution.py:1050
  135.5 12.1 %collective-permute-start.31 = (bf16[2,96,768]{2,1,0:T(8,128)(2,1)S(1)}, bf16[2,96,768]{2,1,0:T(8,128)(2,1)S(1)}, u32[]{:S(2)}, u32[]{:S(2)}) collective-permute-start(bf16[2,96,768]{2,1,0:T(8,128)(2,1)S(1)} %get-tuple-element.309), channel_id=1, source_target_pairs={{0,8},{4,12},{8,0},{12,4},{16,24},{20,28},{24,16},{28,20},{1,9},{5... | collective-permute-start | bytes 884744 | tf_op jit(solution)/shard_map/ppermute | solution.py:1050
  135.7 11.9 %collective-permute-start.32 = (bf16[2,96,768]{2,1,0:T(8,128)(2,1)S(1)}, bf16[2,96,768]{2,1,0:T(8,128)(2,1)S(1)}, u32[]{:S(2)}, u32[]{:S(2)}) collective-permute-start(bf16[2,96,768]{2,1,0:T(8,128)(2,1)S(1)} %get-tuple-element.310), channel_id=1, source_target_pairs={{0,16},{4,20},{8,24},{12,28},{16,0},{20,4},{24,8},{28,12},{1,17},{... | collective-permute-start | bytes 884744 | tf_op jit(solution)/shard_map/ppermute | solution.py:1050
  137.0 11.4 %collective-permute-start.33 = (bf16[2,96,768]{2,1,0:T(8,128)(2,1)S(1)}, bf16[2,96,768]{2,1,0:T(8,128)(2,1)S(1)}, u32[]{:S(2)}, u32[]{:S(2)}) collective-permute-start(bf16[2,96,768]{2,1,0:T(8,128)(2,1)S(1)} %get-tuple-element.311), channel_id=1, source_target_pairs={{0,16},{4,20},{8,24},{12,28},{16,0},{20,4},{24,8},{28,12},{1,17},{... | collective-permute-start | bytes 884744 | tf_op jit(solution)/shard_map/ppermute | solution.py:1050
  148.4 12.8 %collective-permute-start.34 = (bf16[1024,768]{1,0:T(8,128)(2,1)S(1)}, bf16[1024,768]{1,0:T(8,128)(2,1)S(1)}, u32[]{:S(2)}, u32[]{:S(2)}) collective-permute-start(bf16[1024,768]{1,0:T(8,128)(2,1)S(1)} %get-tuple-element.313), channel_id=1, source_target_pairs={{0,4},{4,0},{8,12},{12,8},{16,20},{20,16},{24,28},{28,24},{1,5},{5... | collective-permute-start | bytes 4718600 | tf_op jit(solution)/shard_map/ppermute | solution.py:1050
  151.5 9.7 %collective-permute-start.35 = (bf16[512,768]{1,0:T(8,128)(2,1)S(1)}, bf16[512,768]{1,0:T(8,128)(2,1)S(1)}, u32[]{:S(2)}, u32[]{:S(2)}) collective-permute-start(bf16[512,768]{1,0:T(8,128)(2,1)S(1)} %get-tuple-element.314), channel_id=1, source_target_pairs={{0,4},{4,0},{8,12},{12,8},{16,20},{20,16},{24,28},{28,24},{1,5},{5... | collective-permute-start | bytes 2359304 | tf_op jit(solution)/shard_map/ppermute | solution.py:1050
  162.2 9.8 %collective-permute-start.38 = (bf16[2,96,768]{2,1,0:T(8,128)(2,1)S(1)}, bf16[2,96,768]{2,1,0:T(8,128)(2,1)S(1)}, u32[]{:S(2)}, u32[]{:S(2)}) collective-permute-start(bf16[2,96,768]{2,1,0:T(8,128)(2,1)S(1)} %get-tuple-element.343), channel_id=1, source_target_pairs={{0,1},{1,0},{2,3},{3,2},{4,5},{5,4},{6,7},{7,6},{8,9},{9,8},{10,11... | collective-permute-start | bytes 884744 | tf_op jit(solution)/shard_map/ppermute | solution.py:1050
  164.2 11.6 %collective-permute-start.40 = (bf16[1,4,24,1536]{3,2,1,0:T(8,128)(2,1)S(1)}, bf16[1,4,24,1536]{3,2,1,0:T(8,128)(2,1)S(1)}, u32[]{:S(2)}, u32[]{:S(2)}) collective-permute-start(bf16[1,4,24,1536]{3,2,1,0:T(8,128)(2,1)S(1)} %bitcast.121), channel_id=1, source_target_pairs={{0,8},{4,12},{8,0},{12,4},{16,24},{20,28},{24,16},{28,20},{1,9},{5... | collective-permute-start | bytes 884744 | tf_op jit(solution)/shard_map/ppermute | solution.py:1050
  164.4 11.4 %collective-permute-start.41 = (bf16[1,4,24,1536]{3,2,1,0:T(8,128)(2,1)S(1)}, bf16[1,4,24,1536]{3,2,1,0:T(8,128)(2,1)S(1)}, u32[]{:S(2)}, u32[]{:S(2)}) collective-permute-start(bf16[1,4,24,1536]{3,2,1,0:T(8,128)(2,1)S(1)} %bitcast.120), channel_id=1, source_target_pairs={{0,16},{4,20},{8,24},{12,28},{16,0},{20,4},{24,8},{28,12},{1,17},{... | collective-permute-start | bytes 884744 | tf_op jit(solution)/shard_map/ppermute | solution.py:1050
  164.8 12.0 %collective-permute-start.42 = (bf16[1,4,24,1536]{3,2,1,0:T(8,128)(2,1)S(1)}, bf16[1,4,24,1536]{3,2,1,0:T(8,128)(2,1)S(1)}, u32[]{:S(2)}, u32[]{:S(2)}) collective-permute-start(bf16[1,4,24,1536]{3,2,1,0:T(8,128)(2,1)S(1)} %bitcast.119), channel_id=1, source_target_pairs={{0,16},{4,20},{8,24},{12,28},{16,0},{20,4},{24,8},{28,12},{1,17},{... | collective-permute-start | bytes 884744 | tf_op jit(solution)/shard_map/ppermute | solution.py:1050
  177.4 21.5 %collective-permute-start.46 = (bf16[1,4,24,1536]{3,2,1,0:T(8,128)(2,1)S(1)}, bf16[1,4,24,1536]{3,2,1,0:T(8,128)(2,1)S(1)}, u32[]{:S(2)}, u32[]{:S(2)}) collective-permute-start(bf16[1,4,24,1536]{3,2,1,0:T(8,128)(2,1)S(1)} %get-tuple-element.367), channel_id=1, source_target_pairs={{0,16},{4,20},{8,24},{12,28},{16,0},{20,4},{24,8},{28,12},{1,17},{... | collective-permute-start | bytes 884744 | tf_op jit(solution)/shard_map/ppermute | solution.py:1050
  177.9 21.0 %collective-permute-start.47 = (bf16[1,4,24,1536]{3,2,1,0:T(8,128)(2,1)S(1)}, bf16[1,4,24,1536]{3,2,1,0:T(8,128)(2,1)S(1)}, u32[]{:S(2)}, u32[]{:S(2)}) collective-permute-start(bf16[1,4,24,1536]{3,2,1,0:T(8,128)(2,1)S(1)} %get-tuple-element.368), channel_id=1, source_target_pairs={{0,8},{4,12},{8,0},{12,4},{16,24},{20,28},{24,16},{28,20},{1,9},{5... | collective-permute-start | bytes 884744 | tf_op jit(solution)/shard_map/ppermute | solution.py:1050
  179.9 19.0 %collective-permute-start.44 = (bf16[256,768]{1,0:T(8,128)(2,1)S(1)}, bf16[256,768]{1,0:T(8,128)(2,1)S(1)}, u32[]{:S(2)}, u32[]{:S(2)}) collective-permute-start(bf16[256,768]{1,0:T(8,128)(2,1)S(1)} %get-tuple-element.361), channel_id=1, source_target_pairs={{0,0},{1,1},{4,2},{5,3},{2,4},{3,5},{6,6},{7,7},{8,8},{9,9},{12,10... | collective-permute-start | bytes 1179656 | tf_op jit(solution)/shard_map/ppermute | solution.py:1063
  185.7 18.0 %collective-permute-start.45 = (bf16[256,768]{1,0:T(8,128)(2,1)S(1)}, bf16[256,768]{1,0:T(8,128)(2,1)S(1)}, u32[]{:S(2)}, u32[]{:S(2)}) collective-permute-start(bf16[256,768]{1,0:T(8,128)(2,1)S(1)} %get-tuple-element.362), channel_id=1, source_target_pairs={{1,0},{0,1},{5,2},{4,3},{3,4},{2,5},{7,6},{6,7},{9,8},{8,9},{13,10... | collective-permute-start | bytes 1179656 | tf_op jit(solution)/shard_map/ppermute | solution.py:1063
  185.8 13.1 %collective-permute-start.43 = (bf16[2,96,768]{2,1,0:T(8,128)(2,1)S(1)}, bf16[2,96,768]{2,1,0:T(8,128)(2,1)S(1)}, u32[]{:S(2)}, u32[]{:S(2)}) collective-permute-start(bf16[2,96,768]{2,1,0:T(8,128)(2,1)S(1)} %get-tuple-element.357), channel_id=1, source_target_pairs={{0,4},{4,0},{8,12},{12,8},{16,20},{20,16},{24,28},{28,24},{1,5},{5... | collective-permute-start | bytes 884744 | tf_op jit(solution)/shard_map/ppermute | solution.py:1050
  214.0 13.5 %collective-permute-start.50 = (bf16[2,2,24,1536]{3,2,1,0:T(8,128)(2,1)S(1)}, bf16[2,2,24,1536]{3,2,1,0:T(8,128)(2,1)S(1)}, u32[]{:S(2)}, u32[]{:S(2)}) collective-permute-start(bf16[2,2,24,1536]{3,2,1,0:T(8,128)(2,1)S(1)} %get-tuple-element.389), channel_id=1, source_target_pairs={{0,1},{1,0},{2,3},{3,2},{4,5},{5,4},{6,7},{7,6},{8,9},{9,8},{10,11... | collective-permute-start | bytes 884744 | tf_op jit(solution)/shard_map/ppermute | solution.py:1050
  214.0 24.9 %collective-permute-start.53 = (bf16[2,4,24,1152]{3,2,1,0:T(8,128)(2,1)S(1)}, bf16[2,4,24,1152]{3,2,1,0:T(8,128)(2,1)S(1)}, u32[]{:S(2)}, u32[]{:S(2)}) collective-permute-start(bf16[2,4,24,1152]{3,2,1,0:T(8,128)(2,1)S(1)} %bitcast.118), channel_id=1, source_target_pairs={{0,8},{4,12},{8,0},{12,4},{16,24},{20,28},{24,16},{28,20},{1,9},{5... | collective-permute-start | bytes 1327112 | tf_op jit(solution)/shard_map/ppermute | solution.py:1050
  214.3 24.6 %collective-permute-start.54 = (bf16[2,4,24,1152]{3,2,1,0:T(8,128)(2,1)S(1)}, bf16[2,4,24,1152]{3,2,1,0:T(8,128)(2,1)S(1)}, u32[]{:S(2)}, u32[]{:S(2)}) collective-permute-start(bf16[2,4,24,1152]{3,2,1,0:T(8,128)(2,1)S(1)} %bitcast.117), channel_id=1, source_target_pairs={{0,16},{4,20},{8,24},{12,28},{16,0},{20,4},{24,8},{28,12},{1,17},{... | collective-permute-start | bytes 1327112 | tf_op jit(solution)/shard_map/ppermute | solution.py:1050
  215.5 23.5 %collective-permute-start.55 = (bf16[2,4,24,1152]{3,2,1,0:T(8,128)(2,1)S(1)}, bf16[2,4,24,1152]{3,2,1,0:T(8,128)(2,1)S(1)}, u32[]{:S(2)}, u32[]{:S(2)}) collective-permute-start(bf16[2,4,24,1152]{3,2,1,0:T(8,128)(2,1)S(1)} %bitcast.116), channel_id=1, source_target_pairs={{0,24},{4,28},{8,16},{12,20},{16,8},{20,12},{24,0},{28,4},{1,25},{... | collective-permute-start | bytes 1327112 | tf_op jit(solution)/shard_map/ppermute | solution.py:1050
  216.8 10.7 %collective-permute-start.49 = (bf16[96,768]{1,0:T(8,128)(2,1)S(1)}, bf16[96,768]{1,0:T(8,128)(2,1)S(1)}, u32[]{:S(2)}, u32[]{:S(2)}) collective-permute-start(bf16[96,768]{1,0:T(8,128)(2,1)S(1)} %get-tuple-element.388), channel_id=1, source_target_pairs={{0,2},{1,3},{2,0},{3,1},{4,6},{5,7},{6,4},{7,5},{8,10},{9,11},{10,... | collective-permute-start | bytes 442376 | tf_op jit(solution)/shard_map/ppermute | solution.py:1050
  228.1 10.8 %collective-permute-start.52 = (bf16[2,24,1536]{2,1,0:T(8,128)(2,1)S(1)}, bf16[2,24,1536]{2,1,0:T(8,128)(2,1)S(1)}, u32[]{:S(2)}, u32[]{:S(2)}) collective-permute-start(bf16[2,24,1536]{2,1,0:T(8,128)(2,1)S(1)} %get-tuple-element.410), channel_id=1, source_target_pairs={{0,2},{1,3},{2,0},{3,1},{4,6},{5,7},{6,4},{7,5},{8,10},{9,11},{10,... | collective-permute-start | bytes 442376 | tf_op jit(solution)/shard_map/ppermute | solution.py:1050
  228.8 30.6 %collective-permute-start.51 = (bf16[256,768]{1,0:T(8,128)(2,1)S(1)}, bf16[256,768]{1,0:T(8,128)(2,1)}, u32[]{:S(2)}, u32[]{:S(2)}) collective-permute-start(bf16[256,768]{1,0:T(8,128)(2,1)S(1)} %get-tuple-element.406), channel_id=1, source_target_pairs={{0,0},{1,1},{4,2},{5,3},{2,4},{3,5},{6,6},{7,7},{8,8},{9,9},{12,10... | collective-permute-start | bytes 1179656 | tf_op jit(solution)/shard_map/ppermute | solution.py:1063
  240.4 9.2 %collective-permute-start.59 = (bf16[2,4,24,512]{3,2,1,0:T(8,128)(2,1)S(1)}, bf16[2,4,24,512]{3,2,1,0:T(8,128)(2,1)S(1)}, u32[]{:S(2)}, u32[]{:S(2)}) collective-permute-start(bf16[2,4,24,512]{3,2,1,0:T(8,128)(2,1)S(1)} %bitcast.127), channel_id=1, source_target_pairs={{0,24},{4,28},{8,16},{12,20},{16,8},{20,12},{24,0},{28,4},{1,25},{... | collective-permute-start | bytes 589832 | tf_op jit(solution)/shard_map/ppermute | solution.py:1050
  254.3 25.1 %collective-permute-start.56 = (bf16[256,768]{1,0:T(8,128)(2,1)S(1)}, bf16[256,768]{1,0:T(8,128)(2,1)}, u32[]{:S(2)}, u32[]{:S(2)}) collective-permute-start(bf16[256,768]{1,0:T(8,128)(2,1)S(1)} %get-tuple-element.428), channel_id=1, source_target_pairs={{1,0},{0,1},{5,2},{4,3},{3,4},{2,5},{7,6},{6,7},{9,8},{8,9},{13,10... | collective-permute-start | bytes 1179656 | tf_op jit(solution)/shard_map/ppermute | solution.py:1063
  260.5 9.8 %collective-permute-start.68 = (bf16[24,1536]{1,0:T(8,128)(2,1)S(1)}, bf16[24,1536]{1,0:T(8,128)(2,1)S(1)}, u32[]{:S(2)}, u32[]{:S(2)}) collective-permute-start(bf16[24,1536]{1,0:T(8,128)(2,1)S(1)} %fusion), channel_id=1, source_target_pairs={{0,4},{4,0},{8,12},{12,8},{16,20},{20,16},{24,28},{28,24},{1,5},{5... | collective-permute-start | bytes 221192 | tf_op jit(solution)/shard_map/ppermute | solution.py:1050
  261.7 10.9 %collective-permute-start.64 = (bf16[2,24,1152]{2,1,0:T(8,128)(2,1)}, bf16[2,24,1152]{2,1,0:T(8,128)(2,1)S(1)}, u32[]{:S(2)}, u32[]{:S(2)}) collective-permute-start(bf16[2,24,1152]{2,1,0:T(8,128)(2,1)} %get-tuple-element.439), channel_id=1, source_target_pairs={{0,1},{1,0},{2,3},{3,2},{4,5},{5,4},{6,7},{7,6},{8,9},{9,8},{10,11... | collective-permute-start | bytes 331784 | tf_op jit(solution)/shard_map/ppermute | solution.py:1050
  267.4 11.4 %collective-permute-start.66 = (bf16[2,24,1152]{2,1,0:T(8,128)(2,1)}, bf16[2,24,1152]{2,1,0:T(8,128)(2,1)S(1)}, u32[]{:S(2)}, u32[]{:S(2)}) collective-permute-start(bf16[2,24,1152]{2,1,0:T(8,128)(2,1)} %copy-done.7), channel_id=1, source_target_pairs={{0,3},{1,2},{2,1},{3,0},{4,7},{5,6},{6,5},{7,4},{8,11},{9,10},{10,... | collective-permute-start | bytes 331784 | tf_op jit(solution)/shard_map/ppermute | solution.py:1050
  (38 other events, 271.6 us)

commit v5 on v4

--- a/solution.py
+++ b/solution.py
@@ -101,6 +101,34 @@
     )
 
 
+def fold_shapes(rows, rest):
+    return [shaped((count,) + rest, bf16) for count in (rows, rows, rows, rows // 2, rows // 2)]
+
+
+def fold_copies(held, outs, chip, sem):
+    rows = outs[0].shape[0]
+    half = rows // 2
+    at = lambda distance, second: pl.ds(
+        pl.multiple_of((distance ^ chip) * rows + second * half, half), half
+    )
+    whole = pl.ds(pl.multiple_of(chip * rows, rows), rows)
+    first, second = pl.ds(0, half), pl.ds(half, half)
+    own, to_x, to_y, y_left, x_left = outs
+    pairs = [
+        (0, held.at[whole], own),
+        (3, held.at[at(3, 0)], to_x.at[first]),
+        (1, held.at[at(1, 0)], to_x.at[second]),
+        (3, held.at[at(3, 1)], to_y.at[first]),
+        (2, held.at[at(2, 1)], to_y.at[second]),
+        (2, held.at[at(2, 0)], y_left),
+        (1, held.at[at(1, 1)], x_left),
+    ]
+    return [
+        (pltpu.make_async_copy(a, b, sem.at[i]), distance)
+        for i, (distance, a, b) in enumerate(pairs)
+    ]
+
+
 def run_copies(copies):
     for copy in copies:
         copy.start()
@@ -260,14 +288,25 @@
     return call(cut_kernel, outs, [LOAD] * 2, [info, x, y], limit=8, cost=(0, MIB))
 
 
-def add_kernel(info, a, b, c, d, first, second):
-    first[...] = (a[...].astype(f32) + b[...].astype(f32)).astype(bf16)
-    second[...] = (c[...].astype(f32) + d[...].astype(f32)).astype(bf16)
-
-
-def add_pairs(info, a, b, c, d):
-    out = (shaped(a.shape, bf16), vmem())
-    return call(add_kernel, [out] * 2, [LOAD] * 4, [info, a, b, c, d], limit=8, cost=(0, MIB))
+def add_kernel(info, *refs):
+    for i in range(0, len(refs), 3):
+        a, b, out = refs[i : i + 3]
+        out[...] = (a[...].astype(f32) + b[: out.shape[0]].astype(f32)).astype(bf16)
+
+
+def add_firsts(info, pairs):
+    def kernel(info, *refs):
+        outs = refs[2 * len(pairs) :]
+        add_kernel(info, *[ref for i, out in enumerate(outs) for ref in (*refs[2 * i : 2 * i + 2], out)])
+
+    return call(
+        kernel,
+        [(shaped(a.shape, bf16), vmem()) for a, _ in pairs],
+        [LOAD] * (2 * len(pairs)),
+        [info] + [array for pair in pairs for array in pair],
+        limit=8,
+        cost=(0, MIB),
+    )
 
 
 def pick_kernel(info, blocks, first, second):
@@ -307,23 +346,19 @@
 def front_kernel(blocks, patches, info, *refs):
     tokens_in, refs = refs[:4], refs[4:]
     weights_in, refs = refs[:blocks], refs[blocks:]
-    (q_out, k_out, v_out, start_out, normed_out, small_out, turned_out, seg_out, spot_out) = refs[:9]
-    held, weight, sem = refs[9:]
+    q_out, k_out, v_out, start_out, normed_out, weight, turned_out, seg_out, spot_out = refs[:9]
+    held, sem, weight_sem = refs[9:]
     core, chip, place = info[0], info[1], info[2]
     block, columns = held.shape[1] - 16, weight.shape[1] - SMALL
     part = columns // 3
-    rows = weight.shape[0] // blocks
     copies = []
     for i in range(4):
         side = core if i < 2 else 1 - core
         there = 2 * side + ((i % 2) ^ (place % 2))
         copies.append(pltpu.make_async_copy(tokens_in[i], held.at[there], sem.at[i]))
-    for r in range(blocks):
-        there = pl.ds(pl.multiple_of((r ^ chip) * rows, rows), rows)
-        copies.append(pltpu.make_async_copy(weights_in[r], weight.at[there], sem.at[4 + r]))
+    copies += piece_copies(weights_in, weight, info, weight_sem)
     run_copies(copies)
     small = weight[:, columns:]
-    small_out[...] = small
     turned_out[...] = small.astype(f32).T
     vector = lambda i: turned_out[patches + i : patches + i + 1, :]
     half = pl.ds(pl.multiple_of(core * part, 128), part)
@@ -369,7 +404,7 @@
             (shaped((rows, part), bf16), vmem()),
             (shaped((rows, width), f32), vmem()),
             (shaped((rows, width), bf16), vmem()),
-            (shaped((width, SMALL), bf16), vmem()),
+            (shaped((width, columns), bf16), vmem()),
             (shaped((SMALL, width), f32), vmem()),
             (shaped((8, rows), f32), vmem()),
             (shaped((8, rows), f32), vmem()),
@@ -378,8 +413,8 @@
         [info] + list(tokens) + list(weights),
         scratch=[
             pltpu.VMEM((4, block + 16, width), bf16),
-            pltpu.VMEM((width, columns), bf16),
-            pltpu.SemaphoreType.DMA((4 + blocks,)),
+            pltpu.SemaphoreType.DMA((4,)),
+            pltpu.SemaphoreType.DMA((blocks,)),
         ],
         cost=(2 * rows * width * columns, 12 * MIB),
     )
@@ -632,52 +667,55 @@
     cot_in, refs = refs[:4], refs[4:]
     up_in, refs = refs[:ups], refs[ups:]
     down_in, refs = refs[:downs], refs[downs:]
-    keep_out, send_out, slope_out, refs = refs[0], refs[1], refs[2], refs[3:]
-    cut = 2 if blocks == 4 else 1
-    down_grads, refs = refs[: cut * blocks], refs[cut * blocks :]
-    cot, up, down, out_sum, down_grad, cot_sem, up_sem, down_sem = refs
+    keep_out, send_out, slope_out, up, down, cot, refs = *refs[:6], refs[6:]
+    down_grads, (act, far_sum, down_grad, cot_sem, up_sem, down_sem) = refs[:-6], refs[-6:]
     core, chip = info[0], info[1]
     rows, width = normed.shape
     hidden = up.shape[1]
     chunk = hidden // 4
+    half = rows // 2
     early = piece_copies(up_in, up, info, up_sem)
-    late = cotangent_copies(info, cot_in, cot, [cot_sem.at[i] for i in range(4)])
-    late += block_copies(down_in, down, info, down_sem)
+    late = block_copies(down_in, down, info, down_sem)
+    late += cotangent_copies(info, cot_in, cot, [cot_sem.at[i] for i in range(4)])
     for copy in early + late:
         copy.start()
-    for copy in early + late:
+    for copy in early:
         copy.wait()
-    out_sum[...] = jnp.zeros_like(out_sum)
-
-    def one_chunk(q, carry):
+    own = pl.ds(pl.multiple_of(core * half, half), half)
+    far = pl.ds(pl.multiple_of((1 - core) * half, half), half)
+    outs, flat = [], None
+    for step, distance in enumerate((3, 1, 2, 0)):
+        q = distance ^ chip
         lanes = pl.ds(pl.multiple_of(q * chunk, 128), chunk)
-        down_part = down[pl.ds(q * PLACES, PLACES)].reshape(chunk, width)
         value, slope = gelu_parts(dot(normed[...], up[:, lanes]) + up_bias[0:1, lanes])
         value = value.astype(bf16)
+        act[...] = value
         slope_out[:, lanes] = slope.astype(bf16)
-        out_sum[...] += dot(value, down_part)
-        flat = cot[...].reshape(rows, width)
+        if step == 0:
+            for copy in late:
+                copy.wait()
+            flat = cot[...].reshape(rows, width)
+        blocks_here = pl.ds(pl.multiple_of(q * PLACES, PLACES), PLACES)
         grad = dot_left(value, flat).astype(bf16)
-        down_grad[pl.ds(q * PLACES, PLACES)] = grad.reshape(PLACES, chunk // PLACES, width)
-        return carry
-
-    lax.fori_loop(0, 4, one_chunk, 0)
-    outs = []
-    if blocks == 4:
-        for r in range(blocks):
-            for h in range(2):
-                there = pl.ds((r ^ chip) * PLACES + 2 * h, 2)
-                i = 2 * r + h
-                outs.append(pltpu.make_async_copy(down_grad.at[there], down_grads[i], down_sem.at[i]))
-    else:
+        down_grad[blocks_here] = grad.reshape(PLACES, chunk // PLACES, width)
+        if blocks == 4:
+            outs += [
+                copy
+                for copy, where in fold_copies(down_grad, down_grads, chip, down_sem)
+                if where == distance
+            ]
+            for copy in outs[-2 if distance else -1 :]:
+                copy.start()
+        down_part = down[blocks_here].reshape(chunk, width)
+        keep, send = dot(act[own, :], down_part), dot(act[far, :], down_part)
+        keep_out[...] = keep if step == 0 else keep_out[...] + keep
+        if step < 3:
+            far_sum[...] = send if step == 0 else far_sum[...] + send
+        else:
+            send_out[...] = (far_sum[...] + send).astype(bf16)
+    if blocks != 4:
         outs.append(pltpu.make_async_copy(down_grad, down_grads[0], down_sem.at[0]))
-    for copy in outs:
-        copy.start()
-    half = rows // 2
-    own = pl.ds(pl.multiple_of(core * half, half), half)
-    far = pl.ds(pl.multiple_of((1 - core) * half, half), half)
-    keep_out[...] = out_sum[own, :]
-    send_out[...] = out_sum[far, :].astype(bf16)
+        outs[0].start()
     for copy in outs:
         copy.wait()
 
@@ -686,93 +724,77 @@
     rows, width = normed.shape
     hidden = up_bias.shape[1]
     whole = (4 * PLACES, hidden // (4 * PLACES), width)
-    grads = [(2,) + whole[1:]] * 8 if blocks == 4 else [whole]
+    grads = fold_shapes(PLACES, whole[1:]) if blocks == 4 else [shaped(whole, bf16)]
     return call(
         functools.partial(feed_front_kernel, len(ups), len(downs), blocks),
         [
             (shaped((rows // 2, width), f32), vmem()),
             (shaped((rows // 2, width), bf16), vmem()),
             (shaped((rows, hidden), bf16), vmem()),
+            (shaped((width, hidden), bf16), vmem()),
+            (shaped(whole, bf16), vmem()),
+            (shaped((4, rows // 4, width), bf16), vmem()),
         ]
-        + [(shaped(one, bf16), anywhere()) for one in grads],
+        + [(one, anywhere()) for one in grads],
         [LOAD] * 2 + [HELD] * (4 + len(ups) + len(downs)),
         [info, normed, up_bias] + list(cots) + list(ups) + list(downs),
         scratch=[
-            pltpu.VMEM((4, rows // 4, width), bf16),
-            pltpu.VMEM((width, hidden), bf16),
-            pltpu.VMEM(whole, bf16),
-            pltpu.VMEM((rows, width), f32),
+            pltpu.VMEM((rows, hidden // 4), bf16),
+            pltpu.VMEM((rows // 2, width), f32),
             pltpu.VMEM(whole, bf16),
             pltpu.SemaphoreType.DMA((4,)),
             pltpu.SemaphoreType.DMA((len(ups),)),
             pltpu.SemaphoreType.DMA((8,)),
         ],
-        limit=20,
+        limit=14,
         cost=(6 * rows * width * hidden, 24 * MIB),
     )
 
 
-def feed_back_kernel(ups, downs, info, slope, *refs):
-    cot_in, refs = refs[:4], refs[4:]
-    up_in, refs = refs[:ups], refs[ups:]
-    down_in, refs = refs[:downs], refs[downs:]
-    back_out, low_out, grad_out, bias_out, cot, up, down, cot_sem, up_sem, down_sem = refs
+def feed_back_kernel(info, slope, cot, up, down, back_out, low_out, grad_out, bias_out):
     rows, hidden = slope.shape
     width = up.shape[0]
     chunk = hidden // 4
-    copies = cotangent_copies(info, cot_in, cot, [cot_sem.at[i] for i in range(4)])
-    copies += block_copies(down_in, down, info, down_sem)
-    copies += piece_copies(up_in, up, info, up_sem)
-    run_copies(copies)
-    back_out[...] = jnp.zeros_like(back_out)
-
-    def one_chunk(q, carry):
-        lanes = pl.ds(pl.multiple_of(q * chunk, 128), chunk)
-        down_part = down[pl.ds(q * PLACES, PLACES)].reshape(chunk, width)
-        flat = cot[...].reshape(rows, width)
+    flat = cot[...].reshape(rows, width)
+    for q in range(4):
+        lanes = slice(q * chunk, (q + 1) * chunk)
+        down_part = down[q * PLACES : (q + 1) * PLACES].reshape(chunk, width)
         grad = (dot_right(flat, down_part) * slope[:, lanes].astype(f32)).astype(bf16)
         grad_out[:, lanes] = grad
         bias_out[:, lanes] = jnp.broadcast_to(
             jnp.sum(grad.astype(f32), axis=0, keepdims=True), (8, chunk)
         )
-        back_out[...] += dot_right(grad, up[:, lanes])
-        return carry
-
-    lax.fori_loop(0, 4, one_chunk, 0)
-    low_out[...] = back_out[...].astype(bf16)
-
-
-def feed_back(info, slope, cots, ups, downs, width):
+        back = dot_right(grad, up[:, lanes])
+        if q == 0:
+            back_out[...] = back
+        elif q < 3:
+            back_out[...] += back
+        else:
+            back = back_out[...] + back
+            back_out[...] = back
+            low_out[...] = back.astype(bf16)
+
+
+def feed_back(info, slope, cot, up, down):
     rows, hidden = slope.shape
-    whole = (4 * PLACES, hidden // (4 * PLACES), width)
-    return call(
-        functools.partial(feed_back_kernel, len(ups), len(downs)),
+    width = up.shape[0]
+    return call(
+        feed_back_kernel,
         [
             (shaped((rows, width), f32), vmem()),
             (shaped((rows, width), bf16), vmem()),
             (shaped((rows, hidden), bf16), vmem()),
             (shaped((8, hidden), f32), vmem()),
         ],
-        [LOAD] + [HELD] * (4 + len(ups) + len(downs)),
-        [info, slope] + list(cots) + list(ups) + list(downs),
-        scratch=[
-            pltpu.VMEM((4, rows // 4, width), bf16),
-            pltpu.VMEM((width, hidden), bf16),
-            pltpu.VMEM(whole, bf16),
-            pltpu.SemaphoreType.DMA((4,)),
-            pltpu.SemaphoreType.DMA((len(ups),)),
-            pltpu.SemaphoreType.DMA((len(downs),)),
-        ],
-        limit=20,
+        [LOAD] * 4,
+        [info, slope, cot, up, down],
+        limit=10,
         cost=(4 * rows * width * hidden, 24 * MIB),
     )
 
 
-def weight_kernel(pieces, cut, count, info, left, *refs):
-    parts, outs = refs[:count], refs[count : count + pieces * cut]
-    held, sem = refs[count + pieces * cut :][:2]
-    chip = info[1]
-    width = left.shape[1]
+def weight_kernel(blocks, count, info, left, *refs):
+    parts, outs, held, sem = refs[:count], refs[count:-2], refs[-2], refs[-1]
     base = 0
     for ref in parts:
         for begin in range(0, ref.shape[1], 384):
@@ -780,38 +802,34 @@
             product = dot_left(left[...], ref[:, begin : begin + size]).astype(bf16)
             held[:, base : base + size] = product
             base += size
-    copies = []
-    rows = width // (pieces * cut)
-    for r in range(pieces):
-        for h in range(cut):
-            there = pl.ds(pl.multiple_of(((r ^ chip) * cut + h) * rows, rows), rows)
-            i = cut * r + h
-            copies.append(pltpu.make_async_copy(held.at[there], outs[i], sem.at[i]))
-    run_copies(copies)
-
-
-def weight_grad(info, left, parts, pieces, cut=1):
+    if blocks == 4:
+        run_copies([copy for copy, _ in fold_copies(held, outs, info[1], sem)])
+    else:
+        run_copies([pltpu.make_async_copy(held, outs[0], sem.at[0])])
+
+
+def weight_grad(info, left, parts, blocks):
     rows, width = left.shape
     columns = sum(part.shape[1] for part in parts)
-    count = pieces * cut
-    return call(
-        functools.partial(weight_kernel, pieces, cut, len(parts)),
-        [(shaped((width // count, columns), bf16), anywhere())] * count,
+    outs = [shaped((width, columns), bf16)]
+    if blocks == 4:
+        outs = fold_shapes(width // 4, (columns,))
+    return call(
+        functools.partial(weight_kernel, blocks, len(parts)),
+        [(one, anywhere()) for one in outs],
         [LOAD] * (1 + len(parts)),
         [info, left] + list(parts),
-        scratch=[pltpu.VMEM((width, columns), bf16), pltpu.SemaphoreType.DMA((count,))],
+        scratch=[pltpu.VMEM((width, columns), bf16), pltpu.SemaphoreType.DMA((8,))],
         cost=(2 * rows * width * columns, 8 * MIB),
     )
 
 
-def middle_back_kernel(blocks, patches, info, back, back_far, middle, turned, att, weight, *refs):
-    cot_in, refs = refs[:4], refs[4:]
-    grad_out, attended_out, keep_out, send_out, sums_out, cot, branch, sem = refs
+def middle_back_kernel(blocks, patches, info, back, back_far, middle, turned, att, weight, cot, *refs):
+    grad_out, attended_out, keep_out, send_out, sums_out, branch = refs
     core = info[0]
     rows, width = middle.shape
     tile = rows // 4
     part = width // 2
-    run_copies(cotangent_copies(info, cot_in, cot, [sem.at[i] for i in range(4)]))
     gain = turned[patches + GAIN_TWO : patches + GAIN_TWO + 1, :]
     own_rows = pl.ds(pl.multiple_of(core * part, 128), part)
     for t in range(4):
@@ -855,7 +873,7 @@
         send_out[...] = weight_grad
 
 
-def middle_back(info, back, back_far, middle, turned, att, weight, cots, patches, blocks):
+def middle_back(info, back, back_far, middle, turned, att, weight, cot, patches, blocks):
     rows, width = middle.shape
     part = width // 2
     slab = (2, part // 4, width) if blocks == 4 else (part, width)
@@ -868,63 +886,41 @@
             (shaped(slab, bf16), vmem()),
             (shaped((8, width), f32), vmem()),
         ],
-        [LOAD] * 6 + [HELD] * 4,
-        [info, back, back_far, middle, turned, att, weight] + list(cots),
-        scratch=[
-            pltpu.VMEM((4, rows // 4, width), bf16),
-            pltpu.VMEM((rows, width), bf16),
-            pltpu.SemaphoreType.DMA((4,)),
-        ],
+        [LOAD] * 7,
+        [info, back, back_far, middle, turned, att, weight, cot],
+        scratch=[pltpu.VMEM((rows, width), bf16)],
         cost=(4 * rows * width * part, 14 * MIB),
     )
 
 
-def project_kernel(blocks, info, *refs):
-    dq, dk, dv, refs = refs[0], refs[1], refs[2], refs[3:]
-    weights_in, refs = refs[:blocks], refs[blocks:]
-    keep_out, send_out, weight, sem = refs
-    core, chip = info[0], info[1]
+def project_kernel(info, dq, dk, dv, weight, keep_out, send_out):
+    core = info[0]
     rows, part = dq.shape
-    width = weight.shape[0]
-    up_rows = width // blocks
     half_rows = rows // 2
-    copies = []
-    for r in range(blocks):
-        there = pl.ds(pl.multiple_of((r ^ chip) * up_rows, up_rows), up_rows)
-        copies.append(
-            pltpu.make_async_copy(
-                weights_in[r].at[:, : 3 * part], weight.at[there], sem.at[r]
-            )
-        )
-    run_copies(copies)
 
     def product(first):
         here = pl.ds(pl.multiple_of(first, 128), half_rows)
         return (
             dot_right(dq[here, :], weight[:, :part])
             + dot_right(dk[here, :], weight[:, part : 2 * part])
-            + dot_right(dv[here, :], weight[:, 2 * part :])
+            + dot_right(dv[here, :], weight[:, 2 * part : 3 * part])
         )
 
     send_out[...] = product((1 - core) * half_rows).astype(bf16)
     keep_out[...] = product(core * half_rows)
 
 
-def project_back(info, dq, dk, dv, weights, width):
-    blocks = len(weights)
+def project_back(info, dq, dk, dv, weight):
     rows, part = dq.shape
-    return call(
-        functools.partial(project_kernel, blocks),
+    width = weight.shape[0]
+    return call(
+        project_kernel,
         [
             (shaped((rows // 2, width), f32), vmem()),
             (shaped((rows // 2, width), bf16), vmem()),
         ],
-        [LOAD] * 3 + [HELD] * blocks,
-        [info, dq, dk, dv] + list(weights),
-        scratch=[
-            pltpu.VMEM((width, 3 * part), bf16),
-            pltpu.SemaphoreType.DMA((blocks,)),
-        ],
+        [LOAD] * 4,
+        [info, dq, dk, dv, weight],
         cost=(6 * rows * width * part, 8 * MIB),
     )
 
@@ -933,7 +929,7 @@
     (keep, far, start, grad_middle, turned, sums, bias_grad, spots, dq, dv, out_keep, out_got) = refs[:12]
     refs = refs[12:]
     low_out, refs = refs[0], refs[1:]
-    grads, refs = refs[:blocks], refs[blocks:]
+    grads, refs = refs[:-3], refs[-3:]
     held, rows_held, sem = refs
     core, chip = info[0], info[1]
     rows, part = dq.shape
@@ -983,64 +979,84 @@
                 begin = pl.multiple_of((2 * side + x) * up_rows, up_rows)
                 held[pl.ds(begin, slab), SMALL:] = ref[x, :, : width // 2]
                 held[pl.ds(begin + slab, slab), SMALL:] = ref[x, :, width // 2 :]
-    copies = []
-    for r in range(blocks):
-        there = pl.ds(pl.multiple_of((r ^ chip) * up_rows, up_rows), up_rows)
-        copies.append(pltpu.make_async_copy(held.at[there], grads[r], sem.at[r]))
-    run_copies(copies)
+    if blocks == 4:
+        run_copies([copy for copy, _ in fold_copies(held, grads, chip, sem)])
+    else:
+        run_copies([pltpu.make_async_copy(held, grads[0], sem.at[0])])
 
 
 def start_back(info, blocks, args, patches, chips):
     half_rows, width = args[0].shape
     columns = SMALL + width // 2 if blocks == 4 else SMALL
+    outs = [shaped((width, columns), bf16)]
+    if blocks == 4:
+        outs = fold_shapes(width // 4, (columns,))
     return call(
         functools.partial(start_kernel, blocks, patches, chips),
         [(shaped((half_rows, width), bf16), vmem())]
-        + [(shaped((width // blocks, columns), bf16), anywhere())] * blocks,
+        + [(one, anywhere()) for one in outs],
         [LOAD] * len(args),
         [info] + list(args),
         scratch=[
             pltpu.VMEM((width, columns), bf16),
             pltpu.VMEM((SMALL, width), f32),
-            pltpu.SemaphoreType.DMA((blocks,)),
+            pltpu.SemaphoreType.DMA((8,)),
         ],
         cost=(2 * half_rows * width * SMALL, 10 * MIB),
     )
 
 
-def split_kernel(terms, parts, shift, count, info, *refs):
+def split_kernel(plan, count, shift, info, *refs):
     place = lax.rem(info[2] >> shift, count)
-    outs, held = refs[terms * parts : terms * parts + count], refs[terms * parts + count]
-    totals = []
-    for part in range(parts):
-        total = refs[part * terms][...].astype(f32)
-        for ref in refs[part * terms + 1 : (part + 1) * terms]:
-            total = total + ref[...].astype(f32)
-        totals.append(total)
-    held[...] = (totals[0] if parts == 1 else jnp.concatenate(totals)).reshape(held.shape)
+    inputs, held = refs[: -1 - count], refs[-1]
+    outs = refs[-1 - count : -1]
+    column = 0
+    for parts in plan:
+        totals = []
+        for terms in parts:
+            total = 0.0
+            for index, begin, rows in terms:
+                total = total + inputs[index][begin : begin + rows, :].astype(f32)
+            totals.append(total)
+        whole = totals[0] if len(totals) == 1 else jnp.concatenate(totals)
+        lanes = whole.shape[-1]
+        held[..., column : column + lanes] = whole.reshape(held.shape[:-1] + (lanes,))
+        column += lanes
     lead = (slice(None),) * (len(held.shape) - 3)
     for k in range(count):
         outs[k][...] = held[lead + (k ^ place,)].astype(outs[k].dtype)
 
 
-def split(info, parts, shape, shift=0):
-    columns = parts[0][0].shape[-1]
-    count = shape[-2]
-    outs = [
-        (shaped(shape[:-2] + (shape[-1], columns), f32 if k == 0 else bf16), vmem())
-        for k in range(count)
-    ]
-    arrays = [array.reshape(-1, columns) for part in parts for array in part]
-    total = 1
-    for extent in shape + (columns,):
+def split(info, groups, shape, shift=0):
+    arrays, plan, columns = [], [], 0
+    for group in groups:
+        base = len(arrays)
+        parts = group.parts if isinstance(group, Fold) else [[(i, 0, None) for i in range(len(group))]]
+        terms = group.terms if isinstance(group, Fold) else group
+        flat = [array.reshape((-1,) + array.shape[-1:]) for array in terms]
+        half = flat[0].shape[0] // 2
+        plan.append(
+            [
+                [
+                    (base + i, 0, flat[i].shape[0]) if begin is None else (base + i, begin * half, half)
+                    for i, begin, _ in [(i, None if size is None else begin, size) for i, begin, size in part]
+                ]
+                for part in parts
+            ]
+        )
+        arrays += flat
+        columns += flat[0].shape[-1]
+    count, total = shape[-2], columns
+    for extent in shape:
         total *= extent
-    return call(
-        functools.partial(split_kernel, len(parts[0]), len(parts), shift, count),
-        outs,
+    one = shape[:-2] + (shape[-1], columns)
+    return call(
+        functools.partial(split_kernel, plan, count, shift),
+        [(shaped(one, f32 if k == 0 else bf16), vmem()) for k in range(count)],
         [LOAD] * len(arrays),
         [info] + arrays,
         scratch=[pltpu.VMEM(shape + (columns,), f32)],
-        limit=16,
+        limit=20,
         cost=(0, 8 * total),
     )
 
@@ -1099,31 +1115,24 @@
 
 
 class Fold:
-    def __init__(self, info, pieces, bits):
-        self.info, self.pieces, self.bits = info, pieces, bits
-        if len(pieces[0]) == 2:
-            own, x, y, d = pieces
-            self.near = [swap(d[0], "wide", 2), swap(x[0], "wide", 2), swap(d[1], "wide", 4), swap(y[1], "wide", 4)]
-
-    def second(self, *values):
-        if len(self.pieces[0]) == 2:
-            own, x, y, d = self.pieces
-            count = len(values)
-            values = together(*values, *self.near)
-            values, self.near = values[:count], values[count:]
-            first, second = add_pairs(self.info, y[0], self.near[0], x[1], self.near[2])
-            self.far = [swap(first, "wide", 4), swap(second, "wide", 2)]
-        return values
-
-    def last(self, *values):
-        if len(self.pieces[0]) == 1:
-            self.parts = [fold([piece[0] for piece in self.pieces], self.bits)]
-            return values
-        count = len(values)
-        *values, one, two = together(*values, *self.far)
-        own = self.pieces[0]
-        self.parts = [[own[0], self.near[1], one], [own[1], self.near[3], two]]
-        return values
+    def __init__(self, outs, bits):
+        self.outs, self.bits = list(outs), bits
+        self.plane = len(outs) == 5
+        if self.plane:
+            self.near = [swap(outs[1], "wide", 2), swap(outs[2], "wide", 4)]
+
+    def pairs(self):
+        return [(self.outs[3], self.near[0]), (self.outs[4], self.near[1])] if self.plane else []
+
+    def cross(self, sums):
+        if self.plane:
+            self.far = [swap(sums[0], "wide", 4), swap(sums[1], "wide", 2)]
+            self.terms = [self.outs[0], *self.near, *self.far]
+            first = [(0, 0, 1), (1, 1, 1), (3, 0, 1)]
+            self.parts = [first, [(0, 1, 1), (2, 1, 1), (4, 0, 1)]]
+        else:
+            self.terms = fold(self.outs, self.bits)
+            self.parts = [[(i, 0, None) for i in range(len(self.terms))]]
 
 
 def local(
@@ -1207,20 +1216,39 @@
             return [own, x, y, swap(first, "wide", 2), swap(second, "wide", 4)]
         return pieces
 
-    def gather_sum(pieces):
-        if blocks == 4:
-            return [pieces[0]] + [swap(pieces[i], "wide", 2 * i) for i in range(1, chips)]
-        return fold(pieces, bits)
-
     def place_axis(piece):
         return piece.reshape(piece.shape[:-4] + (PLACES,) + piece.shape[-2:])
 
-    def halves(outs, shape):
-        if blocks == 4:
-            shape = (shape[0] // 2,) + shape[1:]
-            return [[out.reshape(shape) for out in outs[2 * r : 2 * r + 2]] for r in range(4)]
+    def folded(outs, shape):
+        if plane:
+            return Fold(outs, bits)
         whole = outs[0].reshape((chips,) + shape)
-        return [[pick(whole, index ^ chip)] for index in range(chips)]
+        return Fold([pick(whole, index ^ chip) for index in range(chips)], bits)
+
+    def crossed(folds, *values):
+        count = len(values)
+        near = [array for one in folds if one.plane for array in one.near]
+        values = together(*values, *near)
+        values, near = values[:count], list(values[count:])
+        if plane:
+            for one in folds:
+                one.near, near = near[:2], near[2:]
+            sums = add_firsts(info, [pair for one in folds for pair in one.pairs()])
+        for i, one in enumerate(folds):
+            one.cross(sums[2 * i : 2 * i + 2] if plane else None)
+        return values
+
+    def arrived(folds, *values):
+        if not plane:
+            return values
+        count = len(values)
+        far = [array for one in folds for array in one.far]
+        values = together(*values, *far)
+        values, far = values[:count], list(values[count:])
+        for one in folds:
+            one.far, far = far[:2], far[2:]
+            one.terms = [*one.terms[:3], *one.far]
+        return values
 
     rows_in = jnp.concatenate([jnp.stack(vectors), up_bias.reshape(spare, rows)])
     in_keep, in_send = pack_in(info, input_weight, position_table, rows_in)
@@ -1229,7 +1257,7 @@
     raw = jnp.concatenate(raw_parts[:2]) if plane else raw_parts[0]
     up_keep, up_send = pack_up(info, raw_parts[2])
     first, second = sent(info, raw_parts[3], positions, segments)
-    in_far, raw, up_send, first = together(in_far, raw, up_send, first)
+    in_far, raw, up_send = together(in_far, raw, up_send)
 
     in_pair = arrange(info, [in_keep, in_far], 0, 0)
     in_got = [in_pair] + [swap(in_pair, "narrow", k) for k in range(1, PLACES)]
@@ -1262,7 +1290,7 @@
     cot_first, cot_second = pick_turns(info, cotangent)
     cot_low = lax.ppermute(cot_first, ("wide", "narrow"), spread_perm(0))
     in_blocks = by_chip(in_chips)
-    q, k, v, start, normed, small_full, turned, seg, spots = front(
+    q, k, v, start, normed, in_full, turned, seg, spots = front(
         info, token_blocks, in_blocks, patches
     )
     q, k, v, seg, cot_second, up_far, *down_chips = together(
@@ -1296,82 +1324,76 @@
     middle, normed_two, up_bias_own, out_full = middle_front(
         info, att, att_far, start, turned, out_weights, own_hidden, patches, chips
     )
-    keep, send, slope, *down_grads = feed_front(
+    keep, send, slope, up_full, down_full, cot, *down_grads = feed_front(
         info, normed_two, up_bias_own, cots, up_blocks, down_blocks, blocks
     )
     down_rows = own_hidden // (chips * PLACES)
-    down_fold = Fold(info, halves(down_grads, (PLACES, down_rows, width)), bits)
-    fed = feed_back(info, slope, cots, up_blocks, down_blocks, width)
-    back, back_low, grad_hidden, bias_grad, send, normed_two = down_fold.second(
-        *fed, send, normed_two
+    down_fold = folded(down_grads, (PLACES, down_rows, width))
+    fed = feed_back(info, slope, cot, up_full, down_full)
+    back, back_low, grad_hidden, bias_grad, send, normed_two = crossed(
+        [down_fold], *fed, send, normed_two
     )
     back_far = swap(back_low, "wide", 1)
     out_far = swap(send, "wide", 1)
-    up_grads = weight_grad(info, normed_two, [grad_hidden], blocks, 2 if plane else 1)
-    back_far, out_far, *up_grads = down_fold.last(back_far, out_far, *up_grads)
-    up_fold = Fold(info, halves(up_grads, (2, PLACES, rows, own_hidden)), bits)
-    down_keep, down_send = split(info, down_fold.parts, (2, 2, down_rows))
+    up_grads = weight_grad(info, normed_two, [grad_hidden], blocks)
+    back_far, out_far, *up_grads = arrived([down_fold], back_far, out_far, *up_grads)
+    up_fold = folded(up_grads, (2, PLACES, rows, own_hidden))
+    down_keep, down_send = split(info, [down_fold], (2, 2, down_rows))
     down_got = swap(down_send, "narrow", 1)
     grad_middle, grad_att, out_keep, out_send, sums = middle_back(
-        info, back, back_far, middle, turned, att, out_full, cots, patches, blocks
-    )
+        info, back, back_far, middle, turned, att, out_full, cot, patches, blocks
+    )
+    out_far, grad_att = together(out_far, grad_att)
+    out_turns = output_turns(info, middle, keep, out_far, turned, patches)
+    out_turns = [unspread_turn(part, turn) for turn, part in enumerate(out_turns)]
     if blocks == 1:
         shape = (chips // 2, 2, PLACES * rows, width)
         out_keep = pick(out_keep.reshape(shape), core, 1)
         out_send = pick(out_send.reshape(shape), 1 - core, 1)
-    grad_att, out_send, out_far, down_got = up_fold.second(grad_att, out_send, out_far, down_got)
-    out_got = swap(out_send, "wide", 1)
-    out_turns = output_turns(info, middle, keep, out_far, turned, patches)
-    out_turns = [unspread_turn(part, turn) for turn, part in enumerate(out_turns)]
+    grad_att, down_got = crossed([up_fold], grad_att, down_got)
     dq, dk, dv = attend_back(info, q, k, v, att, grad_att, total, seg)
-    dq, dk, dv, out_got, normed, *out_turns = up_fold.last(
-        dq, dk, dv, out_got, normed, *out_turns
-    )
-    start_keep, start_send = project_back(info, dq, dk, dv, in_blocks, width)
-    start_far = swap(start_send, "wide", 1)
-    normed, start_keep = together(normed, start_keep)
+    dq, dk, dv, out_send, normed, *out_turns = arrived(
+        [up_fold], dq, dk, dv, out_send, normed, *out_turns
+    )
+    start_keep, start_send = project_back(info, dq, dk, dv, in_full)
+    start_far, out_got = swap(start_send, "wide", 1), swap(out_send, "wide", 1)
+    up_keep, up_send = split(info, [up_fold], (2, 2, 2, rows))
+    down_keep, down_send = split(info, [[down_keep, down_got]], (2, down_rows), 1)
+    normed, start_keep, up_send, down_send = together(normed, start_keep, up_send, down_send)
+    up_got = swap(up_send, "narrow", 1)
+    down_got = swap(down_send, "narrow", 2)
     in_grads = weight_grad(info, normed, [dq, dk, dv], blocks)
-    start_far, *in_grads = together(start_far, *in_grads)
-    in_sum = gather_sum(by_distance(in_grads, (2, PLACES, rows, 3 * part)))
-    down_keep, down_send = split(info, [[down_keep, down_got]], (2, down_rows), 1)
-    up_keep, up_send = split(info, up_fold.parts, (2, 2, 2, rows))
-    start_far, down_send, up_send = together(start_far, down_send, up_send)
-    down_got = swap(down_send, "narrow", 2)
-    up_got = swap(up_send, "narrow", 1)
+    start_far, out_got, up_got, down_got, *in_grads = together(
+        start_far, out_got, up_got, down_got, *in_grads
+    )
+    in_fold = folded(in_grads, (2, PLACES, rows, 3 * part))
+    up_keep, up_send = split(info, [[up_keep, up_got]], (2, 2, rows), 1)
+    start_far, up_send = together(start_far, up_send)
+    up_got = swap(up_send, "narrow", 2)
     args = [start_keep, start_far, start, grad_middle, turned, sums, bias_grad, spots, dq, dv]
     started = start_back(info, blocks, args + [out_keep, out_got], patches, chips)
-    down_got, up_got, grad_blocks, *small_grads = together(down_got, up_got, *started)
-    up_keep, up_send = split(info, [[up_keep, up_got]], (2, 2, rows), 1)
-    up_got = swap(up_send, "narrow", 2)
-    grad_first, grad_second = pick_turns(info, grad_blocks.reshape(2, block, width))
-    grad_first = unspread_turn(grad_first, 0)
-    up_got, grad_second, *rest = together(up_got, grad_second, *in_sum[1:], *small_grads)
-    in_sum, small_grads = [in_sum[0], *rest[: len(in_sum) - 1]], rest[len(in_sum) - 1 :]
-    if plane:
-        small_sum = gather_sum(by_distance(small_grads, (2, PLACES, rows, SMALL + part)))
-    else:
+    if not plane:
         out_grad = jnp.where(
             first_core,
             jnp.concatenate([out_keep, out_got]),
             jnp.concatenate([out_got, out_keep]),
         ).reshape(chips, PLACES, rows, 2, part)
         out_grad = jnp.transpose(out_grad, (0, 3, 1, 2, 4)).reshape(width, part)
-        small_grads = jnp.concatenate([small_grads[0], out_grad], axis=1)
-        small_sum = gather_sum(by_distance([small_grads], (2, PLACES, rows, SMALL + part)))
-
-    def narrow_sum(cut):
-        whole = cut[0]
-        for index in range(1, PLACES):
-            whole = whole + swap(cut[index], "narrow", index).astype(f32)
-        return whole
-
-    in_cut = split(info, [in_sum], (2, PLACES, rows))
-    down_keep, up_keep, grad_first, *rest = together(
-        down_keep, up_keep, grad_first, *out_turns, *in_cut
-    )
-    out_turns, in_cut = rest[:2], rest[2:]
+        started = [started[0], jnp.concatenate([started[1], out_grad], axis=1)]
+    up_got, grad_blocks, *small_grads = crossed([in_fold], up_got, *started)
+    small_fold = folded(small_grads, (2, PLACES, rows, SMALL + part))
+    grad_first, grad_second = pick_turns(info, grad_blocks.reshape(2, block, width))
+    grad_first = unspread_turn(grad_first, 0)
+    (grad_second,) = crossed([small_fold], *arrived([in_fold], grad_second))
+    grad_second = unspread_turn(grad_second, 1)
+    (grad_first,) = arrived([small_fold], grad_first)
+    in_cut = split(info, [in_fold, small_fold], (2, PLACES, rows))
+    in_got = [swap(in_cut[index], "narrow", index) for index in range(1, PLACES)]
+    in_keep, down_keep, up_keep, up_got, grad_first, grad_second, *out_turns = together(
+        in_cut[0], down_keep, up_keep, up_got, grad_first, grad_second, *out_turns
+    )
     outputs = unspread_join(out_turns, place)
-    grad_tokens = unspread_join([grad_first, unspread_turn(grad_second, 1)], place)
+    grad_tokens = unspread_join([grad_first, grad_second], place)
     down_share = down_keep + down_got.astype(f32)
     up_total = up_keep + up_got.astype(f32)
     up_keep = pick(up_total, core)
@@ -1380,20 +1402,22 @@
     up_share = jnp.where(
         first_core, jnp.concatenate(up_both, axis=2), jnp.concatenate(up_both[::-1], axis=2)
     ).reshape(rows, hidden)
-    in_total = narrow_sum(in_cut)
-    small_total = narrow_sum(split(info, [small_sum], (2, PLACES, rows)))
+    outputs, grad_tokens, down_share, up_share, *in_got = together(
+        outputs, grad_tokens, down_share, up_share, *in_got
+    )
+    in_total = in_keep
+    for array in in_got:
+        in_total = in_total + array.astype(f32)
+    sent_columns = 3 * part + SMALL
     in_keep = pick(in_total, core)
-    in_got = swap(pick(in_total, 1 - core).astype(bf16), "wide", 1).astype(f32)
-    small_far = swap(pick(small_total, 1 - core)[:, :SMALL].astype(bf16), "wide", 1)
-    small_share = pick(small_total, core)[:, :SMALL] + small_far.astype(f32)
-    out_share = jnp.concatenate([small_total[0, :, SMALL:], small_total[1, :, SMALL:]], axis=1)
-    in_both = [
-        in_keep.reshape(rows, 3, 1, part),
-        in_got.reshape(rows, 3, 1, part),
-    ]
+    in_far = pick(in_total, 1 - core)[:, :sent_columns].astype(bf16)
+    in_far = swap(in_far, "wide", 1).astype(f32)
+    in_both = [in_keep[:, : 3 * part].reshape(rows, 3, 1, part), in_far[:, : 3 * part].reshape(rows, 3, 1, part)]
     in_share = jnp.where(
         first_core, jnp.concatenate(in_both, axis=2), jnp.concatenate(in_both[::-1], axis=2)
     ).reshape(rows, 3 * width)
+    small_share = in_keep[:, 3 * part : sent_columns] + in_far[:, 3 * part :]
+    out_share = jnp.concatenate([in_total[0, :, sent_columns:], in_total[1, :, sent_columns:]], axis=1)
     tail = [small_share[:, patches + i] for i in range(8)]
     return (
         outputs,

time: 289 us -> 272 us (0.941)
  the two profiles are of different devices: /device:TPU:9 before, /device:TPU:17 now
where the time goes in v5:
time: 272 us; the launch traced here: 267 us
  Pallas kernels  103 us (38%)
  starting transfers between devices  81.3 us (30%)
  waiting for transfers between devices  64.7 us (24%)
  local copies, waits for them, and re-layouts  10.7 us (4%)
  other arithmetic  5.79 us (2%)
    pallas_call x36, Pallas kernels, call(): pl.pallas_call(loaded if loads else kernel, out_shape=[shape for shape, _...  103 us
    ppermute x55, starting transfers between devices, swap(): return lax.ppermute(values, axis, [(i, i ^ bits) for i in range(size)])  67.6 us
    ppermute x55, waiting for transfers between devices, swap(): return lax.ppermute(values, axis, [(i, i ^ bits) for i in range(size)])  64.7 us
    ppermute x4, starting transfers between devices, unspread_turn(): lax.ppermute(part, ('wide', 'narrow'), [(b, a) for a, b in spread_perm(tu...  8.83 us
  transfers between devices with their start and end apart: 63, of which 22 were waited for; matrix products, arithmetic and copies ran while one was open for 3% of the time, Pallas kernels for 30%

profile of v5, /device:TPU:17, one launch (start us, length us, event | category | flops | bytes accessed | tf_op | source)
XLA Modules:
  0.0 266.8 jit_solution(13531616661775349609)
XLA Ops:
  8.3 1.4 collective-permute-start.3
  9.7 2.3 collective-permute-start.4
  16.6 7.3 %collective-permute-done.4.refs_2_ = bf16[2,24,1280]{2,1,0:T(8,128)(2,1)S(1)} collective-permute-done((bf16[2,24,1280]{2,1,0:T(8,128)(2,1)S(1)}, bf16[2,24,1280]{2,1,0:T(8,128)(2,1)S(1)}, u32[]{:S(2)}, u32[]{:S(2)}) %collective-permute-start.4) | collective-permute-done | bytes 122912 | tf_op jit(solution)/shard_map/ppermute | solution.py:1066
  23.9 5.9 %collective-permute-done.5.refs_3_ = bf16[2,24,1280]{2,1,0:T(8,128)(2,1)S(1)} collective-permute-done((bf16[2,24,1280]{2,1,0:T(8,128)(2,1)S(1)}, bf16[2,24,1280]{2,1,0:T(8,128)(2,1)S(1)}, u32[]{:S(2)}, u32[]{:S(2)}) %collective-permute-start.5) | collective-permute-done | bytes 122912 | tf_op jit(solution)/shard_map/ppermute | solution.py:1066
  31.7 1.3 collective-permute-start.12
  35.0 8.5 %collective-permute-done.7.far = bf16[2,120,768]{2,1,0:T(8,128)(2,1)S(1)} collective-permute-done((bf16[2,120,768]{2,1,0:T(8,128)(2,1)S(1)}, bf16[2,120,768]{2,1,0:T(8,128)(2,1)S(1)}, u32[]{:S(2)}, u32[]{:S(2)}) %collective-permute-start.7) | collective-permute-done | bytes 368672 | tf_op jit(solution)/shard_map/ppermute | solution.py:1066
  43.5 2.2 collective-permute-start.8
  45.7 2.9 %collective-permute-start.9 = (bf16[2,24,1536]{2,1,0:T(8,128)(2,1)S(1)}, bf16[2,24,1536]{2,1,0:T(8,128)(2,1)S(1)}, u32[]{:S(2)}, u32[]{:S(2)}) collective-permute-start(bf16[2,24,1536]{2,1,0:T(8,128)(2,1)S(1)} %shard_map.302.refs_0_), channel_id=1, source_target_pairs={{0,2},{1,3},{2,0},{3,1},{4,6},{5,7},{6,4},{7,5},{8,10},{9,11},{10,... | collective-permute-start | bytes 442376 | tf_op jit(solution)/shard_map/ppermute | solution.py:1066
  49.2 4.5 %collective-permute-done.14 = bf16[2,4,24,1280]{3,2,1,0:T(8,128)(2,1)S(1)} collective-permute-done((bf16[2,4,24,1280]{3,2,1,0:T(8,128)(2,1)S(1)}, bf16[2,4,24,1280]{3,2,1,0:T(8,128)(2,1)S(1)}, u32[]{:S(2)}, u32[]{:S(2)}) %collective-permute-start.14) | collective-permute-done | bytes 491552 | tf_op jit(solution)/shard_map/ppermute | solution.py:1066
  55.1 4.2 %collective-permute-start.10 = (bf16[272,768]{1,0:T(8,128)(2,1)S(1)}, bf16[272,768]{1,0:T(8,128)(2,1)S(1)}, u32[]{:S(2)}, u32[]{:S(2)}) collective-permute-start(bf16[272,768]{1,0:T(8,128)(2,1)S(1)} %collective-permute-done.6.refs_0_), channel_id=1, source_target_pairs={{0,4},{4,0},{8,12},{12,8},{16,20},{20,16},{24,28},{28,24},{1,5},{5... | collective-permute-start | bytes 1253384 | tf_op jit(solution)/shard_map/ppermute | solution.py:1066
  59.3 5.4 %collective-permute-start.11 = (bf16[272,768]{1,0:T(8,128)(2,1)S(1)}, bf16[272,768]{1,0:T(8,128)(2,1)S(1)}, u32[]{:S(2)}, u32[]{:S(2)}) collective-permute-start(bf16[272,768]{1,0:T(8,128)(2,1)S(1)} %collective-permute-done.8.refs_1_), channel_id=1, source_target_pairs={{0,4},{4,0},{8,12},{12,8},{16,20},{20,16},{24,28},{28,24},{1,5},{5... | collective-permute-start | bytes 1253384 | tf_op jit(solution)/shard_map/ppermute | solution.py:1066
  65.3 1.6 collective-permute-start.15
  67.6 7.0 %shard_map.305 = (bf16[1024,384]{1,0:T(8,128)(2,1)S(1)}, bf16[1024,384]{1,0:T(8,128)(2,1)S(1)}, bf16[1024,384]{1,0:T(8,128)(2,1)S(1)}, f32[1024,768]{1,0:T(8,128...) custom-call(s32[4]{0:T(128)S(1)} %pad_add_fusion.info, ...), custom_call_target="tpu_custom_call" | custom-call | flops 2013265920 | bytes 12582912 | tf_op jit(solution)/shard_map/pallas_call | solution.py:61
  75.2 1.3 collective-permute-start.20
  79.9 3.0 %collective-permute-done.20.refs_12_ = bf16[2,96,768]{2,1,0:T(8,128)(2,1)S(1)} collective-permute-done((bf16[2,96,768]{2,1,0:T(8,128)(2,1)S(1)}, bf16[2,96,768]{2,1,0:T(8,128)(2,1)S(1)}, u32[]{:S(2)}, u32[]{:S(2)}) %collective-permute-start.20) | collective-permute-done | bytes 294944 | tf_op jit(solution)/shard_map/ppermute | solution.py:1066
  83.8 13.2 %shard_map.308 = (bf16[1024,384]{1,0:T(8,128)(2,1)S(1)}, f32[3,8,1024]{2,1,0:T(8,128)S(1)}) custom-call(s32[4]{0:T(128)S(1)} %pad_add_fusion.info, bf16[1024,384]{1,0:T(8,128)(2,1)S(1)} %get-tuple-element.275.q, bf16[1024,384]{1,0:T(8,128)(2,1)S(1)} %get-tuple-element.276.k, bf16[1024,384]{1,0:T(8,128)(2,1)S(1)} %get-tuple-element.277.v, ...), custom_call_target="tpu_custom_call" | custom-call | flops 2415919104 | bytes 4194304 | tf_op jit(solution)/shard_map/pallas_call | solution.py:61
  97.1 3.2 %collective-permute-done.21.d.refs_13_ = bf16[3,96,768]{2,1,0:T(8,128)(2,1)S(1)} collective-permute-done((bf16[3,96,768]{2,1,0:T(8,128)(2,1)S(1)}, bf16[3,96,768]{2,1,0:T(8,128)(2,1)S(1)}, u32[]{:S(2)}, u32[]{:S(2)}) %collective-permute-start.21) | collective-permute-done | bytes 442400 | tf_op jit(solution)/shard_map/ppermute | solution.py:1066
  100.3 2.3 collective-permute-start.24
  104.4 1.3 collective-permute-start.28
  107.0 4.2 %shard_map.312 = (f32[1024,768]{1,0:T(8,128)S(1)}, bf16[1024,768]{1,0:T(8,128)(2,1)S(1)}, f32[8,1536]{1,0:T(8,128)S(1)}, bf16[768,768]{1,0:T(8,128)(2,1)S(1)}) custom-call(s32[4]{0:T(128)S(1)} %pad_add_fusion.info, bf16[1024,384]{1,0:T(8,128)(2,1)S(1)} %get-tuple-element.288.att.o, bf16[1024,384]{1,0:T(8,128)(2,1)S(1)} %collective-permute-done.24.att_far, ...), custom_call_target="tpu_custom_call" | custom-call | flops 1207959552 | bytes 12582912 | tf_op jit(solution)/shard_map/pallas_call | solution.py:61
  111.2 1.5 collective-permute-done.28
  113.6 16.7 %shard_map.314 = (f32[512,768]{1,0:T(8,128)S(1)}, bf16[512,768]{1,0:T(8,128)(2,1)S(1)}, bf16[1024,1536]{1,0:T(8,128)(2,1)S(1)}, bf16[768,1536]{1,0:T(8,128)(2,1)...) custom-call(s32[4]{0:T(128)S(1)} %pad_add_fusion.info, ...), custom_call_target="tpu_custom_call" | custom-call | flops 7247757312 | bytes 25165824 | tf_op jit(solution)/shard_map/pallas_call | solution.py:61
  130.3 1.3 collective-permute-start.30
  132.8 7.6 %shard_map.315 = (f32[1024,768]{1,0:T(8,128)S(1)}, bf16[1024,768]{1,0:T(8,128)(2,1)S(1)}, bf16[1024,1536]{1,0:T(8,128)(2,1)S(1)}, f32[8,1536]{1,0:T(8,128)S(1)}) custom-call(s32[4]{0:T(128)S(1)} %pad_add_fusion.info, bf16[1024,1536]{1,0:T(8,128)(2,1)S(1)} %get-tuple-element.305.slope, bf16[4,256,768]{2,1,0:T(8,128)(2,1)S(1)} %get-tuple-element.306.cot, ...), custom_call_target="tpu_custom_call" | custom-call | flops 4831838208 | bytes 25165824 | tf_op jit(solution)/shard_map/pallas_call | solution.py:61
  140.4 3.1 %collective-permute-done.30.refs_1_ = bf16[4,96,768]{2,1,0:T(8,128)(2,1)S(1)} collective-permute-done((bf16[4,96,768]{2,1,0:T(8,128)(2,1)S(1)}, bf16[4,96,768]{2,1,0:T(8,128)(2,1)S(1)}, u32[]{:S(2)}, u32[]{:S(2)}) %collective-permute-start.30) | collective-permute-done | bytes 589856 | tf_op jit(solution)/shard_map/ppermute | solution.py:1066
  143.6 1.4 collective-permute-done.31.refs_3_
  144.9 2.4 collective-permute-start.32
  148.0 1.3 collective-permute-start.34
  149.5 4.6 %shard_map.316 = (bf16[192,1536]{1,0:T(8,128)(2,1)S(1)}, bf16[192,1536]{1,0:T(8,128)(2,1)S(1)}, bf16[192,1536]{1,0:T(8,128)(2,1)S(1)}, bf16[96,1536]{1,0:T(8,128)(2,1)S(1)}, bf16[96,1536]{1,0:T(8,128)(2,1)S(1)}) custom-call(s32[4]{0:T(128)S(1)} %pad_add_fusion.info, bf16[1024,768]{1,0:T(8,128)(2,1)S(1)} %get-tuple-element.318.normed.left, ...), custom_call_target="tpu_custom_call" | custom-call | flops 2415919104 | bytes 8388608 | tf_op jit(solution)/shard_map/pallas_call | solution.py:61
  154.1 2.1 collective-permute-done.34
  159.8 5.6 %shard_map.318 = (f32[512,768]{1,0:T(8,128)S(1)}, bf16[1024,384]{1,0:T(8,128)(2,1)S(1)}, bf16[2,96,768]{2,1,0:T(8,128)(2,1)S(1)}, bf16[2,96,768]{2,1,0:T(8,128)(2,1)S(1)}, f32[8,768]{1,0:T(8,128)S(1)}) custom-call(s32[4]{0:T(128)S(1)} %pad_add_fusion.info, f32[1024,768]{1,0:T(8,128)S(1)} %get-tuple-element.332.back, ...), custom_call_target="tpu_custom_call" | custom-call | flops 1207959552 | bytes 14680064 | tf_op jit(solution)/shard_map/pallas_call | solution.py:61
  167.3 2.9 %collective-permute-done.37.refs_1_ = bf16[192,1536]{1,0:T(8,128)(2,1)S(1)} collective-permute-done((bf16[192,1536]{1,0:T(8,128)(2,1)S(1)}, bf16[192,1536]{1,0:T(8,128)(2,1)S(1)}, u32[]{:S(2)}, u32[]{:S(2)}) %collective-permute-start.37) | collective-permute-done | bytes 589856 | tf_op jit(solution)/shard_map/ppermute | solution.py:1066
  172.7 12.5 %shard_map.320 = (bf16[1024,384]{1,0:T(8,128)(2,1)S(1)}, bf16[1024,384]{1,0:T(8,128)(2,1)S(1)}, bf16[1024,384]{1,0:T(8,128)(2,1)S(1)}) custom-call(s32[4]{0:T(128)S(1)} %pad_add_fusion.info, bf16[1024,384]{1,0:T(8,128)(2,1)S(1)} %get-tuple-element.275.q, bf16[1024,384]{1,0:T(8,128)(2,1)S(1)} %get-tuple-element.276.k, ...), custom_call_target="tpu_custom_call" | custom-call | flops 6039797760 | bytes 6291456 | tf_op jit(solution)/shard_map/pallas_call | solution.py:61
  185.3 3.2 %shard_map.323 = (f32[512,768]{1,0:T(8,128)S(1)}, bf16[512,768]{1,0:T(8,128)(2,1)S(1)}) custom-call(s32[4]{0:T(128)S(1)} %pad_add_fusion.info, bf16[1024,384]{1,0:T(8,128)(2,1)S(1)} %get-tuple-element.361.dq.refs_0_.refs_8_, bf16[1024,384]{1,0:T(8,128)(2,1)S(1)} %get-tuple-element.362.dk.refs_1_, ...), custom_call_target="tpu_custom_call" | custom-call | flops 1811939328 | bytes 8388608 | tf_op jit(solution)/shard_map/pallas_call | solution.py:61
  188.5 5.2 %collective-permute-start.43 = (bf16[512,768]{1,0:T(8,128)(2,1)S(1)}, bf16[512,768]{1,0:T(8,128)(2,1)S(1)}, u32[]{:S(2)}, u32[]{:S(2)}) collective-permute-start(bf16[512,768]{1,0:T(8,128)(2,1)S(1)} %get-tuple-element.365), channel_id=1, source_target_pairs={{0,4},{4,0},{8,12},{12,8},{16,20},{20,16},{24,28},{28,24},{1,5},{5... | collective-permute-start | bytes 2359304 | tf_op jit(solution)/shard_map/ppermute | solution.py:1066
  196.9 5.4 %shard_map.326 = (bf16[192,1152]{1,0:T(8,128)(2,1)S(1)}, bf16[192,1152]{1,0:T(8,128)(2,1)S(1)}, bf16[192,1152]{1,0:T(8,128)(2,1)S(1)}, bf16[96,1152]{1,0:T(8,128)(2,1)S(1)}, bf16[96,1152]{1,0:T(8,128)(2,1)S(1)}) custom-call(s32[4]{0:T(128)S(1)} %pad_add_fusion.info, bf16[1024,768]{1,0:T(8,128)(2,1)S(1)} %get-tuple-element.378.left, ...), custom_call_target="tpu_custom_call" | custom-call | flops 1811939328 | bytes 8388608 | tf_op jit(solution)/shard_map/pallas_call | solution.py:61
  202.3 4.5 %collective-permute-done.46 = bf16[96,768]{1,0:T(8,128)(2,1)S(1)} collective-permute-done((bf16[96,768]{1,0:T(8,128)(2,1)S(1)}, bf16[96,768]{1,0:T(8,128)(2,1)S(1)}, u32[]{:S(2)}, u32[]{:S(2)}) %collective-permute-start.46) | collective-permute-done | bytes 147488 | tf_op jit(solution)/shard_map/ppermute | solution.py:1066
  209.9 4.8 %shard_map.328 = (bf16[512,768]{1,0:T(8,128)(2,1)S(1)}, bf16[192,512]{1,0:T(8,128)(2,1)S(1)}, bf16[192,512]{1,0:T(8,128)(2,1)S(1)}, bf16[192,512]{1,0:T(8,128)(2...) custom-call(s32[4]{0:T(128)S(1)} %pad_add_fusion.info, f32[512,768]{1,0:T(8,128)S(1)} %get-tuple-element.390.refs_0_, ...), custom_call_target="tpu_custom_call" | custom-call | flops 100663296 | bytes 10485760 | tf_op jit(solution)/shard_map/pallas_call | solution.py:61
  214.8 3.0 %collective-permute-done.48.refs_1_ = bf16[192,1152]{1,0:T(8,128)(2,1)S(1)} collective-permute-done((bf16[192,1152]{1,0:T(8,128)(2,1)S(1)}, bf16[192,1152]{1,0:T(8,128)(2,1)S(1)}, u32[]{:S(2)}, u32[]{:S(2)}) %collective-permute-start.48) | collective-permute-done | bytes 442400 | tf_op jit(solution)/shard_map/ppermute | solution.py:1066
  221.4 1.5 shard_map.329
  222.9 4.5 %collective-permute-start.54 = (bf16[256,768]{1,0:T(8,128)(2,1)}, bf16[256,768]{1,0:T(8,128)(2,1)}, u32[]{:S(2)}, u32[]{:S(2)}) collective-permute-start(bf16[256,768]{1,0:T(8,128)(2,1)} %get-tuple-element.422), channel_id=1, source_target_pairs={{0,0},{1,1},{4,2},{5,3},{2,4},{3,5},{6,6},{7,7},{8,8},{9,9},{12,10... | collective-permute-start | bytes 1179656 | tf_op jit(solution)/shard_map/ppermute | solution.py:1079
  227.6 3.2 %collective-permute-start.57 = (bf16[256,768]{1,0:T(8,128)(2,1)}, bf16[256,768]{1,0:T(8,128)(2,1)}, u32[]{:S(2)}, u32[]{:S(2)}) collective-permute-start(bf16[256,768]{1,0:T(8,128)(2,1)} %get-tuple-element.434), channel_id=1, source_target_pairs={{1,0},{0,1},{5,2},{4,3},{3,4},{2,5},{7,6},{6,7},{9,8},{8,9},{13,10... | collective-permute-start | bytes 1179656 | tf_op jit(solution)/shard_map/ppermute | solution.py:1079
  232.7 2.7 collective-permute-done.55.refs_8_
  236.6 1.6 shard_map.332
  238.2 7.6 %collective-permute-start.60 = (bf16[2,24,1664]{2,1,0:T(8,128)(2,1)}, bf16[2,24,1664]{2,1,0:T(8,128)(2,1)S(1)}, u32[]{:S(2)}, u32[]{:S(2)}) collective-permute-start(bf16[2,24,1664]{2,1,0:T(8,128)(2,1)} %get-tuple-element.446), channel_id=1, source_target_pairs={{0,2},{1,3},{2,0},{3,1},{4,6},{5,7},{6,4},{7,5},{8,10},{9,11},{10,... | collective-permute-start | bytes 479240 | tf_op jit(solution)/shard_map/ppermute | solution.py:1066
  246.0 3.3 %collective-permute-start.58 = (bf16[24,1536]{1,0:T(8,128)(2,1)S(1)}, bf16[24,1536]{1,0:T(8,128)(2,1)S(1)}, u32[]{:S(2)}, u32[]{:S(2)}) collective-permute-start(bf16[24,1536]{1,0:T(8,128)(2,1)S(1)} %fusion.1), channel_id=1, source_target_pairs={{0,4},{4,0},{8,12},{12,8},{16,20},{20,16},{24,28},{28,24},{1,5},{5... | collective-permute-start | bytes 221192 | tf_op jit(solution)/shard_map/ppermute | solution.py:1066
  254.5 2.0 collective-permute-done.60
  256.5 5.2 %collective-permute-done.61 = bf16[2,24,1664]{2,1,0:T(8,128)(2,1)S(1)} collective-permute-done((bf16[2,24,1664]{2,1,0:T(8,128)(2,1)}, bf16[2,24,1664]{2,1,0:T(8,128)(2,1)S(1)}, u32[]{:S(2)}, u32[]{:S(2)}) %collective-permute-start.61) | collective-permute-done | bytes 159776 | tf_op jit(solution)/shard_map/ppermute | solution.py:1066
  (181 shorter events, 61.7 us)
Async XLA Ops:
  7.7 22.1 %collective-permute-start.2 = (bf16[120,768]{1,0:T(8,128)(2,1)S(1)}, bf16[120,768]{1,0:T(8,128)(2,1)S(1)}, u32[]{:S(2)}, u32[]{:S(2)}) collective-permute-start(bf16[120,768]{1,0:T(8,128)(2,1)S(1)} %pad_maximum_fusion.2.refs_0_), channel_id=1, source_target_pairs={{0,2},{1,3},{2,0},{3,1},{4,6},{5,7},{6,4},{7,5},{8,10},{9,11},{10,... | collective-permute-start | bytes 552968 | tf_op jit(solution)/shard_map/ppermute | solution.py:1066
  8.3 8.2 %collective-permute-start.3 = (bf16[2,24,1280]{2,1,0:T(8,128)(2,1)S(1)}, bf16[2,24,1280]{2,1,0:T(8,128)(2,1)S(1)}, u32[]{:S(2)}, u32[]{:S(2)}) collective-permute-start(bf16[2,24,1280]{2,1,0:T(8,128)(2,1)S(1)} %shard_map.300.refs_0_), channel_id=1, source_target_pairs={{0,1},{1,0},{2,3},{3,2},{4,5},{5,4},{6,7},{7,6},{8,9},{9,8},{10,11... | collective-permute-start | bytes 368648 | tf_op jit(solution)/shard_map/ppermute | solution.py:1066
  9.7 14.1 %collective-permute-start.4 = (bf16[2,24,1280]{2,1,0:T(8,128)(2,1)S(1)}, bf16[2,24,1280]{2,1,0:T(8,128)(2,1)S(1)}, u32[]{:S(2)}, u32[]{:S(2)}) collective-permute-start(bf16[2,24,1280]{2,1,0:T(8,128)(2,1)S(1)} %shard_map.300.refs_0_), channel_id=1, source_target_pairs={{0,2},{1,3},{2,0},{3,1},{4,6},{5,7},{6,4},{7,5},{8,10},{9,11},{10,... | collective-permute-start | bytes 368648 | tf_op jit(solution)/shard_map/ppermute | solution.py:1066
  12.1 17.7 %collective-permute-start.5 = (bf16[2,24,1280]{2,1,0:T(8,128)(2,1)S(1)}, bf16[2,24,1280]{2,1,0:T(8,128)(2,1)S(1)}, u32[]{:S(2)}, u32[]{:S(2)}) collective-permute-start(bf16[2,24,1280]{2,1,0:T(8,128)(2,1)S(1)} %shard_map.300.refs_0_), channel_id=1, source_target_pairs={{0,3},{1,2},{2,1},{3,0},{4,7},{5,6},{6,5},{7,4},{8,11},{9,10},{10,... | collective-permute-start | bytes 368648 | tf_op jit(solution)/shard_map/ppermute | solution.py:1066
  29.8 13.7 %collective-permute-start.6 = (bf16[272,768]{1,0:T(8,128)(2,1)S(1)}, bf16[272,768]{1,0:T(8,128)(2,1)S(1)}, u32[]{:S(2)}, u32[]{:S(2)}) collective-permute-start(bf16[272,768]{1,0:T(8,128)(2,1)S(1)} %get-tuple-element.247), channel_id=1, source_target_pairs={{0,0},{1,1},{2,4},{3,5},{4,2},{5,3},{6,6},{7,7},{8,8},{9,9},{10,12... | collective-permute-start | bytes 1253384 | tf_op jit(solution)/shard_map/ppermute | solution.py:1272
  31.0 12.4 %collective-permute-start.7 = (bf16[2,120,768]{2,1,0:T(8,128)(2,1)S(1)}, bf16[2,120,768]{2,1,0:T(8,128)(2,1)S(1)}, u32[]{:S(2)}, u32[]{:S(2)}) collective-permute-start(bf16[2,120,768]{2,1,0:T(8,128)(2,1)S(1)} %shard_map.301.own), channel_id=1, source_target_pairs={{0,1},{1,0},{2,3},{3,2},{4,5},{5,4},{6,7},{7,6},{8,9},{9,8},{10,11... | collective-permute-start | bytes 1105928 | tf_op jit(solution)/shard_map/ppermute | solution.py:1066
  31.7 17.5 %collective-permute-start.12 = (bf16[2,4,24,1280]{3,2,1,0:T(8,128)(2,1)S(1)}, bf16[2,4,24,1280]{3,2,1,0:T(8,128)(2,1)S(1)}, u32[]{:S(2)}, u32[]{:S(2)}) collective-permute-start(bf16[2,4,24,1280]{3,2,1,0:T(8,128)(2,1)S(1)} %shard_map.304), channel_id=1, source_target_pairs={{0,8},{4,12},{8,0},{12,4},{16,24},{20,28},{24,16},{28,20},{1,9},{5... | collective-permute-start | bytes 1474568 | tf_op jit(solution)/shard_map/ppermute | solution.py:1066
  33.0 16.2 %collective-permute-start.13 = (bf16[2,4,24,1280]{3,2,1,0:T(8,128)(2,1)S(1)}, bf16[2,4,24,1280]{3,2,1,0:T(8,128)(2,1)S(1)}, u32[]{:S(2)}, u32[]{:S(2)}) collective-permute-start(bf16[2,4,24,1280]{3,2,1,0:T(8,128)(2,1)S(1)} %shard_map.304), channel_id=1, source_target_pairs={{0,16},{4,20},{8,24},{12,28},{16,0},{20,4},{24,8},{28,12},{1,17},{... | collective-permute-start | bytes 1474568 | tf_op jit(solution)/shard_map/ppermute | solution.py:1066
  34.2 19.5 %collective-permute-start.14 = (bf16[2,4,24,1280]{3,2,1,0:T(8,128)(2,1)S(1)}, bf16[2,4,24,1280]{3,2,1,0:T(8,128)(2,1)S(1)}, u32[]{:S(2)}, u32[]{:S(2)}) collective-permute-start(bf16[2,4,24,1280]{3,2,1,0:T(8,128)(2,1)S(1)} %shard_map.304), channel_id=1, source_target_pairs={{0,24},{4,28},{8,16},{12,20},{16,8},{20,12},{24,0},{28,4},{1,25},{... | collective-permute-start | bytes 1474568 | tf_op jit(solution)/shard_map/ppermute | solution.py:1066
  43.5 15.8 %collective-permute-start.8 = (bf16[272,768]{1,0:T(8,128)(2,1)S(1)}, bf16[272,768]{1,0:T(8,128)(2,1)S(1)}, u32[]{:S(2)}, u32[]{:S(2)}) collective-permute-start(bf16[272,768]{1,0:T(8,128)(2,1)S(1)} %get-tuple-element.253), channel_id=1, source_target_pairs={{0,1},{1,0},{2,5},{3,4},{4,3},{5,2},{6,7},{7,6},{8,9},{9,8},{10,13... | collective-permute-start | bytes 1253384 | tf_op jit(solution)/shard_map/ppermute | solution.py:1277
  45.7 13.6 %collective-permute-start.9 = (bf16[2,24,1536]{2,1,0:T(8,128)(2,1)S(1)}, bf16[2,24,1536]{2,1,0:T(8,128)(2,1)S(1)}, u32[]{:S(2)}, u32[]{:S(2)}) collective-permute-start(bf16[2,24,1536]{2,1,0:T(8,128)(2,1)S(1)} %shard_map.302.refs_0_), channel_id=1, source_target_pairs={{0,2},{1,3},{2,0},{3,1},{4,6},{5,7},{6,4},{7,5},{8,10},{9,11},{10,... | collective-permute-start | bytes 442376 | tf_op jit(solution)/shard_map/ppermute | solution.py:1066
  53.7 20.9 %collective-permute-start.16 = (bf16[5,96,768]{2,1,0:T(8,128)(2,1)S(1)}, bf16[5,96,768]{2,1,0:T(8,128)(2,1)S(1)}, u32[]{:S(2)}, u32[]{:S(2)}) collective-permute-start(bf16[5,96,768]{2,1,0:T(8,128)(2,1)S(1)} %shard_map.303.own.refs_9_), channel_id=1, source_target_pairs={{0,8},{4,12},{8,0},{12,4},{16,24},{20,28},{24,16},{28,20},{1,9},{5... | collective-permute-start | bytes 2211848 | tf_op jit(solution)/shard_map/ppermute | solution.py:1066
  54.9 19.7 %collective-permute-start.17 = (bf16[5,96,768]{2,1,0:T(8,128)(2,1)S(1)}, bf16[5,96,768]{2,1,0:T(8,128)(2,1)S(1)}, u32[]{:S(2)}, u32[]{:S(2)}) collective-permute-start(bf16[5,96,768]{2,1,0:T(8,128)(2,1)S(1)} %shard_map.303.own.refs_9_), channel_id=1, source_target_pairs={{0,16},{4,20},{8,24},{12,28},{16,0},{20,4},{24,8},{28,12},{1,17},{... | collective-permute-start | bytes 2211848 | tf_op jit(solution)/shard_map/ppermute | solution.py:1066
  55.1 11.8 %collective-permute-start.10 = (bf16[272,768]{1,0:T(8,128)(2,1)S(1)}, bf16[272,768]{1,0:T(8,128)(2,1)S(1)}, u32[]{:S(2)}, u32[]{:S(2)}) collective-permute-start(bf16[272,768]{1,0:T(8,128)(2,1)S(1)} %collective-permute-done.6.refs_0_), channel_id=1, source_target_pairs={{0,4},{4,0},{8,12},{12,8},{16,20},{20,16},{24,28},{28,24},{1,5},{5... | collective-permute-start | bytes 1253384 | tf_op jit(solution)/shard_map/ppermute | solution.py:1066
  65.3 9.2 %collective-permute-start.15 = (bf16[2,2,24,1536]{3,2,1,0:T(8,128)(2,1)S(1)}, bf16[2,2,24,1536]{3,2,1,0:T(8,128)(2,1)S(1)}, u32[]{:S(2)}, u32[]{:S(2)}) collective-permute-start(bf16[2,2,24,1536]{3,2,1,0:T(8,128)(2,1)S(1)} %shard_map.307.refs_0_), channel_id=1, source_target_pairs={{0,1},{1,0},{2,3},{3,2},{4,5},{5,4},{6,7},{7,6},{8,9},{9,8},{10,11... | collective-permute-start | bytes 884744 | tf_op jit(solution)/shard_map/ppermute | solution.py:1066
  77.1 23.3 %collective-permute-start.22 = (bf16[2,4,24,1536]{3,2,1,0:T(8,128)(2,1)S(1)}, bf16[2,4,24,1536]{3,2,1,0:T(8,128)(2,1)S(1)}, u32[]{:S(2)}, u32[]{:S(2)}) collective-permute-start(bf16[2,4,24,1536]{3,2,1,0:T(8,128)(2,1)S(1)} %bitcast.56), channel_id=1, source_target_pairs={{0,8},{4,12},{8,0},{12,4},{16,24},{20,28},{24,16},{28,20},{1,9},{5... | collective-permute-start | bytes 1769480 | tf_op jit(solution)/shard_map/ppermute | solution.py:1066
  77.4 22.9 %collective-permute-start.23 = (bf16[2,4,24,1536]{3,2,1,0:T(8,128)(2,1)S(1)}, bf16[2,4,24,1536]{3,2,1,0:T(8,128)(2,1)S(1)}, u32[]{:S(2)}, u32[]{:S(2)}) collective-permute-start(bf16[2,4,24,1536]{3,2,1,0:T(8,128)(2,1)S(1)} %bitcast.57), channel_id=1, source_target_pairs={{0,16},{4,20},{8,24},{12,28},{16,0},{20,4},{24,8},{28,12},{1,17},{... | collective-permute-start | bytes 1769480 | tf_op jit(solution)/shard_map/ppermute | solution.py:1066
  78.6 21.7 %collective-permute-start.21 = (bf16[3,96,768]{2,1,0:T(8,128)(2,1)S(1)}, bf16[3,96,768]{2,1,0:T(8,128)(2,1)S(1)}, u32[]{:S(2)}, u32[]{:S(2)}) collective-permute-start(bf16[3,96,768]{2,1,0:T(8,128)(2,1)S(1)} %get-tuple-element.286), channel_id=1, source_target_pairs={{0,16},{4,20},{8,24},{12,28},{16,0},{20,4},{24,8},{28,12},{1,17},{... | collective-permute-start | bytes 1327112 | tf_op jit(solution)/shard_map/ppermute | solution.py:1066
  78.8 18.2 %collective-permute-start.19 = (bf16[256,768]{1,0:T(8,128)(2,1)S(1)}, bf16[256,768]{1,0:T(8,128)(2,1)S(1)}, u32[]{:S(2)}, u32[]{:S(2)}) collective-permute-start(bf16[256,768]{1,0:T(8,128)(2,1)S(1)} %get-tuple-element.281), channel_id=1, source_target_pairs={{0,1},{1,0},{2,5},{3,4},{4,3},{5,2},{6,7},{7,6},{8,9},{9,8},{10,13... | collective-permute-start | bytes 1179656 | tf_op jit(solution)/shard_map/ppermute | solution.py:1301
  83.0 14.1 %collective-permute-start.18 = (bf16[256,768]{1,0:T(8,128)(2,1)S(1)}, bf16[256,768]{1,0:T(8,128)(2,1)S(1)}, u32[]{:S(2)}, u32[]{:S(2)}) collective-permute-start(bf16[256,768]{1,0:T(8,128)(2,1)S(1)} %get-tuple-element.280), channel_id=1, source_target_pairs={{0,0},{1,1},{2,4},{3,5},{4,2},{5,3},{6,6},{7,7},{8,8},{9,9},{10,12... | collective-permute-start | bytes 1179656 | tf_op jit(solution)/shard_map/ppermute | solution.py:1291
  103.3 10.3 %collective-permute-start.26 = (bf16[256,768]{1,0:T(8,128)(2,1)S(1)}, bf16[256,768]{1,0:T(8,128)(2,1)S(1)}, u32[]{:S(2)}, u32[]{:S(2)}) collective-permute-start(bf16[256,768]{1,0:T(8,128)(2,1)S(1)} %collective-permute-done.18.refs_0_), channel_id=1, source_target_pairs={{0,4},{4,0},{8,12},{12,8},{16,20},{20,16},{24,28},{28,24},{1,5},{5... | collective-permute-start | bytes 1179656 | tf_op jit(solution)/shard_map/ppermute | solution.py:1066
  103.8 9.8 %collective-permute-start.27 = (bf16[256,768]{1,0:T(8,128)(2,1)S(1)}, bf16[256,768]{1,0:T(8,128)(2,1)S(1)}, u32[]{:S(2)}, u32[]{:S(2)}) collective-permute-start(bf16[256,768]{1,0:T(8,128)(2,1)S(1)} %collective-permute-done.19.refs_1_), channel_id=1, source_target_pairs={{0,4},{4,0},{8,12},{12,8},{16,20},{20,16},{24,28},{28,24},{1,5},{5... | collective-permute-start | bytes 1179656 | tf_op jit(solution)/shard_map/ppermute | solution.py:1066
  104.4 8.2 %collective-permute-start.28 = (bf16[1,4,24,1536]{3,2,1,0:T(8,128)(2,1)S(1)}, bf16[1,4,24,1536]{3,2,1,0:T(8,128)(2,1)S(1)}, u32[]{:S(2)}, u32[]{:S(2)}) collective-permute-start(bf16[1,4,24,1536]{3,2,1,0:T(8,128)(2,1)S(1)} %get-tuple-element.302), channel_id=1, source_target_pairs={{0,8},{4,12},{8,0},{12,4},{16,24},{20,28},{24,16},{28,20},{1,9},{5... | collective-permute-start | bytes 884744 | tf_op jit(solution)/shard_map/ppermute | solution.py:1066
  130.3 13.3 %collective-permute-start.30 = (bf16[4,96,768]{2,1,0:T(8,128)(2,1)S(1)}, bf16[4,96,768]{2,1,0:T(8,128)(2,1)S(1)}, u32[]{:S(2)}, u32[]{:S(2)}) collective-permute-start(bf16[4,96,768]{2,1,0:T(8,128)(2,1)S(1)} %get-tuple-element.314), channel_id=1, source_target_pairs={{0,8},{4,12},{8,0},{12,4},{16,24},{20,28},{24,16},{28,20},{1,9},{5... | collective-permute-start | bytes 1769480 | tf_op jit(solution)/shard_map/ppermute | solution.py:1066
  131.6 13.3 %collective-permute-start.31 = (bf16[4,96,768]{2,1,0:T(8,128)(2,1)S(1)}, bf16[4,96,768]{2,1,0:T(8,128)(2,1)S(1)}, u32[]{:S(2)}, u32[]{:S(2)}) collective-permute-start(bf16[4,96,768]{2,1,0:T(8,128)(2,1)S(1)} %get-tuple-element.315), channel_id=1, source_target_pairs={{0,16},{4,20},{8,24},{12,28},{16,0},{20,4},{24,8},{28,12},{1,17},{... | collective-permute-start | bytes 1769480 | tf_op jit(solution)/shard_map/ppermute | solution.py:1066
  144.9 12.2 %collective-permute-start.32 = (bf16[1024,768]{1,0:T(8,128)(2,1)S(1)}, bf16[1024,768]{1,0:T(8,128)(2,1)S(1)}, u32[]{:S(2)}, u32[]{:S(2)}) collective-permute-start(bf16[1024,768]{1,0:T(8,128)(2,1)S(1)} %get-tuple-element.316), channel_id=1, source_target_pairs={{0,4},{4,0},{8,12},{12,8},{16,20},{20,16},{24,28},{28,24},{1,5},{5... | collective-permute-start | bytes 4718600 | tf_op jit(solution)/shard_map/ppermute | solution.py:1066
  147.3 9.7 %collective-permute-start.33 = (bf16[512,768]{1,0:T(8,128)(2,1)S(1)}, bf16[512,768]{1,0:T(8,128)(2,1)S(1)}, u32[]{:S(2)}, u32[]{:S(2)}) collective-permute-start(bf16[512,768]{1,0:T(8,128)(2,1)S(1)} %get-tuple-element.317), channel_id=1, source_target_pairs={{0,4},{4,0},{8,12},{12,8},{16,20},{20,16},{24,28},{28,24},{1,5},{5... | collective-permute-start | bytes 2359304 | tf_op jit(solution)/shard_map/ppermute | solution.py:1066
  148.0 8.1 %collective-permute-start.34 = (bf16[2,96,768]{2,1,0:T(8,128)(2,1)S(1)}, bf16[2,96,768]{2,1,0:T(8,128)(2,1)S(1)}, u32[]{:S(2)}, u32[]{:S(2)}) collective-permute-start(bf16[2,96,768]{2,1,0:T(8,128)(2,1)S(1)} %get-tuple-element.329), channel_id=1, source_target_pairs={{0,16},{4,20},{8,24},{12,28},{16,0},{20,4},{24,8},{28,12},{1,17},{... | collective-permute-start | bytes 884744 | tf_op jit(solution)/shard_map/ppermute | solution.py:1066
  157.1 13.1 %collective-permute-start.37 = (bf16[192,1536]{1,0:T(8,128)(2,1)S(1)}, bf16[192,1536]{1,0:T(8,128)(2,1)S(1)}, u32[]{:S(2)}, u32[]{:S(2)}) collective-permute-start(bf16[192,1536]{1,0:T(8,128)(2,1)S(1)} %get-tuple-element.342), channel_id=1, source_target_pairs={{0,8},{4,12},{8,0},{12,4},{16,24},{20,28},{24,16},{28,20},{1,9},{5... | collective-permute-start | bytes 1769480 | tf_op jit(solution)/shard_map/ppermute | solution.py:1066
  157.3 12.9 %collective-permute-start.38 = (bf16[192,1536]{1,0:T(8,128)(2,1)S(1)}, bf16[192,1536]{1,0:T(8,128)(2,1)S(1)}, u32[]{:S(2)}, u32[]{:S(2)}) collective-permute-start(bf16[192,1536]{1,0:T(8,128)(2,1)S(1)} %get-tuple-element.343), channel_id=1, source_target_pairs={{0,16},{4,20},{8,24},{12,28},{16,0},{20,4},{24,8},{28,12},{1,17},{... | collective-permute-start | bytes 1769480 | tf_op jit(solution)/shard_map/ppermute | solution.py:1066
  158.6 8.7 %collective-permute-start.36 = (bf16[2,96,768]{2,1,0:T(8,128)(2,1)S(1)}, bf16[2,96,768]{2,1,0:T(8,128)(2,1)S(1)}, u32[]{:S(2)}, u32[]{:S(2)}) collective-permute-start(bf16[2,96,768]{2,1,0:T(8,128)(2,1)S(1)} %get-tuple-element.341), channel_id=1, source_target_pairs={{0,1},{1,0},{2,3},{3,2},{4,5},{5,4},{6,7},{7,6},{8,9},{9,8},{10,11... | collective-permute-start | bytes 884744 | tf_op jit(solution)/shard_map/ppermute | solution.py:1066
  166.2 19.0 %collective-permute-start.39 = (bf16[256,768]{1,0:T(8,128)(2,1)S(1)}, bf16[256,768]{1,0:T(8,128)(2,1)S(1)}, u32[]{:S(2)}, u32[]{:S(2)}) collective-permute-start(bf16[256,768]{1,0:T(8,128)(2,1)S(1)} %get-tuple-element.353), channel_id=1, source_target_pairs={{0,0},{1,1},{4,2},{5,3},{2,4},{3,5},{6,6},{7,7},{8,8},{9,9},{12,10... | collective-permute-start | bytes 1179656 | tf_op jit(solution)/shard_map/ppermute | solution.py:1079
  166.9 18.4 %collective-permute-start.40 = (bf16[256,768]{1,0:T(8,128)(2,1)S(1)}, bf16[256,768]{1,0:T(8,128)(2,1)S(1)}, u32[]{:S(2)}, u32[]{:S(2)}) collective-permute-start(bf16[256,768]{1,0:T(8,128)(2,1)S(1)} %get-tuple-element.354), channel_id=1, source_target_pairs={{1,0},{0,1},{5,2},{4,3},{3,4},{2,5},{7,6},{6,7},{9,8},{8,9},{13,10... | collective-permute-start | bytes 1179656 | tf_op jit(solution)/shard_map/ppermute | solution.py:1079
  170.9 14.4 %collective-permute-start.41 = (bf16[96,1536]{1,0:T(8,128)(2,1)S(1)}, bf16[96,1536]{1,0:T(8,128)(2,1)S(1)}, u32[]{:S(2)}, u32[]{:S(2)}) collective-permute-start(bf16[96,1536]{1,0:T(8,128)(2,1)S(1)} %get-tuple-element.359), channel_id=1, source_target_pairs={{0,16},{4,20},{8,24},{12,28},{16,0},{20,4},{24,8},{28,12},{1,17},{... | collective-permute-start | bytes 884744 | tf_op jit(solution)/shard_map/ppermute | solution.py:1066
  171.5 13.8 %collective-permute-start.42 = (bf16[96,1536]{1,0:T(8,128)(2,1)S(1)}, bf16[96,1536]{1,0:T(8,128)(2,1)S(1)}, u32[]{:S(2)}, u32[]{:S(2)}) collective-permute-start(bf16[96,1536]{1,0:T(8,128)(2,1)S(1)} %get-tuple-element.360), channel_id=1, source_target_pairs={{0,8},{4,12},{8,0},{12,4},{16,24},{20,28},{24,16},{28,20},{1,9},{5... | collective-permute-start | bytes 884744 | tf_op jit(solution)/shard_map/ppermute | solution.py:1066
  188.5 18.3 %collective-permute-start.43 = (bf16[512,768]{1,0:T(8,128)(2,1)S(1)}, bf16[512,768]{1,0:T(8,128)(2,1)S(1)}, u32[]{:S(2)}, u32[]{:S(2)}) collective-permute-start(bf16[512,768]{1,0:T(8,128)(2,1)S(1)} %get-tuple-element.365), channel_id=1, source_target_pairs={{0,4},{4,0},{8,12},{12,8},{16,20},{20,16},{24,28},{28,24},{1,5},{5... | collective-permute-start | bytes 2359304 | tf_op jit(solution)/shard_map/ppermute | solution.py:1066
  195.3 11.5 %collective-permute-start.45 = (bf16[2,2,24,1536]{3,2,1,0:T(8,128)(2,1)S(1)}, bf16[2,2,24,1536]{3,2,1,0:T(8,128)(2,1)S(1)}, u32[]{:S(2)}, u32[]{:S(2)}) collective-permute-start(bf16[2,2,24,1536]{3,2,1,0:T(8,128)(2,1)S(1)} %get-tuple-element.376), channel_id=1, source_target_pairs={{0,1},{1,0},{2,3},{3,2},{4,5},{5,4},{6,7},{7,6},{8,9},{9,8},{10,11... | collective-permute-start | bytes 884744 | tf_op jit(solution)/shard_map/ppermute | solution.py:1066
  195.8 11.0 %collective-permute-start.44 = (bf16[2,96,768]{2,1,0:T(8,128)(2,1)S(1)}, bf16[2,96,768]{2,1,0:T(8,128)(2,1)S(1)}, u32[]{:S(2)}, u32[]{:S(2)}) collective-permute-start(bf16[2,96,768]{2,1,0:T(8,128)(2,1)S(1)} %get-tuple-element.366), channel_id=1, source_target_pairs={{0,4},{4,0},{8,12},{12,8},{16,20},{20,16},{24,28},{28,24},{1,5},{5... | collective-permute-start | bytes 884744 | tf_op jit(solution)/shard_map/ppermute | solution.py:1066
  196.1 10.7 %collective-permute-start.46 = (bf16[96,768]{1,0:T(8,128)(2,1)S(1)}, bf16[96,768]{1,0:T(8,128)(2,1)S(1)}, u32[]{:S(2)}, u32[]{:S(2)}) collective-permute-start(bf16[96,768]{1,0:T(8,128)(2,1)S(1)} %get-tuple-element.377), channel_id=1, source_target_pairs={{0,2},{1,3},{2,0},{3,1},{4,6},{5,7},{6,4},{7,5},{8,10},{9,11},{10,... | collective-permute-start | bytes 442376 | tf_op jit(solution)/shard_map/ppermute | solution.py:1066
  206.9 10.9 %collective-permute-start.48 = (bf16[192,1152]{1,0:T(8,128)(2,1)S(1)}, bf16[192,1152]{1,0:T(8,128)(2,1)S(1)}, u32[]{:S(2)}, u32[]{:S(2)}) collective-permute-start(bf16[192,1152]{1,0:T(8,128)(2,1)S(1)} %get-tuple-element.404), channel_id=1, source_target_pairs={{0,8},{4,12},{8,0},{12,4},{16,24},{20,28},{24,16},{28,20},{1,9},{5... | collective-permute-start | bytes 1327112 | tf_op jit(solution)/shard_map/ppermute | solution.py:1066
  207.2 10.5 %collective-permute-start.49 = (bf16[192,1152]{1,0:T(8,128)(2,1)S(1)}, bf16[192,1152]{1,0:T(8,128)(2,1)S(1)}, u32[]{:S(2)}, u32[]{:S(2)}) collective-permute-start(bf16[192,1152]{1,0:T(8,128)(2,1)S(1)} %get-tuple-element.405), channel_id=1, source_target_pairs={{0,16},{4,20},{8,24},{12,28},{16,0},{20,4},{24,8},{28,12},{1,17},{... | collective-permute-start | bytes 1327112 | tf_op jit(solution)/shard_map/ppermute | solution.py:1066
  218.4 9.0 %collective-permute-start.50 = (bf16[96,1152]{1,0:T(8,128)(2,1)S(1)}, bf16[96,1152]{1,0:T(8,128)(2,1)S(1)}, u32[]{:S(2)}, u32[]{:S(2)}) collective-permute-start(bf16[96,1152]{1,0:T(8,128)(2,1)S(1)} %get-tuple-element.412), channel_id=1, source_target_pairs={{0,16},{4,20},{8,24},{12,28},{16,0},{20,4},{24,8},{28,12},{1,17},{... | collective-permute-start | bytes 663560 | tf_op jit(solution)/shard_map/ppermute | solution.py:1066
  219.2 8.2 %collective-permute-start.51 = (bf16[96,1152]{1,0:T(8,128)(2,1)S(1)}, bf16[96,1152]{1,0:T(8,128)(2,1)S(1)}, u32[]{:S(2)}, u32[]{:S(2)}) collective-permute-start(bf16[96,1152]{1,0:T(8,128)(2,1)S(1)} %get-tuple-element.413), channel_id=1, source_target_pairs={{0,8},{4,12},{8,0},{12,4},{16,24},{20,28},{24,16},{28,20},{1,9},{5... | collective-permute-start | bytes 663560 | tf_op jit(solution)/shard_map/ppermute | solution.py:1066
  222.9 13.7 %collective-permute-start.54 = (bf16[256,768]{1,0:T(8,128)(2,1)}, bf16[256,768]{1,0:T(8,128)(2,1)}, u32[]{:S(2)}, u32[]{:S(2)}) collective-permute-start(bf16[256,768]{1,0:T(8,128)(2,1)} %get-tuple-element.422), channel_id=1, source_target_pairs={{0,0},{1,1},{4,2},{5,3},{2,4},{3,5},{6,6},{7,7},{8,8},{9,9},{12,10... | collective-permute-start | bytes 1179656 | tf_op jit(solution)/shard_map/ppermute | solution.py:1079
  227.6 18.3 %collective-permute-start.57 = (bf16[256,768]{1,0:T(8,128)(2,1)}, bf16[256,768]{1,0:T(8,128)(2,1)}, u32[]{:S(2)}, u32[]{:S(2)}) collective-permute-start(bf16[256,768]{1,0:T(8,128)(2,1)} %get-tuple-element.434), channel_id=1, source_target_pairs={{1,0},{0,1},{5,2},{4,3},{3,4},{2,5},{7,6},{6,7},{9,8},{8,9},{13,10... | collective-permute-start | bytes 1179656 | tf_op jit(solution)/shard_map/ppermute | solution.py:1079
  238.2 16.3 %collective-permute-start.59 = (bf16[2,24,1664]{2,1,0:T(8,128)(2,1)}, bf16[2,24,1664]{2,1,0:T(8,128)(2,1)S(1)}, u32[]{:S(2)}, u32[]{:S(2)}) collective-permute-start(bf16[2,24,1664]{2,1,0:T(8,128)(2,1)} %get-tuple-element.445), channel_id=1, source_target_pairs={{0,1},{1,0},{2,3},{3,2},{4,5},{5,4},{6,7},{7,6},{8,9},{9,8},{10,11... | collective-permute-start | bytes 479240 | tf_op jit(solution)/shard_map/ppermute | solution.py:1066
  238.2 18.3 %collective-permute-start.60 = (bf16[2,24,1664]{2,1,0:T(8,128)(2,1)}, bf16[2,24,1664]{2,1,0:T(8,128)(2,1)S(1)}, u32[]{:S(2)}, u32[]{:S(2)}) collective-permute-start(bf16[2,24,1664]{2,1,0:T(8,128)(2,1)} %get-tuple-element.446), channel_id=1, source_target_pairs={{0,2},{1,3},{2,0},{3,1},{4,6},{5,7},{6,4},{7,5},{8,10},{9,11},{10,... | collective-permute-start | bytes 479240 | tf_op jit(solution)/shard_map/ppermute | solution.py:1066
  245.8 15.8 %collective-permute-start.61 = (bf16[2,24,1664]{2,1,0:T(8,128)(2,1)}, bf16[2,24,1664]{2,1,0:T(8,128)(2,1)S(1)}, u32[]{:S(2)}, u32[]{:S(2)}) collective-permute-start(bf16[2,24,1664]{2,1,0:T(8,128)(2,1)} %get-tuple-element.447), channel_id=1, source_target_pairs={{0,3},{1,2},{2,1},{3,0},{4,7},{5,6},{6,5},{7,4},{8,11},{9,10},{10,... | collective-permute-start | bytes 479240 | tf_op jit(solution)/shard_map/ppermute | solution.py:1066
  (31 other events, 213.3 us)

commit v6 on v5

--- a/solution.py
+++ b/solution.py
@@ -683,36 +683,38 @@
         copy.wait()
     own = pl.ds(pl.multiple_of(core * half, half), half)
     far = pl.ds(pl.multiple_of((1 - core) * half, half), half)
-    outs, flat = [], None
-    for step, distance in enumerate((3, 1, 2, 0)):
-        q = distance ^ chip
-        lanes = pl.ds(pl.multiple_of(q * chunk, 128), chunk)
-        value, slope = gelu_parts(dot(normed[...], up[:, lanes]) + up_bias[0:1, lanes])
-        value = value.astype(bf16)
-        act[...] = value
-        slope_out[:, lanes] = slope.astype(bf16)
-        if step == 0:
-            for copy in late:
-                copy.wait()
-            flat = cot[...].reshape(rows, width)
-        blocks_here = pl.ds(pl.multiple_of(q * PLACES, PLACES), PLACES)
-        grad = dot_left(value, flat).astype(bf16)
-        down_grad[blocks_here] = grad.reshape(PLACES, chunk // PLACES, width)
+    outs = []
+    pair = 2 * chunk
+    for step, distances in enumerate(((3, 2), (1, 0))):
+        which = (1 - step) ^ (chip // 2)
+        lanes = pl.ds(pl.multiple_of(which * pair, 128), pair)
+        blocks_here = pl.ds(pl.multiple_of(which * 2 * PLACES, 2 * PLACES), 2 * PLACES)
+        for side, here in enumerate((own, far)):
+            value, slope = gelu_parts(dot(normed[here, :], up[:, lanes]) + up_bias[0:1, lanes])
+            value = value.astype(bf16)
+            act[here, :] = value
+            slope_out[here, lanes] = slope.astype(bf16)
+            if step == 0 and side == 0:
+                for copy in late:
+                    copy.wait()
+            part = dot(value, down[blocks_here].reshape(pair, width))
+            if side == 0:
+                keep_out[...] = part if step == 0 else keep_out[...] + part
+            elif step == 0:
+                far_sum[...] = part
+            else:
+                send_out[...] = (far_sum[...] + part).astype(bf16)
+        grad = dot_left(act[...], cot[...].reshape(rows, width)).astype(bf16)
+        down_grad[blocks_here] = grad.reshape(2 * PLACES, chunk // PLACES, width)
         if blocks == 4:
-            outs += [
+            ready = [
                 copy
                 for copy, where in fold_copies(down_grad, down_grads, chip, down_sem)
-                if where == distance
+                if where in distances
             ]
-            for copy in outs[-2 if distance else -1 :]:
+            for copy in ready:
                 copy.start()
-        down_part = down[blocks_here].reshape(chunk, width)
-        keep, send = dot(act[own, :], down_part), dot(act[far, :], down_part)
-        keep_out[...] = keep if step == 0 else keep_out[...] + keep
-        if step < 3:
-            far_sum[...] = send if step == 0 else far_sum[...] + send
-        else:
-            send_out[...] = (far_sum[...] + send).astype(bf16)
+            outs += ready
     if blocks != 4:
         outs.append(pltpu.make_async_copy(down_grad, down_grads[0], down_sem.at[0]))
         outs[0].start()
@@ -739,14 +741,14 @@
         [LOAD] * 2 + [HELD] * (4 + len(ups) + len(downs)),
         [info, normed, up_bias] + list(cots) + list(ups) + list(downs),
         scratch=[
-            pltpu.VMEM((rows, hidden // 4), bf16),
+            pltpu.VMEM((rows, hidden // 2), bf16),
             pltpu.VMEM((rows // 2, width), f32),
             pltpu.VMEM(whole, bf16),
             pltpu.SemaphoreType.DMA((4,)),
             pltpu.SemaphoreType.DMA((len(ups),)),
             pltpu.SemaphoreType.DMA((8,)),
         ],
-        limit=14,
+        limit=16,
         cost=(6 * rows * width * hidden, 24 * MIB),
     )
 
@@ -754,11 +756,11 @@
 def feed_back_kernel(info, slope, cot, up, down, back_out, low_out, grad_out, bias_out):
     rows, hidden = slope.shape
     width = up.shape[0]
-    chunk = hidden // 4
+    chunk = hidden // 2
     flat = cot[...].reshape(rows, width)
-    for q in range(4):
+    for q in range(2):
         lanes = slice(q * chunk, (q + 1) * chunk)
-        down_part = down[q * PLACES : (q + 1) * PLACES].reshape(chunk, width)
+        down_part = down[2 * q * PLACES : 2 * (q + 1) * PLACES].reshape(chunk, width)
         grad = (dot_right(flat, down_part) * slope[:, lanes].astype(f32)).astype(bf16)
         grad_out[:, lanes] = grad
         bias_out[:, lanes] = jnp.broadcast_to(
@@ -767,8 +769,6 @@
         back = dot_right(grad, up[:, lanes])
         if q == 0:
             back_out[...] = back
-        elif q < 3:
-            back_out[...] += back
         else:
             back = back_out[...] + back
             back_out[...] = back
@@ -788,20 +788,20 @@
         ],
         [LOAD] * 4,
         [info, slope, cot, up, down],
-        limit=10,
+        limit=12,
         cost=(4 * rows * width * hidden, 24 * MIB),
     )
 
 
 def weight_kernel(blocks, count, info, left, *refs):
     parts, outs, held, sem = refs[:count], refs[count:-2], refs[-2], refs[-1]
-    base = 0
-    for ref in parts:
-        for begin in range(0, ref.shape[1], 384):
-            size = min(384, ref.shape[1] - begin)
-            product = dot_left(left[...], ref[:, begin : begin + size]).astype(bf16)
-            held[:, base : base + size] = product
-            base += size
+    if count > 1:
+        right = jnp.concatenate([ref[...] for ref in parts], axis=1)
+        held[...] = dot_left(left[...], right).astype(bf16)
+    else:
+        for begin in range(0, held.shape[1], 768):
+            lanes = slice(begin, begin + 768)
+            held[:, lanes] = dot_left(left[...], parts[0][:, lanes]).astype(bf16)
     if blocks == 4:
         run_copies([copy for copy, _ in fold_copies(held, outs, info[1], sem)])
     else:
@@ -1357,19 +1357,11 @@
     )
     start_keep, start_send = project_back(info, dq, dk, dv, in_full)
     start_far, out_got = swap(start_send, "wide", 1), swap(out_send, "wide", 1)
+    down_keep, down_send = split(info, [[down_keep, down_got]], (2, down_rows), 1)
     up_keep, up_send = split(info, [up_fold], (2, 2, 2, rows))
-    down_keep, down_send = split(info, [[down_keep, down_got]], (2, down_rows), 1)
-    normed, start_keep, up_send, down_send = together(normed, start_keep, up_send, down_send)
+    start_far, out_got, up_send, down_send = together(start_far, out_got, up_send, down_send)
     up_got = swap(up_send, "narrow", 1)
     down_got = swap(down_send, "narrow", 2)
-    in_grads = weight_grad(info, normed, [dq, dk, dv], blocks)
-    start_far, out_got, up_got, down_got, *in_grads = together(
-        start_far, out_got, up_got, down_got, *in_grads
-    )
-    in_fold = folded(in_grads, (2, PLACES, rows, 3 * part))
-    up_keep, up_send = split(info, [[up_keep, up_got]], (2, 2, rows), 1)
-    start_far, up_send = together(start_far, up_send)
-    up_got = swap(up_send, "narrow", 2)
     args = [start_keep, start_far, start, grad_middle, turned, sums, bias_grad, spots, dq, dv]
     started = start_back(info, blocks, args + [out_keep, out_got], patches, chips)
     if not plane:
@@ -1380,13 +1372,20 @@
         ).reshape(chips, PLACES, rows, 2, part)
         out_grad = jnp.transpose(out_grad, (0, 3, 1, 2, 4)).reshape(width, part)
         started = [started[0], jnp.concatenate([started[1], out_grad], axis=1)]
-    up_got, grad_blocks, *small_grads = crossed([in_fold], up_got, *started)
+    normed, grad_blocks, *small_grads = together(normed, *started)
     small_fold = folded(small_grads, (2, PLACES, rows, SMALL + part))
     grad_first, grad_second = pick_turns(info, grad_blocks.reshape(2, block, width))
     grad_first = unspread_turn(grad_first, 0)
-    (grad_second,) = crossed([small_fold], *arrived([in_fold], grad_second))
+    in_grads = weight_grad(info, normed, [dq, dk, dv], blocks)
+    up_got, down_got, *in_grads = crossed([small_fold], up_got, down_got, *in_grads)
+    in_fold = folded(in_grads, (2, PLACES, rows, 3 * part))
+    up_keep, up_send = split(info, [[up_keep, up_got]], (2, 2, rows), 1)
+    grad_first, grad_second, up_send = crossed(
+        [in_fold], *arrived([small_fold], grad_first, grad_second, up_send)
+    )
     grad_second = unspread_turn(grad_second, 1)
-    (grad_first,) = arrived([small_fold], grad_first)
+    up_got = swap(up_send, "narrow", 2)
+    (down_keep,) = arrived([in_fold], down_keep)
     in_cut = split(info, [in_fold, small_fold], (2, PLACES, rows))
     in_got = [swap(in_cut[index], "narrow", index) for index in range(1, PLACES)]
     in_keep, down_keep, up_keep, up_got, grad_first, grad_second, *out_turns = together(

time: 272 us -> 267 us (0.982)
  the two profiles are of different devices: /device:TPU:17 before, /device:TPU:11 now
where the time goes in v6:
time: 267 us; the launch traced here: 262 us
  Pallas kernels  99 us (37%)
  waiting for transfers between devices  74.1 us (28%)
  starting transfers between devices  70 us (26%)
  local copies, waits for them, and re-layouts  10.7 us (4%)
  other arithmetic  6.58 us (2%)
    pallas_call x36, Pallas kernels, call(): pl.pallas_call(loaded if loads else kernel, out_shape=[shape for shape, _...  99 us
    ppermute x55, waiting for transfers between devices, swap(): return lax.ppermute(values, axis, [(i, i ^ bits) for i in range(size)])  69.4 us
    ppermute x55, starting transfers between devices, swap(): return lax.ppermute(values, axis, [(i, i ^ bits) for i in range(size)])  48.8 us
    ppermute x4, starting transfers between devices, unspread_turn(): lax.ppermute(part, ('wide', 'narrow'), [(b, a) for a, b in spread_perm(tu...  12.1 us
  transfers between devices with their start and end apart: 63, of which 27 were waited for; matrix products, arithmetic and copies ran while one was open for 3% of the time, Pallas kernels for 31%

profile of v6, /device:TPU:11, one launch (start us, length us, event | category | flops | bytes accessed | tf_op | source)
XLA Modules:
  0.0 261.9 jit_solution(4562414152840608758)
XLA Ops:
  7.7 2.4 collective-permute-start.2
  10.9 2.4 collective-permute-start.5
  17.7 8.5 %collective-permute-done.4.refs_2_ = bf16[2,24,1280]{2,1,0:T(8,128)(2,1)S(1)} collective-permute-done((bf16[2,24,1280]{2,1,0:T(8,128)(2,1)S(1)}, bf16[2,24,1280]{2,1,0:T(8,128)(2,1)S(1)}, u32[]{:S(2)}, u32[]{:S(2)}) %collective-permute-start.4) | collective-permute-done | bytes 122912 | tf_op jit(solution)/shard_map/ppermute | solution.py:1066
  26.2 2.6 %collective-permute-done.5.refs_3_ = bf16[2,24,1280]{2,1,0:T(8,128)(2,1)S(1)} collective-permute-done((bf16[2,24,1280]{2,1,0:T(8,128)(2,1)S(1)}, bf16[2,24,1280]{2,1,0:T(8,128)(2,1)S(1)}, u32[]{:S(2)}, u32[]{:S(2)}) %collective-permute-start.5) | collective-permute-done | bytes 122912 | tf_op jit(solution)/shard_map/ppermute | solution.py:1066
  28.9 2.7 %collective-permute-start.6 = (bf16[272,768]{1,0:T(8,128)(2,1)S(1)}, bf16[272,768]{1,0:T(8,128)(2,1)S(1)}, u32[]{:S(2)}, u32[]{:S(2)}) collective-permute-start(bf16[272,768]{1,0:T(8,128)(2,1)S(1)} %get-tuple-element.247), channel_id=1, source_target_pairs={{0,0},{1,1},{2,4},{3,5},{4,2},{5,3},{6,6},{7,7},{8,8},{9,9},{10,12... | collective-permute-start | bytes 1253384 | tf_op jit(solution)/shard_map/ppermute | solution.py:1272
  32.2 2.9 %collective-permute-start.7 = (bf16[2,120,768]{2,1,0:T(8,128)(2,1)S(1)}, bf16[2,120,768]{2,1,0:T(8,128)(2,1)S(1)}, u32[]{:S(2)}, u32[]{:S(2)}) collective-permute-start(bf16[2,120,768]{2,1,0:T(8,128)(2,1)S(1)} %shard_map.301.own), channel_id=1, source_target_pairs={{0,1},{1,0},{2,3},{3,2},{4,5},{5,4},{6,7},{7,6},{8,9},{9,8},{10,11... | collective-permute-start | bytes 1105928 | tf_op jit(solution)/shard_map/ppermute | solution.py:1066
  39.0 10.0 %collective-permute-done.7.far = bf16[2,120,768]{2,1,0:T(8,128)(2,1)S(1)} collective-permute-done((bf16[2,120,768]{2,1,0:T(8,128)(2,1)S(1)}, bf16[2,120,768]{2,1,0:T(8,128)(2,1)S(1)}, u32[]{:S(2)}, u32[]{:S(2)}) %collective-permute-start.7) | collective-permute-done | bytes 368672 | tf_op jit(solution)/shard_map/ppermute | solution.py:1066
  49.6 5.9 %collective-permute-done.13 = bf16[2,4,24,1280]{3,2,1,0:T(8,128)(2,1)S(1)} collective-permute-done((bf16[2,4,24,1280]{3,2,1,0:T(8,128)(2,1)S(1)}, bf16[2,4,24,1280]{3,2,1,0:T(8,128)(2,1)S(1)}, u32[]{:S(2)}, u32[]{:S(2)}) %collective-permute-start.13) | collective-permute-done | bytes 491552 | tf_op jit(solution)/shard_map/ppermute | solution.py:1066
  57.3 1.6 collective-permute-start.17
  58.9 5.6 %collective-permute-done.9.refs_1_ = bf16[2,24,1536]{2,1,0:T(8,128)(2,1)S(1)} collective-permute-done((bf16[2,24,1536]{2,1,0:T(8,128)(2,1)S(1)}, bf16[2,24,1536]{2,1,0:T(8,128)(2,1)S(1)}, u32[]{:S(2)}, u32[]{:S(2)}) %collective-permute-start.9) | collective-permute-done | bytes 147488 | tf_op jit(solution)/shard_map/ppermute | solution.py:1066
  65.4 3.2 %collective-permute-start.15 = (bf16[2,2,24,1536]{3,2,1,0:T(8,128)(2,1)S(1)}, bf16[2,2,24,1536]{3,2,1,0:T(8,128)(2,1)S(1)}, u32[]{:S(2)}, u32[]{:S(2)}) collective-permute-start(bf16[2,2,24,1536]{3,2,1,0:T(8,128)(2,1)S(1)} %shard_map.307.refs_0_), channel_id=1, source_target_pairs={{0,1},{1,0},{2,3},{3,2},{4,5},{5,4},{6,7},{7,6},{8,9},{9,8},{10,11... | collective-permute-start | bytes 884744 | tf_op jit(solution)/shard_map/ppermute | solution.py:1066
  69.2 7.0 %shard_map.305 = (bf16[1024,384]{1,0:T(8,128)(2,1)S(1)}, bf16[1024,384]{1,0:T(8,128)(2,1)S(1)}, bf16[1024,384]{1,0:T(8,128)(2,1)S(1)}, f32[1024,768]{1,0:T(8,128...) custom-call(s32[4]{0:T(128)S(1)} %pad_add_fusion.info, ...), custom_call_target="tpu_custom_call" | custom-call | flops 2013265920 | bytes 12582912 | tf_op jit(solution)/shard_map/pallas_call | solution.py:61
  80.5 1.5 collective-permute-start.19
  82.0 3.2 %collective-permute-done.20.refs_12_ = bf16[2,96,768]{2,1,0:T(8,128)(2,1)S(1)} collective-permute-done((bf16[2,96,768]{2,1,0:T(8,128)(2,1)S(1)}, bf16[2,96,768]{2,1,0:T(8,128)(2,1)S(1)}, u32[]{:S(2)}, u32[]{:S(2)}) %collective-permute-start.20) | collective-permute-done | bytes 294944 | tf_op jit(solution)/shard_map/ppermute | solution.py:1066
  85.2 4.9 %collective-permute-start.18 = (bf16[256,768]{1,0:T(8,128)(2,1)S(1)}, bf16[256,768]{1,0:T(8,128)(2,1)S(1)}, u32[]{:S(2)}, u32[]{:S(2)}) collective-permute-start(bf16[256,768]{1,0:T(8,128)(2,1)S(1)} %get-tuple-element.280), channel_id=1, source_target_pairs={{0,0},{1,1},{2,4},{3,5},{4,2},{5,3},{6,6},{7,7},{8,8},{9,9},{10,12... | collective-permute-start | bytes 1179656 | tf_op jit(solution)/shard_map/ppermute | solution.py:1291
  90.0 13.2 %shard_map.308 = (bf16[1024,384]{1,0:T(8,128)(2,1)S(1)}, f32[3,8,1024]{2,1,0:T(8,128)S(1)}) custom-call(s32[4]{0:T(128)S(1)} %pad_add_fusion.info, bf16[1024,384]{1,0:T(8,128)(2,1)S(1)} %get-tuple-element.275.q, bf16[1024,384]{1,0:T(8,128)(2,1)S(1)} %get-tuple-element.276.k, bf16[1024,384]{1,0:T(8,128)(2,1)S(1)} %get-tuple-element.277.v, ...), custom_call_target="tpu_custom_call" | custom-call | flops 2415919104 | bytes 4194304 | tf_op jit(solution)/shard_map/pallas_call | solution.py:61
  108.3 4.2 %shard_map.312 = (f32[1024,768]{1,0:T(8,128)S(1)}, bf16[1024,768]{1,0:T(8,128)(2,1)S(1)}, f32[8,1536]{1,0:T(8,128)S(1)}, bf16[768,768]{1,0:T(8,128)(2,1)S(1)}) custom-call(s32[4]{0:T(128)S(1)} %pad_add_fusion.info, bf16[1024,384]{1,0:T(8,128)(2,1)S(1)} %get-tuple-element.288.att.o, bf16[1024,384]{1,0:T(8,128)(2,1)S(1)} %collective-permute-done.24.att_far, ...), custom_call_target="tpu_custom_call" | custom-call | flops 1207959552 | bytes 12582912 | tf_op jit(solution)/shard_map/pallas_call | solution.py:61
  112.5 1.8 collective-permute-done.28
  115.2 14.5 %shard_map.314 = (f32[512,768]{1,0:T(8,128)S(1)}, bf16[512,768]{1,0:T(8,128)(2,1)S(1)}, bf16[1024,1536]{1,0:T(8,128)(2,1)S(1)}, bf16[768,1536]{1,0:T(8,128)(2,1)...) custom-call(s32[4]{0:T(128)S(1)} %pad_add_fusion.info, ...), custom_call_target="tpu_custom_call" | custom-call | flops 7247757312 | bytes 25165824 | tf_op jit(solution)/shard_map/pallas_call | solution.py:61
  131.3 5.8 %shard_map.315 = (f32[1024,768]{1,0:T(8,128)S(1)}, bf16[1024,768]{1,0:T(8,128)(2,1)S(1)}, bf16[1024,1536]{1,0:T(8,128)(2,1)S(1)}, f32[8,1536]{1,0:T(8,128)S(1)}) custom-call(s32[4]{0:T(128)S(1)} %pad_add_fusion.info, bf16[1024,1536]{1,0:T(8,128)(2,1)S(1)} %get-tuple-element.305.slope, bf16[4,256,768]{2,1,0:T(8,128)(2,1)S(1)} %get-tuple-element.306.cot, ...), custom_call_target="tpu_custom_call" | custom-call | flops 4831838208 | bytes 25165824 | tf_op jit(solution)/shard_map/pallas_call | solution.py:61
  137.1 6.3 %collective-permute-done.30.refs_1_ = bf16[4,96,768]{2,1,0:T(8,128)(2,1)S(1)} collective-permute-done((bf16[4,96,768]{2,1,0:T(8,128)(2,1)S(1)}, bf16[4,96,768]{2,1,0:T(8,128)(2,1)S(1)}, u32[]{:S(2)}, u32[]{:S(2)}) %collective-permute-start.30) | collective-permute-done | bytes 589856 | tf_op jit(solution)/shard_map/ppermute | solution.py:1066
  143.5 2.3 collective-permute-start.32
  146.5 1.3 collective-permute-start.34
  149.1 3.7 %shard_map.316 = (bf16[192,1536]{1,0:T(8,128)(2,1)S(1)}, bf16[192,1536]{1,0:T(8,128)(2,1)S(1)}, bf16[192,1536]{1,0:T(8,128)(2,1)S(1)}, bf16[96,1536]{1,0:T(8,128)(2,1)S(1)}, bf16[96,1536]{1,0:T(8,128)(2,1)S(1)}) custom-call(s32[4]{0:T(128)S(1)} %pad_add_fusion.info, bf16[1024,768]{1,0:T(8,128)(2,1)S(1)} %get-tuple-element.318.normed.left, ...), custom_call_target="tpu_custom_call" | custom-call | flops 2415919104 | bytes 8388608 | tf_op jit(solution)/shard_map/pallas_call | solution.py:61
  152.8 1.8 collective-permute-done.34
  159.2 5.6 %shard_map.318 = (f32[512,768]{1,0:T(8,128)S(1)}, bf16[1024,384]{1,0:T(8,128)(2,1)S(1)}, bf16[2,96,768]{2,1,0:T(8,128)(2,1)S(1)}, bf16[2,96,768]{2,1,0:T(8,128)(2,1)S(1)}, f32[8,768]{1,0:T(8,128)S(1)}) custom-call(s32[4]{0:T(128)S(1)} %pad_add_fusion.info, f32[1024,768]{1,0:T(8,128)S(1)} %get-tuple-element.332.back, ...), custom_call_target="tpu_custom_call" | custom-call | flops 1207959552 | bytes 14680064 | tf_op jit(solution)/shard_map/pallas_call | solution.py:61
  165.6 4.0 %collective-permute-start.39 = (bf16[256,768]{1,0:T(8,128)(2,1)S(1)}, bf16[256,768]{1,0:T(8,128)(2,1)S(1)}, u32[]{:S(2)}, u32[]{:S(2)}) collective-permute-start(bf16[256,768]{1,0:T(8,128)(2,1)S(1)} %get-tuple-element.353), channel_id=1, source_target_pairs={{0,0},{1,1},{4,2},{5,3},{2,4},{3,5},{6,6},{7,7},{8,8},{9,9},{12,10... | collective-permute-start | bytes 1179656 | tf_op jit(solution)/shard_map/ppermute | solution.py:1079
  171.9 12.5 %shard_map.320 = (bf16[1024,384]{1,0:T(8,128)(2,1)S(1)}, bf16[1024,384]{1,0:T(8,128)(2,1)S(1)}, bf16[1024,384]{1,0:T(8,128)(2,1)S(1)}) custom-call(s32[4]{0:T(128)S(1)} %pad_add_fusion.info, bf16[1024,384]{1,0:T(8,128)(2,1)S(1)} %get-tuple-element.275.q, bf16[1024,384]{1,0:T(8,128)(2,1)S(1)} %get-tuple-element.276.k, ...), custom_call_target="tpu_custom_call" | custom-call | flops 6039797760 | bytes 6291456 | tf_op jit(solution)/shard_map/pallas_call | solution.py:61
  184.5 3.1 %collective-permute-done.40 = bf16[256,768]{1,0:T(8,128)(2,1)S(1)} collective-permute-done((bf16[256,768]{1,0:T(8,128)(2,1)S(1)}, bf16[256,768]{1,0:T(8,128)(2,1)S(1)}, u32[]{:S(2)}, u32[]{:S(2)}) %collective-permute-start.40) | collective-permute-done | bytes 393248 | tf_op jit(solution)/shard_map/ppermute | solution.py:1079
  187.7 3.2 %shard_map.323 = (f32[512,768]{1,0:T(8,128)S(1)}, bf16[512,768]{1,0:T(8,128)(2,1)S(1)}) custom-call(s32[4]{0:T(128)S(1)} %pad_add_fusion.info, bf16[1024,384]{1,0:T(8,128)(2,1)S(1)} %get-tuple-element.361.dq.refs_8_.refs_0_, bf16[1024,384]{1,0:T(8,128)(2,1)S(1)} %get-tuple-element.362.dk.refs_1_, ...), custom_call_target="tpu_custom_call" | custom-call | flops 1811939328 | bytes 8388608 | tf_op jit(solution)/shard_map/pallas_call | solution.py:61
  193.7 4.8 %shard_map.326 = (bf16[512,768]{1,0:T(8,128)(2,1)S(1)}, bf16[192,512]{1,0:T(8,128)(2,1)S(1)}, bf16[192,512]{1,0:T(8,128)(2,1)S(1)}, bf16[192,512]{1,0:T(8,128)(2...) custom-call(s32[4]{0:T(128)S(1)} %pad_add_fusion.info, f32[512,768]{1,0:T(8,128)S(1)} %get-tuple-element.377.refs_0_, ...), custom_call_target="tpu_custom_call" | custom-call | flops 100663296 | bytes 10485760 | tf_op jit(solution)/shard_map/pallas_call | solution.py:61
  198.5 1.3 collective-permute-start.47
  200.9 1.8 collective-permute-start.46
  202.8 5.1 %shard_map.327 = (bf16[192,1152]{1,0:T(8,128)(2,1)S(1)}, bf16[192,1152]{1,0:T(8,128)(2,1)S(1)}, bf16[192,1152]{1,0:T(8,128)(2,1)S(1)}, bf16[96,1152]{1,0:T(8,128)(2,1)S(1)}, bf16[96,1152]{1,0:T(8,128)(2,1)S(1)}) custom-call(s32[4]{0:T(128)S(1)} %pad_add_fusion.info, bf16[1024,768]{1,0:T(8,128)(2,1)S(1)} %get-tuple-element.391.left, ...), custom_call_target="tpu_custom_call" | custom-call | flops 1811939328 | bytes 8388608 | tf_op jit(solution)/shard_map/pallas_call | solution.py:61
  207.8 1.4 collective-permute-done.46
  209.2 1.3 collective-permute-start.52
  210.8 1.3 shard_map.328
  212.1 5.9 %collective-permute-start.49 = (bf16[256,768]{1,0:T(8,128)(2,1)S(1)}, bf16[256,768]{1,0:T(8,128)(2,1)S(1)}, u32[]{:S(2)}, u32[]{:S(2)}) collective-permute-start(bf16[256,768]{1,0:T(8,128)(2,1)S(1)} %get-tuple-element.401), channel_id=1, source_target_pairs={{0,0},{1,1},{4,2},{5,3},{2,4},{3,5},{6,6},{7,7},{8,8},{9,9},{12,10... | collective-permute-start | bytes 1179656 | tf_op jit(solution)/shard_map/ppermute | solution.py:1079
  220.2 1.3 shard_map.329
  221.5 2.1 collective-permute-done.50.refs_8_
  225.0 2.1 collective-permute-start.57
  227.1 1.4 shard_map.331
  229.7 5.5 %collective-permute-done.54.refs_3_ = bf16[96,1152]{1,0:T(8,128)(2,1)S(1)} collective-permute-done((bf16[96,1152]{1,0:T(8,128)(2,1)}, bf16[96,1152]{1,0:T(8,128)(2,1)S(1)}, u32[]{:S(2)}, u32[]{:S(2)}) %collective-permute-start.54) | collective-permute-done | bytes 221216 | tf_op jit(solution)/shard_map/ppermute | solution.py:1066
  235.2 1.7 collective-permute-done.55.refs_4_
  236.9 1.6 shard_map.332
  238.9 2.4 collective-permute-start.61
  249.7 2.9 %collective-permute-done.60 = bf16[2,24,1664]{2,1,0:T(8,128)(2,1)S(1)} collective-permute-done((bf16[2,24,1664]{2,1,0:T(8,128)(2,1)}, bf16[2,24,1664]{2,1,0:T(8,128)(2,1)S(1)}, u32[]{:S(2)}, u32[]{:S(2)}) %collective-permute-start.60) | collective-permute-done | bytes 159776 | tf_op jit(solution)/shard_map/ppermute | solution.py:1066
  252.6 4.4 %collective-permute-done.61 = bf16[2,24,1664]{2,1,0:T(8,128)(2,1)S(1)} collective-permute-done((bf16[2,24,1664]{2,1,0:T(8,128)(2,1)}, bf16[2,24,1664]{2,1,0:T(8,128)(2,1)S(1)}, u32[]{:S(2)}, u32[]{:S(2)}) %collective-permute-start.61) | collective-permute-done | bytes 159776 | tf_op jit(solution)/shard_map/ppermute | solution.py:1066
  (181 shorter events, 63.9 us)
Async XLA Ops:
  7.7 21.2 %collective-permute-start.2 = (bf16[120,768]{1,0:T(8,128)(2,1)S(1)}, bf16[120,768]{1,0:T(8,128)(2,1)S(1)}, u32[]{:S(2)}, u32[]{:S(2)}) collective-permute-start(bf16[120,768]{1,0:T(8,128)(2,1)S(1)} %pad_maximum_fusion.2.refs_0_), channel_id=1, source_target_pairs={{0,2},{1,3},{2,0},{3,1},{4,6},{5,7},{6,4},{7,5},{8,10},{9,11},{10,... | collective-permute-start | bytes 552968 | tf_op jit(solution)/shard_map/ppermute | solution.py:1066
  10.9 15.4 %collective-permute-start.4 = (bf16[2,24,1280]{2,1,0:T(8,128)(2,1)S(1)}, bf16[2,24,1280]{2,1,0:T(8,128)(2,1)S(1)}, u32[]{:S(2)}, u32[]{:S(2)}) collective-permute-start(bf16[2,24,1280]{2,1,0:T(8,128)(2,1)S(1)} %shard_map.300.refs_0_), channel_id=1, source_target_pairs={{0,2},{1,3},{2,0},{3,1},{4,6},{5,7},{6,4},{7,5},{8,10},{9,11},{10,... | collective-permute-start | bytes 368648 | tf_op jit(solution)/shard_map/ppermute | solution.py:1066
  10.9 17.9 %collective-permute-start.5 = (bf16[2,24,1280]{2,1,0:T(8,128)(2,1)S(1)}, bf16[2,24,1280]{2,1,0:T(8,128)(2,1)S(1)}, u32[]{:S(2)}, u32[]{:S(2)}) collective-permute-start(bf16[2,24,1280]{2,1,0:T(8,128)(2,1)S(1)} %shard_map.300.refs_0_), channel_id=1, source_target_pairs={{0,3},{1,2},{2,1},{3,0},{4,7},{5,6},{6,5},{7,4},{8,11},{9,10},{10,... | collective-permute-start | bytes 368648 | tf_op jit(solution)/shard_map/ppermute | solution.py:1066
  28.9 20.1 %collective-permute-start.6 = (bf16[272,768]{1,0:T(8,128)(2,1)S(1)}, bf16[272,768]{1,0:T(8,128)(2,1)S(1)}, u32[]{:S(2)}, u32[]{:S(2)}) collective-permute-start(bf16[272,768]{1,0:T(8,128)(2,1)S(1)} %get-tuple-element.247), channel_id=1, source_target_pairs={{0,0},{1,1},{2,4},{3,5},{4,2},{5,3},{6,6},{7,7},{8,8},{9,9},{10,12... | collective-permute-start | bytes 1253384 | tf_op jit(solution)/shard_map/ppermute | solution.py:1272
  32.2 16.8 %collective-permute-start.7 = (bf16[2,120,768]{2,1,0:T(8,128)(2,1)S(1)}, bf16[2,120,768]{2,1,0:T(8,128)(2,1)S(1)}, u32[]{:S(2)}, u32[]{:S(2)}) collective-permute-start(bf16[2,120,768]{2,1,0:T(8,128)(2,1)S(1)} %shard_map.301.own), channel_id=1, source_target_pairs={{0,1},{1,0},{2,3},{3,2},{4,5},{5,4},{6,7},{7,6},{8,9},{9,8},{10,11... | collective-permute-start | bytes 1105928 | tf_op jit(solution)/shard_map/ppermute | solution.py:1066
  35.7 13.9 %collective-permute-start.12 = (bf16[2,4,24,1280]{3,2,1,0:T(8,128)(2,1)S(1)}, bf16[2,4,24,1280]{3,2,1,0:T(8,128)(2,1)S(1)}, u32[]{:S(2)}, u32[]{:S(2)}) collective-permute-start(bf16[2,4,24,1280]{3,2,1,0:T(8,128)(2,1)S(1)} %shard_map.304), channel_id=1, source_target_pairs={{0,8},{4,12},{8,0},{12,4},{16,24},{20,28},{24,16},{28,20},{1,9},{5... | collective-permute-start | bytes 1474568 | tf_op jit(solution)/shard_map/ppermute | solution.py:1066
  36.0 19.5 %collective-permute-start.13 = (bf16[2,4,24,1280]{3,2,1,0:T(8,128)(2,1)S(1)}, bf16[2,4,24,1280]{3,2,1,0:T(8,128)(2,1)S(1)}, u32[]{:S(2)}, u32[]{:S(2)}) collective-permute-start(bf16[2,4,24,1280]{3,2,1,0:T(8,128)(2,1)S(1)} %shard_map.304), channel_id=1, source_target_pairs={{0,16},{4,20},{8,24},{12,28},{16,0},{20,4},{24,8},{28,12},{1,17},{... | collective-permute-start | bytes 1474568 | tf_op jit(solution)/shard_map/ppermute | solution.py:1066
  37.3 19.3 %collective-permute-start.14 = (bf16[2,4,24,1280]{3,2,1,0:T(8,128)(2,1)S(1)}, bf16[2,4,24,1280]{3,2,1,0:T(8,128)(2,1)S(1)}, u32[]{:S(2)}, u32[]{:S(2)}) collective-permute-start(bf16[2,4,24,1280]{3,2,1,0:T(8,128)(2,1)S(1)} %shard_map.304), channel_id=1, source_target_pairs={{0,24},{4,28},{8,16},{12,20},{16,8},{20,12},{24,0},{28,4},{1,25},{... | collective-permute-start | bytes 1474568 | tf_op jit(solution)/shard_map/ppermute | solution.py:1066
  49.0 15.8 %collective-permute-start.8 = (bf16[272,768]{1,0:T(8,128)(2,1)S(1)}, bf16[272,768]{1,0:T(8,128)(2,1)S(1)}, u32[]{:S(2)}, u32[]{:S(2)}) collective-permute-start(bf16[272,768]{1,0:T(8,128)(2,1)S(1)} %get-tuple-element.253), channel_id=1, source_target_pairs={{0,1},{1,0},{2,5},{3,4},{4,3},{5,2},{6,7},{7,6},{8,9},{9,8},{10,13... | collective-permute-start | bytes 1253384 | tf_op jit(solution)/shard_map/ppermute | solution.py:1277
  49.0 15.5 %collective-permute-start.9 = (bf16[2,24,1536]{2,1,0:T(8,128)(2,1)S(1)}, bf16[2,24,1536]{2,1,0:T(8,128)(2,1)S(1)}, u32[]{:S(2)}, u32[]{:S(2)}) collective-permute-start(bf16[2,24,1536]{2,1,0:T(8,128)(2,1)S(1)} %shard_map.302.refs_0_), channel_id=1, source_target_pairs={{0,2},{1,3},{2,0},{3,1},{4,6},{5,7},{6,4},{7,5},{8,10},{9,11},{10,... | collective-permute-start | bytes 442376 | tf_op jit(solution)/shard_map/ppermute | solution.py:1066
  56.6 19.6 %collective-permute-start.16 = (bf16[5,96,768]{2,1,0:T(8,128)(2,1)S(1)}, bf16[5,96,768]{2,1,0:T(8,128)(2,1)S(1)}, u32[]{:S(2)}, u32[]{:S(2)}) collective-permute-start(bf16[5,96,768]{2,1,0:T(8,128)(2,1)S(1)} %shard_map.303.own.refs_9_), channel_id=1, source_target_pairs={{0,8},{4,12},{8,0},{12,4},{16,24},{20,28},{24,16},{28,20},{1,9},{5... | collective-permute-start | bytes 2211848 | tf_op jit(solution)/shard_map/ppermute | solution.py:1066
  57.3 18.9 %collective-permute-start.17 = (bf16[5,96,768]{2,1,0:T(8,128)(2,1)S(1)}, bf16[5,96,768]{2,1,0:T(8,128)(2,1)S(1)}, u32[]{:S(2)}, u32[]{:S(2)}) collective-permute-start(bf16[5,96,768]{2,1,0:T(8,128)(2,1)S(1)} %shard_map.303.own.refs_9_), channel_id=1, source_target_pairs={{0,16},{4,20},{8,24},{12,28},{16,0},{20,4},{24,8},{28,12},{1,17},{... | collective-permute-start | bytes 2211848 | tf_op jit(solution)/shard_map/ppermute | solution.py:1066
  58.9 9.7 %collective-permute-start.10 = (bf16[272,768]{1,0:T(8,128)(2,1)S(1)}, bf16[272,768]{1,0:T(8,128)(2,1)S(1)}, u32[]{:S(2)}, u32[]{:S(2)}) collective-permute-start(bf16[272,768]{1,0:T(8,128)(2,1)S(1)} %collective-permute-done.6.refs_0_), channel_id=1, source_target_pairs={{0,4},{4,0},{8,12},{12,8},{16,20},{20,16},{24,28},{28,24},{1,5},{5... | collective-permute-start | bytes 1253384 | tf_op jit(solution)/shard_map/ppermute | solution.py:1066
  65.4 10.8 %collective-permute-start.15 = (bf16[2,2,24,1536]{3,2,1,0:T(8,128)(2,1)S(1)}, bf16[2,2,24,1536]{3,2,1,0:T(8,128)(2,1)S(1)}, u32[]{:S(2)}, u32[]{:S(2)}) collective-permute-start(bf16[2,2,24,1536]{3,2,1,0:T(8,128)(2,1)S(1)} %shard_map.307.refs_0_), channel_id=1, source_target_pairs={{0,1},{1,0},{2,3},{3,2},{4,5},{5,4},{6,7},{7,6},{8,9},{9,8},{10,11... | collective-permute-start | bytes 884744 | tf_op jit(solution)/shard_map/ppermute | solution.py:1066
  76.8 8.3 %collective-permute-start.20 = (bf16[2,96,768]{2,1,0:T(8,128)(2,1)S(1)}, bf16[2,96,768]{2,1,0:T(8,128)(2,1)S(1)}, u32[]{:S(2)}, u32[]{:S(2)}) collective-permute-start(bf16[2,96,768]{2,1,0:T(8,128)(2,1)S(1)} %get-tuple-element.285), channel_id=1, source_target_pairs={{0,8},{4,12},{8,0},{12,4},{16,24},{20,28},{24,16},{28,20},{1,9},{5... | collective-permute-start | bytes 884744 | tf_op jit(solution)/shard_map/ppermute | solution.py:1066
  77.8 25.5 %collective-permute-start.22 = (bf16[2,4,24,1536]{3,2,1,0:T(8,128)(2,1)S(1)}, bf16[2,4,24,1536]{3,2,1,0:T(8,128)(2,1)S(1)}, u32[]{:S(2)}, u32[]{:S(2)}) collective-permute-start(bf16[2,4,24,1536]{3,2,1,0:T(8,128)(2,1)S(1)} %bitcast.56), channel_id=1, source_target_pairs={{0,8},{4,12},{8,0},{12,4},{16,24},{20,28},{24,16},{28,20},{1,9},{5... | collective-permute-start | bytes 1769480 | tf_op jit(solution)/shard_map/ppermute | solution.py:1066
  79.0 24.3 %collective-permute-start.23 = (bf16[2,4,24,1536]{3,2,1,0:T(8,128)(2,1)S(1)}, bf16[2,4,24,1536]{3,2,1,0:T(8,128)(2,1)S(1)}, u32[]{:S(2)}, u32[]{:S(2)}) collective-permute-start(bf16[2,4,24,1536]{3,2,1,0:T(8,128)(2,1)S(1)} %bitcast.57), channel_id=1, source_target_pairs={{0,16},{4,20},{8,24},{12,28},{16,0},{20,4},{24,8},{28,12},{1,17},{... | collective-permute-start | bytes 1769480 | tf_op jit(solution)/shard_map/ppermute | solution.py:1066
  80.3 23.0 %collective-permute-start.21 = (bf16[3,96,768]{2,1,0:T(8,128)(2,1)S(1)}, bf16[3,96,768]{2,1,0:T(8,128)(2,1)S(1)}, u32[]{:S(2)}, u32[]{:S(2)}) collective-permute-start(bf16[3,96,768]{2,1,0:T(8,128)(2,1)S(1)} %get-tuple-element.286), channel_id=1, source_target_pairs={{0,16},{4,20},{8,24},{12,28},{16,0},{20,4},{24,8},{28,12},{1,17},{... | collective-permute-start | bytes 1327112 | tf_op jit(solution)/shard_map/ppermute | solution.py:1066
  80.5 22.8 %collective-permute-start.19 = (bf16[256,768]{1,0:T(8,128)(2,1)S(1)}, bf16[256,768]{1,0:T(8,128)(2,1)S(1)}, u32[]{:S(2)}, u32[]{:S(2)}) collective-permute-start(bf16[256,768]{1,0:T(8,128)(2,1)S(1)} %get-tuple-element.281), channel_id=1, source_target_pairs={{0,1},{1,0},{2,5},{3,4},{4,3},{5,2},{6,7},{7,6},{8,9},{9,8},{10,13... | collective-permute-start | bytes 1179656 | tf_op jit(solution)/shard_map/ppermute | solution.py:1301
  85.2 18.1 %collective-permute-start.18 = (bf16[256,768]{1,0:T(8,128)(2,1)S(1)}, bf16[256,768]{1,0:T(8,128)(2,1)S(1)}, u32[]{:S(2)}, u32[]{:S(2)}) collective-permute-start(bf16[256,768]{1,0:T(8,128)(2,1)S(1)} %get-tuple-element.280), channel_id=1, source_target_pairs={{0,0},{1,1},{2,4},{3,5},{4,2},{5,3},{6,6},{7,7},{8,8},{9,9},{10,12... | collective-permute-start | bytes 1179656 | tf_op jit(solution)/shard_map/ppermute | solution.py:1291
  104.9 10.3 %collective-permute-start.26 = (bf16[256,768]{1,0:T(8,128)(2,1)S(1)}, bf16[256,768]{1,0:T(8,128)(2,1)S(1)}, u32[]{:S(2)}, u32[]{:S(2)}) collective-permute-start(bf16[256,768]{1,0:T(8,128)(2,1)S(1)} %collective-permute-done.18.refs_0_), channel_id=1, source_target_pairs={{0,4},{4,0},{8,12},{12,8},{16,20},{20,16},{24,28},{28,24},{1,5},{5... | collective-permute-start | bytes 1179656 | tf_op jit(solution)/shard_map/ppermute | solution.py:1066
  105.4 9.8 %collective-permute-start.27 = (bf16[256,768]{1,0:T(8,128)(2,1)S(1)}, bf16[256,768]{1,0:T(8,128)(2,1)S(1)}, u32[]{:S(2)}, u32[]{:S(2)}) collective-permute-start(bf16[256,768]{1,0:T(8,128)(2,1)S(1)} %collective-permute-done.19.refs_1_), channel_id=1, source_target_pairs={{0,4},{4,0},{8,12},{12,8},{16,20},{20,16},{24,28},{28,24},{1,5},{5... | collective-permute-start | bytes 1179656 | tf_op jit(solution)/shard_map/ppermute | solution.py:1066
  106.1 8.2 %collective-permute-start.28 = (bf16[1,4,24,1536]{3,2,1,0:T(8,128)(2,1)S(1)}, bf16[1,4,24,1536]{3,2,1,0:T(8,128)(2,1)S(1)}, u32[]{:S(2)}, u32[]{:S(2)}) collective-permute-start(bf16[1,4,24,1536]{3,2,1,0:T(8,128)(2,1)S(1)} %get-tuple-element.302), channel_id=1, source_target_pairs={{0,8},{4,12},{8,0},{12,4},{16,24},{20,28},{24,16},{28,20},{1,9},{5... | collective-permute-start | bytes 884744 | tf_op jit(solution)/shard_map/ppermute | solution.py:1066
  107.0 8.2 %collective-permute-start.29 = (bf16[1,4,24,1536]{3,2,1,0:T(8,128)(2,1)S(1)}, bf16[1,4,24,1536]{3,2,1,0:T(8,128)(2,1)S(1)}, u32[]{:S(2)}, u32[]{:S(2)}) collective-permute-start(bf16[1,4,24,1536]{3,2,1,0:T(8,128)(2,1)S(1)} %get-tuple-element.303), channel_id=1, source_target_pairs={{0,16},{4,20},{8,24},{12,28},{16,0},{20,4},{24,8},{28,12},{1,17},{... | collective-permute-start | bytes 884744 | tf_op jit(solution)/shard_map/ppermute | solution.py:1066
  129.8 13.7 %collective-permute-start.30 = (bf16[4,96,768]{2,1,0:T(8,128)(2,1)S(1)}, bf16[4,96,768]{2,1,0:T(8,128)(2,1)S(1)}, u32[]{:S(2)}, u32[]{:S(2)}) collective-permute-start(bf16[4,96,768]{2,1,0:T(8,128)(2,1)S(1)} %get-tuple-element.314), channel_id=1, source_target_pairs={{0,8},{4,12},{8,0},{12,4},{16,24},{20,28},{24,16},{28,20},{1,9},{5... | collective-permute-start | bytes 1769480 | tf_op jit(solution)/shard_map/ppermute | solution.py:1066
  130.1 13.4 %collective-permute-start.31 = (bf16[4,96,768]{2,1,0:T(8,128)(2,1)S(1)}, bf16[4,96,768]{2,1,0:T(8,128)(2,1)S(1)}, u32[]{:S(2)}, u32[]{:S(2)}) collective-permute-start(bf16[4,96,768]{2,1,0:T(8,128)(2,1)S(1)} %get-tuple-element.315), channel_id=1, source_target_pairs={{0,16},{4,20},{8,24},{12,28},{16,0},{20,4},{24,8},{28,12},{1,17},{... | collective-permute-start | bytes 1769480 | tf_op jit(solution)/shard_map/ppermute | solution.py:1066
  143.5 12.1 %collective-permute-start.32 = (bf16[1024,768]{1,0:T(8,128)(2,1)S(1)}, bf16[1024,768]{1,0:T(8,128)(2,1)S(1)}, u32[]{:S(2)}, u32[]{:S(2)}) collective-permute-start(bf16[1024,768]{1,0:T(8,128)(2,1)S(1)} %get-tuple-element.316), channel_id=1, source_target_pairs={{0,4},{4,0},{8,12},{12,8},{16,20},{20,16},{24,28},{28,24},{1,5},{5... | collective-permute-start | bytes 4718600 | tf_op jit(solution)/shard_map/ppermute | solution.py:1066
  145.8 9.7 %collective-permute-start.33 = (bf16[512,768]{1,0:T(8,128)(2,1)S(1)}, bf16[512,768]{1,0:T(8,128)(2,1)S(1)}, u32[]{:S(2)}, u32[]{:S(2)}) collective-permute-start(bf16[512,768]{1,0:T(8,128)(2,1)S(1)} %get-tuple-element.317), channel_id=1, source_target_pairs={{0,4},{4,0},{8,12},{12,8},{16,20},{20,16},{24,28},{28,24},{1,5},{5... | collective-permute-start | bytes 2359304 | tf_op jit(solution)/shard_map/ppermute | solution.py:1066
  146.5 8.1 %collective-permute-start.34 = (bf16[2,96,768]{2,1,0:T(8,128)(2,1)S(1)}, bf16[2,96,768]{2,1,0:T(8,128)(2,1)S(1)}, u32[]{:S(2)}, u32[]{:S(2)}) collective-permute-start(bf16[2,96,768]{2,1,0:T(8,128)(2,1)S(1)} %get-tuple-element.329), channel_id=1, source_target_pairs={{0,16},{4,20},{8,24},{12,28},{16,0},{20,4},{24,8},{28,12},{1,17},{... | collective-permute-start | bytes 884744 | tf_op jit(solution)/shard_map/ppermute | solution.py:1066
  155.6 14.2 %collective-permute-start.37 = (bf16[192,1536]{1,0:T(8,128)(2,1)S(1)}, bf16[192,1536]{1,0:T(8,128)(2,1)S(1)}, u32[]{:S(2)}, u32[]{:S(2)}) collective-permute-start(bf16[192,1536]{1,0:T(8,128)(2,1)S(1)} %get-tuple-element.342), channel_id=1, source_target_pairs={{0,8},{4,12},{8,0},{12,4},{16,24},{20,28},{24,16},{28,20},{1,9},{5... | collective-permute-start | bytes 1769480 | tf_op jit(solution)/shard_map/ppermute | solution.py:1066
  156.8 12.9 %collective-permute-start.38 = (bf16[192,1536]{1,0:T(8,128)(2,1)S(1)}, bf16[192,1536]{1,0:T(8,128)(2,1)S(1)}, u32[]{:S(2)}, u32[]{:S(2)}) collective-permute-start(bf16[192,1536]{1,0:T(8,128)(2,1)S(1)} %get-tuple-element.343), channel_id=1, source_target_pairs={{0,16},{4,20},{8,24},{12,28},{16,0},{20,4},{24,8},{28,12},{1,17},{... | collective-permute-start | bytes 1769480 | tf_op jit(solution)/shard_map/ppermute | solution.py:1066
  158.2 11.6 %collective-permute-start.36 = (bf16[2,96,768]{2,1,0:T(8,128)(2,1)S(1)}, bf16[2,96,768]{2,1,0:T(8,128)(2,1)S(1)}, u32[]{:S(2)}, u32[]{:S(2)}) collective-permute-start(bf16[2,96,768]{2,1,0:T(8,128)(2,1)S(1)} %get-tuple-element.341), channel_id=1, source_target_pairs={{0,1},{1,0},{2,3},{3,2},{4,5},{5,4},{6,7},{7,6},{8,9},{9,8},{10,11... | collective-permute-start | bytes 884744 | tf_op jit(solution)/shard_map/ppermute | solution.py:1066
  165.6 18.8 %collective-permute-start.39 = (bf16[256,768]{1,0:T(8,128)(2,1)S(1)}, bf16[256,768]{1,0:T(8,128)(2,1)S(1)}, u32[]{:S(2)}, u32[]{:S(2)}) collective-permute-start(bf16[256,768]{1,0:T(8,128)(2,1)S(1)} %get-tuple-element.353), channel_id=1, source_target_pairs={{0,0},{1,1},{4,2},{5,3},{2,4},{3,5},{6,6},{7,7},{8,8},{9,9},{12,10... | collective-permute-start | bytes 1179656 | tf_op jit(solution)/shard_map/ppermute | solution.py:1079
  169.6 18.0 %collective-permute-start.40 = (bf16[256,768]{1,0:T(8,128)(2,1)S(1)}, bf16[256,768]{1,0:T(8,128)(2,1)S(1)}, u32[]{:S(2)}, u32[]{:S(2)}) collective-permute-start(bf16[256,768]{1,0:T(8,128)(2,1)S(1)} %get-tuple-element.354), channel_id=1, source_target_pairs={{1,0},{0,1},{5,2},{4,3},{3,4},{2,5},{7,6},{6,7},{9,8},{8,9},{13,10... | collective-permute-start | bytes 1179656 | tf_op jit(solution)/shard_map/ppermute | solution.py:1079
  170.4 17.2 %collective-permute-start.41 = (bf16[96,1536]{1,0:T(8,128)(2,1)S(1)}, bf16[96,1536]{1,0:T(8,128)(2,1)S(1)}, u32[]{:S(2)}, u32[]{:S(2)}) collective-permute-start(bf16[96,1536]{1,0:T(8,128)(2,1)S(1)} %get-tuple-element.359), channel_id=1, source_target_pairs={{0,16},{4,20},{8,24},{12,28},{16,0},{20,4},{24,8},{28,12},{1,17},{... | collective-permute-start | bytes 884744 | tf_op jit(solution)/shard_map/ppermute | solution.py:1066
  171.7 15.9 %collective-permute-start.42 = (bf16[96,1536]{1,0:T(8,128)(2,1)S(1)}, bf16[96,1536]{1,0:T(8,128)(2,1)S(1)}, u32[]{:S(2)}, u32[]{:S(2)}) collective-permute-start(bf16[96,1536]{1,0:T(8,128)(2,1)S(1)} %get-tuple-element.360), channel_id=1, source_target_pairs={{0,8},{4,12},{8,0},{12,4},{16,24},{20,28},{24,16},{28,20},{1,9},{5... | collective-permute-start | bytes 884744 | tf_op jit(solution)/shard_map/ppermute | solution.py:1066
  193.7 15.6 %collective-permute-start.45 = (bf16[2,2,24,1536]{3,2,1,0:T(8,128)(2,1)S(1)}, bf16[2,2,24,1536]{3,2,1,0:T(8,128)(2,1)S(1)}, u32[]{:S(2)}, u32[]{:S(2)}) collective-permute-start(bf16[2,2,24,1536]{3,2,1,0:T(8,128)(2,1)S(1)} %get-tuple-element.374), channel_id=1, source_target_pairs={{0,1},{1,0},{2,3},{3,2},{4,5},{5,4},{6,7},{7,6},{8,9},{9,8},{10,11... | collective-permute-start | bytes 884744 | tf_op jit(solution)/shard_map/ppermute | solution.py:1066
  198.5 10.7 %collective-permute-start.47 = (bf16[192,512]{1,0:T(8,128)(2,1)S(1)}, bf16[192,512]{1,0:T(8,128)(2,1)S(1)}, u32[]{:S(2)}, u32[]{:S(2)}) collective-permute-start(bf16[192,512]{1,0:T(8,128)(2,1)S(1)} %get-tuple-element.397), channel_id=1, source_target_pairs={{0,8},{4,12},{8,0},{12,4},{16,24},{20,28},{24,16},{28,20},{1,9},{5... | collective-permute-start | bytes 589832 | tf_op jit(solution)/shard_map/ppermute | solution.py:1066
  199.8 9.4 %collective-permute-start.48 = (bf16[192,512]{1,0:T(8,128)(2,1)S(1)}, bf16[192,512]{1,0:T(8,128)(2,1)S(1)}, u32[]{:S(2)}, u32[]{:S(2)}) collective-permute-start(bf16[192,512]{1,0:T(8,128)(2,1)S(1)} %get-tuple-element.398), channel_id=1, source_target_pairs={{0,16},{4,20},{8,24},{12,28},{16,0},{20,4},{24,8},{28,12},{1,17},{... | collective-permute-start | bytes 589832 | tf_op jit(solution)/shard_map/ppermute | solution.py:1066
  200.9 8.3 %collective-permute-start.46 = (bf16[96,768]{1,0:T(8,128)(2,1)S(1)}, bf16[96,768]{1,0:T(8,128)(2,1)S(1)}, u32[]{:S(2)}, u32[]{:S(2)}) collective-permute-start(bf16[96,768]{1,0:T(8,128)(2,1)S(1)} %get-tuple-element.375), channel_id=1, source_target_pairs={{0,2},{1,3},{2,0},{3,1},{4,6},{5,7},{6,4},{7,5},{8,10},{9,11},{10,... | collective-permute-start | bytes 442376 | tf_op jit(solution)/shard_map/ppermute | solution.py:1066
  209.2 15.7 %collective-permute-start.52 = (bf16[192,1152]{1,0:T(8,128)(2,1)S(1)}, bf16[192,1152]{1,0:T(8,128)(2,1)S(1)}, u32[]{:S(2)}, u32[]{:S(2)}) collective-permute-start(bf16[192,1152]{1,0:T(8,128)(2,1)S(1)} %get-tuple-element.415), channel_id=1, source_target_pairs={{0,8},{4,12},{8,0},{12,4},{16,24},{20,28},{24,16},{28,20},{1,9},{5... | collective-permute-start | bytes 1327112 | tf_op jit(solution)/shard_map/ppermute | solution.py:1066
  210.5 14.4 %collective-permute-start.53 = (bf16[192,1152]{1,0:T(8,128)(2,1)S(1)}, bf16[192,1152]{1,0:T(8,128)(2,1)S(1)}, u32[]{:S(2)}, u32[]{:S(2)}) collective-permute-start(bf16[192,1152]{1,0:T(8,128)(2,1)S(1)} %get-tuple-element.416), channel_id=1, source_target_pairs={{0,16},{4,20},{8,24},{12,28},{16,0},{20,4},{24,8},{28,12},{1,17},{... | collective-permute-start | bytes 1327112 | tf_op jit(solution)/shard_map/ppermute | solution.py:1066
  212.1 12.8 %collective-permute-start.49 = (bf16[256,768]{1,0:T(8,128)(2,1)S(1)}, bf16[256,768]{1,0:T(8,128)(2,1)S(1)}, u32[]{:S(2)}, u32[]{:S(2)}) collective-permute-start(bf16[256,768]{1,0:T(8,128)(2,1)S(1)} %get-tuple-element.401), channel_id=1, source_target_pairs={{0,0},{1,1},{4,2},{5,3},{2,4},{3,5},{6,6},{7,7},{8,8},{9,9},{12,10... | collective-permute-start | bytes 1179656 | tf_op jit(solution)/shard_map/ppermute | solution.py:1079
  225.0 17.3 %collective-permute-start.57 = (bf16[256,768]{1,0:T(8,128)(2,1)}, bf16[256,768]{1,0:T(8,128)(2,1)}, u32[]{:S(2)}, u32[]{:S(2)}) collective-permute-start(bf16[256,768]{1,0:T(8,128)(2,1)} %get-tuple-element.434), channel_id=1, source_target_pairs={{1,0},{0,1},{5,2},{4,3},{3,4},{2,5},{7,6},{6,7},{9,8},{8,9},{13,10... | collective-permute-start | bytes 1179656 | tf_op jit(solution)/shard_map/ppermute | solution.py:1079
  229.7 12.6 %collective-permute-start.56 = (bf16[2,24,1536]{2,1,0:T(8,128)(2,1)}, bf16[2,24,1536]{2,1,0:T(8,128)(2,1)}, u32[]{:S(2)}, u32[]{:S(2)}) collective-permute-start(bf16[2,24,1536]{2,1,0:T(8,128)(2,1)} %get-tuple-element.432), channel_id=1, source_target_pairs={{0,2},{1,3},{2,0},{3,1},{4,6},{5,7},{6,4},{7,5},{8,10},{9,11},{10,... | collective-permute-start | bytes 442376 | tf_op jit(solution)/shard_map/ppermute | solution.py:1066
  238.6 11.1 %collective-permute-start.59 = (bf16[2,24,1664]{2,1,0:T(8,128)(2,1)}, bf16[2,24,1664]{2,1,0:T(8,128)(2,1)S(1)}, u32[]{:S(2)}, u32[]{:S(2)}) collective-permute-start(bf16[2,24,1664]{2,1,0:T(8,128)(2,1)} %get-tuple-element.445), channel_id=1, source_target_pairs={{0,1},{1,0},{2,3},{3,2},{4,5},{5,4},{6,7},{7,6},{8,9},{9,8},{10,11... | collective-permute-start | bytes 479240 | tf_op jit(solution)/shard_map/ppermute | solution.py:1066
  238.9 13.7 %collective-permute-start.60 = (bf16[2,24,1664]{2,1,0:T(8,128)(2,1)}, bf16[2,24,1664]{2,1,0:T(8,128)(2,1)S(1)}, u32[]{:S(2)}, u32[]{:S(2)}) collective-permute-start(bf16[2,24,1664]{2,1,0:T(8,128)(2,1)} %get-tuple-element.446), channel_id=1, source_target_pairs={{0,2},{1,3},{2,0},{3,1},{4,6},{5,7},{6,4},{7,5},{8,10},{9,11},{10,... | collective-permute-start | bytes 479240 | tf_op jit(solution)/shard_map/ppermute | solution.py:1066
  238.9 18.1 %collective-permute-start.61 = (bf16[2,24,1664]{2,1,0:T(8,128)(2,1)}, bf16[2,24,1664]{2,1,0:T(8,128)(2,1)S(1)}, u32[]{:S(2)}, u32[]{:S(2)}) collective-permute-start(bf16[2,24,1664]{2,1,0:T(8,128)(2,1)} %get-tuple-element.447), channel_id=1, source_target_pairs={{0,3},{1,2},{2,1},{3,0},{4,7},{5,6},{6,5},{7,4},{8,11},{9,10},{10,... | collective-permute-start | bytes 479240 | tf_op jit(solution)/shard_map/ppermute | solution.py:1066
  (31 other events, 173.4 us)

commit v7 on v6

--- a/solution.py
+++ b/solution.py
@@ -504,7 +504,7 @@
     for b in range(4):
         many = (b + 1) * block
         here = slice(b * block, (b + 1) * block)
-        grads = []
+        low_probs, low_scores, own_qs, own_gs = [], [], [], []
         for h in range(2):
             ask = jnp.where(side == h, turned_q[:, here].astype(f32), 0.0).astype(bf16)
             ask_g = jnp.where(side == h, turned_g[:, here].astype(f32), 0.0).astype(bf16)
@@ -512,12 +512,16 @@
             probs = jnp.exp(scores - total[0, h : h + 1, here])
             grad_probs = dot(v[:many, :], ask_g)
             grad_scores = (probs * (grad_probs - inner[h][:, here])).astype(bf16)
-            own_q = jnp.where(flat == h, q[here, :].astype(f32), 0.0).astype(bf16)
-            own_g = jnp.where(flat == h, g[here, :].astype(f32), 0.0).astype(bf16)
-            dv_sum[:many, :] += dot(probs.astype(bf16), own_g)
-            dk_sum[:many, :] += dot(grad_scores, own_q)
-            grads.append(dot(turned_k[64 * h : 64 * h + 64, :many], grad_scores))
-        dq[here, :] = (jnp.concatenate(grads, axis=0).T * 0.125).astype(bf16)
+            own_qs.append(jnp.where(flat == h, q[here, :].astype(f32), 0.0).astype(bf16))
+            own_gs.append(jnp.where(flat == h, g[here, :].astype(f32), 0.0).astype(bf16))
+            low_probs.append(probs.astype(bf16))
+            low_scores.append(grad_scores)
+        dv_sum[:many, :] += dot(jnp.concatenate(low_probs, axis=1), jnp.concatenate(own_gs))
+        dk_sum[:many, :] += dot(jnp.concatenate(low_scores, axis=1), jnp.concatenate(own_qs))
+        both = dot(turned_k[:, :many], jnp.concatenate(low_scores, axis=1))
+        half = both.shape[1] // 2
+        mixed = jnp.concatenate([both[:64, :half], both[64:, half:]], axis=0)
+        dq[here, :] = (mixed.T * 0.125).astype(bf16)
         base += many
     dk[...] = dk_sum[...].astype(bf16)
     dv[...] = dv_sum[...].astype(bf16)
@@ -753,19 +757,18 @@
     )
 
 
-def feed_back_kernel(info, slope, cot, up, down, back_out, low_out, grad_out, bias_out):
+def feed_back_kernel(chips, info, slope, cot, up, down, back_out, low_out, grad_out, bias_out):
     rows, hidden = slope.shape
     width = up.shape[0]
     chunk = hidden // 2
     flat = cot[...].reshape(rows, width)
+    sums = []
     for q in range(2):
         lanes = slice(q * chunk, (q + 1) * chunk)
         down_part = down[2 * q * PLACES : 2 * (q + 1) * PLACES].reshape(chunk, width)
         grad = (dot_right(flat, down_part) * slope[:, lanes].astype(f32)).astype(bf16)
         grad_out[:, lanes] = grad
-        bias_out[:, lanes] = jnp.broadcast_to(
-            jnp.sum(grad.astype(f32), axis=0, keepdims=True), (8, chunk)
-        )
+        sums.append(jnp.sum(grad.astype(f32), axis=0, keepdims=True))
         back = dot_right(grad, up[:, lanes])
         if q == 0:
             back_out[...] = back
@@ -773,18 +776,26 @@
             back = back_out[...] + back
             back_out[...] = back
             low_out[...] = back.astype(bf16)
-
-
-def feed_back(info, slope, cot, up, down):
+    spare = 2 * hidden // width
+    turns = hidden_turns(spare, hidden, chips)
+    biases = jnp.where(turns, jnp.concatenate(sums, axis=1), 0.0)
+    high = biases.astype(bf16)
+    both = jnp.concatenate([high.astype(f32), biases - high.astype(f32)]).astype(bf16)
+    placed = dot(both, hidden_places(info[0], hidden, width, chips))
+    bias_out[...] = jnp.zeros_like(bias_out)
+    bias_out[:spare, :] = placed[:spare] + placed[spare:]
+
+
+def feed_back(info, slope, cot, up, down, chips):
     rows, hidden = slope.shape
     width = up.shape[0]
     return call(
-        feed_back_kernel,
+        functools.partial(feed_back_kernel, chips),
         [
             (shaped((rows, width), f32), vmem()),
             (shaped((rows, width), bf16), vmem()),
             (shaped((rows, hidden), bf16), vmem()),
-            (shaped((8, hidden), f32), vmem()),
+            (shaped((8, width), f32), vmem()),
         ],
         [LOAD] * 4,
         [info, slope, cot, up, down],
@@ -925,7 +936,7 @@
     )
 
 
-def start_kernel(blocks, patches, chips, info, *refs):
+def start_kernel(blocks, patches, spare, info, *refs):
     (keep, far, start, grad_middle, turned, sums, bias_grad, spots, dq, dv, out_keep, out_got) = refs[:12]
     refs = refs[12:]
     low_out, refs = refs[0], refs[1:]
@@ -964,13 +975,7 @@
     put(SHIFT_TWO, sums[3:4, :])
     put(GAIN_ONE, jnp.sum(grad_normed * normal, axis=0, keepdims=True))
     put(SHIFT_ONE, jnp.sum(grad_normed, axis=0, keepdims=True))
-    hidden = bias_grad.shape[1]
-    spare = 2 * hidden // width
-    biases = jnp.where(hidden_turns(spare, hidden, chips), bias_grad[0:1, :], 0.0)
-    high = biases.astype(bf16)
-    both = jnp.concatenate([high.astype(f32), biases - high.astype(f32)]).astype(bf16)
-    placed = dot(both, hidden_places(core, hidden, width, chips))
-    rows_held[patches + 8 : patches + 8 + spare, :] = placed[:spare] + placed[spare:]
+    rows_held[patches + 8 : patches + 8 + spare, :] = bias_grad[:spare, :]
     held[:, :SMALL] = rows_held[...].T.astype(bf16)
     if blocks == 4:
         slab = up_rows // 2
@@ -985,14 +990,14 @@
         run_copies([pltpu.make_async_copy(held, grads[0], sem.at[0])])
 
 
-def start_back(info, blocks, args, patches, chips):
+def start_back(info, blocks, args, patches, spare):
     half_rows, width = args[0].shape
     columns = SMALL + width // 2 if blocks == 4 else SMALL
     outs = [shaped((width, columns), bf16)]
     if blocks == 4:
         outs = fold_shapes(width // 4, (columns,))
     return call(
-        functools.partial(start_kernel, blocks, patches, chips),
+        functools.partial(start_kernel, blocks, patches, spare),
         [(shaped((half_rows, width), bf16), vmem())]
         + [(one, anywhere()) for one in outs],
         [LOAD] * len(args),
@@ -1250,7 +1255,7 @@
             one.terms = [*one.terms[:3], *one.far]
         return values
 
-    rows_in = jnp.concatenate([jnp.stack(vectors), up_bias.reshape(spare, rows)])
+    rows_in = jnp.stack([*vectors, *(up_bias[i * rows : (i + 1) * rows] for i in range(spare))])
     in_keep, in_send = pack_in(info, input_weight, position_table, rows_in)
     in_far = swap(in_send, "wide", 1)
     raw_parts = together(down_weight, output_weight, up_sorted, tokens, in_keep)
@@ -1329,7 +1334,7 @@
     )
     down_rows = own_hidden // (chips * PLACES)
     down_fold = folded(down_grads, (PLACES, down_rows, width))
-    fed = feed_back(info, slope, cot, up_full, down_full)
+    fed = feed_back(info, slope, cot, up_full, down_full, chips)
     back, back_low, grad_hidden, bias_grad, send, normed_two = crossed(
         [down_fold], *fed, send, normed_two
     )
@@ -1363,7 +1368,7 @@
     up_got = swap(up_send, "narrow", 1)
     down_got = swap(down_send, "narrow", 2)
     args = [start_keep, start_far, start, grad_middle, turned, sums, bias_grad, spots, dq, dv]
-    started = start_back(info, blocks, args + [out_keep, out_got], patches, chips)
+    started = start_back(info, blocks, args + [out_keep, out_got], patches, spare)
     if not plane:
         out_grad = jnp.where(
             first_core,

time: 267 us -> 267 us (level)
  the two profiles are of different devices: /device:TPU:11 before, /device:TPU:7 now
where the time goes in v7:
time: 267 us; the launch traced here: 262 us
  Pallas kernels  98.1 us (37%)
  starting transfers between devices  81.7 us (31%)
  waiting for transfers between devices  63.1 us (24%)
  local copies, waits for them, and re-layouts  10.8 us (4%)
  other arithmetic  6.59 us (2%)
    pallas_call x36, Pallas kernels, call(): pl.pallas_call(loaded if loads else kernel, out_shape=[shape for shape, _...  98.1 us
    ppermute x55, waiting for transfers between devices, swap(): return lax.ppermute(values, axis, [(i, i ^ bits) for i in range(size)])  58.5 us
    ppermute x55, starting transfers between devices, swap(): return lax.ppermute(values, axis, [(i, i ^ bits) for i in range(size)])  57.1 us
    ppermute x4, starting transfers between devices, unspread_turn(): lax.ppermute(part, ('wide', 'narrow'), [(b, a) for a, b in spread_perm(tu...  9.52 us
    ppermute x1, starting transfers between devices, local(): low = lax.ppermute(first, ('wide', 'narrow'), spread_perm(0))  7.52 us
  transfers between devices with their start and end apart: 63, of which 19 were waited for; matrix products, arithmetic and copies ran while one was open for 3% of the time, Pallas kernels for 30%

profile of v7, /device:TPU:7, one launch (start us, length us, event | category | flops | bytes accessed | tf_op | source)
XLA Modules:
  0.0 261.9 jit_solution(14169032390309320467)
XLA Ops:
  7.8 2.4 collective-permute-start.2
  10.8 1.4 collective-permute-start.3
  12.2 2.2 collective-permute-start.5
  18.7 8.2 %collective-permute-done.4.refs_2_ = bf16[2,24,1280]{2,1,0:T(8,128)(2,1)S(1)} collective-permute-done((bf16[2,24,1280]{2,1,0:T(8,128)(2,1)S(1)}, bf16[2,24,1280]{2,1,0:T(8,128)(2,1)S(1)}, u32[]{:S(2)}, u32[]{:S(2)}) %collective-permute-start.4) | collective-permute-done | bytes 122912 | tf_op jit(solution)/shard_map/ppermute | solution.py:1071
  26.9 7.5 %collective-permute-start.6 = (bf16[272,768]{1,0:T(8,128)(2,1)S(1)}, bf16[272,768]{1,0:T(8,128)(2,1)S(1)}, u32[]{:S(2)}, u32[]{:S(2)}) collective-permute-start(bf16[272,768]{1,0:T(8,128)(2,1)S(1)} %get-tuple-element.247), channel_id=1, source_target_pairs={{0,0},{1,1},{2,4},{3,5},{4,2},{5,3},{6,6},{7,7},{8,8},{9,9},{10,12... | collective-permute-start | bytes 1253384 | tf_op jit(solution)/shard_map/ppermute | solution.py:1277
  36.3 2.2 collective-permute-start.14
  39.0 9.2 %collective-permute-done.7.far = bf16[2,120,768]{2,1,0:T(8,128)(2,1)S(1)} collective-permute-done((bf16[2,120,768]{2,1,0:T(8,128)(2,1)S(1)}, bf16[2,120,768]{2,1,0:T(8,128)(2,1)S(1)}, u32[]{:S(2)}, u32[]{:S(2)}) %collective-permute-start.7) | collective-permute-done | bytes 368672 | tf_op jit(solution)/shard_map/ppermute | solution.py:1071
  49.3 8.2 %collective-permute-done.13 = bf16[2,4,24,1280]{3,2,1,0:T(8,128)(2,1)S(1)} collective-permute-done((bf16[2,4,24,1280]{3,2,1,0:T(8,128)(2,1)S(1)}, bf16[2,4,24,1280]{3,2,1,0:T(8,128)(2,1)S(1)}, u32[]{:S(2)}, u32[]{:S(2)}) %collective-permute-start.13) | collective-permute-done | bytes 491552 | tf_op jit(solution)/shard_map/ppermute | solution.py:1071
  57.5 1.5 collective-permute-start.16
  59.0 2.6 collective-permute-done.9.refs_1_
  61.6 6.3 %collective-permute-start.11 = (bf16[272,768]{1,0:T(8,128)(2,1)S(1)}, bf16[272,768]{1,0:T(8,128)(2,1)S(1)}, u32[]{:S(2)}, u32[]{:S(2)}) collective-permute-start(bf16[272,768]{1,0:T(8,128)(2,1)S(1)} %collective-permute-done.8.refs_1_), channel_id=1, source_target_pairs={{0,4},{4,0},{8,12},{12,8},{16,20},{20,16},{24,28},{28,24},{1,5},{5... | collective-permute-start | bytes 1253384 | tf_op jit(solution)/shard_map/ppermute | solution.py:1071
  69.9 7.0 %shard_map.305 = (bf16[1024,384]{1,0:T(8,128)(2,1)S(1)}, bf16[1024,384]{1,0:T(8,128)(2,1)S(1)}, bf16[1024,384]{1,0:T(8,128)(2,1)S(1)}, f32[1024,768]{1,0:T(8,128...) custom-call(s32[4]{0:T(128)S(1)} %pad_add_fusion.info, ...), custom_call_target="tpu_custom_call" | custom-call | flops 2013265920 | bytes 12582912 | tf_op jit(solution)/shard_map/pallas_call | solution.py:61
  81.5 2.3 collective-permute-start.19
  83.8 1.8 collective-permute-done.20.refs_12_
  85.6 4.9 %collective-permute-start.18 = (bf16[256,768]{1,0:T(8,128)(2,1)S(1)}, bf16[256,768]{1,0:T(8,128)(2,1)S(1)}, u32[]{:S(2)}, u32[]{:S(2)}) collective-permute-start(bf16[256,768]{1,0:T(8,128)(2,1)S(1)} %get-tuple-element.280), channel_id=1, source_target_pairs={{0,0},{1,1},{2,4},{3,5},{4,2},{5,3},{6,6},{7,7},{8,8},{9,9},{10,12... | collective-permute-start | bytes 1179656 | tf_op jit(solution)/shard_map/ppermute | solution.py:1296
  90.5 13.2 %shard_map.308 = (bf16[1024,384]{1,0:T(8,128)(2,1)S(1)}, f32[3,8,1024]{2,1,0:T(8,128)S(1)}) custom-call(s32[4]{0:T(128)S(1)} %pad_add_fusion.info, bf16[1024,384]{1,0:T(8,128)(2,1)S(1)} %get-tuple-element.275.q, bf16[1024,384]{1,0:T(8,128)(2,1)S(1)} %get-tuple-element.276.k, bf16[1024,384]{1,0:T(8,128)(2,1)S(1)} %get-tuple-element.277.v, ...), custom_call_target="tpu_custom_call" | custom-call | flops 2415919104 | bytes 4194304 | tf_op jit(solution)/shard_map/pallas_call | solution.py:61
  103.8 1.5 collective-permute-start.24
  108.2 4.2 %shard_map.312 = (f32[1024,768]{1,0:T(8,128)S(1)}, bf16[1024,768]{1,0:T(8,128)(2,1)S(1)}, f32[8,1536]{1,0:T(8,128)S(1)}, bf16[768,768]{1,0:T(8,128)(2,1)S(1)}) custom-call(s32[4]{0:T(128)S(1)} %pad_add_fusion.info, bf16[1024,384]{1,0:T(8,128)(2,1)S(1)} %get-tuple-element.288.att.o, bf16[1024,384]{1,0:T(8,128)(2,1)S(1)} %collective-permute-done.24.att_far, ...), custom_call_target="tpu_custom_call" | custom-call | flops 1207959552 | bytes 12582912 | tf_op jit(solution)/shard_map/pallas_call | solution.py:61
  112.4 2.9 %collective-permute-done.28 = bf16[1,4,24,1536]{3,2,1,0:T(8,128)(2,1)S(1)} collective-permute-done((bf16[1,4,24,1536]{3,2,1,0:T(8,128)(2,1)S(1)}, bf16[1,4,24,1536]{3,2,1,0:T(8,128)(2,1)S(1)}, u32[]{:S(2)}, u32[]{:S(2)}) %collective-permute-start.28) | collective-permute-done | bytes 294944 | tf_op jit(solution)/shard_map/ppermute | solution.py:1071
  116.2 14.5 %shard_map.314 = (f32[512,768]{1,0:T(8,128)S(1)}, bf16[512,768]{1,0:T(8,128)(2,1)S(1)}, bf16[1024,1536]{1,0:T(8,128)(2,1)S(1)}, bf16[768,1536]{1,0:T(8,128)(2,1)...) custom-call(s32[4]{0:T(128)S(1)} %pad_add_fusion.info, ...), custom_call_target="tpu_custom_call" | custom-call | flops 7247757312 | bytes 25165824 | tf_op jit(solution)/shard_map/pallas_call | solution.py:61
  131.3 6.8 %shard_map.315 = (f32[1024,768]{1,0:T(8,128)S(1)}, bf16[1024,768]{1,0:T(8,128)(2,1)S(1)}, bf16[1024,1536]{1,0:T(8,128)(2,1)S(1)}, f32[8,768]{1,0:T(8,128)S(1)}) custom-call(s32[4]{0:T(128)S(1)} %pad_add_fusion.info, bf16[1024,1536]{1,0:T(8,128)(2,1)S(1)} %get-tuple-element.305.slope, bf16[4,256,768]{2,1,0:T(8,128)(2,1)S(1)} %get-tuple-element.306.cot, ...), custom_call_target="tpu_custom_call" | custom-call | flops 4831838208 | bytes 25165824 | tf_op jit(solution)/shard_map/pallas_call | solution.py:61
  138.0 6.4 %collective-permute-done.30.refs_1_ = bf16[4,96,768]{2,1,0:T(8,128)(2,1)S(1)} collective-permute-done((bf16[4,96,768]{2,1,0:T(8,128)(2,1)S(1)}, bf16[4,96,768]{2,1,0:T(8,128)(2,1)S(1)}, u32[]{:S(2)}, u32[]{:S(2)}) %collective-permute-start.30) | collective-permute-done | bytes 589856 | tf_op jit(solution)/shard_map/ppermute | solution.py:1071
  144.5 2.3 collective-permute-start.32
  149.0 3.7 %shard_map.316 = (bf16[192,1536]{1,0:T(8,128)(2,1)S(1)}, bf16[192,1536]{1,0:T(8,128)(2,1)S(1)}, bf16[192,1536]{1,0:T(8,128)(2,1)S(1)}, bf16[96,1536]{1,0:T(8,128)(2,1)S(1)}, bf16[96,1536]{1,0:T(8,128)(2,1)S(1)}) custom-call(s32[4]{0:T(128)S(1)} %pad_add_fusion.info, bf16[1024,768]{1,0:T(8,128)(2,1)S(1)} %get-tuple-element.318.normed.left, ...), custom_call_target="tpu_custom_call" | custom-call | flops 2415919104 | bytes 8388608 | tf_op jit(solution)/shard_map/pallas_call | solution.py:61
  152.8 2.8 %collective-permute-done.34 = bf16[2,96,768]{2,1,0:T(8,128)(2,1)S(1)} collective-permute-done((bf16[2,96,768]{2,1,0:T(8,128)(2,1)S(1)}, bf16[2,96,768]{2,1,0:T(8,128)(2,1)S(1)}, u32[]{:S(2)}, u32[]{:S(2)}) %collective-permute-start.34) | collective-permute-done | bytes 294944 | tf_op jit(solution)/shard_map/ppermute | solution.py:1071
  159.5 5.7 %shard_map.318 = (f32[512,768]{1,0:T(8,128)S(1)}, bf16[1024,384]{1,0:T(8,128)(2,1)S(1)}, bf16[2,96,768]{2,1,0:T(8,128)(2,1)S(1)}, bf16[2,96,768]{2,1,0:T(8,128)(2,1)S(1)}, f32[8,768]{1,0:T(8,128)S(1)}) custom-call(s32[4]{0:T(128)S(1)} %pad_add_fusion.info, f32[1024,768]{1,0:T(8,128)S(1)} %get-tuple-element.332.back, ...), custom_call_target="tpu_custom_call" | custom-call | flops 1207959552 | bytes 14680064 | tf_op jit(solution)/shard_map/pallas_call | solution.py:61
  166.0 4.8 %collective-permute-start.39 = (bf16[256,768]{1,0:T(8,128)(2,1)S(1)}, bf16[256,768]{1,0:T(8,128)(2,1)S(1)}, u32[]{:S(2)}, u32[]{:S(2)}) collective-permute-start(bf16[256,768]{1,0:T(8,128)(2,1)S(1)} %get-tuple-element.353), channel_id=1, source_target_pairs={{0,0},{1,1},{4,2},{5,3},{2,4},{3,5},{6,6},{7,7},{8,8},{9,9},{12,10... | collective-permute-start | bytes 1179656 | tf_op jit(solution)/shard_map/ppermute | solution.py:1084
  172.7 12.2 %shard_map.320 = (bf16[1024,384]{1,0:T(8,128)(2,1)S(1)}, bf16[1024,384]{1,0:T(8,128)(2,1)S(1)}, bf16[1024,384]{1,0:T(8,128)(2,1)S(1)}) custom-call(s32[4]{0:T(128)S(1)} %pad_add_fusion.info, bf16[1024,384]{1,0:T(8,128)(2,1)S(1)} %get-tuple-element.275.q, bf16[1024,384]{1,0:T(8,128)(2,1)S(1)} %get-tuple-element.276.k, ...), custom_call_target="tpu_custom_call" | custom-call | flops 6039797760 | bytes 6291456 | tf_op jit(solution)/shard_map/pallas_call | solution.py:61
  185.0 3.2 %shard_map.323 = (f32[512,768]{1,0:T(8,128)S(1)}, bf16[512,768]{1,0:T(8,128)(2,1)S(1)}) custom-call(s32[4]{0:T(128)S(1)} %pad_add_fusion.info, bf16[1024,384]{1,0:T(8,128)(2,1)S(1)} %get-tuple-element.361.dq.refs_8_.refs_0_, bf16[1024,384]{1,0:T(8,128)(2,1)S(1)} %get-tuple-element.362.dk.refs_1_, ...), custom_call_target="tpu_custom_call" | custom-call | flops 1811939328 | bytes 8388608 | tf_op jit(solution)/shard_map/pallas_call | solution.py:61
  188.2 2.7 %collective-permute-start.43 = (bf16[512,768]{1,0:T(8,128)(2,1)S(1)}, bf16[512,768]{1,0:T(8,128)(2,1)S(1)}, u32[]{:S(2)}, u32[]{:S(2)}) collective-permute-start(bf16[512,768]{1,0:T(8,128)(2,1)S(1)} %get-tuple-element.365), channel_id=1, source_target_pairs={{0,4},{4,0},{8,12},{12,8},{16,20},{20,16},{24,28},{28,24},{1,5},{5... | collective-permute-start | bytes 2359304 | tf_op jit(solution)/shard_map/ppermute | solution.py:1071
  193.2 1.9 collective-permute-start.45
  195.1 3.6 %shard_map.326 = (bf16[512,768]{1,0:T(8,128)(2,1)S(1)}, bf16[192,512]{1,0:T(8,128)(2,1)S(1)}, bf16[192,512]{1,0:T(8,128)(2,1)S(1)}, bf16[192,512]{1,0:T(8,128)(2...) custom-call(s32[4]{0:T(128)S(1)} %pad_add_fusion.info, f32[512,768]{1,0:T(8,128)S(1)} %get-tuple-element.377.refs_0_, ...), custom_call_target="tpu_custom_call" | custom-call | flops 100663296 | bytes 10485760 | tf_op jit(solution)/shard_map/pallas_call | solution.py:61
  199.2 1.3 collective-permute-start.46
  200.6 4.8 %shard_map.327 = (bf16[192,1152]{1,0:T(8,128)(2,1)S(1)}, bf16[192,1152]{1,0:T(8,128)(2,1)S(1)}, bf16[192,1152]{1,0:T(8,128)(2,1)S(1)}, bf16[96,1152]{1,0:T(8,128)(2,1)S(1)}, bf16[96,1152]{1,0:T(8,128)(2,1)S(1)}) custom-call(s32[4]{0:T(128)S(1)} %pad_add_fusion.info, bf16[1024,768]{1,0:T(8,128)(2,1)S(1)} %get-tuple-element.391.left, ...), custom_call_target="tpu_custom_call" | custom-call | flops 1811939328 | bytes 8388608 | tf_op jit(solution)/shard_map/pallas_call | solution.py:61
  205.4 4.0 %collective-permute-start.52 = (bf16[192,1152]{1,0:T(8,128)(2,1)S(1)}, bf16[192,1152]{1,0:T(8,128)(2,1)S(1)}, u32[]{:S(2)}, u32[]{:S(2)}) collective-permute-start(bf16[192,1152]{1,0:T(8,128)(2,1)S(1)} %get-tuple-element.415), channel_id=1, source_target_pairs={{0,8},{4,12},{8,0},{12,4},{16,24},{20,28},{24,16},{28,20},{1,9},{5... | collective-permute-start | bytes 1327112 | tf_op jit(solution)/shard_map/ppermute | solution.py:1071
  209.5 1.8 collective-permute-start.53
  211.3 1.3 shard_map.328
  212.6 2.7 %collective-permute-start.49 = (bf16[256,768]{1,0:T(8,128)(2,1)S(1)}, bf16[256,768]{1,0:T(8,128)(2,1)S(1)}, u32[]{:S(2)}, u32[]{:S(2)}) collective-permute-start(bf16[256,768]{1,0:T(8,128)(2,1)S(1)} %get-tuple-element.401), channel_id=1, source_target_pairs={{0,0},{1,1},{4,2},{5,3},{2,4},{3,5},{6,6},{7,7},{8,8},{9,9},{12,10... | collective-permute-start | bytes 1179656 | tf_op jit(solution)/shard_map/ppermute | solution.py:1084
  216.4 1.3 shard_map.329
  217.8 4.5 %collective-permute-done.50.refs_8_ = bf16[96,512]{1,0:T(8,128)(2,1)S(1)} collective-permute-done((bf16[96,512]{1,0:T(8,128)(2,1)S(1)}, bf16[96,512]{1,0:T(8,128)(2,1)S(1)}, u32[]{:S(2)}, u32[]{:S(2)}) %collective-permute-start.50) | collective-permute-done | bytes 98336 | tf_op jit(solution)/shard_map/ppermute | solution.py:1071
  222.3 4.6 %collective-permute-done.49 = bf16[256,768]{1,0:T(8,128)(2,1)S(1)} collective-permute-done((bf16[256,768]{1,0:T(8,128)(2,1)S(1)}, bf16[256,768]{1,0:T(8,128)(2,1)S(1)}, u32[]{:S(2)}, u32[]{:S(2)}) %collective-permute-start.49) | collective-permute-done | bytes 393248 | tf_op jit(solution)/shard_map/ppermute | solution.py:1084
  226.8 1.5 collective-permute-start.57
  228.3 1.4 shard_map.331
  230.2 4.5 %collective-permute-done.54.refs_3_ = bf16[96,1152]{1,0:T(8,128)(2,1)S(1)} collective-permute-done((bf16[96,1152]{1,0:T(8,128)(2,1)}, bf16[96,1152]{1,0:T(8,128)(2,1)S(1)}, u32[]{:S(2)}, u32[]{:S(2)}) %collective-permute-start.54) | collective-permute-done | bytes 221216 | tf_op jit(solution)/shard_map/ppermute | solution.py:1071
  235.6 1.6 shard_map.332
  237.6 3.2 %collective-permute-start.61 = (bf16[2,24,1664]{2,1,0:T(8,128)(2,1)}, bf16[2,24,1664]{2,1,0:T(8,128)(2,1)S(1)}, u32[]{:S(2)}, u32[]{:S(2)}) collective-permute-start(bf16[2,24,1664]{2,1,0:T(8,128)(2,1)} %get-tuple-element.447), channel_id=1, source_target_pairs={{0,3},{1,2},{2,1},{3,0},{4,7},{5,6},{6,5},{7,4},{8,11},{9,10},{10,... | collective-permute-start | bytes 479240 | tf_op jit(solution)/shard_map/ppermute | solution.py:1071
  240.8 2.6 %collective-permute-done.56 = bf16[2,24,1536]{2,1,0:T(8,128)(2,1)} collective-permute-done((bf16[2,24,1536]{2,1,0:T(8,128)(2,1)}, bf16[2,24,1536]{2,1,0:T(8,128)(2,1)}, u32[]{:S(2)}, u32[]{:S(2)}) %collective-permute-start.56) | collective-permute-done | bytes 147488 | tf_op jit(solution)/shard_map/ppermute | solution.py:1071
  244.4 7.8 %collective-permute-start.58 = (bf16[24,1536]{1,0:T(8,128)(2,1)S(1)}, bf16[24,1536]{1,0:T(8,128)(2,1)S(1)}, u32[]{:S(2)}, u32[]{:S(2)}) collective-permute-start(bf16[24,1536]{1,0:T(8,128)(2,1)S(1)} %fusion.1), channel_id=1, source_target_pairs={{0,4},{4,0},{8,12},{12,8},{16,20},{20,16},{24,28},{28,24},{1,5},{5... | collective-permute-start | bytes 221192 | tf_op jit(solution)/shard_map/ppermute | solution.py:1071
  (181 shorter events, 51.2 us)
Async XLA Ops:
  7.8 19.1 %collective-permute-start.2 = (bf16[120,768]{1,0:T(8,128)(2,1)S(1)}, bf16[120,768]{1,0:T(8,128)(2,1)S(1)}, u32[]{:S(2)}, u32[]{:S(2)}) collective-permute-start(bf16[120,768]{1,0:T(8,128)(2,1)S(1)} %pad_maximum_fusion.2.refs_0_), channel_id=1, source_target_pairs={{0,2},{1,3},{2,0},{3,1},{4,6},{5,7},{6,4},{7,5},{8,10},{9,11},{10,... | collective-permute-start | bytes 552968 | tf_op jit(solution)/shard_map/ppermute | solution.py:1071
  10.8 7.9 %collective-permute-start.3 = (bf16[2,24,1280]{2,1,0:T(8,128)(2,1)S(1)}, bf16[2,24,1280]{2,1,0:T(8,128)(2,1)S(1)}, u32[]{:S(2)}, u32[]{:S(2)}) collective-permute-start(bf16[2,24,1280]{2,1,0:T(8,128)(2,1)S(1)} %shard_map.300.refs_0_), channel_id=1, source_target_pairs={{0,1},{1,0},{2,3},{3,2},{4,5},{5,4},{6,7},{7,6},{8,9},{9,8},{10,11... | collective-permute-start | bytes 368648 | tf_op jit(solution)/shard_map/ppermute | solution.py:1071
  12.1 14.8 %collective-permute-start.4 = (bf16[2,24,1280]{2,1,0:T(8,128)(2,1)S(1)}, bf16[2,24,1280]{2,1,0:T(8,128)(2,1)S(1)}, u32[]{:S(2)}, u32[]{:S(2)}) collective-permute-start(bf16[2,24,1280]{2,1,0:T(8,128)(2,1)S(1)} %shard_map.300.refs_0_), channel_id=1, source_target_pairs={{0,2},{1,3},{2,0},{3,1},{4,6},{5,7},{6,4},{7,5},{8,10},{9,11},{10,... | collective-permute-start | bytes 368648 | tf_op jit(solution)/shard_map/ppermute | solution.py:1071
  12.2 14.7 %collective-permute-start.5 = (bf16[2,24,1280]{2,1,0:T(8,128)(2,1)S(1)}, bf16[2,24,1280]{2,1,0:T(8,128)(2,1)S(1)}, u32[]{:S(2)}, u32[]{:S(2)}) collective-permute-start(bf16[2,24,1280]{2,1,0:T(8,128)(2,1)S(1)} %shard_map.300.refs_0_), channel_id=1, source_target_pairs={{0,3},{1,2},{2,1},{3,0},{4,7},{5,6},{6,5},{7,4},{8,11},{9,10},{10,... | collective-permute-start | bytes 368648 | tf_op jit(solution)/shard_map/ppermute | solution.py:1071
  26.9 21.3 %collective-permute-start.6 = (bf16[272,768]{1,0:T(8,128)(2,1)S(1)}, bf16[272,768]{1,0:T(8,128)(2,1)S(1)}, u32[]{:S(2)}, u32[]{:S(2)}) collective-permute-start(bf16[272,768]{1,0:T(8,128)(2,1)S(1)} %get-tuple-element.247), channel_id=1, source_target_pairs={{0,0},{1,1},{2,4},{3,5},{4,2},{5,3},{6,6},{7,7},{8,8},{9,9},{10,12... | collective-permute-start | bytes 1253384 | tf_op jit(solution)/shard_map/ppermute | solution.py:1277
  35.0 13.2 %collective-permute-start.7 = (bf16[2,120,768]{2,1,0:T(8,128)(2,1)S(1)}, bf16[2,120,768]{2,1,0:T(8,128)(2,1)S(1)}, u32[]{:S(2)}, u32[]{:S(2)}) collective-permute-start(bf16[2,120,768]{2,1,0:T(8,128)(2,1)S(1)} %shard_map.301.own), channel_id=1, source_target_pairs={{0,1},{1,0},{2,3},{3,2},{4,5},{5,4},{6,7},{7,6},{8,9},{9,8},{10,11... | collective-permute-start | bytes 1105928 | tf_op jit(solution)/shard_map/ppermute | solution.py:1071
  35.7 13.6 %collective-permute-start.12 = (bf16[2,4,24,1280]{3,2,1,0:T(8,128)(2,1)S(1)}, bf16[2,4,24,1280]{3,2,1,0:T(8,128)(2,1)S(1)}, u32[]{:S(2)}, u32[]{:S(2)}) collective-permute-start(bf16[2,4,24,1280]{3,2,1,0:T(8,128)(2,1)S(1)} %shard_map.304), channel_id=1, source_target_pairs={{0,8},{4,12},{8,0},{12,4},{16,24},{20,28},{24,16},{28,20},{1,9},{5... | collective-permute-start | bytes 1474568 | tf_op jit(solution)/shard_map/ppermute | solution.py:1071
  36.0 21.5 %collective-permute-start.13 = (bf16[2,4,24,1280]{3,2,1,0:T(8,128)(2,1)S(1)}, bf16[2,4,24,1280]{3,2,1,0:T(8,128)(2,1)S(1)}, u32[]{:S(2)}, u32[]{:S(2)}) collective-permute-start(bf16[2,4,24,1280]{3,2,1,0:T(8,128)(2,1)S(1)} %shard_map.304), channel_id=1, source_target_pairs={{0,16},{4,20},{8,24},{12,28},{16,0},{20,4},{24,8},{28,12},{1,17},{... | collective-permute-start | bytes 1474568 | tf_op jit(solution)/shard_map/ppermute | solution.py:1071
  36.3 21.3 %collective-permute-start.14 = (bf16[2,4,24,1280]{3,2,1,0:T(8,128)(2,1)S(1)}, bf16[2,4,24,1280]{3,2,1,0:T(8,128)(2,1)S(1)}, u32[]{:S(2)}, u32[]{:S(2)}) collective-permute-start(bf16[2,4,24,1280]{3,2,1,0:T(8,128)(2,1)S(1)} %shard_map.304), channel_id=1, source_target_pairs={{0,24},{4,28},{8,16},{12,20},{16,8},{20,12},{24,0},{28,4},{1,25},{... | collective-permute-start | bytes 1474568 | tf_op jit(solution)/shard_map/ppermute | solution.py:1071
  48.2 13.4 %collective-permute-start.8 = (bf16[272,768]{1,0:T(8,128)(2,1)S(1)}, bf16[272,768]{1,0:T(8,128)(2,1)S(1)}, u32[]{:S(2)}, u32[]{:S(2)}) collective-permute-start(bf16[272,768]{1,0:T(8,128)(2,1)S(1)} %get-tuple-element.253), channel_id=1, source_target_pairs={{0,1},{1,0},{2,5},{3,4},{4,3},{5,2},{6,7},{7,6},{8,9},{9,8},{10,13... | collective-permute-start | bytes 1253384 | tf_op jit(solution)/shard_map/ppermute | solution.py:1282
  48.7 13.0 %collective-permute-start.9 = (bf16[2,24,1536]{2,1,0:T(8,128)(2,1)S(1)}, bf16[2,24,1536]{2,1,0:T(8,128)(2,1)S(1)}, u32[]{:S(2)}, u32[]{:S(2)}) collective-permute-start(bf16[2,24,1536]{2,1,0:T(8,128)(2,1)S(1)} %shard_map.302.refs_0_), channel_id=1, source_target_pairs={{0,2},{1,3},{2,0},{3,1},{4,6},{5,7},{6,4},{7,5},{8,10},{9,11},{10,... | collective-permute-start | bytes 442376 | tf_op jit(solution)/shard_map/ppermute | solution.py:1071
  57.5 19.7 %collective-permute-start.16 = (bf16[5,96,768]{2,1,0:T(8,128)(2,1)S(1)}, bf16[5,96,768]{2,1,0:T(8,128)(2,1)S(1)}, u32[]{:S(2)}, u32[]{:S(2)}) collective-permute-start(bf16[5,96,768]{2,1,0:T(8,128)(2,1)S(1)} %shard_map.303.own.refs_9_), channel_id=1, source_target_pairs={{0,8},{4,12},{8,0},{12,4},{16,24},{20,28},{24,16},{28,20},{1,9},{5... | collective-permute-start | bytes 2211848 | tf_op jit(solution)/shard_map/ppermute | solution.py:1071
  59.0 18.2 %collective-permute-start.17 = (bf16[5,96,768]{2,1,0:T(8,128)(2,1)S(1)}, bf16[5,96,768]{2,1,0:T(8,128)(2,1)S(1)}, u32[]{:S(2)}, u32[]{:S(2)}) collective-permute-start(bf16[5,96,768]{2,1,0:T(8,128)(2,1)S(1)} %shard_map.303.own.refs_9_), channel_id=1, source_target_pairs={{0,16},{4,20},{8,24},{12,28},{16,0},{20,4},{24,8},{28,12},{1,17},{... | collective-permute-start | bytes 2211848 | tf_op jit(solution)/shard_map/ppermute | solution.py:1071
  59.0 9.6 %collective-permute-start.10 = (bf16[272,768]{1,0:T(8,128)(2,1)S(1)}, bf16[272,768]{1,0:T(8,128)(2,1)S(1)}, u32[]{:S(2)}, u32[]{:S(2)}) collective-permute-start(bf16[272,768]{1,0:T(8,128)(2,1)S(1)} %collective-permute-done.6.refs_0_), channel_id=1, source_target_pairs={{0,4},{4,0},{8,12},{12,8},{16,20},{20,16},{24,28},{28,24},{1,5},{5... | collective-permute-start | bytes 1253384 | tf_op jit(solution)/shard_map/ppermute | solution.py:1071
  68.5 8.7 %collective-permute-start.15 = (bf16[2,2,24,1536]{3,2,1,0:T(8,128)(2,1)S(1)}, bf16[2,2,24,1536]{3,2,1,0:T(8,128)(2,1)S(1)}, u32[]{:S(2)}, u32[]{:S(2)}) collective-permute-start(bf16[2,2,24,1536]{3,2,1,0:T(8,128)(2,1)S(1)} %shard_map.307.refs_0_), channel_id=1, source_target_pairs={{0,1},{1,0},{2,3},{3,2},{4,5},{5,4},{6,7},{7,6},{8,9},{9,8},{10,11... | collective-permute-start | bytes 884744 | tf_op jit(solution)/shard_map/ppermute | solution.py:1071
  77.8 7.8 %collective-permute-start.20 = (bf16[2,96,768]{2,1,0:T(8,128)(2,1)S(1)}, bf16[2,96,768]{2,1,0:T(8,128)(2,1)S(1)}, u32[]{:S(2)}, u32[]{:S(2)}) collective-permute-start(bf16[2,96,768]{2,1,0:T(8,128)(2,1)S(1)} %get-tuple-element.285), channel_id=1, source_target_pairs={{0,8},{4,12},{8,0},{12,4},{16,24},{20,28},{24,16},{28,20},{1,9},{5... | collective-permute-start | bytes 884744 | tf_op jit(solution)/shard_map/ppermute | solution.py:1071
  78.7 25.0 %collective-permute-start.22 = (bf16[2,4,24,1536]{3,2,1,0:T(8,128)(2,1)S(1)}, bf16[2,4,24,1536]{3,2,1,0:T(8,128)(2,1)S(1)}, u32[]{:S(2)}, u32[]{:S(2)}) collective-permute-start(bf16[2,4,24,1536]{3,2,1,0:T(8,128)(2,1)S(1)} %bitcast.64), channel_id=1, source_target_pairs={{0,8},{4,12},{8,0},{12,4},{16,24},{20,28},{24,16},{28,20},{1,9},{5... | collective-permute-start | bytes 1769480 | tf_op jit(solution)/shard_map/ppermute | solution.py:1071
  80.0 23.8 %collective-permute-start.23 = (bf16[2,4,24,1536]{3,2,1,0:T(8,128)(2,1)S(1)}, bf16[2,4,24,1536]{3,2,1,0:T(8,128)(2,1)S(1)}, u32[]{:S(2)}, u32[]{:S(2)}) collective-permute-start(bf16[2,4,24,1536]{3,2,1,0:T(8,128)(2,1)S(1)} %bitcast.65), channel_id=1, source_target_pairs={{0,16},{4,20},{8,24},{12,28},{16,0},{20,4},{24,8},{28,12},{1,17},{... | collective-permute-start | bytes 1769480 | tf_op jit(solution)/shard_map/ppermute | solution.py:1071
  80.2 23.5 %collective-permute-start.21 = (bf16[3,96,768]{2,1,0:T(8,128)(2,1)S(1)}, bf16[3,96,768]{2,1,0:T(8,128)(2,1)S(1)}, u32[]{:S(2)}, u32[]{:S(2)}) collective-permute-start(bf16[3,96,768]{2,1,0:T(8,128)(2,1)S(1)} %get-tuple-element.286), channel_id=1, source_target_pairs={{0,16},{4,20},{8,24},{12,28},{16,0},{20,4},{24,8},{28,12},{1,17},{... | collective-permute-start | bytes 1327112 | tf_op jit(solution)/shard_map/ppermute | solution.py:1071
  81.5 22.2 %collective-permute-start.19 = (bf16[256,768]{1,0:T(8,128)(2,1)S(1)}, bf16[256,768]{1,0:T(8,128)(2,1)S(1)}, u32[]{:S(2)}, u32[]{:S(2)}) collective-permute-start(bf16[256,768]{1,0:T(8,128)(2,1)S(1)} %get-tuple-element.281), channel_id=1, source_target_pairs={{0,1},{1,0},{2,5},{3,4},{4,3},{5,2},{6,7},{7,6},{8,9},{9,8},{10,13... | collective-permute-start | bytes 1179656 | tf_op jit(solution)/shard_map/ppermute | solution.py:1306
  85.6 18.1 %collective-permute-start.18 = (bf16[256,768]{1,0:T(8,128)(2,1)S(1)}, bf16[256,768]{1,0:T(8,128)(2,1)S(1)}, u32[]{:S(2)}, u32[]{:S(2)}) collective-permute-start(bf16[256,768]{1,0:T(8,128)(2,1)S(1)} %get-tuple-element.280), channel_id=1, source_target_pairs={{0,0},{1,1},{2,4},{3,5},{4,2},{5,3},{6,6},{7,7},{8,8},{9,9},{10,12... | collective-permute-start | bytes 1179656 | tf_op jit(solution)/shard_map/ppermute | solution.py:1296
  105.9 10.3 %collective-permute-start.26 = (bf16[256,768]{1,0:T(8,128)(2,1)S(1)}, bf16[256,768]{1,0:T(8,128)(2,1)S(1)}, u32[]{:S(2)}, u32[]{:S(2)}) collective-permute-start(bf16[256,768]{1,0:T(8,128)(2,1)S(1)} %collective-permute-done.18.refs_0_), channel_id=1, source_target_pairs={{0,4},{4,0},{8,12},{12,8},{16,20},{20,16},{24,28},{28,24},{1,5},{5... | collective-permute-start | bytes 1179656 | tf_op jit(solution)/shard_map/ppermute | solution.py:1071
  106.4 9.8 %collective-permute-start.27 = (bf16[256,768]{1,0:T(8,128)(2,1)S(1)}, bf16[256,768]{1,0:T(8,128)(2,1)S(1)}, u32[]{:S(2)}, u32[]{:S(2)}) collective-permute-start(bf16[256,768]{1,0:T(8,128)(2,1)S(1)} %collective-permute-done.19.refs_1_), channel_id=1, source_target_pairs={{0,4},{4,0},{8,12},{12,8},{16,20},{20,16},{24,28},{28,24},{1,5},{5... | collective-permute-start | bytes 1179656 | tf_op jit(solution)/shard_map/ppermute | solution.py:1071
  107.1 8.2 %collective-permute-start.28 = (bf16[1,4,24,1536]{3,2,1,0:T(8,128)(2,1)S(1)}, bf16[1,4,24,1536]{3,2,1,0:T(8,128)(2,1)S(1)}, u32[]{:S(2)}, u32[]{:S(2)}) collective-permute-start(bf16[1,4,24,1536]{3,2,1,0:T(8,128)(2,1)S(1)} %get-tuple-element.302), channel_id=1, source_target_pairs={{0,8},{4,12},{8,0},{12,4},{16,24},{20,28},{24,16},{28,20},{1,9},{5... | collective-permute-start | bytes 884744 | tf_op jit(solution)/shard_map/ppermute | solution.py:1071
  108.0 8.2 %collective-permute-start.29 = (bf16[1,4,24,1536]{3,2,1,0:T(8,128)(2,1)S(1)}, bf16[1,4,24,1536]{3,2,1,0:T(8,128)(2,1)S(1)}, u32[]{:S(2)}, u32[]{:S(2)}) collective-permute-start(bf16[1,4,24,1536]{3,2,1,0:T(8,128)(2,1)S(1)} %get-tuple-element.303), channel_id=1, source_target_pairs={{0,16},{4,20},{8,24},{12,28},{16,0},{20,4},{24,8},{28,12},{1,17},{... | collective-permute-start | bytes 884744 | tf_op jit(solution)/shard_map/ppermute | solution.py:1071
  130.8 13.7 %collective-permute-start.30 = (bf16[4,96,768]{2,1,0:T(8,128)(2,1)S(1)}, bf16[4,96,768]{2,1,0:T(8,128)(2,1)S(1)}, u32[]{:S(2)}, u32[]{:S(2)}) collective-permute-start(bf16[4,96,768]{2,1,0:T(8,128)(2,1)S(1)} %get-tuple-element.314), channel_id=1, source_target_pairs={{0,8},{4,12},{8,0},{12,4},{16,24},{20,28},{24,16},{28,20},{1,9},{5... | collective-permute-start | bytes 1769480 | tf_op jit(solution)/shard_map/ppermute | solution.py:1071
  131.1 13.4 %collective-permute-start.31 = (bf16[4,96,768]{2,1,0:T(8,128)(2,1)S(1)}, bf16[4,96,768]{2,1,0:T(8,128)(2,1)S(1)}, u32[]{:S(2)}, u32[]{:S(2)}) collective-permute-start(bf16[4,96,768]{2,1,0:T(8,128)(2,1)S(1)} %get-tuple-element.315), channel_id=1, source_target_pairs={{0,16},{4,20},{8,24},{12,28},{16,0},{20,4},{24,8},{28,12},{1,17},{... | collective-permute-start | bytes 1769480 | tf_op jit(solution)/shard_map/ppermute | solution.py:1071
  144.5 11.2 %collective-permute-start.32 = (bf16[1024,768]{1,0:T(8,128)(2,1)S(1)}, bf16[1024,768]{1,0:T(8,128)(2,1)S(1)}, u32[]{:S(2)}, u32[]{:S(2)}) collective-permute-start(bf16[1024,768]{1,0:T(8,128)(2,1)S(1)} %get-tuple-element.316), channel_id=1, source_target_pairs={{0,4},{4,0},{8,12},{12,8},{16,20},{20,16},{24,28},{28,24},{1,5},{5... | collective-permute-start | bytes 4718600 | tf_op jit(solution)/shard_map/ppermute | solution.py:1071
  146.8 8.8 %collective-permute-start.33 = (bf16[512,768]{1,0:T(8,128)(2,1)S(1)}, bf16[512,768]{1,0:T(8,128)(2,1)S(1)}, u32[]{:S(2)}, u32[]{:S(2)}) collective-permute-start(bf16[512,768]{1,0:T(8,128)(2,1)S(1)} %get-tuple-element.317), channel_id=1, source_target_pairs={{0,4},{4,0},{8,12},{12,8},{16,20},{20,16},{24,28},{28,24},{1,5},{5... | collective-permute-start | bytes 2359304 | tf_op jit(solution)/shard_map/ppermute | solution.py:1071
  147.5 8.1 %collective-permute-start.34 = (bf16[2,96,768]{2,1,0:T(8,128)(2,1)S(1)}, bf16[2,96,768]{2,1,0:T(8,128)(2,1)S(1)}, u32[]{:S(2)}, u32[]{:S(2)}) collective-permute-start(bf16[2,96,768]{2,1,0:T(8,128)(2,1)S(1)} %get-tuple-element.329), channel_id=1, source_target_pairs={{0,16},{4,20},{8,24},{12,28},{16,0},{20,4},{24,8},{28,12},{1,17},{... | collective-permute-start | bytes 884744 | tf_op jit(solution)/shard_map/ppermute | solution.py:1071
  147.8 7.8 %collective-permute-start.35 = (bf16[2,96,768]{2,1,0:T(8,128)(2,1)S(1)}, bf16[2,96,768]{2,1,0:T(8,128)(2,1)S(1)}, u32[]{:S(2)}, u32[]{:S(2)}) collective-permute-start(bf16[2,96,768]{2,1,0:T(8,128)(2,1)S(1)} %get-tuple-element.330), channel_id=1, source_target_pairs={{0,8},{4,12},{8,0},{12,4},{16,24},{20,28},{24,16},{28,20},{1,9},{5... | collective-permute-start | bytes 884744 | tf_op jit(solution)/shard_map/ppermute | solution.py:1071
  155.6 15.7 %collective-permute-start.37 = (bf16[192,1536]{1,0:T(8,128)(2,1)S(1)}, bf16[192,1536]{1,0:T(8,128)(2,1)S(1)}, u32[]{:S(2)}, u32[]{:S(2)}) collective-permute-start(bf16[192,1536]{1,0:T(8,128)(2,1)S(1)} %get-tuple-element.342), channel_id=1, source_target_pairs={{0,8},{4,12},{8,0},{12,4},{16,24},{20,28},{24,16},{28,20},{1,9},{5... | collective-permute-start | bytes 1769480 | tf_op jit(solution)/shard_map/ppermute | solution.py:1071
  156.9 14.4 %collective-permute-start.38 = (bf16[192,1536]{1,0:T(8,128)(2,1)S(1)}, bf16[192,1536]{1,0:T(8,128)(2,1)S(1)}, u32[]{:S(2)}, u32[]{:S(2)}) collective-permute-start(bf16[192,1536]{1,0:T(8,128)(2,1)S(1)} %get-tuple-element.343), channel_id=1, source_target_pairs={{0,16},{4,20},{8,24},{12,28},{16,0},{20,4},{24,8},{28,12},{1,17},{... | collective-permute-start | bytes 1769480 | tf_op jit(solution)/shard_map/ppermute | solution.py:1071
  159.0 12.4 %collective-permute-start.36 = (bf16[2,96,768]{2,1,0:T(8,128)(2,1)S(1)}, bf16[2,96,768]{2,1,0:T(8,128)(2,1)S(1)}, u32[]{:S(2)}, u32[]{:S(2)}) collective-permute-start(bf16[2,96,768]{2,1,0:T(8,128)(2,1)S(1)} %get-tuple-element.341), channel_id=1, source_target_pairs={{0,1},{1,0},{2,3},{3,2},{4,5},{5,4},{6,7},{7,6},{8,9},{9,8},{10,11... | collective-permute-start | bytes 884744 | tf_op jit(solution)/shard_map/ppermute | solution.py:1071
  166.0 18.9 %collective-permute-start.39 = (bf16[256,768]{1,0:T(8,128)(2,1)S(1)}, bf16[256,768]{1,0:T(8,128)(2,1)S(1)}, u32[]{:S(2)}, u32[]{:S(2)}) collective-permute-start(bf16[256,768]{1,0:T(8,128)(2,1)S(1)} %get-tuple-element.353), channel_id=1, source_target_pairs={{0,0},{1,1},{4,2},{5,3},{2,4},{3,5},{6,6},{7,7},{8,8},{9,9},{12,10... | collective-permute-start | bytes 1179656 | tf_op jit(solution)/shard_map/ppermute | solution.py:1084
  170.7 14.2 %collective-permute-start.40 = (bf16[256,768]{1,0:T(8,128)(2,1)S(1)}, bf16[256,768]{1,0:T(8,128)(2,1)S(1)}, u32[]{:S(2)}, u32[]{:S(2)}) collective-permute-start(bf16[256,768]{1,0:T(8,128)(2,1)S(1)} %get-tuple-element.354), channel_id=1, source_target_pairs={{1,0},{0,1},{5,2},{4,3},{3,4},{2,5},{7,6},{6,7},{9,8},{8,9},{13,10... | collective-permute-start | bytes 1179656 | tf_op jit(solution)/shard_map/ppermute | solution.py:1084
  172.0 12.9 %collective-permute-start.41 = (bf16[96,1536]{1,0:T(8,128)(2,1)S(1)}, bf16[96,1536]{1,0:T(8,128)(2,1)S(1)}, u32[]{:S(2)}, u32[]{:S(2)}) collective-permute-start(bf16[96,1536]{1,0:T(8,128)(2,1)S(1)} %get-tuple-element.359), channel_id=1, source_target_pairs={{0,16},{4,20},{8,24},{12,28},{16,0},{20,4},{24,8},{28,12},{1,17},{... | collective-permute-start | bytes 884744 | tf_op jit(solution)/shard_map/ppermute | solution.py:1071
  172.5 12.5 %collective-permute-start.42 = (bf16[96,1536]{1,0:T(8,128)(2,1)S(1)}, bf16[96,1536]{1,0:T(8,128)(2,1)S(1)}, u32[]{:S(2)}, u32[]{:S(2)}) collective-permute-start(bf16[96,1536]{1,0:T(8,128)(2,1)S(1)} %get-tuple-element.360), channel_id=1, source_target_pairs={{0,8},{4,12},{8,0},{12,4},{16,24},{20,28},{24,16},{28,20},{1,9},{5... | collective-permute-start | bytes 884744 | tf_op jit(solution)/shard_map/ppermute | solution.py:1071
  193.2 12.2 %collective-permute-start.45 = (bf16[2,2,24,1536]{3,2,1,0:T(8,128)(2,1)S(1)}, bf16[2,2,24,1536]{3,2,1,0:T(8,128)(2,1)S(1)}, u32[]{:S(2)}, u32[]{:S(2)}) collective-permute-start(bf16[2,2,24,1536]{3,2,1,0:T(8,128)(2,1)S(1)} %get-tuple-element.374), channel_id=1, source_target_pairs={{0,1},{1,0},{2,3},{3,2},{4,5},{5,4},{6,7},{7,6},{8,9},{9,8},{10,11... | collective-permute-start | bytes 884744 | tf_op jit(solution)/shard_map/ppermute | solution.py:1071
  205.4 21.4 %collective-permute-start.52 = (bf16[192,1152]{1,0:T(8,128)(2,1)S(1)}, bf16[192,1152]{1,0:T(8,128)(2,1)S(1)}, u32[]{:S(2)}, u32[]{:S(2)}) collective-permute-start(bf16[192,1152]{1,0:T(8,128)(2,1)S(1)} %get-tuple-element.415), channel_id=1, source_target_pairs={{0,8},{4,12},{8,0},{12,4},{16,24},{20,28},{24,16},{28,20},{1,9},{5... | collective-permute-start | bytes 1327112 | tf_op jit(solution)/shard_map/ppermute | solution.py:1071
  209.5 17.4 %collective-permute-start.53 = (bf16[192,1152]{1,0:T(8,128)(2,1)S(1)}, bf16[192,1152]{1,0:T(8,128)(2,1)S(1)}, u32[]{:S(2)}, u32[]{:S(2)}) collective-permute-start(bf16[192,1152]{1,0:T(8,128)(2,1)S(1)} %get-tuple-element.416), channel_id=1, source_target_pairs={{0,16},{4,20},{8,24},{12,28},{16,0},{20,4},{24,8},{28,12},{1,17},{... | collective-permute-start | bytes 1327112 | tf_op jit(solution)/shard_map/ppermute | solution.py:1071
  212.6 14.2 %collective-permute-start.49 = (bf16[256,768]{1,0:T(8,128)(2,1)S(1)}, bf16[256,768]{1,0:T(8,128)(2,1)S(1)}, u32[]{:S(2)}, u32[]{:S(2)}) collective-permute-start(bf16[256,768]{1,0:T(8,128)(2,1)S(1)} %get-tuple-element.401), channel_id=1, source_target_pairs={{0,0},{1,1},{4,2},{5,3},{2,4},{3,5},{6,6},{7,7},{8,8},{9,9},{12,10... | collective-permute-start | bytes 1179656 | tf_op jit(solution)/shard_map/ppermute | solution.py:1084
  226.8 16.6 %collective-permute-start.57 = (bf16[256,768]{1,0:T(8,128)(2,1)}, bf16[256,768]{1,0:T(8,128)(2,1)}, u32[]{:S(2)}, u32[]{:S(2)}) collective-permute-start(bf16[256,768]{1,0:T(8,128)(2,1)} %get-tuple-element.434), channel_id=1, source_target_pairs={{1,0},{0,1},{5,2},{4,3},{3,4},{2,5},{7,6},{6,7},{9,8},{8,9},{13,10... | collective-permute-start | bytes 1179656 | tf_op jit(solution)/shard_map/ppermute | solution.py:1084
  230.2 13.3 %collective-permute-start.56 = (bf16[2,24,1536]{2,1,0:T(8,128)(2,1)}, bf16[2,24,1536]{2,1,0:T(8,128)(2,1)}, u32[]{:S(2)}, u32[]{:S(2)}) collective-permute-start(bf16[2,24,1536]{2,1,0:T(8,128)(2,1)} %get-tuple-element.432), channel_id=1, source_target_pairs={{0,2},{1,3},{2,0},{3,1},{4,6},{5,7},{6,4},{7,5},{8,10},{9,11},{10,... | collective-permute-start | bytes 442376 | tf_op jit(solution)/shard_map/ppermute | solution.py:1071
  237.2 20.2 %collective-permute-start.59 = (bf16[2,24,1664]{2,1,0:T(8,128)(2,1)}, bf16[2,24,1664]{2,1,0:T(8,128)(2,1)S(1)}, u32[]{:S(2)}, u32[]{:S(2)}) collective-permute-start(bf16[2,24,1664]{2,1,0:T(8,128)(2,1)} %get-tuple-element.445), channel_id=1, source_target_pairs={{0,1},{1,0},{2,3},{3,2},{4,5},{5,4},{6,7},{7,6},{8,9},{9,8},{10,11... | collective-permute-start | bytes 479240 | tf_op jit(solution)/shard_map/ppermute | solution.py:1071
  237.5 19.8 %collective-permute-start.60 = (bf16[2,24,1664]{2,1,0:T(8,128)(2,1)}, bf16[2,24,1664]{2,1,0:T(8,128)(2,1)S(1)}, u32[]{:S(2)}, u32[]{:S(2)}) collective-permute-start(bf16[2,24,1664]{2,1,0:T(8,128)(2,1)} %get-tuple-element.446), channel_id=1, source_target_pairs={{0,2},{1,3},{2,0},{3,1},{4,6},{5,7},{6,4},{7,5},{8,10},{9,11},{10,... | collective-permute-start | bytes 479240 | tf_op jit(solution)/shard_map/ppermute | solution.py:1071
  237.6 19.8 %collective-permute-start.61 = (bf16[2,24,1664]{2,1,0:T(8,128)(2,1)}, bf16[2,24,1664]{2,1,0:T(8,128)(2,1)S(1)}, u32[]{:S(2)}, u32[]{:S(2)}) collective-permute-start(bf16[2,24,1664]{2,1,0:T(8,128)(2,1)} %get-tuple-element.447), channel_id=1, source_target_pairs={{0,3},{1,2},{2,1},{3,0},{4,7},{5,6},{6,5},{7,4},{8,11},{9,10},{10,... | collective-permute-start | bytes 479240 | tf_op jit(solution)/shard_map/ppermute | solution.py:1071
  244.4 11.6 %collective-permute-start.58 = (bf16[24,1536]{1,0:T(8,128)(2,1)S(1)}, bf16[24,1536]{1,0:T(8,128)(2,1)S(1)}, u32[]{:S(2)}, u32[]{:S(2)}) collective-permute-start(bf16[24,1536]{1,0:T(8,128)(2,1)S(1)} %fusion.1), channel_id=1, source_target_pairs={{0,4},{4,0},{8,12},{12,8},{16,20},{20,16},{24,28},{28,24},{1,5},{5... | collective-permute-start | bytes 221192 | tf_op jit(solution)/shard_map/ppermute | solution.py:1071
  (31 other events, 195.5 us)

commit v8 on v7

--- a/solution.py
+++ b/solution.py
@@ -1311,14 +1311,19 @@
     att, cot_low, cot_high, *rest = together(att, cot_low, cot_high, *down_chips, *up_chips)
     down_chips, up_chips = rest[:count], rest[count:]
 
+    if plane:
+        up_own, up_x, up_y = up_chips
+        up_first, up_second = cut(info, up_x, up_y)
+        att, cot_low, cot_high, up_first, up_second, *down_chips = together(
+            att, cot_low, cot_high, up_first, up_second, *down_chips
+        )
+        up_chips = [up_own, up_x, up_y, swap(up_first, "wide", 2), swap(up_second, "wide", 4)]
     att_far = swap(att, "wide", 1)
     if plane:
         out_rows = last_blocks(info, *down_chips[:3], down_chips[4])
         out_weights = [out_rows, swap(out_rows, "wide", 1)]
     else:
         out_weights = [lax.all_gather(output_weight, ("wide", "narrow"), axis=0, tiled=True)]
-    if plane:
-        up_chips = cross_two(up_chips)
     cots = [cot_low, cot_high, swap(cot_low, "wide", 1), swap(cot_high, "wide", 1)]
     if plane:
         up_blocks = [part.reshape((-1,) + part.shape[-1:]) for part in up_chips]

time: 267 us -> 268 us (level)
  no operation moved by 1% of the time
where the time goes in v8:
time: 268 us; the launch traced here: 263 us
  Pallas kernels  98.1 us (37%)
  starting transfers between devices  81.6 us (30%)
  waiting for transfers between devices  64 us (24%)
  local copies, waits for them, and re-layouts  10.8 us (4%)
  other arithmetic  6.59 us (2%)
    pallas_call x36, Pallas kernels, call(): pl.pallas_call(loaded if loads else kernel, out_shape=[shape for shape, _...  98.1 us
    ppermute x55, waiting for transfers between devices, swap(): return lax.ppermute(values, axis, [(i, i ^ bits) for i in range(size)])  59.5 us
    ppermute x55, starting transfers between devices, swap(): return lax.ppermute(values, axis, [(i, i ^ bits) for i in range(size)])  57.1 us
    ppermute x4, starting transfers between devices, unspread_turn(): lax.ppermute(part, ('wide', 'narrow'), [(b, a) for a, b in spread_perm(tu...  9.32 us
    ppermute x1, starting transfers between devices, local(): low = lax.ppermute(first, ('wide', 'narrow'), spread_perm(0))  7.52 us
  transfers between devices with their start and end apart: 63, of which 19 were waited for; matrix products, arithmetic and copies ran while one was open for 3% of the time, Pallas kernels for 30%

profile of v8, /device:TPU:7, one launch (start us, length us, event | category | flops | bytes accessed | tf_op | source)
XLA Modules:
  0.0 262.7 jit_solution(6709361630855945095)
XLA Ops:
  7.8 2.4 collective-permute-start.2
  10.8 1.4 collective-permute-start.3
  12.2 2.2 collective-permute-start.5
  18.7 8.2 %collective-permute-done.4.refs_2_ = bf16[2,24,1280]{2,1,0:T(8,128)(2,1)S(1)} collective-permute-done((bf16[2,24,1280]{2,1,0:T(8,128)(2,1)S(1)}, bf16[2,24,1280]{2,1,0:T(8,128)(2,1)S(1)}, u32[]{:S(2)}, u32[]{:S(2)}) %collective-permute-start.4) | collective-permute-done | bytes 122912 | tf_op jit(solution)/shard_map/ppermute | solution.py:1071
  26.9 7.5 %collective-permute-start.6 = (bf16[272,768]{1,0:T(8,128)(2,1)S(1)}, bf16[272,768]{1,0:T(8,128)(2,1)S(1)}, u32[]{:S(2)}, u32[]{:S(2)}) collective-permute-start(bf16[272,768]{1,0:T(8,128)(2,1)S(1)} %get-tuple-element.257), channel_id=1, source_target_pairs={{0,0},{1,1},{2,4},{3,5},{4,2},{5,3},{6,6},{7,7},{8,8},{9,9},{10,12... | collective-permute-start | bytes 1253384 | tf_op jit(solution)/shard_map/ppermute | solution.py:1277
  36.3 2.2 collective-permute-start.14
  39.0 9.2 %collective-permute-done.7.far = bf16[2,120,768]{2,1,0:T(8,128)(2,1)S(1)} collective-permute-done((bf16[2,120,768]{2,1,0:T(8,128)(2,1)S(1)}, bf16[2,120,768]{2,1,0:T(8,128)(2,1)S(1)}, u32[]{:S(2)}, u32[]{:S(2)}) %collective-permute-start.7) | collective-permute-done | bytes 368672 | tf_op jit(solution)/shard_map/ppermute | solution.py:1071
  49.3 8.2 %collective-permute-done.13 = bf16[2,4,24,1280]{3,2,1,0:T(8,128)(2,1)S(1)} collective-permute-done((bf16[2,4,24,1280]{3,2,1,0:T(8,128)(2,1)S(1)}, bf16[2,4,24,1280]{3,2,1,0:T(8,128)(2,1)S(1)}, u32[]{:S(2)}, u32[]{:S(2)}) %collective-permute-start.13) | collective-permute-done | bytes 491552 | tf_op jit(solution)/shard_map/ppermute | solution.py:1071
  57.5 1.5 collective-permute-start.16
  59.0 2.6 collective-permute-done.9.refs_1_
  61.6 6.3 %collective-permute-start.11 = (bf16[272,768]{1,0:T(8,128)(2,1)S(1)}, bf16[272,768]{1,0:T(8,128)(2,1)S(1)}, u32[]{:S(2)}, u32[]{:S(2)}) collective-permute-start(bf16[272,768]{1,0:T(8,128)(2,1)S(1)} %collective-permute-done.8.refs_1_), channel_id=1, source_target_pairs={{0,4},{4,0},{8,12},{12,8},{16,20},{20,16},{24,28},{28,24},{1,5},{5... | collective-permute-start | bytes 1253384 | tf_op jit(solution)/shard_map/ppermute | solution.py:1071
  69.9 7.0 %shard_map.305 = (bf16[1024,384]{1,0:T(8,128)(2,1)S(1)}, bf16[1024,384]{1,0:T(8,128)(2,1)S(1)}, bf16[1024,384]{1,0:T(8,128)(2,1)S(1)}, f32[1024,768]{1,0:T(8,128...) custom-call(s32[4]{0:T(128)S(1)} %pad_add_fusion.info, ...), custom_call_target="tpu_custom_call" | custom-call | flops 2013265920 | bytes 12582912 | tf_op jit(solution)/shard_map/pallas_call | solution.py:61
  81.5 2.3 collective-permute-start.19
  83.8 1.8 collective-permute-done.20.refs_12_
  85.6 4.9 %collective-permute-start.18 = (bf16[256,768]{1,0:T(8,128)(2,1)S(1)}, bf16[256,768]{1,0:T(8,128)(2,1)S(1)}, u32[]{:S(2)}, u32[]{:S(2)}) collective-permute-start(bf16[256,768]{1,0:T(8,128)(2,1)S(1)} %get-tuple-element.290), channel_id=1, source_target_pairs={{0,0},{1,1},{2,4},{3,5},{4,2},{5,3},{6,6},{7,7},{8,8},{9,9},{10,12... | collective-permute-start | bytes 1179656 | tf_op jit(solution)/shard_map/ppermute | solution.py:1296
  90.5 13.2 %shard_map.308 = (bf16[1024,384]{1,0:T(8,128)(2,1)S(1)}, f32[3,8,1024]{2,1,0:T(8,128)S(1)}) custom-call(s32[4]{0:T(128)S(1)} %pad_add_fusion.info, bf16[1024,384]{1,0:T(8,128)(2,1)S(1)} %get-tuple-element.285.q, bf16[1024,384]{1,0:T(8,128)(2,1)S(1)} %get-tuple-element.286.k, bf16[1024,384]{1,0:T(8,128)(2,1)S(1)} %get-tuple-element.287.v, ...), custom_call_target="tpu_custom_call" | custom-call | flops 2415919104 | bytes 4194304 | tf_op jit(solution)/shard_map/pallas_call | solution.py:61
  104.4 1.5 collective-permute-start.24
  108.9 4.2 %shard_map.313 = (f32[1024,768]{1,0:T(8,128)S(1)}, bf16[1024,768]{1,0:T(8,128)(2,1)S(1)}, f32[8,1536]{1,0:T(8,128)S(1)}, bf16[768,768]{1,0:T(8,128)(2,1)S(1)}) custom-call(s32[4]{0:T(128)S(1)} %pad_add_fusion.info, bf16[1024,384]{1,0:T(8,128)(2,1)S(1)} %get-tuple-element.310.att.o, bf16[1024,384]{1,0:T(8,128)(2,1)S(1)} %collective-permute-done.24.att_far, ...), custom_call_target="tpu_custom_call" | custom-call | flops 1207959552 | bytes 12582912 | tf_op jit(solution)/shard_map/pallas_call | solution.py:61
  113.1 2.2 collective-permute-done.28
  115.3 1.6 collective-permute-done.29
  116.9 14.5 %shard_map.314 = (f32[512,768]{1,0:T(8,128)S(1)}, bf16[512,768]{1,0:T(8,128)(2,1)S(1)}, bf16[1024,1536]{1,0:T(8,128)(2,1)S(1)}, bf16[768,1536]{1,0:T(8,128)(2,1)...) custom-call(s32[4]{0:T(128)S(1)} %pad_add_fusion.info, ...), custom_call_target="tpu_custom_call" | custom-call | flops 7247757312 | bytes 25165824 | tf_op jit(solution)/shard_map/pallas_call | solution.py:61
  131.9 6.8 %shard_map.315 = (f32[1024,768]{1,0:T(8,128)S(1)}, bf16[1024,768]{1,0:T(8,128)(2,1)S(1)}, bf16[1024,1536]{1,0:T(8,128)(2,1)S(1)}, f32[8,768]{1,0:T(8,128)S(1)}) custom-call(s32[4]{0:T(128)S(1)} %pad_add_fusion.info, bf16[1024,1536]{1,0:T(8,128)(2,1)S(1)} %get-tuple-element.325.slope, bf16[4,256,768]{2,1,0:T(8,128)(2,1)S(1)} %get-tuple-element.326.cot, ...), custom_call_target="tpu_custom_call" | custom-call | flops 4831838208 | bytes 25165824 | tf_op jit(solution)/shard_map/pallas_call | solution.py:61
  138.7 6.4 %collective-permute-done.30.refs_1_ = bf16[4,96,768]{2,1,0:T(8,128)(2,1)S(1)} collective-permute-done((bf16[4,96,768]{2,1,0:T(8,128)(2,1)S(1)}, bf16[4,96,768]{2,1,0:T(8,128)(2,1)S(1)}, u32[]{:S(2)}, u32[]{:S(2)}) %collective-permute-start.30) | collective-permute-done | bytes 589856 | tf_op jit(solution)/shard_map/ppermute | solution.py:1071
  145.1 2.3 collective-permute-start.32
  149.7 3.7 %shard_map.316 = (bf16[192,1536]{1,0:T(8,128)(2,1)S(1)}, bf16[192,1536]{1,0:T(8,128)(2,1)S(1)}, bf16[192,1536]{1,0:T(8,128)(2,1)S(1)}, bf16[96,1536]{1,0:T(8,128)(2,1)S(1)}, bf16[96,1536]{1,0:T(8,128)(2,1)S(1)}) custom-call(s32[4]{0:T(128)S(1)} %pad_add_fusion.info, bf16[1024,768]{1,0:T(8,128)(2,1)S(1)} %get-tuple-element.338.normed.left, ...), custom_call_target="tpu_custom_call" | custom-call | flops 2415919104 | bytes 8388608 | tf_op jit(solution)/shard_map/pallas_call | solution.py:61
  153.4 2.8 %collective-permute-done.34 = bf16[2,96,768]{2,1,0:T(8,128)(2,1)S(1)} collective-permute-done((bf16[2,96,768]{2,1,0:T(8,128)(2,1)S(1)}, bf16[2,96,768]{2,1,0:T(8,128)(2,1)S(1)}, u32[]{:S(2)}, u32[]{:S(2)}) %collective-permute-start.34) | collective-permute-done | bytes 294944 | tf_op jit(solution)/shard_map/ppermute | solution.py:1071
  160.1 5.7 %shard_map.318 = (f32[512,768]{1,0:T(8,128)S(1)}, bf16[1024,384]{1,0:T(8,128)(2,1)S(1)}, bf16[2,96,768]{2,1,0:T(8,128)(2,1)S(1)}, bf16[2,96,768]{2,1,0:T(8,128)(2,1)S(1)}, f32[8,768]{1,0:T(8,128)S(1)}) custom-call(s32[4]{0:T(128)S(1)} %pad_add_fusion.info, f32[1024,768]{1,0:T(8,128)S(1)} %get-tuple-element.352.back, ...), custom_call_target="tpu_custom_call" | custom-call | flops 1207959552 | bytes 14680064 | tf_op jit(solution)/shard_map/pallas_call | solution.py:61
  166.6 4.8 %collective-permute-start.39 = (bf16[256,768]{1,0:T(8,128)(2,1)S(1)}, bf16[256,768]{1,0:T(8,128)(2,1)S(1)}, u32[]{:S(2)}, u32[]{:S(2)}) collective-permute-start(bf16[256,768]{1,0:T(8,128)(2,1)S(1)} %get-tuple-element.373), channel_id=1, source_target_pairs={{0,0},{1,1},{4,2},{5,3},{2,4},{3,5},{6,6},{7,7},{8,8},{9,9},{12,10... | collective-permute-start | bytes 1179656 | tf_op jit(solution)/shard_map/ppermute | solution.py:1084
  173.3 12.2 %shard_map.320 = (bf16[1024,384]{1,0:T(8,128)(2,1)S(1)}, bf16[1024,384]{1,0:T(8,128)(2,1)S(1)}, bf16[1024,384]{1,0:T(8,128)(2,1)S(1)}) custom-call(s32[4]{0:T(128)S(1)} %pad_add_fusion.info, bf16[1024,384]{1,0:T(8,128)(2,1)S(1)} %get-tuple-element.285.q, bf16[1024,384]{1,0:T(8,128)(2,1)S(1)} %get-tuple-element.286.k, ...), custom_call_target="tpu_custom_call" | custom-call | flops 6039797760 | bytes 6291456 | tf_op jit(solution)/shard_map/pallas_call | solution.py:61
  185.6 3.2 %shard_map.323 = (f32[512,768]{1,0:T(8,128)S(1)}, bf16[512,768]{1,0:T(8,128)(2,1)S(1)}) custom-call(s32[4]{0:T(128)S(1)} %pad_add_fusion.info, bf16[1024,384]{1,0:T(8,128)(2,1)S(1)} %get-tuple-element.381.dq.refs_8_.refs_0_, bf16[1024,384]{1,0:T(8,128)(2,1)S(1)} %get-tuple-element.382.dk.refs_1_, ...), custom_call_target="tpu_custom_call" | custom-call | flops 1811939328 | bytes 8388608 | tf_op jit(solution)/shard_map/pallas_call | solution.py:61
  188.8 2.7 %collective-permute-start.43 = (bf16[512,768]{1,0:T(8,128)(2,1)S(1)}, bf16[512,768]{1,0:T(8,128)(2,1)S(1)}, u32[]{:S(2)}, u32[]{:S(2)}) collective-permute-start(bf16[512,768]{1,0:T(8,128)(2,1)S(1)} %get-tuple-element.385), channel_id=1, source_target_pairs={{0,4},{4,0},{8,12},{12,8},{16,20},{20,16},{24,28},{28,24},{1,5},{5... | collective-permute-start | bytes 2359304 | tf_op jit(solution)/shard_map/ppermute | solution.py:1071
  193.8 2.0 collective-permute-start.45
  195.8 3.6 %shard_map.326 = (bf16[512,768]{1,0:T(8,128)(2,1)S(1)}, bf16[192,512]{1,0:T(8,128)(2,1)S(1)}, bf16[192,512]{1,0:T(8,128)(2,1)S(1)}, bf16[192,512]{1,0:T(8,128)(2...) custom-call(s32[4]{0:T(128)S(1)} %pad_add_fusion.info, f32[512,768]{1,0:T(8,128)S(1)} %get-tuple-element.397.refs_0_, ...), custom_call_target="tpu_custom_call" | custom-call | flops 100663296 | bytes 10485760 | tf_op jit(solution)/shard_map/pallas_call | solution.py:61
  199.9 1.3 collective-permute-start.46
  201.2 4.8 %shard_map.327 = (bf16[192,1152]{1,0:T(8,128)(2,1)S(1)}, bf16[192,1152]{1,0:T(8,128)(2,1)S(1)}, bf16[192,1152]{1,0:T(8,128)(2,1)S(1)}, bf16[96,1152]{1,0:T(8,128)(2,1)S(1)}, bf16[96,1152]{1,0:T(8,128)(2,1)S(1)}) custom-call(s32[4]{0:T(128)S(1)} %pad_add_fusion.info, bf16[1024,768]{1,0:T(8,128)(2,1)S(1)} %get-tuple-element.411.left, ...), custom_call_target="tpu_custom_call" | custom-call | flops 1811939328 | bytes 8388608 | tf_op jit(solution)/shard_map/pallas_call | solution.py:61
  206.1 4.1 %collective-permute-start.52 = (bf16[192,1152]{1,0:T(8,128)(2,1)S(1)}, bf16[192,1152]{1,0:T(8,128)(2,1)S(1)}, u32[]{:S(2)}, u32[]{:S(2)}) collective-permute-start(bf16[192,1152]{1,0:T(8,128)(2,1)S(1)} %get-tuple-element.435), channel_id=1, source_target_pairs={{0,8},{4,12},{8,0},{12,4},{16,24},{20,28},{24,16},{28,20},{1,9},{5... | collective-permute-start | bytes 1327112 | tf_op jit(solution)/shard_map/ppermute | solution.py:1071
  210.2 1.9 collective-permute-start.53
  212.0 1.3 shard_map.328
  213.4 2.6 collective-permute-start.49
  218.4 4.7 %collective-permute-done.50.refs_8_ = bf16[96,512]{1,0:T(8,128)(2,1)S(1)} collective-permute-done((bf16[96,512]{1,0:T(8,128)(2,1)S(1)}, bf16[96,512]{1,0:T(8,128)(2,1)S(1)}, u32[]{:S(2)}, u32[]{:S(2)}) %collective-permute-start.50) | collective-permute-done | bytes 98336 | tf_op jit(solution)/shard_map/ppermute | solution.py:1071
  223.1 4.5 %collective-permute-done.49 = bf16[256,768]{1,0:T(8,128)(2,1)S(1)} collective-permute-done((bf16[256,768]{1,0:T(8,128)(2,1)S(1)}, bf16[256,768]{1,0:T(8,128)(2,1)S(1)}, u32[]{:S(2)}, u32[]{:S(2)}) %collective-permute-start.49) | collective-permute-done | bytes 393248 | tf_op jit(solution)/shard_map/ppermute | solution.py:1084
  227.6 1.4 collective-permute-start.57
  229.0 1.4 shard_map.331
  230.8 4.6 %collective-permute-done.54.refs_3_ = bf16[96,1152]{1,0:T(8,128)(2,1)S(1)} collective-permute-done((bf16[96,1152]{1,0:T(8,128)(2,1)}, bf16[96,1152]{1,0:T(8,128)(2,1)S(1)}, u32[]{:S(2)}, u32[]{:S(2)}) %collective-permute-start.54) | collective-permute-done | bytes 221216 | tf_op jit(solution)/shard_map/ppermute | solution.py:1071
  236.3 1.6 shard_map.332
  238.3 3.3 %collective-permute-start.61 = (bf16[2,24,1664]{2,1,0:T(8,128)(2,1)}, bf16[2,24,1664]{2,1,0:T(8,128)(2,1)S(1)}, u32[]{:S(2)}, u32[]{:S(2)}) collective-permute-start(bf16[2,24,1664]{2,1,0:T(8,128)(2,1)} %get-tuple-element.467), channel_id=1, source_target_pairs={{0,3},{1,2},{2,1},{3,0},{4,7},{5,6},{6,5},{7,4},{8,11},{9,10},{10,... | collective-permute-start | bytes 479240 | tf_op jit(solution)/shard_map/ppermute | solution.py:1071
  241.5 2.6 %collective-permute-done.56 = bf16[2,24,1536]{2,1,0:T(8,128)(2,1)} collective-permute-done((bf16[2,24,1536]{2,1,0:T(8,128)(2,1)}, bf16[2,24,1536]{2,1,0:T(8,128)(2,1)}, u32[]{:S(2)}, u32[]{:S(2)}) %collective-permute-start.56) | collective-permute-done | bytes 147488 | tf_op jit(solution)/shard_map/ppermute | solution.py:1071
  245.2 7.8 %collective-permute-start.58 = (bf16[24,1536]{1,0:T(8,128)(2,1)S(1)}, bf16[24,1536]{1,0:T(8,128)(2,1)S(1)}, u32[]{:S(2)}, u32[]{:S(2)}) collective-permute-start(bf16[24,1536]{1,0:T(8,128)(2,1)S(1)} %fusion.1), channel_id=1, source_target_pairs={{0,4},{4,0},{8,12},{12,8},{16,20},{20,16},{24,28},{28,24},{1,5},{5... | collective-permute-start | bytes 221192 | tf_op jit(solution)/shard_map/ppermute | solution.py:1071
  (181 shorter events, 52.2 us)
Async XLA Ops:
  7.8 19.1 %collective-permute-start.2 = (bf16[120,768]{1,0:T(8,128)(2,1)S(1)}, bf16[120,768]{1,0:T(8,128)(2,1)S(1)}, u32[]{:S(2)}, u32[]{:S(2)}) collective-permute-start(bf16[120,768]{1,0:T(8,128)(2,1)S(1)} %pad_maximum_fusion.2.refs_0_), channel_id=1, source_target_pairs={{0,2},{1,3},{2,0},{3,1},{4,6},{5,7},{6,4},{7,5},{8,10},{9,11},{10,... | collective-permute-start | bytes 552968 | tf_op jit(solution)/shard_map/ppermute | solution.py:1071
  10.8 7.9 %collective-permute-start.3 = (bf16[2,24,1280]{2,1,0:T(8,128)(2,1)S(1)}, bf16[2,24,1280]{2,1,0:T(8,128)(2,1)S(1)}, u32[]{:S(2)}, u32[]{:S(2)}) collective-permute-start(bf16[2,24,1280]{2,1,0:T(8,128)(2,1)S(1)} %shard_map.300.refs_0_), channel_id=1, source_target_pairs={{0,1},{1,0},{2,3},{3,2},{4,5},{5,4},{6,7},{7,6},{8,9},{9,8},{10,11... | collective-permute-start | bytes 368648 | tf_op jit(solution)/shard_map/ppermute | solution.py:1071
  12.1 14.8 %collective-permute-start.4 = (bf16[2,24,1280]{2,1,0:T(8,128)(2,1)S(1)}, bf16[2,24,1280]{2,1,0:T(8,128)(2,1)S(1)}, u32[]{:S(2)}, u32[]{:S(2)}) collective-permute-start(bf16[2,24,1280]{2,1,0:T(8,128)(2,1)S(1)} %shard_map.300.refs_0_), channel_id=1, source_target_pairs={{0,2},{1,3},{2,0},{3,1},{4,6},{5,7},{6,4},{7,5},{8,10},{9,11},{10,... | collective-permute-start | bytes 368648 | tf_op jit(solution)/shard_map/ppermute | solution.py:1071
  12.2 14.7 %collective-permute-start.5 = (bf16[2,24,1280]{2,1,0:T(8,128)(2,1)S(1)}, bf16[2,24,1280]{2,1,0:T(8,128)(2,1)S(1)}, u32[]{:S(2)}, u32[]{:S(2)}) collective-permute-start(bf16[2,24,1280]{2,1,0:T(8,128)(2,1)S(1)} %shard_map.300.refs_0_), channel_id=1, source_target_pairs={{0,3},{1,2},{2,1},{3,0},{4,7},{5,6},{6,5},{7,4},{8,11},{9,10},{10,... | collective-permute-start | bytes 368648 | tf_op jit(solution)/shard_map/ppermute | solution.py:1071
  26.9 21.3 %collective-permute-start.6 = (bf16[272,768]{1,0:T(8,128)(2,1)S(1)}, bf16[272,768]{1,0:T(8,128)(2,1)S(1)}, u32[]{:S(2)}, u32[]{:S(2)}) collective-permute-start(bf16[272,768]{1,0:T(8,128)(2,1)S(1)} %get-tuple-element.257), channel_id=1, source_target_pairs={{0,0},{1,1},{2,4},{3,5},{4,2},{5,3},{6,6},{7,7},{8,8},{9,9},{10,12... | collective-permute-start | bytes 1253384 | tf_op jit(solution)/shard_map/ppermute | solution.py:1277
  35.0 13.2 %collective-permute-start.7 = (bf16[2,120,768]{2,1,0:T(8,128)(2,1)S(1)}, bf16[2,120,768]{2,1,0:T(8,128)(2,1)S(1)}, u32[]{:S(2)}, u32[]{:S(2)}) collective-permute-start(bf16[2,120,768]{2,1,0:T(8,128)(2,1)S(1)} %shard_map.301.own), channel_id=1, source_target_pairs={{0,1},{1,0},{2,3},{3,2},{4,5},{5,4},{6,7},{7,6},{8,9},{9,8},{10,11... | collective-permute-start | bytes 1105928 | tf_op jit(solution)/shard_map/ppermute | solution.py:1071
  35.7 13.6 %collective-permute-start.12 = (bf16[2,4,24,1280]{3,2,1,0:T(8,128)(2,1)S(1)}, bf16[2,4,24,1280]{3,2,1,0:T(8,128)(2,1)S(1)}, u32[]{:S(2)}, u32[]{:S(2)}) collective-permute-start(bf16[2,4,24,1280]{3,2,1,0:T(8,128)(2,1)S(1)} %shard_map.304), channel_id=1, source_target_pairs={{0,8},{4,12},{8,0},{12,4},{16,24},{20,28},{24,16},{28,20},{1,9},{5... | collective-permute-start | bytes 1474568 | tf_op jit(solution)/shard_map/ppermute | solution.py:1071
  36.0 21.5 %collective-permute-start.13 = (bf16[2,4,24,1280]{3,2,1,0:T(8,128)(2,1)S(1)}, bf16[2,4,24,1280]{3,2,1,0:T(8,128)(2,1)S(1)}, u32[]{:S(2)}, u32[]{:S(2)}) collective-permute-start(bf16[2,4,24,1280]{3,2,1,0:T(8,128)(2,1)S(1)} %shard_map.304), channel_id=1, source_target_pairs={{0,16},{4,20},{8,24},{12,28},{16,0},{20,4},{24,8},{28,12},{1,17},{... | collective-permute-start | bytes 1474568 | tf_op jit(solution)/shard_map/ppermute | solution.py:1071
  36.3 21.3 %collective-permute-start.14 = (bf16[2,4,24,1280]{3,2,1,0:T(8,128)(2,1)S(1)}, bf16[2,4,24,1280]{3,2,1,0:T(8,128)(2,1)S(1)}, u32[]{:S(2)}, u32[]{:S(2)}) collective-permute-start(bf16[2,4,24,1280]{3,2,1,0:T(8,128)(2,1)S(1)} %shard_map.304), channel_id=1, source_target_pairs={{0,24},{4,28},{8,16},{12,20},{16,8},{20,12},{24,0},{28,4},{1,25},{... | collective-permute-start | bytes 1474568 | tf_op jit(solution)/shard_map/ppermute | solution.py:1071
  48.2 13.4 %collective-permute-start.8 = (bf16[272,768]{1,0:T(8,128)(2,1)S(1)}, bf16[272,768]{1,0:T(8,128)(2,1)S(1)}, u32[]{:S(2)}, u32[]{:S(2)}) collective-permute-start(bf16[272,768]{1,0:T(8,128)(2,1)S(1)} %get-tuple-element.263), channel_id=1, source_target_pairs={{0,1},{1,0},{2,5},{3,4},{4,3},{5,2},{6,7},{7,6},{8,9},{9,8},{10,13... | collective-permute-start | bytes 1253384 | tf_op jit(solution)/shard_map/ppermute | solution.py:1282
  48.7 13.0 %collective-permute-start.9 = (bf16[2,24,1536]{2,1,0:T(8,128)(2,1)S(1)}, bf16[2,24,1536]{2,1,0:T(8,128)(2,1)S(1)}, u32[]{:S(2)}, u32[]{:S(2)}) collective-permute-start(bf16[2,24,1536]{2,1,0:T(8,128)(2,1)S(1)} %shard_map.302.refs_0_), channel_id=1, source_target_pairs={{0,2},{1,3},{2,0},{3,1},{4,6},{5,7},{6,4},{7,5},{8,10},{9,11},{10,... | collective-permute-start | bytes 442376 | tf_op jit(solution)/shard_map/ppermute | solution.py:1071
  57.5 19.7 %collective-permute-start.16 = (bf16[5,96,768]{2,1,0:T(8,128)(2,1)S(1)}, bf16[5,96,768]{2,1,0:T(8,128)(2,1)S(1)}, u32[]{:S(2)}, u32[]{:S(2)}) collective-permute-start(bf16[5,96,768]{2,1,0:T(8,128)(2,1)S(1)} %shard_map.303.own.refs_9_), channel_id=1, source_target_pairs={{0,8},{4,12},{8,0},{12,4},{16,24},{20,28},{24,16},{28,20},{1,9},{5... | collective-permute-start | bytes 2211848 | tf_op jit(solution)/shard_map/ppermute | solution.py:1071
  59.0 18.2 %collective-permute-start.17 = (bf16[5,96,768]{2,1,0:T(8,128)(2,1)S(1)}, bf16[5,96,768]{2,1,0:T(8,128)(2,1)S(1)}, u32[]{:S(2)}, u32[]{:S(2)}) collective-permute-start(bf16[5,96,768]{2,1,0:T(8,128)(2,1)S(1)} %shard_map.303.own.refs_9_), channel_id=1, source_target_pairs={{0,16},{4,20},{8,24},{12,28},{16,0},{20,4},{24,8},{28,12},{1,17},{... | collective-permute-start | bytes 2211848 | tf_op jit(solution)/shard_map/ppermute | solution.py:1071
  59.0 9.6 %collective-permute-start.10 = (bf16[272,768]{1,0:T(8,128)(2,1)S(1)}, bf16[272,768]{1,0:T(8,128)(2,1)S(1)}, u32[]{:S(2)}, u32[]{:S(2)}) collective-permute-start(bf16[272,768]{1,0:T(8,128)(2,1)S(1)} %collective-permute-done.6.refs_0_), channel_id=1, source_target_pairs={{0,4},{4,0},{8,12},{12,8},{16,20},{20,16},{24,28},{28,24},{1,5},{5... | collective-permute-start | bytes 1253384 | tf_op jit(solution)/shard_map/ppermute | solution.py:1071
  68.5 8.7 %collective-permute-start.15 = (bf16[2,2,24,1536]{3,2,1,0:T(8,128)(2,1)S(1)}, bf16[2,2,24,1536]{3,2,1,0:T(8,128)(2,1)S(1)}, u32[]{:S(2)}, u32[]{:S(2)}) collective-permute-start(bf16[2,2,24,1536]{3,2,1,0:T(8,128)(2,1)S(1)} %shard_map.307.refs_0_), channel_id=1, source_target_pairs={{0,1},{1,0},{2,3},{3,2},{4,5},{5,4},{6,7},{7,6},{8,9},{9,8},{10,11... | collective-permute-start | bytes 884744 | tf_op jit(solution)/shard_map/ppermute | solution.py:1071
  77.8 7.8 %collective-permute-start.20 = (bf16[2,96,768]{2,1,0:T(8,128)(2,1)S(1)}, bf16[2,96,768]{2,1,0:T(8,128)(2,1)S(1)}, u32[]{:S(2)}, u32[]{:S(2)}) collective-permute-start(bf16[2,96,768]{2,1,0:T(8,128)(2,1)S(1)} %get-tuple-element.295), channel_id=1, source_target_pairs={{0,8},{4,12},{8,0},{12,4},{16,24},{20,28},{24,16},{28,20},{1,9},{5... | collective-permute-start | bytes 884744 | tf_op jit(solution)/shard_map/ppermute | solution.py:1071
  78.7 25.0 %collective-permute-start.22 = (bf16[2,4,24,1536]{3,2,1,0:T(8,128)(2,1)S(1)}, bf16[2,4,24,1536]{3,2,1,0:T(8,128)(2,1)S(1)}, u32[]{:S(2)}, u32[]{:S(2)}) collective-permute-start(bf16[2,4,24,1536]{3,2,1,0:T(8,128)(2,1)S(1)} %bitcast.64), channel_id=1, source_target_pairs={{0,8},{4,12},{8,0},{12,4},{16,24},{20,28},{24,16},{28,20},{1,9},{5... | collective-permute-start | bytes 1769480 | tf_op jit(solution)/shard_map/ppermute | solution.py:1071
  80.0 23.8 %collective-permute-start.23 = (bf16[2,4,24,1536]{3,2,1,0:T(8,128)(2,1)S(1)}, bf16[2,4,24,1536]{3,2,1,0:T(8,128)(2,1)S(1)}, u32[]{:S(2)}, u32[]{:S(2)}) collective-permute-start(bf16[2,4,24,1536]{3,2,1,0:T(8,128)(2,1)S(1)} %bitcast.65), channel_id=1, source_target_pairs={{0,16},{4,20},{8,24},{12,28},{16,0},{20,4},{24,8},{28,12},{1,17},{... | collective-permute-start | bytes 1769480 | tf_op jit(solution)/shard_map/ppermute | solution.py:1071
  80.2 23.5 %collective-permute-start.21 = (bf16[3,96,768]{2,1,0:T(8,128)(2,1)S(1)}, bf16[3,96,768]{2,1,0:T(8,128)(2,1)S(1)}, u32[]{:S(2)}, u32[]{:S(2)}) collective-permute-start(bf16[3,96,768]{2,1,0:T(8,128)(2,1)S(1)} %get-tuple-element.296), channel_id=1, source_target_pairs={{0,16},{4,20},{8,24},{12,28},{16,0},{20,4},{24,8},{28,12},{1,17},{... | collective-permute-start | bytes 1327112 | tf_op jit(solution)/shard_map/ppermute | solution.py:1071
  81.5 22.2 %collective-permute-start.19 = (bf16[256,768]{1,0:T(8,128)(2,1)S(1)}, bf16[256,768]{1,0:T(8,128)(2,1)S(1)}, u32[]{:S(2)}, u32[]{:S(2)}) collective-permute-start(bf16[256,768]{1,0:T(8,128)(2,1)S(1)} %get-tuple-element.291), channel_id=1, source_target_pairs={{0,1},{1,0},{2,5},{3,4},{4,3},{5,2},{6,7},{7,6},{8,9},{9,8},{10,13... | collective-permute-start | bytes 1179656 | tf_op jit(solution)/shard_map/ppermute | solution.py:1306
  85.6 18.1 %collective-permute-start.18 = (bf16[256,768]{1,0:T(8,128)(2,1)S(1)}, bf16[256,768]{1,0:T(8,128)(2,1)S(1)}, u32[]{:S(2)}, u32[]{:S(2)}) collective-permute-start(bf16[256,768]{1,0:T(8,128)(2,1)S(1)} %get-tuple-element.290), channel_id=1, source_target_pairs={{0,0},{1,1},{2,4},{3,5},{4,2},{5,3},{6,6},{7,7},{8,8},{9,9},{10,12... | collective-permute-start | bytes 1179656 | tf_op jit(solution)/shard_map/ppermute | solution.py:1296
  106.6 10.3 %collective-permute-start.26 = (bf16[256,768]{1,0:T(8,128)(2,1)S(1)}, bf16[256,768]{1,0:T(8,128)(2,1)S(1)}, u32[]{:S(2)}, u32[]{:S(2)}) collective-permute-start(bf16[256,768]{1,0:T(8,128)(2,1)S(1)} %collective-permute-done.18.refs_0_), channel_id=1, source_target_pairs={{0,4},{4,0},{8,12},{12,8},{16,20},{20,16},{24,28},{28,24},{1,5},{5... | collective-permute-start | bytes 1179656 | tf_op jit(solution)/shard_map/ppermute | solution.py:1071
  107.1 9.8 %collective-permute-start.27 = (bf16[256,768]{1,0:T(8,128)(2,1)S(1)}, bf16[256,768]{1,0:T(8,128)(2,1)S(1)}, u32[]{:S(2)}, u32[]{:S(2)}) collective-permute-start(bf16[256,768]{1,0:T(8,128)(2,1)S(1)} %collective-permute-done.19.refs_1_), channel_id=1, source_target_pairs={{0,4},{4,0},{8,12},{12,8},{16,20},{20,16},{24,28},{28,24},{1,5},{5... | collective-permute-start | bytes 1179656 | tf_op jit(solution)/shard_map/ppermute | solution.py:1071
  107.1 8.2 %collective-permute-start.28 = (bf16[1,4,24,1536]{3,2,1,0:T(8,128)(2,1)S(1)}, bf16[1,4,24,1536]{3,2,1,0:T(8,128)(2,1)S(1)}, u32[]{:S(2)}, u32[]{:S(2)}) collective-permute-start(bf16[1,4,24,1536]{3,2,1,0:T(8,128)(2,1)S(1)} %get-tuple-element.322), channel_id=1, source_target_pairs={{0,8},{4,12},{8,0},{12,4},{16,24},{20,28},{24,16},{28,20},{1,9},{5... | collective-permute-start | bytes 884744 | tf_op jit(solution)/shard_map/ppermute | solution.py:1071
  108.6 8.2 %collective-permute-start.29 = (bf16[1,4,24,1536]{3,2,1,0:T(8,128)(2,1)S(1)}, bf16[1,4,24,1536]{3,2,1,0:T(8,128)(2,1)S(1)}, u32[]{:S(2)}, u32[]{:S(2)}) collective-permute-start(bf16[1,4,24,1536]{3,2,1,0:T(8,128)(2,1)S(1)} %get-tuple-element.323), channel_id=1, source_target_pairs={{0,16},{4,20},{8,24},{12,28},{16,0},{20,4},{24,8},{28,12},{1,17},{... | collective-permute-start | bytes 884744 | tf_op jit(solution)/shard_map/ppermute | solution.py:1071
  131.4 13.7 %collective-permute-start.30 = (bf16[4,96,768]{2,1,0:T(8,128)(2,1)S(1)}, bf16[4,96,768]{2,1,0:T(8,128)(2,1)S(1)}, u32[]{:S(2)}, u32[]{:S(2)}) collective-permute-start(bf16[4,96,768]{2,1,0:T(8,128)(2,1)S(1)} %get-tuple-element.334), channel_id=1, source_target_pairs={{0,8},{4,12},{8,0},{12,4},{16,24},{20,28},{24,16},{28,20},{1,9},{5... | collective-permute-start | bytes 1769480 | tf_op jit(solution)/shard_map/ppermute | solution.py:1071
  131.7 13.4 %collective-permute-start.31 = (bf16[4,96,768]{2,1,0:T(8,128)(2,1)S(1)}, bf16[4,96,768]{2,1,0:T(8,128)(2,1)S(1)}, u32[]{:S(2)}, u32[]{:S(2)}) collective-permute-start(bf16[4,96,768]{2,1,0:T(8,128)(2,1)S(1)} %get-tuple-element.335), channel_id=1, source_target_pairs={{0,16},{4,20},{8,24},{12,28},{16,0},{20,4},{24,8},{28,12},{1,17},{... | collective-permute-start | bytes 1769480 | tf_op jit(solution)/shard_map/ppermute | solution.py:1071
  145.1 11.2 %collective-permute-start.32 = (bf16[1024,768]{1,0:T(8,128)(2,1)S(1)}, bf16[1024,768]{1,0:T(8,128)(2,1)S(1)}, u32[]{:S(2)}, u32[]{:S(2)}) collective-permute-start(bf16[1024,768]{1,0:T(8,128)(2,1)S(1)} %get-tuple-element.336), channel_id=1, source_target_pairs={{0,4},{4,0},{8,12},{12,8},{16,20},{20,16},{24,28},{28,24},{1,5},{5... | collective-permute-start | bytes 4718600 | tf_op jit(solution)/shard_map/ppermute | solution.py:1071
  147.4 8.8 %collective-permute-start.33 = (bf16[512,768]{1,0:T(8,128)(2,1)S(1)}, bf16[512,768]{1,0:T(8,128)(2,1)S(1)}, u32[]{:S(2)}, u32[]{:S(2)}) collective-permute-start(bf16[512,768]{1,0:T(8,128)(2,1)S(1)} %get-tuple-element.337), channel_id=1, source_target_pairs={{0,4},{4,0},{8,12},{12,8},{16,20},{20,16},{24,28},{28,24},{1,5},{5... | collective-permute-start | bytes 2359304 | tf_op jit(solution)/shard_map/ppermute | solution.py:1071
  148.1 8.1 %collective-permute-start.34 = (bf16[2,96,768]{2,1,0:T(8,128)(2,1)S(1)}, bf16[2,96,768]{2,1,0:T(8,128)(2,1)S(1)}, u32[]{:S(2)}, u32[]{:S(2)}) collective-permute-start(bf16[2,96,768]{2,1,0:T(8,128)(2,1)S(1)} %get-tuple-element.349), channel_id=1, source_target_pairs={{0,16},{4,20},{8,24},{12,28},{16,0},{20,4},{24,8},{28,12},{1,17},{... | collective-permute-start | bytes 884744 | tf_op jit(solution)/shard_map/ppermute | solution.py:1071
  148.4 7.8 %collective-permute-start.35 = (bf16[2,96,768]{2,1,0:T(8,128)(2,1)S(1)}, bf16[2,96,768]{2,1,0:T(8,128)(2,1)S(1)}, u32[]{:S(2)}, u32[]{:S(2)}) collective-permute-start(bf16[2,96,768]{2,1,0:T(8,128)(2,1)S(1)} %get-tuple-element.350), channel_id=1, source_target_pairs={{0,8},{4,12},{8,0},{12,4},{16,24},{20,28},{24,16},{28,20},{1,9},{5... | collective-permute-start | bytes 884744 | tf_op jit(solution)/shard_map/ppermute | solution.py:1071
  156.3 15.7 %collective-permute-start.37 = (bf16[192,1536]{1,0:T(8,128)(2,1)S(1)}, bf16[192,1536]{1,0:T(8,128)(2,1)S(1)}, u32[]{:S(2)}, u32[]{:S(2)}) collective-permute-start(bf16[192,1536]{1,0:T(8,128)(2,1)S(1)} %get-tuple-element.362), channel_id=1, source_target_pairs={{0,8},{4,12},{8,0},{12,4},{16,24},{20,28},{24,16},{28,20},{1,9},{5... | collective-permute-start | bytes 1769480 | tf_op jit(solution)/shard_map/ppermute | solution.py:1071
  157.6 14.4 %collective-permute-start.38 = (bf16[192,1536]{1,0:T(8,128)(2,1)S(1)}, bf16[192,1536]{1,0:T(8,128)(2,1)S(1)}, u32[]{:S(2)}, u32[]{:S(2)}) collective-permute-start(bf16[192,1536]{1,0:T(8,128)(2,1)S(1)} %get-tuple-element.363), channel_id=1, source_target_pairs={{0,16},{4,20},{8,24},{12,28},{16,0},{20,4},{24,8},{28,12},{1,17},{... | collective-permute-start | bytes 1769480 | tf_op jit(solution)/shard_map/ppermute | solution.py:1071
  159.6 12.4 %collective-permute-start.36 = (bf16[2,96,768]{2,1,0:T(8,128)(2,1)S(1)}, bf16[2,96,768]{2,1,0:T(8,128)(2,1)S(1)}, u32[]{:S(2)}, u32[]{:S(2)}) collective-permute-start(bf16[2,96,768]{2,1,0:T(8,128)(2,1)S(1)} %get-tuple-element.361), channel_id=1, source_target_pairs={{0,1},{1,0},{2,3},{3,2},{4,5},{5,4},{6,7},{7,6},{8,9},{9,8},{10,11... | collective-permute-start | bytes 884744 | tf_op jit(solution)/shard_map/ppermute | solution.py:1071
  166.6 18.9 %collective-permute-start.39 = (bf16[256,768]{1,0:T(8,128)(2,1)S(1)}, bf16[256,768]{1,0:T(8,128)(2,1)S(1)}, u32[]{:S(2)}, u32[]{:S(2)}) collective-permute-start(bf16[256,768]{1,0:T(8,128)(2,1)S(1)} %get-tuple-element.373), channel_id=1, source_target_pairs={{0,0},{1,1},{4,2},{5,3},{2,4},{3,5},{6,6},{7,7},{8,8},{9,9},{12,10... | collective-permute-start | bytes 1179656 | tf_op jit(solution)/shard_map/ppermute | solution.py:1084
  171.4 14.2 %collective-permute-start.40 = (bf16[256,768]{1,0:T(8,128)(2,1)S(1)}, bf16[256,768]{1,0:T(8,128)(2,1)S(1)}, u32[]{:S(2)}, u32[]{:S(2)}) collective-permute-start(bf16[256,768]{1,0:T(8,128)(2,1)S(1)} %get-tuple-element.374), channel_id=1, source_target_pairs={{1,0},{0,1},{5,2},{4,3},{3,4},{2,5},{7,6},{6,7},{9,8},{8,9},{13,10... | collective-permute-start | bytes 1179656 | tf_op jit(solution)/shard_map/ppermute | solution.py:1084
  172.7 12.9 %collective-permute-start.41 = (bf16[96,1536]{1,0:T(8,128)(2,1)S(1)}, bf16[96,1536]{1,0:T(8,128)(2,1)S(1)}, u32[]{:S(2)}, u32[]{:S(2)}) collective-permute-start(bf16[96,1536]{1,0:T(8,128)(2,1)S(1)} %get-tuple-element.379), channel_id=1, source_target_pairs={{0,16},{4,20},{8,24},{12,28},{16,0},{20,4},{24,8},{28,12},{1,17},{... | collective-permute-start | bytes 884744 | tf_op jit(solution)/shard_map/ppermute | solution.py:1071
  173.1 12.5 %collective-permute-start.42 = (bf16[96,1536]{1,0:T(8,128)(2,1)S(1)}, bf16[96,1536]{1,0:T(8,128)(2,1)S(1)}, u32[]{:S(2)}, u32[]{:S(2)}) collective-permute-start(bf16[96,1536]{1,0:T(8,128)(2,1)S(1)} %get-tuple-element.380), channel_id=1, source_target_pairs={{0,8},{4,12},{8,0},{12,4},{16,24},{20,28},{24,16},{28,20},{1,9},{5... | collective-permute-start | bytes 884744 | tf_op jit(solution)/shard_map/ppermute | solution.py:1071
  193.8 12.3 %collective-permute-start.45 = (bf16[2,2,24,1536]{3,2,1,0:T(8,128)(2,1)S(1)}, bf16[2,2,24,1536]{3,2,1,0:T(8,128)(2,1)S(1)}, u32[]{:S(2)}, u32[]{:S(2)}) collective-permute-start(bf16[2,2,24,1536]{3,2,1,0:T(8,128)(2,1)S(1)} %get-tuple-element.394), channel_id=1, source_target_pairs={{0,1},{1,0},{2,3},{3,2},{4,5},{5,4},{6,7},{7,6},{8,9},{9,8},{10,11... | collective-permute-start | bytes 884744 | tf_op jit(solution)/shard_map/ppermute | solution.py:1071
  206.1 21.5 %collective-permute-start.52 = (bf16[192,1152]{1,0:T(8,128)(2,1)S(1)}, bf16[192,1152]{1,0:T(8,128)(2,1)S(1)}, u32[]{:S(2)}, u32[]{:S(2)}) collective-permute-start(bf16[192,1152]{1,0:T(8,128)(2,1)S(1)} %get-tuple-element.435), channel_id=1, source_target_pairs={{0,8},{4,12},{8,0},{12,4},{16,24},{20,28},{24,16},{28,20},{1,9},{5... | collective-permute-start | bytes 1327112 | tf_op jit(solution)/shard_map/ppermute | solution.py:1071
  210.2 17.4 %collective-permute-start.53 = (bf16[192,1152]{1,0:T(8,128)(2,1)S(1)}, bf16[192,1152]{1,0:T(8,128)(2,1)S(1)}, u32[]{:S(2)}, u32[]{:S(2)}) collective-permute-start(bf16[192,1152]{1,0:T(8,128)(2,1)S(1)} %get-tuple-element.436), channel_id=1, source_target_pairs={{0,16},{4,20},{8,24},{12,28},{16,0},{20,4},{24,8},{28,12},{1,17},{... | collective-permute-start | bytes 1327112 | tf_op jit(solution)/shard_map/ppermute | solution.py:1071
  213.4 14.2 %collective-permute-start.49 = (bf16[256,768]{1,0:T(8,128)(2,1)S(1)}, bf16[256,768]{1,0:T(8,128)(2,1)S(1)}, u32[]{:S(2)}, u32[]{:S(2)}) collective-permute-start(bf16[256,768]{1,0:T(8,128)(2,1)S(1)} %get-tuple-element.421), channel_id=1, source_target_pairs={{0,0},{1,1},{4,2},{5,3},{2,4},{3,5},{6,6},{7,7},{8,8},{9,9},{12,10... | collective-permute-start | bytes 1179656 | tf_op jit(solution)/shard_map/ppermute | solution.py:1084
  227.6 16.6 %collective-permute-start.57 = (bf16[256,768]{1,0:T(8,128)(2,1)}, bf16[256,768]{1,0:T(8,128)(2,1)}, u32[]{:S(2)}, u32[]{:S(2)}) collective-permute-start(bf16[256,768]{1,0:T(8,128)(2,1)} %get-tuple-element.454), channel_id=1, source_target_pairs={{1,0},{0,1},{5,2},{4,3},{3,4},{2,5},{7,6},{6,7},{9,8},{8,9},{13,10... | collective-permute-start | bytes 1179656 | tf_op jit(solution)/shard_map/ppermute | solution.py:1084
  230.8 13.4 %collective-permute-start.56 = (bf16[2,24,1536]{2,1,0:T(8,128)(2,1)}, bf16[2,24,1536]{2,1,0:T(8,128)(2,1)}, u32[]{:S(2)}, u32[]{:S(2)}) collective-permute-start(bf16[2,24,1536]{2,1,0:T(8,128)(2,1)} %get-tuple-element.452), channel_id=1, source_target_pairs={{0,2},{1,3},{2,0},{3,1},{4,6},{5,7},{6,4},{7,5},{8,10},{9,11},{10,... | collective-permute-start | bytes 442376 | tf_op jit(solution)/shard_map/ppermute | solution.py:1071
  237.9 20.2 %collective-permute-start.59 = (bf16[2,24,1664]{2,1,0:T(8,128)(2,1)}, bf16[2,24,1664]{2,1,0:T(8,128)(2,1)S(1)}, u32[]{:S(2)}, u32[]{:S(2)}) collective-permute-start(bf16[2,24,1664]{2,1,0:T(8,128)(2,1)} %get-tuple-element.465), channel_id=1, source_target_pairs={{0,1},{1,0},{2,3},{3,2},{4,5},{5,4},{6,7},{7,6},{8,9},{9,8},{10,11... | collective-permute-start | bytes 479240 | tf_op jit(solution)/shard_map/ppermute | solution.py:1071
  238.3 19.8 %collective-permute-start.60 = (bf16[2,24,1664]{2,1,0:T(8,128)(2,1)}, bf16[2,24,1664]{2,1,0:T(8,128)(2,1)S(1)}, u32[]{:S(2)}, u32[]{:S(2)}) collective-permute-start(bf16[2,24,1664]{2,1,0:T(8,128)(2,1)} %get-tuple-element.466), channel_id=1, source_target_pairs={{0,2},{1,3},{2,0},{3,1},{4,6},{5,7},{6,4},{7,5},{8,10},{9,11},{10,... | collective-permute-start | bytes 479240 | tf_op jit(solution)/shard_map/ppermute | solution.py:1071
  238.3 19.8 %collective-permute-start.61 = (bf16[2,24,1664]{2,1,0:T(8,128)(2,1)}, bf16[2,24,1664]{2,1,0:T(8,128)(2,1)S(1)}, u32[]{:S(2)}, u32[]{:S(2)}) collective-permute-start(bf16[2,24,1664]{2,1,0:T(8,128)(2,1)} %get-tuple-element.467), channel_id=1, source_target_pairs={{0,3},{1,2},{2,1},{3,0},{4,7},{5,6},{6,5},{7,4},{8,11},{9,10},{10,... | collective-permute-start | bytes 479240 | tf_op jit(solution)/shard_map/ppermute | solution.py:1071
  245.2 11.6 %collective-permute-start.58 = (bf16[24,1536]{1,0:T(8,128)(2,1)S(1)}, bf16[24,1536]{1,0:T(8,128)(2,1)S(1)}, u32[]{:S(2)}, u32[]{:S(2)}) collective-permute-start(bf16[24,1536]{1,0:T(8,128)(2,1)S(1)} %fusion.1), channel_id=1, source_target_pairs={{0,4},{4,0},{8,12},{12,8},{16,20},{20,16},{24,28},{28,24},{1,5},{5... | collective-permute-start | bytes 221192 | tf_op jit(solution)/shard_map/ppermute | solution.py:1071
  (31 other events, 196.1 us)
